TPU v7x, 32 devices: a whole 2x2x4 slice. The times are simulated.
32 devices in a mesh: rep: 8 (over y, x, core), exp: 4 (over z).
Axes of the slice: x: 2, y: 2, z: 4, core: 2. Of those that a mesh axis runs over, the one named last changes fastest.
Arguments:
- replay_buffer_rows: bfloat16 [4096, 3584], P(('rep', 'exp')), may hold values from -6 to 6
- shard_request_index: int32 [32, 8, 32], P(('rep', 'exp')), may hold values from 0 to 127
- replica_fetch_count: int32 [32, 8], P(('rep', 'exp')), may hold values from 0 to 32, as said below
- routes: int32 [4096, 1], P(('rep', 'exp')), may hold values from 0 to 3; in each aligned block of 128 rows (0 to 127, 128 to 255, ...) at most 56 rows name the same one
- router_route_weight: float32 [4096, 1], P(('rep', 'exp')), may hold values from 0.25 to 1
- output_gradient: bfloat16 [4096, 1024], P(('rep', 'exp')), may hold values from -0.119628906 to 0.119628906
- frozen_gate_weight: bfloat16 [4, 3584, 1024], P('exp'), may hold values from -0.09375 to 0.09375
- adapter_down_weight: bfloat16 [4, 3584, 128], P('exp'), may hold values from -0.09375 to 0.09375
- adapter_up_weight: bfloat16 [4, 128, 1024], P('exp'), may hold values from -0.5 to 0.5
Outputs:
- out_rows: bfloat16 [4096, 1024], P(('rep', 'exp'))
- down_adapter_gradient: float32 [4, 3584, 128], P('exp', 'rep')
- up_adapter_gradient: float32 [4, 128, 1024], P('exp', 'rep')
Inputs may be any that keep to these rules, and one draw needn't show every extreme that they name: Each row replica_fetch_count[d, :] sums to 128, and every row has an entry equal to 32. `shard_request_index`: entry [s * 4 + c, r, j] is read only where j < replica_fetch_count[r * 4 + c, s]. `routes`: among the 128 rows of one device no expert is named more than 56 times, and that bound is reached.
All inputs are finite; a program needn't handle non-finite values.
Results may differ from a plain program's by a relative error of at most 0.0061.
Values may be sent and summed in bfloat16 or wider, within the bound.
No kernel may reach another device: no remote copies, remote signals or barrier semaphores. Data moves between devices by JAX's collectives and lax.ppermute only.
A program may use at most 64 MiB of HBM per device.

v0:
```python
import jax
import jax.numpy as jnp
from jax import lax
from jax.sharding import PartitionSpec as P


def silu_slope(pre_act):
    gate_value = jax.nn.sigmoid(pre_act)
    return gate_value * (1.0 + pre_act * (1.0 - gate_value))


def body(
    replay_buffer_rows,
    shard_request_index,
    replica_fetch_count,
    routes,
    router_route_weight,
    output_gradient,
    frozen_gate_weight,
    adapter_down_weight,
    adapter_up_weight,
):
    rep_count = lax.axis_size("rep")
    exp_count = lax.axis_size("exp")
    token_count = routes.shape[0]
    route_count = routes.shape[1]
    fetch_slots = shard_request_index.shape[2]
    model_width = replay_buffer_rows.shape[1]
    hidden_units = frozen_gate_weight.shape[2]
    capacity = 7 * token_count * route_count // (4 * exp_count)
    tile_rows = exp_count * capacity
    served = jnp.take(replay_buffer_rows, shard_request_index[0], axis=0)
    arrived = lax.all_to_all(served, "rep", split_axis=0, concat_axis=0, tiled=True)
    flat_rows = arrived.reshape(rep_count * fetch_slots, model_width)
    counts = replica_fetch_count[0]
    row_ends = jnp.cumsum(counts)
    row_starts = row_ends - counts
    positions = jnp.arange(token_count, dtype=jnp.int32)
    source = jnp.sum((row_ends[None, :] <= positions[:, None]).astype(jnp.int32), axis=1)
    offset = positions - jnp.take(row_starts, source)
    tokens = jnp.take(flat_rows, source * fetch_slots + offset, axis=0)
    expert_ids = lax.broadcasted_iota(jnp.int32, (token_count * route_count, exp_count), 1)
    chosen = (routes == expert_ids).astype(jnp.int32)
    slot_rank = jnp.sum((jnp.cumsum(chosen, axis=0) - 1) * chosen, axis=1)
    target = (routes[:, 0] * capacity + slot_rank).reshape(token_count, route_count)
    row_ids = lax.broadcasted_iota(jnp.int32, (tile_rows, token_count), 0)
    pickers = [(row_ids == target[:, 0][None, :]).astype(jnp.bfloat16)]
    which_route = 0
    row_sum = jnp.dot(pickers[which_route], tokens, preferred_element_type=jnp.float32)
    sent_rows = row_sum.astype(jnp.bfloat16).reshape(exp_count, capacity, model_width)
    tile_in = lax.all_to_all(sent_rows, "exp", split_axis=0, concat_axis=0, tiled=True)
    input_tile = tile_in.reshape(tile_rows, model_width)
    adapted_hidden = jnp.dot(
        input_tile, adapter_down_weight[0], preferred_element_type=jnp.float32
    ).astype(jnp.bfloat16)
    pre_act = jnp.dot(
        input_tile, frozen_gate_weight[0], preferred_element_type=jnp.float32
    ) + jnp.dot(adapted_hidden, adapter_up_weight[0], preferred_element_type=jnp.float32)
    activated = jax.nn.silu(pre_act).astype(jnp.bfloat16)
    results = lax.all_to_all(
        activated.reshape(exp_count, capacity, hidden_units),
        "exp",
        split_axis=0,
        concat_axis=0,
        tiled=True,
    )
    result_rows = results.reshape(tile_rows, hidden_units)
    which_route = 0
    picked = jnp.take(result_rows, target[:, which_route], axis=0).astype(jnp.float32)
    combined = router_route_weight * picked
    out_rows = combined.astype(jnp.bfloat16)
    which_route = 0
    scaled = (router_route_weight * output_gradient.astype(jnp.float32)).astype(jnp.bfloat16)
    grad_sum = jnp.dot(pickers[which_route], scaled, preferred_element_type=jnp.float32)
    grad_in = lax.all_to_all(
        grad_sum.astype(jnp.bfloat16).reshape(exp_count, capacity, hidden_units),
        "exp",
        split_axis=0,
        concat_axis=0,
        tiled=True,
    )
    grad_tile = grad_in.reshape(tile_rows, hidden_units)
    preact_gradient = (grad_tile.astype(jnp.float32) * silu_slope(pre_act)).astype(jnp.bfloat16)
    up_term = lax.dot_general(
        adapted_hidden,
        preact_gradient,
        (((0,), (0,)), ((), ())),
        preferred_element_type=jnp.float32,
    )
    back_reduced = lax.dot_general(
        preact_gradient,
        adapter_up_weight[0],
        (((1,), (1,)), ((), ())),
        preferred_element_type=jnp.float32,
    ).astype(jnp.bfloat16)
    down_term = lax.dot_general(
        input_tile, back_reduced, (((0,), (0,)), ((), ())), preferred_element_type=jnp.float32
    )
    down_grad, up_grad = (
        lax.psum_scatter(down_term, "rep", scatter_dimension=0, tiled=True),
        lax.psum_scatter(up_term, "rep", scatter_dimension=0, tiled=True),
    )
    return (out_rows, down_grad[None], up_grad[None])


def solution(mesh):
    placed = (
        P(("rep", "exp"), None),
        P(("rep", "exp"), None, None),
        P(("rep", "exp"), None),
        P(("rep", "exp"), None),
        P(("rep", "exp"), None),
        P(("rep", "exp"), None),
        P("exp", None, None),
        P("exp", None, None),
        P("exp", None, None),
    )
    return jax.shard_map(
        body,
        mesh=mesh,
        in_specs=placed,
        out_specs=(P(("rep", "exp"), None), P("exp", "rep", None), P("exp", "rep", None)),
        check_vma=False,
    )
```

profile of v0, /device:TPU:0, one launch (start us, length us, event | category | flops | bytes accessed | tf_op | source)
XLA Modules:
  0.0 192.0 jit_solution(13429322130435242267)
XLA Ops:
  7.2 0.0 copy-start
  7.2 0.8 compare_and_fusion
  8.0 0.7 compare_select_fusion
  8.6 0.1 reshape.192
  8.7 0.0 copy-done
  8.7 1.7 gather_fusion
  10.5 1.5 broadcast_select_fusion
  11.9 0.0 copy-start.5
  11.9 0.0 copy-start.3
  11.9 5.3 %all-to-all-start = ((bf16[8,32,3584]{2,1,0:T(8,128)(2,1)}), bf16[8,32,3584]{2,1,0:T(8,128)(2,1)S(1)}, u32[]{:S(2)}, u32[]{:S(2)}) async-start(bf16[8,32,3584]{2,1,0:T(8,128)(2,1)} %broadcast_select_fusion), calls=%async_computation | async-start | bytes 3670016 | tf_op jit(solution)/shard_map/all_to_all | solution.py:33
  17.2 0.0 copy-done.5
  17.2 0.2 reduce-window.8
  17.4 0.0 copy-done.3
  17.4 0.1 fusion.12
  17.5 0.2 reduce_window_sum.18
  17.7 0.7 fusion.21
  18.4 0.1 convert_reduce_fusion
  18.5 5.1 %compare_and_fusion.1 = (pred[128]{0:T(512)(128)(4,1)S(1)}, s32[128]{0:T(128)S(1)}) fusion(s32[128]{0:T(128)S(1)} %convert_reduce_fusion, s32[]{:T(128)} %bitcast.16, s32[]{:T(128)} %bitcast.15, s32[]{:T(128)} %bitcast.14, s32[]{:T(128)} %bitcast.13, s32[]{:T(128)} %bitcast.12, s32[]{:T(128)} %bitcast.11, s32[]{:T(128)} %bitcast.10, s32[]{:T(128)} %bitcast.9), kind=kLoop, calls=%fused_computation.52 | loop fusion | flops 4224 | bytes 1184 | tf_op jit(solution)/shard_map/jit(_take)/and | solution.py:41
  23.6 0.2 select_reduce_fusion
  23.8 17.3 %all-to-all-done = bf16[8,32,3584]{2,1,0:T(8,128)(2,1)S(1)} async-done(((bf16[8,32,3584]{2,1,0:T(8,128)(2,1)}), bf16[8,32,3584]{2,1,0:T(8,128)(2,1)S(1)}, u32[]{:S(2)}, u32[]{:S(2)}) %all-to-all-start) | async-done | bytes 1835040 | tf_op jit(solution)/shard_map/all_to_all | solution.py:33
  41.1 2.1 %gather_fusion.1 = bf16[128,3584]{1,0:T(8,128)(2,1)} fusion(bf16[256,3584]{1,0:T(8,128)(2,1)S(1)} %bitcast.91, s32[1024]{0:T(1024)S(1)} %pad_clamp_fusion.1), kind=kCustom, calls=%fused_computation.1 | custom fusion | bytes 1835520 | tf_op jit(solution)/shard_map/jit(_take)/gather | solution.py:41
  43.1 3.0 %convolution_convert_fusion = bf16[224,3584]{1,0:T(8,128)(2,1)} fusion(bf16[128,3584]{1,0:T(8,128)(2,1)} %gather_fusion.1, pred[128]{0:T(512)(128)(4,1)S(1)} %get-tuple-element.5, s32[128]{0:T(128)S(1)} %multiply_add_fusion), kind=kOutput, calls=%fused_computation.5 | convolution fusion | flops 206811136 | bytes 2523776 | tf_op jit(solution)/shard_map/dot_general | solution.py:49
  46.1 0.0 copy-start.4
  46.1 0.0 copy-start.1
  46.1 5.0 %all-to-all-start.1 = ((bf16[4,56,3584]{2,1,0:T(8,128)(2,1)}), bf16[4,56,3584]{2,1,0:T(8,128)(2,1)S(1)}, u32[]{:S(2)}, u32[]{:S(2)}) async-start(bf16[4,56,3584]{2,1,0:T(8,128)(2,1)} %bitcast.97), calls=%async_computation.1 | async-start | bytes 3211264 | tf_op jit(solution)/shard_map/all_to_all | solution.py:51
  51.1 0.0 copy-done.4
  51.1 2.1 %convolution_convert_fusion.1 = bf16[224,1024]{1,0:T(8,128)(2,1)} fusion(bf16[128,1024]{1,0:T(8,128)(2,1)} %param.14, f32[128]{0:T(128)S(1)} %bitcast.101, s32[128]{0:T(128)S(1)} %multiply_add_fusion), kind=kOutput, calls=%fused_computation.8 | convolution fusion | flops 59371520 | bytes 721920 | tf_op jit(solution)/shard_map/dot_general | solution.py:74
  53.2 32.8 %all-to-all-done.1 = bf16[4,56,3584]{2,1,0:T(8,128)(2,1)S(1)} async-done(((bf16[4,56,3584]{2,1,0:T(8,128)(2,1)}), bf16[4,56,3584]{2,1,0:T(8,128)(2,1)S(1)}, u32[]{:S(2)}, u32[]{:S(2)}) %all-to-all-start.1) | async-done | bytes 1605664 | tf_op jit(solution)/shard_map/all_to_all | solution.py:51
  86.0 4.1 %all-to-all-start.3 = ((bf16[4,56,1024]{2,1,0:T(8,128)(2,1)}), bf16[4,56,1024]{2,1,0:T(8,128)(2,1)}, u32[]{:S(2)}, u32[]{:S(2)}) async-start(bf16[4,56,1024]{2,1,0:T(8,128)(2,1)} %bitcast.32), calls=%async_computation.3 | async-start | bytes 917504 | tf_op jit(solution)/shard_map/all_to_all | solution.py:75
  90.1 0.0 reduce-scatter.5.cloned.1.call-start
  90.2 0.0 copy-done.1
  90.2 0.6 convolution_convert_fusion.3
  90.8 0.0 copy-start.2
  90.8 5.9 %fusion = f32[224,1024]{1,0:T(8,128)} fusion(bf16[224,3584]{1,0:T(8,128)(2,1)S(1)} %bitcast.93, bf16[1,3584,1024]{2,1,0:T(8,128)(2,1)} %param.15), kind=kOutput, calls=%fused_computation.3 | convolution fusion | flops 1644167168 | bytes 9863168 | tf_op jit(solution)/shard_map/dot_general | solution.py:56
  96.7 6.1 %all-to-all-done.3 = bf16[4,56,1024]{2,1,0:T(8,128)(2,1)} async-done(((bf16[4,56,1024]{2,1,0:T(8,128)(2,1)}), bf16[4,56,1024]{2,1,0:T(8,128)(2,1)}, u32[]{:S(2)}, u32[]{:S(2)}) %all-to-all-start.3) | async-done | bytes 458784 | tf_op jit(solution)/shard_map/all_to_all | solution.py:75
  102.8 0.0 copy-done.2
  102.8 2.7 %fusion.3 = (bf16[224,1024]{1,0:T(8,128)(2,1)S(1)}, bf16[224,1024]{1,0:T(8,128)(2,1)}) fusion(bf16[4,56,1024]{2,1,0:T(8,128)(2,1)} %all-to-all-done.3, f32[224,1024]{1,0:T(8,128)} %fusion, bf16[224,128]{1,0:T(8,128)(2,1)S(1)} %convolution_convert_fusion.3, bf16[1,128,1024]{2,1,0:T(8,128)(2,1)S(1)} %copy-done.2), kind=kOutput, calls=%fused_computation.13 | convolution fusion | flops 61702144 | bytes 2613248 | tf_op jit(solution)/shard_map/dot_general | solution.py:58
  105.5 1.1 fusion.22
  106.5 0.0 reduce-scatter.5.cloned.1.call-update
  106.6 0.0 reduce-scatter.3.cloned.1.call-start
  106.6 2.4 %fusion.2 = f32[3584,128]{1,0:T(8,128)} fusion(bf16[224,3584]{1,0:T(8,128)(2,1)S(1)} %bitcast.94, bf16[224,1024]{1,0:T(8,128)(2,1)S(1)} %get-tuple-element.7, bf16[1,128,1024]{2,1,0:T(8,128)(2,1)S(1)} %copy-done.2), kind=kOutput, calls=%fused_computation.11 | convolution fusion | flops 264269824 | bytes 4161536 | tf_op jit(solution)/shard_map/dot_general | solution.py:96
  109.0 0.0 reduce-scatter.3.cloned.1.call-update
  109.0 3.5 %all-to-all-start.2 = ((bf16[4,56,1024]{2,1,0:T(8,128)(2,1)}), bf16[4,56,1024]{2,1,0:T(8,128)(2,1)S(1)}, u32[]{:S(2)}, u32[]{:S(2)}) async-start(bf16[4,56,1024]{2,1,0:T(8,128)(2,1)} %bitcast.29), calls=%async_computation.2 | async-start | bytes 917504 | tf_op jit(solution)/shard_map/all_to_all | solution.py:60
  112.5 12.6 %all-to-all-done.2 = bf16[4,56,1024]{2,1,0:T(8,128)(2,1)S(1)} async-done(((bf16[4,56,1024]{2,1,0:T(8,128)(2,1)}), bf16[4,56,1024]{2,1,0:T(8,128)(2,1)S(1)}, u32[]{:S(2)}, u32[]{:S(2)}) %all-to-all-start.2) | async-done | bytes 458784 | tf_op jit(solution)/shard_map/all_to_all | solution.py:60
  125.1 0.9 gather_fusion.2
  126.0 0.9 multiply_convert_fusion.2
  126.8 14.3 %reduce-scatter.5.cloned.1.call-done = f32[16,1024]{1,0:T(8,128)} async-done(((f32[128,1024]{1,0:T(8,128)}), f32[16,1024]{1,0:T(8,128)}) %reduce-scatter.5.cloned.1.call-update) | async-done | bytes 65552 | tf_op jit(solution)/shard_map/reduce_scatter | solution.py:101
  141.1 44.1 %reduce-scatter.3.cloned.1.call-done = f32[448,128]{1,0:T(8,128)} async-done(((f32[3584,128]{1,0:T(8,128)}), f32[448,128]{1,0:T(8,128)}) %reduce-scatter.3.cloned.1.call-update) | async-done | bytes 229392 | tf_op jit(solution)/shard_map/reduce_scatter | solution.py:100
  (7 shorter events, 0.0 us)
Async XLA Ops:
  7.2 1.6 copy-start
  11.9 5.3 %copy-start.5 = (s32[1,8]{1,0:T(1,128)S(1)}, s32[1,8]{1,0:T(1,128)}, u32[]{:S(2)}) copy-start(s32[1,8]{1,0:T(1,128)} %param.11) | copy-start | bytes 100
  11.9 5.5 %copy-start.3 = (s32[128,1]{0,1:T(1,128)S(1)}, s32[128,1]{0,1:T(1,128)}, u32[]{:S(2)}) copy-start(s32[128,1]{0,1:T(1,128)} %param.12) | copy-start | bytes 1540
  11.9 29.1 %all-to-all-start = ((bf16[8,32,3584]{2,1,0:T(8,128)(2,1)}), bf16[8,32,3584]{2,1,0:T(8,128)(2,1)S(1)}, u32[]{:S(2)}, u32[]{:S(2)}) async-start(bf16[8,32,3584]{2,1,0:T(8,128)(2,1)} %broadcast_select_fusion), calls=%async_computation | async-start | bytes 3670016 | tf_op jit(solution)/shard_map/all_to_all | solution.py:33
  46.1 5.0 %copy-start.4 = (f32[128,1]{0,1:T(1,128)S(1)}, f32[128,1]{0,1:T(1,128)}, u32[]{:S(2)}) copy-start(f32[128,1]{0,1:T(1,128)} %param.13) | copy-start | bytes 1540
  46.1 44.1 %copy-start.1 = (bf16[1,3584,128]{2,1,0:T(8,128)(2,1)S(1)}, bf16[1,3584,128]{2,1,0:T(8,128)(2,1)}, u32[]{:S(2)}) copy-start(bf16[1,3584,128]{2,1,0:T(8,128)(2,1)} %param.16) | copy-start | bytes 2752516
  46.1 39.9 %all-to-all-start.1 = ((bf16[4,56,3584]{2,1,0:T(8,128)(2,1)}), bf16[4,56,3584]{2,1,0:T(8,128)(2,1)S(1)}, u32[]{:S(2)}, u32[]{:S(2)}) async-start(bf16[4,56,3584]{2,1,0:T(8,128)(2,1)} %bitcast.97), calls=%async_computation.1 | async-start | bytes 3211264 | tf_op jit(solution)/shard_map/all_to_all | solution.py:51
  86.0 16.8 %all-to-all-start.3 = ((bf16[4,56,1024]{2,1,0:T(8,128)(2,1)}), bf16[4,56,1024]{2,1,0:T(8,128)(2,1)}, u32[]{:S(2)}, u32[]{:S(2)}) async-start(bf16[4,56,1024]{2,1,0:T(8,128)(2,1)} %bitcast.32), calls=%async_computation.3 | async-start | bytes 917504 | tf_op jit(solution)/shard_map/all_to_all | solution.py:75
  90.1 50.9 %reduce-scatter.5.cloned.1.call-start = ((), (), s32[]{:S(2)}) async-start(), calls=%async_computation.7 | async-start | bytes 589824 | tf_op jit(solution)/shard_map/reduce_scatter | solution.py:101
  90.8 12.0 %copy-start.2 = (bf16[1,128,1024]{2,1,0:T(8,128)(2,1)S(1)}, bf16[1,128,1024]{2,1,0:T(8,128)(2,1)}, u32[]{:S(2)}) copy-start(bf16[1,128,1024]{2,1,0:T(8,128)(2,1)} %param.17) | copy-start | bytes 786436
  106.6 78.6 %reduce-scatter.3.cloned.1.call-start = ((), (), s32[]{:S(2)}) async-start(), calls=%async_computation.6 | async-start | bytes 2064384 | tf_op jit(solution)/shard_map/reduce_scatter | solution.py:100
  109.0 16.1 %all-to-all-start.2 = ((bf16[4,56,1024]{2,1,0:T(8,128)(2,1)}), bf16[4,56,1024]{2,1,0:T(8,128)(2,1)S(1)}, u32[]{:S(2)}, u32[]{:S(2)}) async-start(bf16[4,56,1024]{2,1,0:T(8,128)(2,1)} %bitcast.29), calls=%async_computation.2 | async-start | bytes 917504 | tf_op jit(solution)/shard_map/all_to_all | solution.py:60
Sparse Core Ops, SparseCore 0:
  106.7 34.3 reduce-scatter.4
  145.4 39.6 reduce-scatter.2
where the time goes:
time: 193 us; the launch traced here: 192 us
  waiting for transfers between devices  127 us (66%)
  starting transfers between devices  18 us (9%)
  matrix products  17.7 us (9%)
  between operations  14.2 us (7%)
  other arithmetic  9.63 us (5%)
  local copies, waits for them, and re-layouts  5.42 us (3%)
    reduce_scatter x1, waiting for transfers between devices, body(): lax.psum_scatter(down_term, 'rep', scatter_dimension=0, tiled=True)  44.1 us
    all_to_all x1, waiting for transfers between devices, body(): lax.all_to_all(sent_rows, 'exp', split_axis=0, concat_axis=0, tiled=True)  32.8 us
    all_to_all x1, waiting for transfers between devices, body(): lax.all_to_all(served, 'rep', split_axis=0, concat_axis=0, tiled=True)  17.3 us
    reduce_scatter x1, waiting for transfers between devices, body(): lax.psum_scatter(up_term, 'rep', scatter_dimension=0, tiled=True)  14.3 us
    all_to_all x1, waiting for transfers between devices, body(): lax.all_to_all(activated.reshape(exp_count, capacity, hidden_units), 'exp...  12.6 us
    all_to_all x1, waiting for transfers between devices, body(): lax.all_to_all(grad_sum.astype(jnp.bfloat16).reshape(exp_count, capacity,...  6.09 us
    dot_general x1, matrix products, body(): jnp.dot(input_tile, frozen_gate_weight[0], preferred_element_type=jnp.flo...  5.9 us
    all_to_all x1, starting transfers between devices, body(): lax.all_to_all(served, 'rep', split_axis=0, concat_axis=0, tiled=True)  5.3 us
  transfers between devices with their start and end apart: 6, of which 6 were waited for; matrix products, arithmetic and copies ran while one was open for 10% of the time, Pallas kernels for 0%

commit v1 on v0

v1 whole, which is shorter than its diff:
```python
import jax
import jax.numpy as jnp
from jax import lax
from jax.sharding import PartitionSpec as P

CHUNKS = 2


def silu_slope(pre_act):
    gate_value = jax.nn.sigmoid(pre_act)
    return gate_value * (1.0 + pre_act * (1.0 - gate_value))


def swap(block, step, exp_count):
    if step == 0:
        return block
    return lax.ppermute(block, "exp", [(i, i ^ step) for i in range(exp_count)])


def body(
    replay_buffer_rows,
    shard_request_index,
    replica_fetch_count,
    routes,
    router_route_weight,
    output_gradient,
    frozen_gate_weight,
    adapter_down_weight,
    adapter_up_weight,
):
    rep_count = lax.axis_size("rep")
    exp_count = lax.axis_size("exp")
    column = lax.axis_index("exp")
    token_count = routes.shape[0]
    shard_rows, model_width = replay_buffer_rows.shape
    fetch_slots = shard_request_index.shape[2]
    hidden_units = frozen_gate_weight.shape[2]
    rank_width = adapter_down_weight.shape[2]
    capacity = 7 * token_count // (4 * exp_count)
    tile_rows = exp_count * capacity
    fetched_rows = rep_count * fetch_slots
    bf16 = jnp.bfloat16
    f32 = jnp.float32

    asked = shard_request_index.reshape(fetched_rows, 1)
    serve = (asked == lax.broadcasted_iota(jnp.int32, (fetched_rows, shard_rows), 1)).astype(bf16)
    chunk_width = model_width // CHUNKS
    arrived = []
    for chunk in range(CHUNKS):
        part = replay_buffer_rows[:, chunk * chunk_width : (chunk + 1) * chunk_width]
        served = jnp.dot(serve, part, preferred_element_type=f32).astype(bf16)
        arrived.append(
            lax.all_to_all(
                served.reshape(rep_count, fetch_slots, chunk_width),
                "rep",
                split_axis=0,
                concat_axis=0,
                tiled=True,
            ).reshape(fetched_rows, chunk_width)
        )

    counts = replica_fetch_count.reshape(1, rep_count)
    row_ends = jnp.cumsum(counts, axis=1)
    row_starts = row_ends - counts
    positions = lax.broadcasted_iota(jnp.int32, (token_count, rep_count), 0)
    passed = row_ends <= positions
    source = jnp.sum(passed.astype(jnp.int32), axis=1, keepdims=True)
    here = lax.broadcasted_iota(jnp.int32, (token_count, rep_count), 1) == source
    start = jnp.sum(jnp.where(here, row_starts, 0), axis=1, keepdims=True)
    place = source * fetch_slots + positions[:, :1] - start
    block = jnp.bitwise_xor(routes, column)
    chosen = (block == lax.broadcasted_iota(jnp.int32, (token_count, exp_count), 1)).astype(jnp.int32)
    rank = jnp.sum((jnp.cumsum(chosen, axis=0) - 1) * chosen, axis=1, keepdims=True)
    target = block * capacity + rank
    slot_of = target == lax.broadcasted_iota(jnp.int32, (token_count, tile_rows), 1)
    home = slot_of.astype(bf16)
    place_of = (place == lax.broadcasted_iota(jnp.int32, (token_count, fetched_rows), 1)).astype(bf16)
    pick_rows = lax.dot_general(
        home, place_of, (((0,), (0,)), ((), ())), preferred_element_type=f32
    ).astype(bf16)

    scaled = (router_route_weight * output_gradient.astype(f32)).astype(bf16)
    grad_blocks = []
    for step in range(exp_count):
        lanes = slice(step * capacity, (step + 1) * capacity)
        sent = lax.dot_general(
            home[:, lanes], scaled, (((0,), (0,)), ((), ())), preferred_element_type=f32
        ).astype(bf16)
        grad_blocks.append(swap(sent, step, exp_count))
    grad_tile = jnp.concatenate(grad_blocks, axis=0)

    pre_act = jnp.zeros((tile_rows, hidden_units), f32)
    adapted = jnp.zeros((tile_rows, rank_width), f32)
    tiles = []
    for chunk in range(CHUNKS):
        blocks = []
        for step in range(exp_count):
            lanes = slice(step * capacity, (step + 1) * capacity)
            sent = jnp.dot(pick_rows[lanes], arrived[chunk], preferred_element_type=f32).astype(bf16)
            blocks.append(swap(sent, step, exp_count))
        tile = jnp.concatenate(blocks, axis=0)
        tiles.append(tile)
        part = slice(chunk * chunk_width, (chunk + 1) * chunk_width)
        adapted = adapted + jnp.dot(tile, adapter_down_weight[0, part], preferred_element_type=f32)
        pre_act = pre_act + jnp.dot(tile, frozen_gate_weight[0, part], preferred_element_type=f32)
    adapted = adapted.astype(bf16)
    pre_act = pre_act + jnp.dot(adapted, adapter_up_weight[0], preferred_element_type=f32)
    activated = jax.nn.silu(pre_act).astype(bf16)

    results = [
        swap(activated[step * capacity : (step + 1) * capacity], step, exp_count)
        for step in range(exp_count)
    ]
    picked = jnp.dot(home, jnp.concatenate(results, axis=0), preferred_element_type=f32)
    out_rows = (router_route_weight * picked).astype(bf16)

    preact_gradient = (grad_tile.astype(f32) * silu_slope(pre_act)).astype(bf16)
    up_term = lax.dot_general(
        adapted, preact_gradient, (((0,), (0,)), ((), ())), preferred_element_type=f32
    )
    back_reduced = lax.dot_general(
        preact_gradient, adapter_up_weight[0], (((1,), (1,)), ((), ())), preferred_element_type=f32
    ).astype(bf16)
    down_terms = [
        lax.dot_general(tile, back_reduced, (((0,), (0,)), ((), ())), preferred_element_type=f32)
        for tile in tiles
    ]
    down_term = jnp.concatenate(down_terms, axis=0).astype(bf16)
    down_sent = down_term.reshape(rep_count, model_width // rep_count, rank_width)
    up_rows = rank_width // rep_count
    up_lanes = hidden_units // rank_width
    up_sent = (
        up_term.astype(bf16)
        .reshape(rep_count, up_rows, up_lanes, rank_width)
        .transpose(0, 2, 1, 3)
        .reshape(rep_count, up_rows * up_lanes, rank_width)
    )
    terms = lax.all_to_all(
        jnp.concatenate([down_sent, up_sent], axis=1), "rep", split_axis=0, concat_axis=0, tiled=True
    )
    total = jnp.sum(terms.astype(f32), axis=0)
    down_grad = total[: model_width // rep_count]
    up_grad = (
        total[model_width // rep_count :]
        .reshape(up_lanes, up_rows, rank_width)
        .transpose(1, 0, 2)
        .reshape(up_rows, hidden_units)
    )
    return (out_rows, down_grad[None], up_grad[None])


def solution(mesh):
    placed = (
        P(("rep", "exp"), None),
        P(("rep", "exp"), None, None),
        P(("rep", "exp"), None),
        P(("rep", "exp"), None),
        P(("rep", "exp"), None),
        P(("rep", "exp"), None),
        P("exp", None, None),
        P("exp", None, None),
        P("exp", None, None),
    )
    return jax.shard_map(
        body,
        mesh=mesh,
        in_specs=placed,
        out_specs=(P(("rep", "exp"), None), P("exp", "rep", None), P("exp", "rep", None)),
        check_vma=False,
    )
```

time: 193 us -> 118 us (0.61)
  waiting for transfers between devices: 127 us -> 50.4 us
  starting transfers between devices: 18 us -> 39 us
  between operations: 14.2 us -> 0.98 us
  other arithmetic: 9.63 us -> 4.87 us
  local copies, waits for them, and re-layouts: 5.42 us -> 2.83 us
    reduce_scatter x2 -> x0, waiting for transfers between devices: 58.3 us -> none  [the longest x1 44.1 us: body(): lax.psum_scatter(down_term, 'rep', scatter_dimension=0, tiled=True)]
    all_to_all x4 -> x3, waiting for transfers between devices: 68.8 us -> 25.1 us  [the longest x2 23.8 us: body(): lax.all_to_all(served.reshape(rep_count, fetch_slots, chunk_width), 'rep'...]
    ppermute x0 -> x12, starting transfers between devices: none -> 27.3 us  [swap(): return lax.ppermute(block, 'exp', [(i, i ^ step) for i in range(exp_count)])]
    ppermute x0 -> x12, waiting for transfers between devices: none -> 25.3 us  [swap(): return lax.ppermute(block, 'exp', [(i, i ^ step) for i in range(exp_count)])]
    all_to_all x4 -> x3, starting transfers between devices: 17.9 us -> 11.7 us  [the longest x2 7.41 us: body(): lax.all_to_all(served.reshape(rep_count, fetch_slots, chunk_width), 'rep'...]
    and x2 -> x0, other arithmetic: 5.87 us -> none  [the longest x1 5.09 us: body(): tokens = jnp.take(flat_rows, source * fetch_slots + offset, axis=0)]
    gather x4 -> x0, local copies, waits for them, and re-layouts: 5.31 us -> none  [the longest x1 2.06 us: body(): tokens = jnp.take(flat_rows, source * fetch_slots + offset, axis=0)]
    select_n x3 -> x0, other arithmetic: 2.17 us -> none  [the longest x2 2.16 us: body(): served = jnp.take(replay_buffer_rows, shard_request_index[0], axis=0)]
  transfers between devices with their start and end apart: 6 -> 15, of which waited for: 6 -> 8; matrix products, arithmetic and copies ran while one was open for 10% -> 13% of each run, Pallas kernels for 0% -> 0%
where the time goes in v1:
time: 118 us; the launch traced here: 117 us
  waiting for transfers between devices  50.4 us (43%)
  starting transfers between devices  39 us (33%)
  matrix products  19 us (16%)
  other arithmetic  4.87 us (4%)
  local copies, waits for them, and re-layouts  2.83 us (2%)
    ppermute x12, starting transfers between devices, swap(): return lax.ppermute(block, 'exp', [(i, i ^ step) for i in range(exp_count)])  27.3 us
    ppermute x12, waiting for transfers between devices, swap(): return lax.ppermute(block, 'exp', [(i, i ^ step) for i in range(exp_count)])  25.3 us
    all_to_all x2, waiting for transfers between devices, body(): lax.all_to_all(served.reshape(rep_count, fetch_slots, chunk_width), 'rep'...  23.8 us
    all_to_all x2, starting transfers between devices, body(): lax.all_to_all(served.reshape(rep_count, fetch_slots, chunk_width), 'rep'...  7.41 us
    dot_general x2, matrix products, body(): jnp.dot(tile, frozen_gate_weight[0, part], preferred_element_type=f32)  5.37 us
    all_to_all x1, starting transfers between devices, body(): lax.all_to_all(jnp.concatenate([down_sent, up_sent], axis=1), 'rep', spli...  4.3 us
    dot_general x2, matrix products, body(): served = jnp.dot(serve, part, preferred_element_type=f32).astype(bf16)  3.87 us
    dot_general x4, matrix products, body(): lax.dot_general(home[:, lanes], scaled, (((0,), (0,)), ((), ())), preferr...  3.71 us
  transfers between devices with their start and end apart: 15, of which 8 were waited for; matrix products, arithmetic and copies ran while one was open for 13% of the time, Pallas kernels for 0%

profile of v1, /device:TPU:0, one launch (start us, length us, event | category | flops | bytes accessed | tf_op | source)
XLA Modules:
  0.0 117.0 jit_solution(9475405958578517485)
XLA Ops:
  0.6 0.0 copy-start
  0.6 0.9 reduce_window_sum.23
  1.5 0.7 subtract_bitcast_fusion
  2.2 0.1 convert_reduce_fusion.1
  2.3 0.7 xor_bitcast_fusion
  2.9 0.1 fusion.37
  3.0 0.2 reduce_window_sum.22
  3.2 0.2 select_reduce_fusion
  3.4 0.1 select_reduce_fusion.1
  3.4 0.7 fusion.50
  4.1 0.1 iota_compare_fusion.4
  4.2 1.3 %convolution_convert_fusion.15 = bf16[56,1024]{1,0:T(8,128)(2,1)S(1)} fusion(pred[128,224]{1,0:T(32,128)(4,1)S(1)} %iota_compare_fusion.4, bf16[128,1024]{1,0:T(8,128)(2,1)} %param.14, f32[128]{0:T(128)} %bitcast.92), kind=kOutput, calls=%fused_computation.28 | convolution fusion | flops 15130624 | bytes 393728 | tf_op jit(solution)/shard_map/dot_general | solution.py:86
  5.5 4.1 %collective-permute-start.10 = (bf16[56,1024]{1,0:T(8,128)(2,1)S(1)}, bf16[56,1024]{1,0:T(8,128)(2,1)S(1)}, u32[]{:S(2)}, u32[]{:S(2)}) collective-permute-start(bf16[56,1024]{1,0:T(8,128)(2,1)S(1)} %convolution_convert_fusion.15), channel_id=1, source_target_pairs={{0,2},{1,3},{2,0},{3,1},{4,6},{5,7},{6,4},{7,5},{8,10},{9,11},{10,... | collective-permute-start | bytes 344072 | tf_op jit(solution)/shard_map/ppermute | solution.py:17
  9.6 1.2 %convolution_convert_fusion.14 = bf16[56,1024]{1,0:T(8,128)(2,1)S(1)} fusion(pred[128,224]{1,0:T(32,128)(4,1)S(1)} %iota_compare_fusion.4, bf16[128,1024]{1,0:T(8,128)(2,1)} %param.14, f32[128]{0:T(128)} %bitcast.93), kind=kOutput, calls=%fused_computation.27 | convolution fusion | flops 15130624 | bytes 393728 | tf_op jit(solution)/shard_map/dot_general | solution.py:86
  10.8 1.4 %collective-permute-start.11 = (bf16[56,1024]{1,0:T(8,128)(2,1)S(1)}, bf16[56,1024]{1,0:T(8,128)(2,1)}, u32[]{:S(2)}, u32[]{:S(2)}) collective-permute-start(bf16[56,1024]{1,0:T(8,128)(2,1)S(1)} %convolution_convert_fusion.14), channel_id=1, source_target_pairs={{0,3},{1,2},{2,1},{3,0},{4,7},{5,6},{6,5},{7,4},{8,11},{9,10},{10,... | collective-permute-start | bytes 344072 | tf_op jit(solution)/shard_map/ppermute | solution.py:17
  12.2 0.8 eq.59
  13.0 2.4 %convolution_convert_fusion = bf16[256,1792]{1,0:T(8,128)(2,1)} fusion(bf16[128,3584]{1,0:T(8,128)(2,1)} %param.9, s32[256]{0:T(256)S(1)} %eq.59), kind=kOutput, calls=%fused_computation.6 | convolution fusion | flops 117932032 | bytes 1377280 | tf_op jit(solution)/shard_map/dot_general | solution.py:51
  15.4 3.9 %all-to-all-start.1 = ((bf16[8,32,1792]{2,1,0:T(8,128)(2,1)}), bf16[8,32,1792]{2,1,0:T(8,128)(2,1)S(1)}, u32[]{:S(2)}, u32[]{:S(2)}) async-start(bf16[8,32,1792]{2,1,0:T(8,128)(2,1)} %bitcast.12), calls=%async_computation.1 | async-start | bytes 1835008 | tf_op jit(solution)/shard_map/all_to_all | solution.py:53
  19.3 0.3 convolution_convert_fusion.13
  19.6 1.0 convolution_convert_fusion.16
  20.6 0.3 convolution_convert_fusion.17
  20.9 1.4 %convolution_convert_fusion.1 = bf16[256,1792]{1,0:T(8,128)(2,1)} fusion(bf16[128,3584]{1,0:T(8,128)(2,1)S(1)} %copy-done.2, s32[256]{0:T(256)S(1)} %eq.59), kind=kOutput, calls=%fused_computation.7 | convolution fusion | flops 117932032 | bytes 1377280 | tf_op jit(solution)/shard_map/dot_general | solution.py:51
  22.3 11.0 %all-to-all-done.1 = bf16[8,32,1792]{2,1,0:T(8,128)(2,1)S(1)} async-done(((bf16[8,32,1792]{2,1,0:T(8,128)(2,1)}), bf16[8,32,1792]{2,1,0:T(8,128)(2,1)S(1)}, u32[]{:S(2)}, u32[]{:S(2)}) %all-to-all-start.1) | async-done | bytes 917536 | tf_op jit(solution)/shard_map/all_to_all | solution.py:53
  33.3 3.6 %all-to-all-start = ((bf16[8,32,1792]{2,1,0:T(8,128)(2,1)}), bf16[8,32,1792]{2,1,0:T(8,128)(2,1)S(1)}, u32[]{:S(2)}, u32[]{:S(2)}) async-start(bf16[8,32,1792]{2,1,0:T(8,128)(2,1)} %bitcast.9), calls=%async_computation | async-start | bytes 1835008 | tf_op jit(solution)/shard_map/all_to_all | solution.py:53
  36.9 0.3 convolution_convert_fusion.7
  37.2 0.3 convolution_convert_fusion.4
  37.5 0.3 convolution_convert_fusion.5
  37.8 0.3 convolution_convert_fusion.6
  38.1 12.7 %all-to-all-done = bf16[8,32,1792]{2,1,0:T(8,128)(2,1)S(1)} async-done(((bf16[8,32,1792]{2,1,0:T(8,128)(2,1)}), bf16[8,32,1792]{2,1,0:T(8,128)(2,1)S(1)}, u32[]{:S(2)}, u32[]{:S(2)}) %all-to-all-start) | async-done | bytes 917536 | tf_op jit(solution)/shard_map/all_to_all | solution.py:53
  50.8 0.3 convolution_convert_fusion.11
  51.1 0.3 convolution_convert_fusion.8
  51.4 0.3 convolution_convert_fusion.9
  51.7 0.3 collective-permute-start.3
  52.0 2.8 %collective-permute-start.4 = (bf16[56,1792]{1,0:T(8,128)(2,1)S(1)}, bf16[56,1792]{1,0:T(8,128)(2,1)S(1)}, u32[]{:S(2)}, u32[]{:S(2)}) collective-permute-start(bf16[56,1792]{1,0:T(8,128)(2,1)S(1)} %convolution_convert_fusion.5), channel_id=1, source_target_pairs={{0,2},{1,3},{2,0},{3,1},{4,6},{5,7},{6,4},{7,5},{8,10},{9,11},{10,... | collective-permute-start | bytes 602120 | tf_op jit(solution)/shard_map/ppermute | solution.py:17
  54.8 1.4 %collective-permute-start.5 = (bf16[56,1792]{1,0:T(8,128)(2,1)S(1)}, bf16[56,1792]{1,0:T(8,128)(2,1)S(1)}, u32[]{:S(2)}, u32[]{:S(2)}) collective-permute-start(bf16[56,1792]{1,0:T(8,128)(2,1)S(1)} %convolution_convert_fusion.4), channel_id=1, source_target_pairs={{0,3},{1,2},{2,1},{3,0},{4,7},{5,6},{6,5},{7,4},{8,11},{9,10},{10,... | collective-permute-start | bytes 602120 | tf_op jit(solution)/shard_map/ppermute | solution.py:17
  56.2 0.3 convolution_convert_fusion.10
  56.5 4.7 %collective-permute-done.3 = bf16[56,1792]{1,0:T(8,128)(2,1)S(1)} collective-permute-done((bf16[56,1792]{1,0:T(8,128)(2,1)S(1)}, bf16[56,1792]{1,0:T(8,128)(2,1)S(1)}, u32[]{:S(2)}, u32[]{:S(2)}) %collective-permute-start.3) | collective-permute-done | bytes 200736 | tf_op jit(solution)/shard_map/ppermute | solution.py:17
  61.2 8.5 %collective-permute-done.4 = bf16[56,1792]{1,0:T(8,128)(2,1)S(1)} collective-permute-done((bf16[56,1792]{1,0:T(8,128)(2,1)S(1)}, bf16[56,1792]{1,0:T(8,128)(2,1)S(1)}, u32[]{:S(2)}, u32[]{:S(2)}) %collective-permute-start.4) | collective-permute-done | bytes 200736 | tf_op jit(solution)/shard_map/ppermute | solution.py:17
  69.7 2.8 %collective-permute-start.2 = (bf16[56,1792]{1,0:T(8,128)(2,1)S(1)}, bf16[56,1792]{1,0:T(8,128)(2,1)S(1)}, u32[]{:S(2)}, u32[]{:S(2)}) collective-permute-start(bf16[56,1792]{1,0:T(8,128)(2,1)S(1)} %convolution_convert_fusion.8), channel_id=1, source_target_pairs={{0,3},{1,2},{2,1},{3,0},{4,7},{5,6},{6,5},{7,4},{8,11},{9,10},{10,... | collective-permute-start | bytes 602120 | tf_op jit(solution)/shard_map/ppermute | solution.py:17
  72.5 3.1 %fusion = f32[224,1024]{1,0:T(8,128)S(1)} fusion(bf16[1,3584,1024]{2,1,0:T(8,128)(2,1)} %param.15, bf16[56,1792]{1,0:T(8,128)(2,1)S(1)} %collective-permute-done.5, bf16[56,1792]{1,0:T(8,128)(2,1)S(1)} %collective-permute-done.4, bf16[56,1792]{1,0:T(8,128)(2,1)S(1)} %collective-permute-done.3, bf16[56,1792]{1,0:T(8,128)(2,1)S(1)} %convolution_convert_fusion.7), kind=kOutput, calls=%fused_computation | convolution fusion | flops 825294848 | bytes 5390336 | tf_op jit(solution)/shard_map/dot_general | solution.py:105
  75.6 0.4 fusion.22
  76.0 0.5 copy-done.3
  76.5 10.0 %collective-permute-start.9 = (bf16[56,1024]{1,0:T(8,128)(2,1)S(1)}, bf16[56,1024]{1,0:T(8,128)(2,1)S(1)}, u32[]{:S(2)}, u32[]{:S(2)}) collective-permute-start(bf16[56,1024]{1,0:T(8,128)(2,1)S(1)} %copy-done.3), channel_id=1, source_target_pairs={{0,1},{1,0},{2,3},{3,2},{4,5},{5,4},{6,7},{7,6},{8,9},{9,8},{10,11... | collective-permute-start | bytes 344072 | tf_op jit(solution)/shard_map/ppermute | solution.py:17
  86.5 0.4 fusion.14
  86.9 0.3 fusion.30
  87.2 2.1 %collective-permute-done.9 = bf16[56,1024]{1,0:T(8,128)(2,1)S(1)} collective-permute-done((bf16[56,1024]{1,0:T(8,128)(2,1)S(1)}, bf16[56,1024]{1,0:T(8,128)(2,1)S(1)}, u32[]{:S(2)}, u32[]{:S(2)}) %collective-permute-start.9) | collective-permute-done | bytes 114720 | tf_op jit(solution)/shard_map/ppermute | solution.py:17
  89.2 2.3 %multiply_convert_fusion = (bf16[224,1024]{1,0:T(8,128)(2,1)S(1)}, bf16[224,1024]{1,0:T(8,128)(2,1)S(1)}) fusion(bf16[56,1024]{1,0:T(8,128)(2,1)} %collective-permute-done.11, bf16[56,1024]{1,0:T(8,128)(2,1)S(1)} %collective-permute-done.10, bf16[56,1024]{1,0:T(8,128)(2,1)S(1)} %collective-permute-done.9, ...), kind=kOutput, calls=%fused_computation.35 | convolution fusion | flops 830111744 | bytes 7684096 | tf_op jit(solution)/shard_map/dot_general | solution.py:105
  91.6 0.3 convolution_convert_fusion.18
  91.8 0.2 fusion.13
  92.2 0.5 convolution_convert_fusion.2
  92.7 0.5 convolution_convert_fusion.3
  93.2 0.1 pad_maximum_fusion.1
  93.2 1.1 pad_maximum_fusion
  94.3 4.3 %all-to-all-start.2 = ((bf16[8,576,128]{2,1,0:T(8,128)(2,1)}), bf16[8,576,128]{2,1,0:T(8,128)(2,1)S(1)}, u32[]{:S(2)}, u32[]{:S(2)}) async-start(bf16[8,576,128]{2,1,0:T(8,128)(2,1)} %pad_maximum_fusion), calls=%async_computation.2 | async-start | bytes 2359296 | tf_op jit(solution)/shard_map/all_to_all | solution.py:138
  98.7 1.0 collective-permute-start.8
  99.7 2.6 %collective-permute-start.7 = (bf16[56,1024]{1,0:T(8,128)(2,1)S(1)}, bf16[56,1024]{1,0:T(8,128)(2,1)S(1)}, u32[]{:S(2)}, u32[]{:S(2)}) collective-permute-start(bf16[56,1024]{1,0:T(8,128)(2,1)S(1)} %get-tuple-element.7), channel_id=1, source_target_pairs={{0,2},{1,3},{2,0},{3,1},{4,6},{5,7},{6,4},{7,5},{8,10},{9,11},{10,... | collective-permute-start | bytes 344072 | tf_op jit(solution)/shard_map/ppermute | solution.py:17
  102.2 0.9 collective-permute-start.6
  103.1 3.5 %collective-permute-done.8 = bf16[56,1024]{1,0:T(8,128)(2,1)S(1)} collective-permute-done((bf16[56,1024]{1,0:T(8,128)(2,1)S(1)}, bf16[56,1024]{1,0:T(8,128)(2,1)S(1)}, u32[]{:S(2)}, u32[]{:S(2)}) %collective-permute-start.8) | collective-permute-done | bytes 114720 | tf_op jit(solution)/shard_map/ppermute | solution.py:17
  106.6 6.5 %collective-permute-done.7 = bf16[56,1024]{1,0:T(8,128)(2,1)S(1)} collective-permute-done((bf16[56,1024]{1,0:T(8,128)(2,1)S(1)}, bf16[56,1024]{1,0:T(8,128)(2,1)S(1)}, u32[]{:S(2)}, u32[]{:S(2)}) %collective-permute-start.7) | collective-permute-done | bytes 114720 | tf_op jit(solution)/shard_map/ppermute | solution.py:17
  113.1 1.0 fusion.12
  114.1 1.3 %all-to-all-done.2 = bf16[8,576,128]{2,1,0:T(8,128)(2,1)S(1)} async-done(((bf16[8,576,128]{2,1,0:T(8,128)(2,1)}), bf16[8,576,128]{2,1,0:T(8,128)(2,1)S(1)}, u32[]{:S(2)}, u32[]{:S(2)}) %all-to-all-start.2) | async-done | bytes 1179680 | tf_op jit(solution)/shard_map/all_to_all | solution.py:138
  115.4 0.2 convert_reduce_fusion
  115.6 0.7 slice_bitcast_fusion
  116.4 0.6 broadcast_in_dim_reshape.3
  (31 shorter events, 0.2 us)
Async XLA Ops:
  0.6 86.2 %copy-start = (bf16[1,128,1024]{2,1,0:T(8,128)(2,1)S(1)}, bf16[1,128,1024]{2,1,0:T(8,128)(2,1)}, u32[]{:S(2)}) copy-start(bf16[1,128,1024]{2,1,0:T(8,128)(2,1)} %param.17) | copy-start | bytes 786436
  5.5 81.7 %collective-permute-start.10 = (bf16[56,1024]{1,0:T(8,128)(2,1)S(1)}, bf16[56,1024]{1,0:T(8,128)(2,1)S(1)}, u32[]{:S(2)}, u32[]{:S(2)}) collective-permute-start(bf16[56,1024]{1,0:T(8,128)(2,1)S(1)} %convolution_convert_fusion.15), channel_id=1, source_target_pairs={{0,2},{1,3},{2,0},{3,1},{4,6},{5,7},{6,4},{7,5},{8,10},{9,11},{10,... | collective-permute-start | bytes 344072 | tf_op jit(solution)/shard_map/ppermute | solution.py:17
  10.8 76.3 %collective-permute-start.11 = (bf16[56,1024]{1,0:T(8,128)(2,1)S(1)}, bf16[56,1024]{1,0:T(8,128)(2,1)}, u32[]{:S(2)}, u32[]{:S(2)}) collective-permute-start(bf16[56,1024]{1,0:T(8,128)(2,1)S(1)} %convolution_convert_fusion.14), channel_id=1, source_target_pairs={{0,3},{1,2},{2,1},{3,0},{4,7},{5,6},{6,5},{7,4},{8,11},{9,10},{10,... | collective-permute-start | bytes 344072 | tf_op jit(solution)/shard_map/ppermute | solution.py:17
  13.0 6.6 %copy-start.1 = (bf16[128,1024]{1,0:T(8,128)(2,1)S(1)}, bf16[128,1024]{1,0:T(8,128)(2,1)}, u32[]{:S(2)}) copy-start(bf16[128,1024]{1,0:T(8,128)(2,1)} %param.14) | copy-start | bytes 786436
  13.0 6.6 %copy-start.4 = (f32[128,1]{0,1:T(1,128)S(1)}, f32[128,1]{0,1:T(1,128)}, u32[]{:S(2)}) copy-start(f32[128,1]{0,1:T(1,128)} %param.13) | copy-start | bytes 1540
  15.4 5.4 %copy-start.2 = (bf16[128,3584]{1,0:T(8,128)(2,1)S(1)}, bf16[128,3584]{1,0:T(8,128)(2,1)}, u32[]{:S(2)}) copy-start(bf16[128,3584]{1,0:T(8,128)(2,1)} %param.9) | copy-start | bytes 2752516
  15.4 17.9 %all-to-all-start.1 = ((bf16[8,32,1792]{2,1,0:T(8,128)(2,1)}), bf16[8,32,1792]{2,1,0:T(8,128)(2,1)S(1)}, u32[]{:S(2)}, u32[]{:S(2)}) async-start(bf16[8,32,1792]{2,1,0:T(8,128)(2,1)} %bitcast.12), calls=%async_computation.1 | async-start | bytes 1835008 | tf_op jit(solution)/shard_map/all_to_all | solution.py:53
  33.3 17.5 %all-to-all-start = ((bf16[8,32,1792]{2,1,0:T(8,128)(2,1)}), bf16[8,32,1792]{2,1,0:T(8,128)(2,1)S(1)}, u32[]{:S(2)}, u32[]{:S(2)}) async-start(bf16[8,32,1792]{2,1,0:T(8,128)(2,1)} %bitcast.9), calls=%async_computation | async-start | bytes 1835008 | tf_op jit(solution)/shard_map/all_to_all | solution.py:53
  51.7 9.5 %collective-permute-start.3 = (bf16[56,1792]{1,0:T(8,128)(2,1)S(1)}, bf16[56,1792]{1,0:T(8,128)(2,1)S(1)}, u32[]{:S(2)}, u32[]{:S(2)}) collective-permute-start(bf16[56,1792]{1,0:T(8,128)(2,1)S(1)} %convolution_convert_fusion.6), channel_id=1, source_target_pairs={{0,1},{1,0},{2,3},{3,2},{4,5},{5,4},{6,7},{7,6},{8,9},{9,8},{10,11... | collective-permute-start | bytes 602120 | tf_op jit(solution)/shard_map/ppermute | solution.py:17
  52.0 17.6 %collective-permute-start.4 = (bf16[56,1792]{1,0:T(8,128)(2,1)S(1)}, bf16[56,1792]{1,0:T(8,128)(2,1)S(1)}, u32[]{:S(2)}, u32[]{:S(2)}) collective-permute-start(bf16[56,1792]{1,0:T(8,128)(2,1)S(1)} %convolution_convert_fusion.5), channel_id=1, source_target_pairs={{0,2},{1,3},{2,0},{3,1},{4,6},{5,7},{6,4},{7,5},{8,10},{9,11},{10,... | collective-permute-start | bytes 602120 | tf_op jit(solution)/shard_map/ppermute | solution.py:17
  54.8 14.9 %collective-permute-start.5 = (bf16[56,1792]{1,0:T(8,128)(2,1)S(1)}, bf16[56,1792]{1,0:T(8,128)(2,1)S(1)}, u32[]{:S(2)}, u32[]{:S(2)}) collective-permute-start(bf16[56,1792]{1,0:T(8,128)(2,1)S(1)} %convolution_convert_fusion.4), channel_id=1, source_target_pairs={{0,3},{1,2},{2,1},{3,0},{4,7},{5,6},{6,5},{7,4},{8,11},{9,10},{10,... | collective-permute-start | bytes 602120 | tf_op jit(solution)/shard_map/ppermute | solution.py:17
  56.1 33.1 %slice-start = ((s8[7340032]{0:T(1024)(128)(4,1)}), s8[4194304]{0:T(1024)(128)(4,1)S(1)}, s32[]{:S(2)}) async-start(s8[7340032]{0:T(1024)(128)(4,1)} %bitcast.97), calls=%async_computation.3 | async-start | bytes 8388608
  56.4 19.1 %copy-start.5 = (bf16[1,3584,128]{2,1,0:T(8,128)(2,1)S(1)}, bf16[1,3584,128]{2,1,0:T(8,128)(2,1)}, u32[]{:S(2)}) copy-start(bf16[1,3584,128]{2,1,0:T(8,128)(2,1)} %param.16) | copy-start | bytes 2752516
  56.5 32.8 %slice-start.1 = ((s8[7340032]{0:T(1024)(128)(4,1)}), s8[3145728]{0:T(1024)(128)(4,1)S(1)}, s32[]{:S(2)}) async-start(s8[7340032]{0:T(1024)(128)(4,1)} %bitcast.97), calls=%async_computation.4 | async-start | bytes 6291456
  61.2 14.8 %collective-permute-start = (bf16[56,1792]{1,0:T(8,128)(2,1)S(1)}, bf16[56,1792]{1,0:T(8,128)(2,1)S(1)}, u32[]{:S(2)}, u32[]{:S(2)}) collective-permute-start(bf16[56,1792]{1,0:T(8,128)(2,1)S(1)} %convolution_convert_fusion.10), channel_id=1, source_target_pairs={{0,1},{1,0},{2,3},{3,2},{4,5},{5,4},{6,7},{7,6},{8,9},{9,8},{10,11... | collective-permute-start | bytes 602120 | tf_op jit(solution)/shard_map/ppermute | solution.py:17
  69.6 16.8 %collective-permute-start.1 = (bf16[56,1792]{1,0:T(8,128)(2,1)S(1)}, bf16[56,1792]{1,0:T(8,128)(2,1)S(1)}, u32[]{:S(2)}, u32[]{:S(2)}) collective-permute-start(bf16[56,1792]{1,0:T(8,128)(2,1)S(1)} %convolution_convert_fusion.9), channel_id=1, source_target_pairs={{0,2},{1,3},{2,0},{3,1},{4,6},{5,7},{6,4},{7,5},{8,10},{9,11},{10,... | collective-permute-start | bytes 602120 | tf_op jit(solution)/shard_map/ppermute | solution.py:17
  69.7 16.8 %collective-permute-start.2 = (bf16[56,1792]{1,0:T(8,128)(2,1)S(1)}, bf16[56,1792]{1,0:T(8,128)(2,1)S(1)}, u32[]{:S(2)}, u32[]{:S(2)}) collective-permute-start(bf16[56,1792]{1,0:T(8,128)(2,1)S(1)} %convolution_convert_fusion.8), channel_id=1, source_target_pairs={{0,3},{1,2},{2,1},{3,0},{4,7},{5,6},{6,5},{7,4},{8,11},{9,10},{10,... | collective-permute-start | bytes 602120 | tf_op jit(solution)/shard_map/ppermute | solution.py:17
  75.6 0.9 copy-start.3
  76.5 12.8 %collective-permute-start.9 = (bf16[56,1024]{1,0:T(8,128)(2,1)S(1)}, bf16[56,1024]{1,0:T(8,128)(2,1)S(1)}, u32[]{:S(2)}, u32[]{:S(2)}) collective-permute-start(bf16[56,1024]{1,0:T(8,128)(2,1)S(1)} %copy-done.3), channel_id=1, source_target_pairs={{0,1},{1,0},{2,3},{3,2},{4,5},{5,4},{6,7},{7,6},{8,9},{9,8},{10,11... | collective-permute-start | bytes 344072 | tf_op jit(solution)/shard_map/ppermute | solution.py:17
  94.3 21.1 %all-to-all-start.2 = ((bf16[8,576,128]{2,1,0:T(8,128)(2,1)}), bf16[8,576,128]{2,1,0:T(8,128)(2,1)S(1)}, u32[]{:S(2)}, u32[]{:S(2)}) async-start(bf16[8,576,128]{2,1,0:T(8,128)(2,1)} %pad_maximum_fusion), calls=%async_computation.2 | async-start | bytes 2359296 | tf_op jit(solution)/shard_map/all_to_all | solution.py:138
  98.7 7.9 %collective-permute-start.8 = (bf16[56,1024]{1,0:T(8,128)(2,1)S(1)}, bf16[56,1024]{1,0:T(8,128)(2,1)S(1)}, u32[]{:S(2)}, u32[]{:S(2)}) collective-permute-start(bf16[56,1024]{1,0:T(8,128)(2,1)S(1)} %get-tuple-element.6), channel_id=1, source_target_pairs={{0,3},{1,2},{2,1},{3,0},{4,7},{5,6},{6,5},{7,4},{8,11},{9,10},{10,... | collective-permute-start | bytes 344072 | tf_op jit(solution)/shard_map/ppermute | solution.py:17
  99.7 13.5 %collective-permute-start.7 = (bf16[56,1024]{1,0:T(8,128)(2,1)S(1)}, bf16[56,1024]{1,0:T(8,128)(2,1)S(1)}, u32[]{:S(2)}, u32[]{:S(2)}) collective-permute-start(bf16[56,1024]{1,0:T(8,128)(2,1)S(1)} %get-tuple-element.7), channel_id=1, source_target_pairs={{0,2},{1,3},{2,0},{3,1},{4,6},{5,7},{6,4},{7,5},{8,10},{9,11},{10,... | collective-permute-start | bytes 344072 | tf_op jit(solution)/shard_map/ppermute | solution.py:17
  102.2 10.9 %collective-permute-start.6 = (bf16[56,1024]{1,0:T(8,128)(2,1)S(1)}, bf16[56,1024]{1,0:T(8,128)(2,1)S(1)}, u32[]{:S(2)}, u32[]{:S(2)}) collective-permute-start(bf16[56,1024]{1,0:T(8,128)(2,1)S(1)} %get-tuple-element.8), channel_id=1, source_target_pairs={{0,1},{1,0},{2,3},{3,2},{4,5},{5,4},{6,7},{7,6},{8,9},{9,8},{10,11... | collective-permute-start | bytes 344072 | tf_op jit(solution)/shard_map/ppermute | solution.py:17

commit v2 on v0

v2 whole, which is shorter than its diff:
```python
import functools

import jax
import jax.numpy as jnp
from jax import lax
from jax.experimental import pallas as pl
from jax.experimental.pallas import tpu as pltpu
from jax.sharding import PartitionSpec as P

CHUNKS = 2
VMEM_BYTES = 48 * 1024 * 1024
bf16 = jnp.bfloat16
f32 = jnp.float32
i32 = jnp.int32


def dot(a, b, contract=((1,), (0,))):
    return lax.dot_general(a, b, (contract, ((), ())), preferred_element_type=f32)


def call(kernel, out_shape, in_specs, scratch=(), flops=0, transcendentals=0, moved=0, name=None):
    return pl.pallas_call(
        kernel,
        out_shape=out_shape,
        grid=(1,),
        in_specs=in_specs,
        out_specs=jax.tree.map(whole, out_shape),
        scratch_shapes=list(scratch),
        cost_estimate=pl.CostEstimate(flops=flops, bytes_accessed=moved, transcendentals=transcendentals),
        compiler_params=pltpu.CompilerParams(vmem_limit_bytes=VMEM_BYTES),
        name=name,
    )


def whole(array):
    zeros = (0,) * len(array.shape)
    return pl.BlockSpec(array.shape, lambda i: zeros)


def smem(array):
    zeros = (0,) * len(array.shape)
    return pl.BlockSpec(array.shape, lambda i: zeros, memory_space=pltpu.SMEM)


def shape(dims, kind):
    return jax.ShapeDtypeStruct(dims, kind)


def swap_exp(block, step, exp_count):
    if step == 0:
        return block
    return lax.ppermute(block, "exp", [(i, i ^ step) for i in range(exp_count)])


def swap_rep(block, step, rep_count):
    if step == 0:
        return block
    return lax.ppermute(block, "rep", [(i, i ^ step) for i in range(rep_count)])


def prepare_kernel(fetch_slots, capacity, padded, counts, routes, weight, grads, pick, home, *sent):
    tokens = routes.shape[0]
    rep_count = counts.shape[1]
    exp_count = len(sent)
    replica = lax.axis_index("rep")
    column = lax.axis_index("exp")
    position = lax.broadcasted_iota(i32, (tokens, 1), 0)
    source = jnp.zeros((tokens, 1), i32)
    start = jnp.zeros((tokens, 1), i32)
    end = jnp.int32(0)
    for shard in range(rep_count):
        end = end + counts[0, shard]
        passed = position >= end
        source = source + passed.astype(i32)
        start = jnp.where(passed, end, start)
    place = jnp.bitwise_xor(source, replica) * fetch_slots + position - start
    place_of = place == lax.broadcasted_iota(i32, (tokens, rep_count * fetch_slots), 1)

    block = jnp.bitwise_xor(routes[...], column)
    chosen = block == lax.broadcasted_iota(i32, (tokens, exp_count), 1)
    above = lax.broadcasted_iota(i32, (tokens, tokens), 1) < lax.broadcasted_iota(i32, (tokens, tokens), 0)
    ranks = dot(above.astype(f32).astype(bf16), chosen.astype(f32).astype(bf16))
    rank = jnp.sum(jnp.where(chosen, ranks, 0.0), axis=1, keepdims=True).astype(i32)
    target = block * padded + rank
    slots = exp_count * padded
    home_of = (target == lax.broadcasted_iota(i32, (tokens, slots), 1)).astype(f32).astype(bf16)
    home[...] = home_of
    pick[...] = dot(home_of, place_of.astype(f32).astype(bf16), ((0,), (0,))).astype(bf16)
    scaled = (weight[...] * grads[...].astype(f32)).astype(bf16)
    by_slot = dot(home_of, scaled, ((0,), (0,))).astype(bf16)
    for step in range(exp_count):
        sent[step][...] = by_slot[step * padded : step * padded + capacity]


def serve_kernel(own_rows, pair_rows, own_table, pair_table, *sent):
    rep_count, fetch_slots = own_table.shape[1:]
    shard_rows = own_rows.shape[0]
    replica = lax.axis_index("rep")
    asked = []
    for step in range(0, rep_count, 2):
        wanted = jnp.bitwise_xor(replica, step)
        asked.append(own_table[0, pl.ds(wanted, 1), :])
        asked.append(pair_table[0, pl.ds(wanted, 1), :] + shard_rows)
    asked = jnp.concatenate(asked, axis=1)
    serve = (asked == lax.broadcasted_iota(i32, (2 * shard_rows, rep_count * fetch_slots), 0)).astype(f32).astype(bf16)
    rows = jnp.concatenate([own_rows[...], pair_rows[...]], axis=0)
    served = dot(serve, rows, ((0,), (0,))).astype(bf16)
    for number, block in enumerate(sent):
        block[...] = served[number * 2 * fetch_slots : (number + 1) * 2 * fetch_slots]


def pick_kernel(capacity, padded, sources, pick, *refs):
    arrived, sent = refs[:sources], refs[sources:]
    rows = jnp.concatenate([block[...] for block in arrived], axis=0)
    by_slot = dot(pick[...], rows).astype(bf16)
    for step in range(len(sent)):
        sent[step][...] = by_slot[step * padded : step * padded + capacity]


def fill(tile, blocks, capacity, padded):
    tile[...] = jnp.zeros(tile.shape, tile.dtype)
    for step, block in enumerate(blocks):
        tile[step * padded : step * padded + capacity, :] = block[...]


def partial_kernel(capacity, padded, gate, down, *refs):
    blocks = refs[:-3]
    tile, pre_act, adapted = refs[-3:]
    fill(tile, blocks, capacity, padded)
    pre_act[...] = dot(tile[...], gate[0])
    adapted[...] = dot(tile[...], down[0])


def finish_kernel(
    capacity, padded, exp_count, first, pre_first, adapted_first, gate, down, up, *refs
):
    blocks, refs = refs[:exp_count], refs[exp_count:]
    grads, refs = refs[:exp_count], refs[exp_count:]
    activated, refs = refs[:exp_count], refs[exp_count:]
    keep, give, tile, grad_tile, down_term, up_term = refs
    fill(tile, blocks, capacity, padded)
    fill(grad_tile, grads, capacity, padded)
    adapted = (adapted_first[...] + dot(tile[...], down[0])).astype(bf16)
    pre_act = pre_first[...] + dot(tile[...], gate[0]) + dot(adapted, up[0])
    gate_value = jax.nn.sigmoid(pre_act)
    rows = (pre_act * gate_value).astype(bf16)
    for step in range(exp_count):
        activated[step][...] = rows[step * padded : step * padded + capacity]
    slope = gate_value * (1.0 + pre_act * (1.0 - gate_value))
    grad_pre = (grad_tile[...].astype(f32) * slope).astype(bf16)
    back = dot(grad_pre, up[0], ((1,), (1,))).astype(bf16)
    pairs = keep.shape[0]
    down_rows = down_term.shape[1]
    up_rows, hidden_units = up_term.shape[1:]
    lanes = keep.shape[2]
    by_owner = first.shape[1] // down_rows
    for half, rows in enumerate((first, tile)):
        part = dot(rows[...], back, ((0,), (0,))).astype(bf16)
        for number in range(by_owner):
            down_term[half * by_owner + number] = part[number * down_rows : (number + 1) * down_rows]
    part = dot(adapted, grad_pre, ((0,), (0,)))
    for number in range(2 * pairs):
        up_term[number] = part[number * up_rows : (number + 1) * up_rows].astype(bf16)

    replica = lax.axis_index("rep")
    for number in range(pairs):
        for flip, target in ((0, keep), (1, give)):
            owner = jnp.bitwise_xor(replica, 2 * number + flip)
            target[number, :down_rows] = down_term[owner]
            mine = up_term[owner]
            for part in range(hidden_units // lanes):
                base = down_rows + part * up_rows
                target[number, base : base + up_rows] = mine[:, part * lanes : (part + 1) * lanes]


def combine_kernel(capacity, padded, home, weight, *refs):
    blocks = refs[:-2]
    out, tile = refs[-2:]
    fill(tile, blocks, capacity, padded)
    out[...] = (weight[...] * dot(home[...], tile[...])).astype(bf16)


def total_kernel(*refs):
    terms, (down_grad, up_grad) = refs[:-2], refs[-2:]
    total = terms[0][...].astype(f32)
    for term in terms[1:]:
        total = total + term[...].astype(f32)
    down_rows = down_grad.shape[1]
    up_rows, hidden_units = up_grad.shape[1:]
    lanes = total.shape[1]
    down_grad[0] = total[:down_rows]
    for part in range(hidden_units // lanes):
        base = down_rows + part * up_rows
        up_grad[0, :, part * lanes : (part + 1) * lanes] = total[base : base + up_rows]


def body(
    replay_buffer_rows,
    shard_request_index,
    replica_fetch_count,
    routes,
    router_route_weight,
    output_gradient,
    frozen_gate_weight,
    adapter_down_weight,
    adapter_up_weight,
):
    rep_count = lax.axis_size("rep")
    exp_count = lax.axis_size("exp")
    pairs = rep_count // 2
    token_count = routes.shape[0]
    shard_rows, model_width = replay_buffer_rows.shape
    fetch_slots = shard_request_index.shape[2]
    hidden_units = frozen_gate_weight.shape[2]
    rank_width = adapter_down_weight.shape[2]
    capacity = 7 * token_count // (4 * exp_count)
    padded = -(-capacity // 16) * 16
    slots = exp_count * padded
    fetched_rows = rep_count * fetch_slots
    chunk_width = model_width // CHUNKS

    pair_table = swap_rep(shard_request_index, 1, rep_count)
    pair_rows = swap_rep(replay_buffer_rows, 1, rep_count)

    prepared = call(
        functools.partial(prepare_kernel, fetch_slots, capacity, padded),
        [shape((slots, fetched_rows), bf16), shape((token_count, slots), bf16)]
        + [shape((capacity, hidden_units), bf16)] * exp_count,
        [smem(replica_fetch_count), whole(routes), whole(router_route_weight), whole(output_gradient)],
        flops=2 * token_count * slots * (hidden_units + fetched_rows),
        name="prepare",
    )(replica_fetch_count, routes, router_route_weight, output_gradient)
    pick, home, grads = prepared[0], prepared[1], prepared[2:]

    def columns(rows, chunk):
        return pl.BlockSpec((rows, chunk_width), lambda i: (0, chunk))

    def weight_rows(array, chunk):
        return pl.BlockSpec((1, chunk_width, array.shape[2]), lambda i: (0, chunk, 0))

    arrived = []
    for chunk in range(CHUNKS):
        served = call(
            serve_kernel,
            [shape((2 * fetch_slots, chunk_width), bf16)] * pairs,
            [columns(shard_rows, chunk)] * 2 + [whole(shard_request_index)] * 2,
            flops=4 * fetched_rows * shard_rows * chunk_width,
            name="serve",
        )(replay_buffer_rows, pair_rows, shard_request_index, pair_table)
        arrived.append([swap_rep(block, 2 * number, rep_count) for number, block in enumerate(served)])

    grads = [swap_exp(block, step, exp_count) for step, block in enumerate(grads)]

    blocks = []
    for chunk in range(CHUNKS):
        sent = call(
            functools.partial(pick_kernel, capacity, padded, pairs),
            [shape((capacity, chunk_width), bf16)] * exp_count,
            [whole(pick)] + [whole(block) for block in arrived[chunk]],
            flops=2 * slots * fetched_rows * chunk_width,
            name="pick",
        )(pick, *arrived[chunk])
        blocks.append([swap_exp(block, step, exp_count) for step, block in enumerate(sent)])

    first, pre_first, adapted_first = call(
        functools.partial(partial_kernel, capacity, padded),
        [shape((slots, chunk_width), bf16), shape((slots, hidden_units), f32), shape((slots, rank_width), f32)],
        [weight_rows(frozen_gate_weight, 0), weight_rows(adapter_down_weight, 0)]
        + [whole(block) for block in blocks[0]],
        flops=2 * slots * chunk_width * (hidden_units + rank_width),
        name="partial",
    )(frozen_gate_weight, adapter_down_weight, *blocks[0])

    term_rows = (model_width + rank_width * hidden_units // rank_width) // rep_count
    finished = call(
        functools.partial(finish_kernel, capacity, padded, exp_count),
        [shape((capacity, hidden_units), bf16)] * exp_count + [shape((pairs, term_rows, rank_width), bf16)] * 2,
        [whole(first), whole(pre_first), whole(adapted_first)]
        + [weight_rows(frozen_gate_weight, 1), weight_rows(adapter_down_weight, 1), whole(adapter_up_weight)]
        + [whole(block) for block in blocks[1]]
        + [whole(block) for block in grads],
        scratch=[
            pltpu.VMEM((slots, chunk_width), bf16),
            pltpu.VMEM((slots, hidden_units), bf16),
            pltpu.VMEM((rep_count, model_width // rep_count, rank_width), bf16),
            pltpu.VMEM((rep_count, rank_width // rep_count, hidden_units), bf16),
        ],
        flops=4 * slots * chunk_width * (hidden_units + rank_width),
        name="finish",
    )(
        first,
        pre_first,
        adapted_first,
        frozen_gate_weight,
        adapter_down_weight,
        adapter_up_weight,
        *blocks[1],
        *grads,
    )
    activated, (keep, give) = finished[:exp_count], finished[exp_count:]

    pair_terms = swap_rep(give, 1, rep_count)
    results = [swap_exp(block, step, exp_count) for step, block in enumerate(activated)]
    chip_terms = (keep.astype(f32) + pair_terms.astype(f32)).astype(bf16)
    terms = [swap_rep(chip_terms[number], 2 * number, rep_count) for number in range(pairs)]

    out_rows = call(
        functools.partial(combine_kernel, capacity, padded),
        shape((token_count, hidden_units), bf16),
        [whole(home), whole(router_route_weight)] + [whole(block) for block in results],
        scratch=[pltpu.VMEM((slots, hidden_units), bf16)],
        flops=2 * token_count * slots * hidden_units,
        name="combine",
    )(home, router_route_weight, *results)

    down_grad, up_grad = call(
        total_kernel,
        [
            shape((1, model_width // rep_count, rank_width), f32),
            shape((1, rank_width // rep_count, hidden_units), f32),
        ],
        [whole(term) for term in terms],
        name="total",
    )(*terms)
    return (out_rows, down_grad, up_grad)


def solution(mesh):
    placed = (
        P(("rep", "exp"), None),
        P(("rep", "exp"), None, None),
        P(("rep", "exp"), None),
        P(("rep", "exp"), None),
        P(("rep", "exp"), None),
        P(("rep", "exp"), None),
        P("exp", None, None),
        P("exp", None, None),
        P("exp", None, None),
    )
    return jax.shard_map(
        body,
        mesh=mesh,
        in_specs=placed,
        out_specs=(P(("rep", "exp"), None), P("exp", "rep", None), P("exp", "rep", None)),
        check_vma=False,
    )
```

time: 193 us -> 94.9 us (0.49)
  waiting for transfers between devices: 127 us -> 40.9 us
  starting transfers between devices: 18 us -> 37.6 us
  matrix products: 17.7 us -> 0 us
  between operations: 14.2 us -> 0.82 us
  Pallas kernels: 0 us -> 13.1 us
  other arithmetic: 9.63 us -> 0.16 us
  local copies, waits for them, and re-layouts: 5.42 us -> 2.17 us
    all_to_all x4 -> x0, waiting for transfers between devices: 68.8 us -> none  [the longest x1 32.8 us: body(): lax.all_to_all(sent_rows, 'exp', split_axis=0, concat_axis=0, tiled=True)]
    reduce_scatter x2 -> x0, waiting for transfers between devices: 58.3 us -> none  [the longest x1 44.1 us: body(): lax.psum_scatter(down_term, 'rep', scatter_dimension=0, tiled=True)]
    ppermute x0 -> x24, waiting for transfers between devices: none -> 40.9 us  [the longest x12 32.3 us: swap_exp(): return lax.ppermute(block, 'exp', [(i, i ^ step) for i in range(exp_count)])]
    ppermute x0 -> x24, starting transfers between devices: none -> 37.6 us  [the longest x12 22.4 us: swap_exp(): return lax.ppermute(block, 'exp', [(i, i ^ step) for i in range(exp_count)])]
    all_to_all x4 -> x0, starting transfers between devices: 17.9 us -> none  [the longest x1 5.3 us: body(): lax.all_to_all(served, 'rep', split_axis=0, concat_axis=0, tiled=True)]
    dot_general x7 -> x0, matrix products: 17.7 us -> none  [the longest x1 5.9 us: body(): jnp.dot(input_tile, frozen_gate_weight[0], preferred_element_type=jnp.flo...]
    pallas_call x0 -> x9, Pallas kernels: none -> 13.1 us  [the longest x1 4.76 us: body(): call(functools.partial(finish_kernel, capacity, padded, exp_count), [shap...]
    and x2 -> x0, other arithmetic: 5.87 us -> none  [the longest x1 5.09 us: body(): tokens = jnp.take(flat_rows, source * fetch_slots + offset, axis=0)]
  transfers between devices with their start and end apart: 6 -> 24, of which waited for: 6 -> 10; matrix products, arithmetic and copies ran while one was open for 10% -> 0% of each run, Pallas kernels for 0% -> 7%
where the time goes in v2:
time: 94.9 us; the launch traced here: 94.7 us
  waiting for transfers between devices  40.9 us (43%)
  starting transfers between devices  37.6 us (40%)
  Pallas kernels  13.1 us (14%)
  local copies, waits for them, and re-layouts  2.17 us (2%)
    ppermute x12, waiting for transfers between devices, swap_exp(): return lax.ppermute(block, 'exp', [(i, i ^ step) for i in range(exp_count)])  32.3 us
    ppermute x12, starting transfers between devices, swap_exp(): return lax.ppermute(block, 'exp', [(i, i ^ step) for i in range(exp_count)])  22.4 us
    ppermute x12, starting transfers between devices, swap_rep(): return lax.ppermute(block, 'rep', [(i, i ^ step) for i in range(rep_count)])  15.2 us
    ppermute x12, waiting for transfers between devices, swap_rep(): return lax.ppermute(block, 'rep', [(i, i ^ step) for i in range(rep_count)])  8.59 us
    pallas_call x1, Pallas kernels, body(): call(functools.partial(finish_kernel, capacity, padded, exp_count), [shap...  4.76 us
    pallas_call x1, Pallas kernels, body(): call(functools.partial(partial_kernel, capacity, padded), [shape((slots,...  3.45 us
    unnamed x18, local copies, waits for them, and re-layouts  2.13 us
  transfers between devices with their start and end apart: 24, of which 10 were waited for; matrix products, arithmetic and copies ran while one was open for 0% of the time, Pallas kernels for 7%

profile of v2, /device:TPU:0, one launch (start us, length us, event | category | flops | bytes accessed | tf_op | source)
XLA Modules:
  0.0 94.7 jit_solution(2572228413155393356)
XLA Ops:
  0.6 0.5 collective-permute-start
  1.1 0.1 collective-permute-start.1
  1.2 2.2 %collective-permute-done.1.pair_table = s32[1,8,32]{2,1,0:T(8,128)S(1)} collective-permute-done((s32[1,8,32]{2,1,0:T(8,128)}, s32[1,8,32]{2,1,0:T(8,128)S(1)}, u32[]{:S(2)}, u32[]{:S(2)}) %collective-permute-start.1) | collective-permute-done | bytes 1056 | tf_op jit(solution)/shard_map/ppermute | solution.py:58
  3.5 0.0 collective-permute-done.pair_rows
  3.5 1.2 %copy-done.1 = bf16[128,3584]{1,0:T(8,128)(2,1)S(1)} copy-done((bf16[128,3584]{1,0:T(8,128)(2,1)S(1)}, bf16[128,3584]{1,0:T(8,128)(2,1)}, u32[]{:S(2)}) %copy-start.1) | copy-done | bytes 917528
  4.7 0.7 copy-done.4
  5.3 0.5 serve.2
  5.9 0.0 copy-start.6
  5.9 0.0 copy-start.7
  5.9 0.0 copy-start.3
  5.9 0.0 copy-start.5
  5.9 2.9 %collective-permute-start.2 = (bf16[64,1792]{1,0:T(8,128)(2,1)S(1)}, bf16[64,1792]{1,0:T(8,128)(2,1)S(1)}, u32[]{:S(2)}, u32[]{:S(2)}) collective-permute-start(bf16[64,1792]{1,0:T(8,128)(2,1)S(1)} %get-tuple-element.39), channel_id=1, source_target_pairs={{0,8},{4,12},{8,0},{12,4},{16,24},{20,28},{24,16},{28,20},{1,9},{5... | collective-permute-start | bytes 688136 | tf_op jit(solution)/shard_map/ppermute | solution.py:58
  8.8 1.5 %collective-permute-start.3 = (bf16[64,1792]{1,0:T(8,128)(2,1)S(1)}, bf16[64,1792]{1,0:T(8,128)(2,1)S(1)}, u32[]{:S(2)}, u32[]{:S(2)}) collective-permute-start(bf16[64,1792]{1,0:T(8,128)(2,1)S(1)} %get-tuple-element.40), channel_id=1, source_target_pairs={{0,16},{4,20},{8,24},{12,28},{16,0},{20,4},{24,8},{28,12},{1,17},{... | collective-permute-start | bytes 688136 | tf_op jit(solution)/shard_map/ppermute | solution.py:58
  10.4 0.0 collective-permute-start.4
  10.4 0.5 serve.3
  10.9 2.0 %collective-permute-start.8 = (bf16[64,1792]{1,0:T(8,128)(2,1)S(1)}, bf16[64,1792]{1,0:T(8,128)(2,1)S(1)}, u32[]{:S(2)}, u32[]{:S(2)}) collective-permute-start(bf16[64,1792]{1,0:T(8,128)(2,1)S(1)} %get-tuple-element.50), channel_id=1, source_target_pairs={{0,8},{4,12},{8,0},{12,4},{16,24},{20,28},{24,16},{28,20},{1,9},{5... | collective-permute-start | bytes 688136 | tf_op jit(solution)/shard_map/ppermute | solution.py:58
  12.9 1.5 %collective-permute-start.9 = (bf16[64,1792]{1,0:T(8,128)(2,1)S(1)}, bf16[64,1792]{1,0:T(8,128)(2,1)S(1)}, u32[]{:S(2)}, u32[]{:S(2)}) collective-permute-start(bf16[64,1792]{1,0:T(8,128)(2,1)S(1)} %get-tuple-element.51), channel_id=1, source_target_pairs={{0,16},{4,20},{8,24},{12,28},{16,0},{20,4},{24,8},{28,12},{1,17},{... | collective-permute-start | bytes 688136 | tf_op jit(solution)/shard_map/ppermute | solution.py:58
  14.5 0.8 collective-permute-done.2.refs_1_
  15.2 3.0 %collective-permute-start.10 = (bf16[64,1792]{1,0:T(8,128)(2,1)S(1)}, bf16[64,1792]{1,0:T(8,128)(2,1)S(1)}, u32[]{:S(2)}, u32[]{:S(2)}) collective-permute-start(bf16[64,1792]{1,0:T(8,128)(2,1)S(1)} %get-tuple-element.52), channel_id=1, source_target_pairs={{0,24},{4,28},{8,16},{12,20},{16,8},{20,12},{24,0},{28,4},{1,25},{... | collective-permute-start | bytes 688136 | tf_op jit(solution)/shard_map/ppermute | solution.py:58
  18.3 0.1 copy.13.weight
  18.4 0.1 copy.12.routes
  18.5 0.0 copy-start
  18.5 1.3 %prepare.1 = (bf16[256,256]{1,0:T(8,128)(2,1)S(1)}, bf16[128,256]{1,0:T(8,128)(2,1)S(1)}, bf16[56,1024]{1,0:T(8,128)(2,1)S(1)}, bf16[56,1024]{1,0:T(8,128)(2,1)S...) custom-call(s32[1,8]{1,0:T(1,128)S(1)} %copy-done.5, s32[128,1]{1,0:T(8,128)S(1)} %copy.12.routes, ...), custom_call_target="tpu_custom_call" | custom-call | flops 83886080 | tf_op jit(solution)/shard_map/prepare/pallas_call | solution.py:225
  19.8 2.5 %collective-permute-done.3.refs_2_ = bf16[64,1792]{1,0:T(8,128)(2,1)S(1)} collective-permute-done((bf16[64,1792]{1,0:T(8,128)(2,1)S(1)}, bf16[64,1792]{1,0:T(8,128)(2,1)S(1)}, u32[]{:S(2)}, u32[]{:S(2)}) %collective-permute-start.3) | collective-permute-done | bytes 229408 | tf_op jit(solution)/shard_map/ppermute | solution.py:58
  22.3 0.0 collective-permute-done.4.refs_3_
  22.3 0.4 pick.2
  22.7 1.6 %collective-permute-start.5 = (bf16[56,1792]{1,0:T(8,128)(2,1)S(1)}, bf16[56,1792]{1,0:T(8,128)(2,1)S(1)}, u32[]{:S(2)}, u32[]{:S(2)}) collective-permute-start(bf16[56,1792]{1,0:T(8,128)(2,1)S(1)} %get-tuple-element.43), channel_id=1, source_target_pairs={{0,1},{1,0},{2,3},{3,2},{4,5},{5,4},{6,7},{7,6},{8,9},{9,8},{10,11... | collective-permute-start | bytes 602120 | tf_op jit(solution)/shard_map/ppermute | solution.py:52
  24.3 0.5 collective-permute-start.14
  24.8 0.3 collective-permute-done.8.refs_1_
  25.1 3.2 %collective-permute-start.6 = (bf16[56,1792]{1,0:T(8,128)(2,1)S(1)}, bf16[56,1792]{1,0:T(8,128)(2,1)S(1)}, u32[]{:S(2)}, u32[]{:S(2)}) collective-permute-start(bf16[56,1792]{1,0:T(8,128)(2,1)S(1)} %get-tuple-element.44), channel_id=1, source_target_pairs={{0,2},{1,3},{2,0},{3,1},{4,6},{5,7},{6,4},{7,5},{8,10},{9,11},{10,... | collective-permute-start | bytes 602120 | tf_op jit(solution)/shard_map/ppermute | solution.py:52
  28.3 2.7 %collective-permute-done.9.refs_2_ = bf16[64,1792]{1,0:T(8,128)(2,1)S(1)} collective-permute-done((bf16[64,1792]{1,0:T(8,128)(2,1)S(1)}, bf16[64,1792]{1,0:T(8,128)(2,1)S(1)}, u32[]{:S(2)}, u32[]{:S(2)}) %collective-permute-start.9) | collective-permute-done | bytes 229408 | tf_op jit(solution)/shard_map/ppermute | solution.py:58
  31.0 3.6 %collective-permute-start.7 = (bf16[56,1792]{1,0:T(8,128)(2,1)S(1)}, bf16[56,1792]{1,0:T(8,128)(2,1)S(1)}, u32[]{:S(2)}, u32[]{:S(2)}) collective-permute-start(bf16[56,1792]{1,0:T(8,128)(2,1)S(1)} %get-tuple-element.45), channel_id=1, source_target_pairs={{0,3},{1,2},{2,1},{3,0},{4,7},{5,6},{6,5},{7,4},{8,11},{9,10},{10,... | collective-permute-start | bytes 602120 | tf_op jit(solution)/shard_map/ppermute | solution.py:52
  34.6 0.4 pick.3
  35.0 0.1 collective-permute-start.11
  35.1 0.0 collective-permute-done.14.refs_5_
  35.1 0.8 collective-permute-start.12
  35.8 0.0 collective-permute-done.5.refs_1_
  35.8 3.6 %collective-permute-start.13 = (bf16[56,1792]{1,0:T(8,128)(2,1)S(1)}, bf16[56,1792]{1,0:T(8,128)(2,1)S(1)}, u32[]{:S(2)}, u32[]{:S(2)}) collective-permute-start(bf16[56,1792]{1,0:T(8,128)(2,1)S(1)} %get-tuple-element.56), channel_id=1, source_target_pairs={{0,3},{1,2},{2,1},{3,0},{4,7},{5,6},{6,5},{7,4},{8,11},{9,10},{10,... | collective-permute-start | bytes 602120 | tf_op jit(solution)/shard_map/ppermute | solution.py:52
  39.4 1.5 %collective-permute-done.6.refs_2_ = bf16[56,1792]{1,0:T(8,128)(2,1)S(1)} collective-permute-done((bf16[56,1792]{1,0:T(8,128)(2,1)S(1)}, bf16[56,1792]{1,0:T(8,128)(2,1)S(1)}, u32[]{:S(2)}, u32[]{:S(2)}) %collective-permute-start.6) | collective-permute-done | bytes 200736 | tf_op jit(solution)/shard_map/ppermute | solution.py:52
  41.0 0.0 collective-permute-start.15
  41.0 2.9 %collective-permute-done.7.refs_3_ = bf16[56,1792]{1,0:T(8,128)(2,1)S(1)} collective-permute-done((bf16[56,1792]{1,0:T(8,128)(2,1)S(1)}, bf16[56,1792]{1,0:T(8,128)(2,1)S(1)}, u32[]{:S(2)}, u32[]{:S(2)}) %collective-permute-start.7) | collective-permute-done | bytes 200736 | tf_op jit(solution)/shard_map/ppermute | solution.py:52
  43.8 2.9 %collective-permute-start.16 = (bf16[56,1024]{1,0:T(8,128)(2,1)S(1)}, bf16[56,1024]{1,0:T(8,128)(2,1)S(1)}, u32[]{:S(2)}, u32[]{:S(2)}) collective-permute-start(bf16[56,1024]{1,0:T(8,128)(2,1)S(1)} %get-tuple-element.60), channel_id=1, source_target_pairs={{0,3},{1,2},{2,1},{3,0},{4,7},{5,6},{6,5},{7,4},{8,11},{9,10},{10,... | collective-permute-start | bytes 344072 | tf_op jit(solution)/shard_map/ppermute | solution.py:52
  46.7 3.4 %partial.1 = (bf16[256,1792]{1,0:T(8,128)(2,1)S(1)}, f32[256,1024]{1,0:T(8,128)S(1)}, f32[256,128]{1,0:T(8,128)S(1)}) custom-call(bf16[1,3584,1024]{2,1,0:T(8,128)(2,1)} %gate.3, bf16[1,3584,128]{2,1,0:T(8,128)(2,1)S(1)} %copy-done, bf16[56,1792]{1,0:T(8,128)(2,1)S(1)} %get-tuple-element.42.refs_0_, bf16[56,1792]{1,0:T(8,128)(2,1)S(1)} %collective-permute-done.5.refs_1_, ...), custom_call_target="tpu_custom_call" | custom-call | flops 1056964608 | tf_op jit(solution)/shard_map/partial/pallas_call | solution.py:265
  50.2 20.6 %collective-permute-done.15.refs_6_ = bf16[56,1024]{1,0:T(8,128)(2,1)S(1)} collective-permute-done((bf16[56,1024]{1,0:T(8,128)(2,1)S(1)}, bf16[56,1024]{1,0:T(8,128)(2,1)S(1)}, u32[]{:S(2)}, u32[]{:S(2)}) %collective-permute-start.15) | collective-permute-done | bytes 114720 | tf_op jit(solution)/shard_map/ppermute | solution.py:52
  70.8 0.0 collective-permute-done.16.refs_7_
  70.8 0.0 collective-permute-done.11.refs_1_
  70.8 0.0 collective-permute-done.12.refs_2_
  70.8 0.0 collective-permute-done.13.refs_3_
  70.8 4.8 %finish.1 = (bf16[56,1024]{1,0:T(8,128)(2,1)S(1)}, bf16[56,1024]{1,0:T(8,128)(2,1)S(1)}, bf16[56,1024]{1,0:T(8,128)(2,1)S(1)}, bf16[56,1024]{1,0:T(8,128)(2,1)S(...) custom-call(bf16[256,1792]{1,0:T(8,128)(2,1)S(1)} %get-tuple-element.46.first, ...), custom_call_target="tpu_custom_call" | custom-call | flops 2113929216 | tf_op jit(solution)/shard_map/finish/pallas_call | solution.py:275
  75.6 0.1 collective-permute-start.20
  75.7 1.9 %collective-permute-start.17 = (bf16[56,1024]{1,0:T(8,128)(2,1)S(1)}, bf16[56,1024]{1,0:T(8,128)(2,1)S(1)}, u32[]{:S(2)}, u32[]{:S(2)}) collective-permute-start(bf16[56,1024]{1,0:T(8,128)(2,1)S(1)} %get-tuple-element.62), channel_id=1, source_target_pairs={{0,1},{1,0},{2,3},{3,2},{4,5},{5,4},{6,7},{7,6},{8,9},{9,8},{10,11... | collective-permute-start | bytes 344072 | tf_op jit(solution)/shard_map/ppermute | solution.py:52
  77.6 0.1 collective-permute-done.20
  77.7 0.2 add_convert_fusion
  77.9 2.5 %collective-permute-start.23 = (bf16[576,128]{1,0:T(8,128)(2,1)S(1)}, bf16[576,128]{1,0:T(8,128)(2,1)S(1)}, u32[]{:S(2)}, u32[]{:S(2)}) collective-permute-start(bf16[576,128]{1,0:T(8,128)(2,1)S(1)} %get-tuple-element.69), channel_id=1, source_target_pairs={{0,24},{4,28},{8,16},{12,20},{16,8},{20,12},{24,0},{28,4},{1,25},{... | collective-permute-start | bytes 442376 | tf_op jit(solution)/shard_map/ppermute | solution.py:58
  80.4 0.5 collective-permute-start.22
  80.8 0.6 collective-permute-start.21
  81.4 3.8 %collective-permute-start.18 = (bf16[56,1024]{1,0:T(8,128)(2,1)S(1)}, bf16[56,1024]{1,0:T(8,128)(2,1)S(1)}, u32[]{:S(2)}, u32[]{:S(2)}) collective-permute-start(bf16[56,1024]{1,0:T(8,128)(2,1)S(1)} %get-tuple-element.63), channel_id=1, source_target_pairs={{0,2},{1,3},{2,0},{3,1},{4,6},{5,7},{6,4},{7,5},{8,10},{9,11},{10,... | collective-permute-start | bytes 344072 | tf_op jit(solution)/shard_map/ppermute | solution.py:52
  85.2 0.0 collective-permute-done.17.refs_1_
  85.2 0.4 collective-permute-start.19
  85.7 7.3 %collective-permute-done.18.refs_2_ = bf16[56,1024]{1,0:T(8,128)(2,1)S(1)} collective-permute-done((bf16[56,1024]{1,0:T(8,128)(2,1)S(1)}, bf16[56,1024]{1,0:T(8,128)(2,1)S(1)}, u32[]{:S(2)}, u32[]{:S(2)}) %collective-permute-start.18) | collective-permute-done | bytes 114720 | tf_op jit(solution)/shard_map/ppermute | solution.py:52
  93.0 0.0 collective-permute-done.19.refs_3_
  93.0 0.9 combine.1
  93.9 0.0 collective-permute-done.23.refs_3_
  94.0 0.8 total.1
  (13 shorter events, 0.1 us)
Async XLA Ops:
  0.6 2.8 %collective-permute-start = (bf16[128,3584]{1,0:T(8,128)(2,1)}, bf16[128,3584]{1,0:T(8,128)(2,1)S(1)}, u32[]{:S(2)}, u32[]{:S(2)}) collective-permute-start(bf16[128,3584]{1,0:T(8,128)(2,1)} %own_rows.3), channel_id=1, source_target_pairs={{0,4},{4,0},{8,12},{12,8},{16,20},{20,16},{24,28},{28,24},{1,5},{5... | collective-permute-start | bytes 2752520 | tf_op jit(solution)/shard_map/ppermute | solution.py:58
  1.1 2.3 %collective-permute-start.1 = (s32[1,8,32]{2,1,0:T(8,128)}, s32[1,8,32]{2,1,0:T(8,128)S(1)}, u32[]{:S(2)}, u32[]{:S(2)}) collective-permute-start(s32[1,8,32]{2,1,0:T(8,128)} %own_table.3), channel_id=1, source_target_pairs={{0,4},{4,0},{8,12},{12,8},{16,20},{20,16},{24,28},{28,24},{1,5},{5... | collective-permute-start | bytes 3080 | tf_op jit(solution)/shard_map/ppermute | solution.py:58
  3.5 1.2 %copy-start.1 = (bf16[128,3584]{1,0:T(8,128)(2,1)S(1)}, bf16[128,3584]{1,0:T(8,128)(2,1)}, u32[]{:S(2)}) copy-start(bf16[128,3584]{1,0:T(8,128)(2,1)} %own_rows.3) | copy-start | bytes 2752516
  4.6 0.7 copy-start.4
  5.9 12.4 %copy-start.6 = (f32[128,1]{0,1:T(1,128)S(1)}, f32[128,1]{0,1:T(1,128)}, u32[]{:S(2)}) copy-start(f32[128,1]{0,1:T(1,128)} %param.13) | copy-start | bytes 1540
  5.9 12.5 %copy-start.7 = (s32[128,1]{0,1:T(1,128)S(1)}, s32[128,1]{0,1:T(1,128)}, u32[]{:S(2)}) copy-start(s32[128,1]{0,1:T(1,128)} %param.12) | copy-start | bytes 1540
  5.9 12.6 %copy-start.3 = (bf16[128,1024]{1,0:T(8,128)(2,1)S(1)}, bf16[128,1024]{1,0:T(8,128)(2,1)}, u32[]{:S(2)}) copy-start(bf16[128,1024]{1,0:T(8,128)(2,1)} %grads.1) | copy-start | bytes 786436
  5.9 12.6 %copy-start.5 = (s32[1,8]{1,0:T(1,128)S(1)}, s32[1,8]{1,0:T(1,128)}, u32[]{:S(2)}) copy-start(s32[1,8]{1,0:T(1,128)} %counts.1) | copy-start | bytes 100
  5.9 9.3 %collective-permute-start.2 = (bf16[64,1792]{1,0:T(8,128)(2,1)S(1)}, bf16[64,1792]{1,0:T(8,128)(2,1)S(1)}, u32[]{:S(2)}, u32[]{:S(2)}) collective-permute-start(bf16[64,1792]{1,0:T(8,128)(2,1)S(1)} %get-tuple-element.39), channel_id=1, source_target_pairs={{0,8},{4,12},{8,0},{12,4},{16,24},{20,28},{24,16},{28,20},{1,9},{5... | collective-permute-start | bytes 688136 | tf_op jit(solution)/shard_map/ppermute | solution.py:58
  8.8 13.4 %collective-permute-start.3 = (bf16[64,1792]{1,0:T(8,128)(2,1)S(1)}, bf16[64,1792]{1,0:T(8,128)(2,1)S(1)}, u32[]{:S(2)}, u32[]{:S(2)}) collective-permute-start(bf16[64,1792]{1,0:T(8,128)(2,1)S(1)} %get-tuple-element.40), channel_id=1, source_target_pairs={{0,16},{4,20},{8,24},{12,28},{16,0},{20,4},{24,8},{28,12},{1,17},{... | collective-permute-start | bytes 688136 | tf_op jit(solution)/shard_map/ppermute | solution.py:58
  10.4 11.9 %collective-permute-start.4 = (bf16[64,1792]{1,0:T(8,128)(2,1)S(1)}, bf16[64,1792]{1,0:T(8,128)(2,1)S(1)}, u32[]{:S(2)}, u32[]{:S(2)}) collective-permute-start(bf16[64,1792]{1,0:T(8,128)(2,1)S(1)} %get-tuple-element.41), channel_id=1, source_target_pairs={{0,24},{4,28},{8,16},{12,20},{16,8},{20,12},{24,0},{28,4},{1,25},{... | collective-permute-start | bytes 688136 | tf_op jit(solution)/shard_map/ppermute | solution.py:58
  10.9 14.2 %collective-permute-start.8 = (bf16[64,1792]{1,0:T(8,128)(2,1)S(1)}, bf16[64,1792]{1,0:T(8,128)(2,1)S(1)}, u32[]{:S(2)}, u32[]{:S(2)}) collective-permute-start(bf16[64,1792]{1,0:T(8,128)(2,1)S(1)} %get-tuple-element.50), channel_id=1, source_target_pairs={{0,8},{4,12},{8,0},{12,4},{16,24},{20,28},{24,16},{28,20},{1,9},{5... | collective-permute-start | bytes 688136 | tf_op jit(solution)/shard_map/ppermute | solution.py:58
  12.9 18.0 %collective-permute-start.9 = (bf16[64,1792]{1,0:T(8,128)(2,1)S(1)}, bf16[64,1792]{1,0:T(8,128)(2,1)S(1)}, u32[]{:S(2)}, u32[]{:S(2)}) collective-permute-start(bf16[64,1792]{1,0:T(8,128)(2,1)S(1)} %get-tuple-element.51), channel_id=1, source_target_pairs={{0,16},{4,20},{8,24},{12,28},{16,0},{20,4},{24,8},{28,12},{1,17},{... | collective-permute-start | bytes 688136 | tf_op jit(solution)/shard_map/ppermute | solution.py:58
  15.2 19.3 %collective-permute-start.10 = (bf16[64,1792]{1,0:T(8,128)(2,1)S(1)}, bf16[64,1792]{1,0:T(8,128)(2,1)S(1)}, u32[]{:S(2)}, u32[]{:S(2)}) collective-permute-start(bf16[64,1792]{1,0:T(8,128)(2,1)S(1)} %get-tuple-element.52), channel_id=1, source_target_pairs={{0,24},{4,28},{8,16},{12,20},{16,8},{20,12},{24,0},{28,4},{1,25},{... | collective-permute-start | bytes 688136 | tf_op jit(solution)/shard_map/ppermute | solution.py:58
  18.5 28.2 %copy-start = (bf16[1,3584,128]{2,1,0:T(8,128)(2,1)S(1)}, bf16[1,3584,128]{2,1,0:T(8,128)(2,1)}, u32[]{:S(2)}) copy-start(bf16[1,3584,128]{2,1,0:T(8,128)(2,1)} %down.3) | copy-start | bytes 2752516
  22.7 13.2 %collective-permute-start.5 = (bf16[56,1792]{1,0:T(8,128)(2,1)S(1)}, bf16[56,1792]{1,0:T(8,128)(2,1)S(1)}, u32[]{:S(2)}, u32[]{:S(2)}) collective-permute-start(bf16[56,1792]{1,0:T(8,128)(2,1)S(1)} %get-tuple-element.43), channel_id=1, source_target_pairs={{0,1},{1,0},{2,3},{3,2},{4,5},{5,4},{6,7},{7,6},{8,9},{9,8},{10,11... | collective-permute-start | bytes 602120 | tf_op jit(solution)/shard_map/ppermute | solution.py:52
  24.3 10.8 %collective-permute-start.14 = (bf16[56,1024]{1,0:T(8,128)(2,1)S(1)}, bf16[56,1024]{1,0:T(8,128)(2,1)S(1)}, u32[]{:S(2)}, u32[]{:S(2)}) collective-permute-start(bf16[56,1024]{1,0:T(8,128)(2,1)S(1)} %get-tuple-element.58), channel_id=1, source_target_pairs={{0,1},{1,0},{2,3},{3,2},{4,5},{5,4},{6,7},{7,6},{8,9},{9,8},{10,11... | collective-permute-start | bytes 344072 | tf_op jit(solution)/shard_map/ppermute | solution.py:52
  25.1 15.9 %collective-permute-start.6 = (bf16[56,1792]{1,0:T(8,128)(2,1)S(1)}, bf16[56,1792]{1,0:T(8,128)(2,1)S(1)}, u32[]{:S(2)}, u32[]{:S(2)}) collective-permute-start(bf16[56,1792]{1,0:T(8,128)(2,1)S(1)} %get-tuple-element.44), channel_id=1, source_target_pairs={{0,2},{1,3},{2,0},{3,1},{4,6},{5,7},{6,4},{7,5},{8,10},{9,11},{10,... | collective-permute-start | bytes 602120 | tf_op jit(solution)/shard_map/ppermute | solution.py:52
  31.0 12.9 %collective-permute-start.7 = (bf16[56,1792]{1,0:T(8,128)(2,1)S(1)}, bf16[56,1792]{1,0:T(8,128)(2,1)S(1)}, u32[]{:S(2)}, u32[]{:S(2)}) collective-permute-start(bf16[56,1792]{1,0:T(8,128)(2,1)S(1)} %get-tuple-element.45), channel_id=1, source_target_pairs={{0,3},{1,2},{2,1},{3,0},{4,7},{5,6},{6,5},{7,4},{8,11},{9,10},{10,... | collective-permute-start | bytes 602120 | tf_op jit(solution)/shard_map/ppermute | solution.py:52
  35.0 35.8 %collective-permute-start.11 = (bf16[56,1792]{1,0:T(8,128)(2,1)S(1)}, bf16[56,1792]{1,0:T(8,128)(2,1)S(1)}, u32[]{:S(2)}, u32[]{:S(2)}) collective-permute-start(bf16[56,1792]{1,0:T(8,128)(2,1)S(1)} %get-tuple-element.54), channel_id=1, source_target_pairs={{0,1},{1,0},{2,3},{3,2},{4,5},{5,4},{6,7},{7,6},{8,9},{9,8},{10,11... | collective-permute-start | bytes 602120 | tf_op jit(solution)/shard_map/ppermute | solution.py:52
  35.1 35.7 %collective-permute-start.12 = (bf16[56,1792]{1,0:T(8,128)(2,1)S(1)}, bf16[56,1792]{1,0:T(8,128)(2,1)S(1)}, u32[]{:S(2)}, u32[]{:S(2)}) collective-permute-start(bf16[56,1792]{1,0:T(8,128)(2,1)S(1)} %get-tuple-element.55), channel_id=1, source_target_pairs={{0,2},{1,3},{2,0},{3,1},{4,6},{5,7},{6,4},{7,5},{8,10},{9,11},{10,... | collective-permute-start | bytes 602120 | tf_op jit(solution)/shard_map/ppermute | solution.py:52
  35.8 35.0 %collective-permute-start.13 = (bf16[56,1792]{1,0:T(8,128)(2,1)S(1)}, bf16[56,1792]{1,0:T(8,128)(2,1)S(1)}, u32[]{:S(2)}, u32[]{:S(2)}) collective-permute-start(bf16[56,1792]{1,0:T(8,128)(2,1)S(1)} %get-tuple-element.56), channel_id=1, source_target_pairs={{0,3},{1,2},{2,1},{3,0},{4,7},{5,6},{6,5},{7,4},{8,11},{9,10},{10,... | collective-permute-start | bytes 602120 | tf_op jit(solution)/shard_map/ppermute | solution.py:52
  41.0 29.8 %collective-permute-start.15 = (bf16[56,1024]{1,0:T(8,128)(2,1)S(1)}, bf16[56,1024]{1,0:T(8,128)(2,1)S(1)}, u32[]{:S(2)}, u32[]{:S(2)}) collective-permute-start(bf16[56,1024]{1,0:T(8,128)(2,1)S(1)} %get-tuple-element.59), channel_id=1, source_target_pairs={{0,2},{1,3},{2,0},{3,1},{4,6},{5,7},{6,4},{7,5},{8,10},{9,11},{10,... | collective-permute-start | bytes 344072 | tf_op jit(solution)/shard_map/ppermute | solution.py:52
  43.8 27.0 %collective-permute-start.16 = (bf16[56,1024]{1,0:T(8,128)(2,1)S(1)}, bf16[56,1024]{1,0:T(8,128)(2,1)S(1)}, u32[]{:S(2)}, u32[]{:S(2)}) collective-permute-start(bf16[56,1024]{1,0:T(8,128)(2,1)S(1)} %get-tuple-element.60), channel_id=1, source_target_pairs={{0,3},{1,2},{2,1},{3,0},{4,7},{5,6},{6,5},{7,4},{8,11},{9,10},{10,... | collective-permute-start | bytes 344072 | tf_op jit(solution)/shard_map/ppermute | solution.py:52
  46.7 24.1 %copy-start.2 = (bf16[1,128,1024]{2,1,0:T(8,128)(2,1)S(1)}, bf16[1,128,1024]{2,1,0:T(8,128)(2,1)}, u32[]{:S(2)}) copy-start(bf16[1,128,1024]{2,1,0:T(8,128)(2,1)} %up.1) | copy-start | bytes 786436
  75.6 2.1 %collective-permute-start.20 = (bf16[4,576,128]{2,1,0:T(8,128)(2,1)S(1)}, bf16[4,576,128]{2,1,0:T(8,128)(2,1)S(1)}, u32[]{:S(2)}, u32[]{:S(2)}) collective-permute-start(bf16[4,576,128]{2,1,0:T(8,128)(2,1)S(1)} %get-tuple-element.66), channel_id=1, source_target_pairs={{0,4},{4,0},{8,12},{12,8},{16,20},{20,16},{24,28},{28,24},{1,5},{5... | collective-permute-start | bytes 1769480 | tf_op jit(solution)/shard_map/ppermute | solution.py:58
  75.7 9.5 %collective-permute-start.17 = (bf16[56,1024]{1,0:T(8,128)(2,1)S(1)}, bf16[56,1024]{1,0:T(8,128)(2,1)S(1)}, u32[]{:S(2)}, u32[]{:S(2)}) collective-permute-start(bf16[56,1024]{1,0:T(8,128)(2,1)S(1)} %get-tuple-element.62), channel_id=1, source_target_pairs={{0,1},{1,0},{2,3},{3,2},{4,5},{5,4},{6,7},{7,6},{8,9},{9,8},{10,11... | collective-permute-start | bytes 344072 | tf_op jit(solution)/shard_map/ppermute | solution.py:52
  77.9 16.1 %collective-permute-start.23 = (bf16[576,128]{1,0:T(8,128)(2,1)S(1)}, bf16[576,128]{1,0:T(8,128)(2,1)S(1)}, u32[]{:S(2)}, u32[]{:S(2)}) collective-permute-start(bf16[576,128]{1,0:T(8,128)(2,1)S(1)} %get-tuple-element.69), channel_id=1, source_target_pairs={{0,24},{4,28},{8,16},{12,20},{16,8},{20,12},{24,0},{28,4},{1,25},{... | collective-permute-start | bytes 442376 | tf_op jit(solution)/shard_map/ppermute | solution.py:58
  80.4 13.6 %collective-permute-start.22 = (bf16[576,128]{1,0:T(8,128)(2,1)S(1)}, bf16[576,128]{1,0:T(8,128)(2,1)S(1)}, u32[]{:S(2)}, u32[]{:S(2)}) collective-permute-start(bf16[576,128]{1,0:T(8,128)(2,1)S(1)} %get-tuple-element.70), channel_id=1, source_target_pairs={{0,16},{4,20},{8,24},{12,28},{16,0},{20,4},{24,8},{28,12},{1,17},{... | collective-permute-start | bytes 442376 | tf_op jit(solution)/shard_map/ppermute | solution.py:58
  80.8 13.1 %collective-permute-start.21 = (bf16[576,128]{1,0:T(8,128)(2,1)S(1)}, bf16[576,128]{1,0:T(8,128)(2,1)S(1)}, u32[]{:S(2)}, u32[]{:S(2)}) collective-permute-start(bf16[576,128]{1,0:T(8,128)(2,1)S(1)} %get-tuple-element.71), channel_id=1, source_target_pairs={{0,8},{4,12},{8,0},{12,4},{16,24},{20,28},{24,16},{28,20},{1,9},{5... | collective-permute-start | bytes 442376 | tf_op jit(solution)/shard_map/ppermute | solution.py:58
  81.4 11.6 %collective-permute-start.18 = (bf16[56,1024]{1,0:T(8,128)(2,1)S(1)}, bf16[56,1024]{1,0:T(8,128)(2,1)S(1)}, u32[]{:S(2)}, u32[]{:S(2)}) collective-permute-start(bf16[56,1024]{1,0:T(8,128)(2,1)S(1)} %get-tuple-element.63), channel_id=1, source_target_pairs={{0,2},{1,3},{2,0},{3,1},{4,6},{5,7},{6,4},{7,5},{8,10},{9,11},{10,... | collective-permute-start | bytes 344072 | tf_op jit(solution)/shard_map/ppermute | solution.py:52
  85.2 7.8 %collective-permute-start.19 = (bf16[56,1024]{1,0:T(8,128)(2,1)S(1)}, bf16[56,1024]{1,0:T(8,128)(2,1)S(1)}, u32[]{:S(2)}, u32[]{:S(2)}) collective-permute-start(bf16[56,1024]{1,0:T(8,128)(2,1)S(1)} %get-tuple-element.64), channel_id=1, source_target_pairs={{0,3},{1,2},{2,1},{3,0},{4,7},{5,6},{6,5},{7,4},{8,11},{9,10},{10,... | collective-permute-start | bytes 344072 | tf_op jit(solution)/shard_map/ppermute | solution.py:52

commit v3 on v2

v3 whole, which is shorter than its diff:
```python
import functools

import jax
import jax.numpy as jnp
from jax import lax
from jax.experimental import pallas as pl
from jax.experimental.pallas import tpu as pltpu
from jax.sharding import PartitionSpec as P

CHUNKS = 2
bf16 = jnp.bfloat16
f32 = jnp.float32
i32 = jnp.int32


def dot(a, b, contract=((1,), (0,))):
    return lax.dot_general(a, b, (contract, ((), ())), preferred_element_type=f32)


def call(kernel, out_shape, operands, counts=None, resident=(), far=(), stored=(), scratch=(), flops=0, vmem=16, name=None):
    first_out = len(operands)
    away = [number for number, array in enumerate(operands) if any(array is other for other in far)]
    moved = [*away, *(first_out + number for number in stored)]
    arrays = [*operands, *out_shape]

    def moving(*refs):
        inner = list(refs)
        copies = {}
        if moved:
            *inner, sems = inner
            near = inner[len(inner) - len(moved) :]
            inner = inner[: len(inner) - len(moved)]
            for place, number in enumerate(moved):
                ends = (inner[number], near[place]) if number < first_out else (near[place], inner[number])
                copies[number] = pltpu.make_async_copy(*ends, sems.at[place])
                inner[number] = near[place]
        for number in away:
            copies[number].start()
        for number in away:
            copies[number].wait()
        kernel(*inner)
        for number in moved[len(away) :]:
            copies[number].start()
        for number in moved[len(away) :]:
            copies[number].wait()

    def space(number):
        array = arrays[number]
        zeros = (0,) * len(array.shape)
        if number in moved:
            return pl.BlockSpec(memory_space=pltpu.HBM)
        if any(array is other for other in resident):
            return pl.BlockSpec(memory_space=pltpu.VMEM)
        if array is counts:
            return pl.BlockSpec(memory_space=pltpu.SMEM)
        return pl.BlockSpec(array.shape, lambda i: zeros)

    near = [pltpu.VMEM(arrays[number].shape, arrays[number].dtype) for number in moved]
    operands = [
        pltpu.with_memory_space_constraint(array, pltpu.HBM) if number in away else array
        for number, array in enumerate(operands)
    ]
    return pl.pallas_call(
        moving,
        out_shape=[
            pltpu.HBM(out.shape, out.dtype) if number in stored else out for number, out in enumerate(out_shape)
        ],
        grid=(1,),
        in_specs=[space(number) for number in range(first_out)],
        out_specs=[space(first_out + number) for number in range(len(out_shape))],
        scratch_shapes=[*scratch, *near] + ([pltpu.SemaphoreType.DMA((len(moved),))] if moved else []),
        cost_estimate=pl.CostEstimate(flops=flops, bytes_accessed=flops // 300, transcendentals=0),
        compiler_params=pltpu.CompilerParams(vmem_limit_bytes=vmem * 1024 * 1024),
        name=name,
    )(*operands)


def shape(dims, kind):
    return jax.ShapeDtypeStruct(dims, kind)


def swap_exp(block, step, exp_count):
    if step == 0:
        return block
    return lax.ppermute(block, "exp", [(i, i ^ step) for i in range(exp_count)])


def swap_core(block, rep_count):
    return lax.ppermute(block, "rep", [(i, i ^ 1) for i in range(rep_count)])


def swap_chip(block, step, rep_count):
    if step == 0:
        return block
    return lax.ppermute(block, "rep", [(i, i ^ (2 * step)) for i in range(rep_count)])


def between_chips(blocks, rep_count):
    cores = [list(range(core, rep_count, 2)) for core in range(2)]
    return lax.all_to_all(blocks, "rep", 0, 0, axis_index_groups=cores, tiled=True)


def upright(row):
    count = row.shape[1]
    same = lax.broadcasted_iota(i32, (count, count), 0) == lax.broadcasted_iota(i32, (count, count), 1)
    return jnp.sum(jnp.where(same, row, jnp.zeros_like(row)), axis=1, keepdims=True)


def one_hot(spots):
    return spots.astype(f32).astype(bf16)


def slot_spots(capacity, padded, exp_count, routes):
    tokens = routes.shape[1]
    block = jnp.bitwise_xor(upright(routes[...]), lax.axis_index("exp"))
    chosen = block == lax.broadcasted_iota(i32, (tokens, exp_count), 1)
    above = lax.broadcasted_iota(i32, (tokens, tokens), 1) < lax.broadcasted_iota(i32, (tokens, tokens), 0)
    ranks = dot(one_hot(above), one_hot(chosen))
    rank = jnp.sum(jnp.where(chosen, ranks, 0.0), axis=1, keepdims=True).astype(i32)
    target = block * padded + rank
    return one_hot(target == lax.broadcasted_iota(i32, (tokens, exp_count * padded), 1))


def prepare_kernel(fetch_slots, capacity, padded, exp_count, counts, routes, pick, pick_swapped, home):
    tokens = routes.shape[1]
    rep_count = counts.shape[1]
    replica = lax.axis_index("rep")
    position = lax.broadcasted_iota(i32, (tokens, 1), 0)
    source = jnp.zeros((tokens, 1), i32)
    start = jnp.zeros((tokens, 1), i32)
    end = jnp.int32(0)
    for shard in range(rep_count):
        end = end + counts[0, shard]
        passed = position >= end
        source = source + passed.astype(i32)
        start = jnp.where(passed, end, start)
    home_of = slot_spots(capacity, padded, exp_count, routes)
    home[...] = home_of

    places = lax.broadcasted_iota(i32, (tokens, rep_count * fetch_slots), 1)
    other = jnp.bitwise_and(jnp.bitwise_xor(source, replica), 1)
    even = source - jnp.bitwise_and(source, 1)
    apart = jnp.bitwise_xor(even, replica - jnp.bitwise_and(replica, 1))
    for chip, matrix in ((even, pick), (apart, pick_swapped)):
        place = (chip + other) * fetch_slots + position - start
        matrix[...] = dot(home_of, one_hot(place == places), ((0,), (0,))).astype(bf16)


def part_of(chunk, width):
    return slice(chunk * width, (chunk + 1) * width)


def serve(table, rows, first):
    rep_count, fetch_slots = table.shape[1:]
    core = jnp.bitwise_and(lax.axis_index("rep"), 1)
    asked = [table[0, pl.ds(jnp.bitwise_xor(2 * chip, first) + core, 1), :] for chip in range(rep_count // 2)]
    asked = jnp.concatenate(asked, axis=1)
    chosen = asked == lax.broadcasted_iota(i32, (rows.shape[0], asked.shape[1]), 0)
    found = dot(one_hot(chosen), rows, ((0,), (0,))).astype(bf16)
    return [found[chip * fetch_slots : (chip + 1) * fetch_slots] for chip in range(rep_count // 2)]


def begin_kernel(capacity, padded, table, rows, routes, weight, grads, served, *sent):
    for chip, found in enumerate(serve(table, rows[:, : served.shape[2]], 0)):
        served[chip] = found
    home = slot_spots(capacity, padded, len(sent), routes)
    scaled = (upright(weight[...]) * grads[...].astype(f32)).astype(bf16)
    by_slot = dot(home, scaled, ((0,), (0,))).astype(bf16)
    for step in range(len(sent)):
        sent[step][...] = by_slot[step * padded : step * padded + capacity]


def serve_first_kernel(table, rows, own, served):
    fetch_slots = own.shape[1]
    for chip, found in enumerate(serve(table, rows[:, : served.shape[2]], 0)):
        served[chip, :fetch_slots] = own[chip]
        served[chip, fetch_slots:] = found


def serve_last_kernel(own_table, own_rows, pair_table, pair_rows, *served):
    fetch_slots = own_table.shape[2]
    part = part_of(1, served[0].shape[1])
    replica = lax.axis_index("rep")
    first = replica - jnp.bitwise_and(replica, 1)
    for block, found in zip(served, serve(own_table, own_rows[:, part], first)):
        block[:fetch_slots] = found
    for block, found in zip(served, serve(pair_table, pair_rows[:, part], first)):
        block[fetch_slots:] = found


def pick_first_kernel(capacity, padded, pick, arrived, *refs):
    *grads, sent, grad_tile = refs
    fill(grad_tile, grads, capacity, padded)
    chips, rows, width = arrived.shape
    by_slot = dot(pick[...], arrived[...].reshape(chips * rows, width)).astype(bf16)
    column = lax.axis_index("exp")
    for step in range(sent.shape[0]):
        sent[jnp.bitwise_xor(column, step)] = by_slot[step * padded : step * padded + capacity]


def pick_last_kernel(capacity, padded, chips, pick, *refs):
    arrived, sent = refs[:chips], refs[chips:]
    rows = jnp.concatenate([block[...] for block in arrived], axis=0)
    by_slot = dot(pick[...], rows).astype(bf16)
    for step in range(len(sent)):
        sent[step][...] = by_slot[step * padded : step * padded + capacity]


def fill(tile, blocks, capacity, padded):
    tile[...] = jnp.zeros(tile.shape, tile.dtype)
    for step, block in enumerate(blocks):
        tile[step * padded : step * padded + capacity, :] = block[...]


def partial_kernel(capacity, padded, gate, down, arrived, tile, pre_act, adapted):
    column = lax.axis_index("exp")
    tile[...] = jnp.zeros(tile.shape, tile.dtype)
    for step in range(arrived.shape[0]):
        tile[step * padded : step * padded + capacity, :] = arrived[jnp.bitwise_xor(column, step)]
    part = part_of(0, tile.shape[1])
    pre_act[...] = dot(tile[...], gate[0, part])
    adapted[...] = dot(tile[...], down[0, part])


def finish_kernel(
    capacity, padded, exp_count, grad_tile, first, pre_first, adapted_first, gate, down, up, *refs
):
    blocks, refs = refs[:exp_count], refs[exp_count:]
    activated, refs = refs[:exp_count], refs[exp_count:]
    keep, give, tile, down_term, up_term = refs
    fill(tile, blocks, capacity, padded)
    part = part_of(1, tile.shape[1])
    adapted = (adapted_first[...] + dot(tile[...], down[0, part])).astype(bf16)
    pre_act = pre_first[...] + dot(tile[...], gate[0, part]) + dot(adapted, up[0])
    gate_value = jax.nn.sigmoid(pre_act)
    rows = (pre_act * gate_value).astype(bf16)
    for step in range(exp_count):
        activated[step][...] = rows[step * padded : step * padded + capacity]
    slope = gate_value * (1.0 + pre_act * (1.0 - gate_value))
    grad_pre = (grad_tile[...].astype(f32) * slope).astype(bf16)
    back = dot(grad_pre, up[0], ((1,), (1,))).astype(bf16)
    pairs = keep.shape[0]
    down_rows = down_term.shape[1]
    up_rows, hidden_units = up_term.shape[1:]
    lanes = keep.shape[2]
    by_owner = first.shape[1] // down_rows
    for half, rows in enumerate((first, tile)):
        part = dot(rows[...], back, ((0,), (0,)))
        for number in range(by_owner):
            down_term[half * by_owner + number] = part[number * down_rows : (number + 1) * down_rows]
    part = dot(adapted, grad_pre, ((0,), (0,)))
    for number in range(2 * pairs):
        up_term[number] = part[number * up_rows : (number + 1) * up_rows]

    replica = lax.axis_index("rep")
    for chip in range(pairs):
        for flip, target in ((0, keep), (1, give)):
            owner = jnp.bitwise_xor(replica, 2 * chip + flip)
            target[chip, :down_rows] = down_term[owner].astype(target.dtype)
            mine = up_term[owner].astype(target.dtype)
            for part in range(hidden_units // lanes):
                base = down_rows + part * up_rows
                target[chip, base : base + up_rows] = mine[:, part * lanes : (part + 1) * lanes]


def combine_kernel(capacity, padded, home, weight, *refs):
    blocks = refs[:-2]
    out, tile = refs[-2:]
    fill(tile, blocks, capacity, padded)
    out[...] = (upright(weight[...]) * dot(home[...], tile[...])).astype(bf16)


def total_kernel(*refs):
    *terms, down_grad, up_grad = refs
    total = terms[0][...].astype(f32)
    for term in terms[1:]:
        total = total + term[...].astype(f32)
    down_rows = down_grad.shape[1]
    up_rows, hidden_units = up_grad.shape[1:]
    lanes = total.shape[1]
    down_grad[0] = total[:down_rows]
    for part in range(hidden_units // lanes):
        base = down_rows + part * up_rows
        up_grad[0, :, part * lanes : (part + 1) * lanes] = total[base : base + up_rows]


def body(
    replay_buffer_rows,
    shard_request_index,
    replica_fetch_count,
    routes,
    router_route_weight,
    output_gradient,
    frozen_gate_weight,
    adapter_down_weight,
    adapter_up_weight,
):
    rep_count = lax.axis_size("rep")
    exp_count = lax.axis_size("exp")
    pairs = rep_count // 2
    token_count = routes.shape[0]
    shard_rows, model_width = replay_buffer_rows.shape
    fetch_slots = shard_request_index.shape[2]
    hidden_units = frozen_gate_weight.shape[2]
    rank_width = adapter_down_weight.shape[2]
    capacity = 7 * token_count // (4 * exp_count)
    padded = -(-capacity // 16) * 16
    slots = exp_count * padded
    fetched_rows = rep_count * fetch_slots
    chunk_width = model_width // CHUNKS

    routes_row = routes.reshape(1, token_count)
    weight_row = router_route_weight.reshape(1, token_count)

    pair_rows = swap_core(replay_buffer_rows, rep_count)
    pair_table = swap_core(shard_request_index, rep_count)
    operands = [shard_request_index, replay_buffer_rows, routes_row, weight_row, output_gradient]
    own_served, *grads = call(
        functools.partial(begin_kernel, capacity, padded),
        [shape((pairs, fetch_slots, chunk_width), bf16)] + [shape((capacity, hidden_units), bf16)] * exp_count,
        operands,
        far=operands,
        flops=2 * token_count * slots * hidden_units,
        name="begin",
    )
    (served,) = call(
        serve_first_kernel,
        [shape((pairs, 2 * fetch_slots, chunk_width), bf16)],
        [pair_table, pair_rows, own_served],
        stored=[0],
        flops=2 * fetched_rows * shard_rows * chunk_width,
        name="serve_first",
    )
    served, *grads, routes_row = lax.optimization_barrier((served, *grads, routes_row))
    arrived = between_chips(served, rep_count)
    grads = [swap_exp(block, step, exp_count) for step, block in enumerate(grads)]
    pick, pick_swapped, home = call(
        functools.partial(prepare_kernel, fetch_slots, capacity, padded, exp_count),
        [shape((slots, fetched_rows), bf16)] * 2 + [shape((token_count, slots), bf16)],
        [replica_fetch_count, routes_row],
        counts=replica_fetch_count,
        stored=[0, 1, 2],
        flops=4 * token_count * slots * fetched_rows,
        name="prepare",
    )
    sent, grad_tile = call(
        functools.partial(pick_first_kernel, capacity, padded),
        [shape((exp_count, capacity, chunk_width), bf16), shape((slots, hidden_units), bf16)],
        [pick, arrived, *grads],
        far=[pick],
        stored=[0, 1],
        flops=2 * slots * fetched_rows * chunk_width,
        name="pick_first",
    )

    pair_rows, sent = lax.optimization_barrier((pair_rows, sent))
    first_blocks = lax.all_to_all(sent, "exp", 0, 0, tiled=True)
    served = call(
        serve_last_kernel,
        [shape((2 * fetch_slots, chunk_width), bf16)] * pairs,
        [shard_request_index, replay_buffer_rows, pair_table, pair_rows],
        far=[shard_request_index, pair_table],
        flops=2 * fetched_rows * shard_rows * chunk_width,
        name="serve_last",
    )
    arrived = [swap_chip(block, step, rep_count) for step, block in enumerate(served)]
    sent = call(
        functools.partial(pick_last_kernel, capacity, padded, pairs),
        [shape((capacity, chunk_width), bf16)] * exp_count,
        [pick_swapped, *arrived],
        flops=2 * slots * fetched_rows * chunk_width,
        name="pick_last",
    )
    last_blocks = [swap_exp(block, step, exp_count) for step, block in enumerate(sent)]

    first, pre_first, adapted_first = call(
        functools.partial(partial_kernel, capacity, padded),
        [shape((slots, chunk_width), bf16), shape((slots, hidden_units), f32), shape((slots, rank_width), f32)],
        [frozen_gate_weight, adapter_down_weight, first_blocks],
        resident=[frozen_gate_weight, adapter_down_weight],
        flops=2 * slots * chunk_width * (hidden_units + rank_width),
        name="partial",
    )

    term_rows = (model_width + rank_width * hidden_units // rank_width) // rep_count
    *activated, keep, give = call(
        functools.partial(finish_kernel, capacity, padded, exp_count),
        [shape((capacity, hidden_units), bf16)] * exp_count + [shape((pairs, term_rows, rank_width), kind) for kind in (f32, bf16)],
        [
            grad_tile,
            first,
            pre_first,
            adapted_first,
            frozen_gate_weight,
            adapter_down_weight,
            adapter_up_weight,
            *last_blocks,
        ],
        resident=[frozen_gate_weight, adapter_down_weight],
        scratch=[
            pltpu.VMEM((slots, chunk_width), bf16),
            pltpu.VMEM((rep_count, model_width // rep_count, rank_width), f32),
            pltpu.VMEM((rep_count, rank_width // rep_count, hidden_units), f32),
        ],
        flops=4 * slots * chunk_width * (hidden_units + rank_width),
        name="finish",
    )

    pair_terms = swap_core(give, rep_count)
    results = [swap_exp(block, step, exp_count) for step, block in enumerate(activated)]
    terms = keep + pair_terms.astype(f32)
    while terms.shape[0] > 2:
        half = terms.shape[0] // 2
        terms = terms[:half] + swap_chip(terms[half:].astype(bf16), half, rep_count).astype(f32)
    last_terms = [terms[0], swap_chip(terms[1].astype(bf16), 1, rep_count)]

    down_grad, up_grad = call(
        total_kernel,
        [
            shape((1, model_width // rep_count, rank_width), f32),
            shape((1, rank_width // rep_count, hidden_units), f32),
        ],
        last_terms,
        name="total",
    )
    down_grad, *results = lax.optimization_barrier((down_grad, *results))
    (out_rows,) = call(
        functools.partial(combine_kernel, capacity, padded),
        [shape((token_count, hidden_units), bf16)],
        [home, weight_row, *results],
        scratch=[pltpu.VMEM((slots, hidden_units), bf16)],
        flops=2 * token_count * slots * hidden_units,
        name="combine",
    )
    return (out_rows, down_grad, up_grad)


def solution(mesh):
    placed = (
        P(("rep", "exp"), None),
        P(("rep", "exp"), None, None),
        P(("rep", "exp"), None),
        P(("rep", "exp"), None),
        P(("rep", "exp"), None),
        P(("rep", "exp"), None),
        P("exp", None, None),
        P("exp", None, None),
        P("exp", None, None),
    )
    return jax.shard_map(
        body,
        mesh=mesh,
        in_specs=placed,
        out_specs=(P(("rep", "exp"), None), P("exp", "rep", None), P("exp", "rep", None)),
        check_vma=False,
    )
```

time: 94.9 us -> 87.8 us (0.925)
  waiting for transfers between devices: 40.9 us -> 33.9 us
  starting transfers between devices: 37.6 us -> 31.5 us
  Pallas kernels: 13.1 us -> 17.1 us
  local copies, waits for them, and re-layouts: 2.17 us -> 3.9 us
    ppermute x12 -> x9, waiting for transfers between devices: 32.3 us -> 13.8 us  [swap_exp(): return lax.ppermute(block, 'exp', [(i, i ^ step) for i in range(exp_count)])]
    all_to_all x0 -> x2, starting transfers between devices: none -> 9.32 us  [the longest x1 5.09 us: between_chips(): lax.all_to_all(blocks, 'rep', 0, 0, axis_index_groups=cores, tiled=True)]
    ppermute x12 -> x8, starting transfers between devices: 15.2 us -> 7.28 us  [the longest x5 6.61 us: swap_chip(): lax.ppermute(block, 'rep', [(i, i ^ 2 * step) for i in range(rep_count)])]
    ppermute x12 -> x8, waiting for transfers between devices: 8.59 us -> 16 us  [the longest x5 13.9 us: swap_chip(): lax.ppermute(block, 'rep', [(i, i ^ 2 * step) for i in range(rep_count)])]
    ppermute x12 -> x9, starting transfers between devices: 22.4 us -> 14.9 us  [swap_exp(): return lax.ppermute(block, 'exp', [(i, i ^ step) for i in range(exp_count)])]
    all_to_all x0 -> x2, waiting for transfers between devices: none -> 4.09 us  [the longest x1 4.09 us: body(): first_blocks = lax.all_to_all(sent, 'exp', 0, 0, tiled=True)]
    pallas_call x9 -> x10, Pallas kernels: 13.1 us -> 17.1 us  [call(): pl.pallas_call(moving, out_shape=[pltpu.HBM(out.shape, out.dtype) if numb...]
    unnamed x18 -> x28, local copies, waits for them, and re-layouts: 2.13 us -> 3.82 us
  transfers between devices with their start and end apart: 24 -> 19, of which waited for: 10 -> 10; matrix products, arithmetic and copies ran while one was open for 0% -> 0% of each run, Pallas kernels for 7% -> 10%
where the time goes in v3:
time: 87.8 us; the launch traced here: 87.5 us
  waiting for transfers between devices  33.9 us (39%)
  starting transfers between devices  31.5 us (36%)
  Pallas kernels  17.1 us (19%)
  local copies, waits for them, and re-layouts  3.9 us (4%)
    pallas_call x10, Pallas kernels, call(): pl.pallas_call(moving, out_shape=[pltpu.HBM(out.shape, out.dtype) if numb...  17.1 us
    ppermute x9, starting transfers between devices, swap_exp(): return lax.ppermute(block, 'exp', [(i, i ^ step) for i in range(exp_count)])  14.9 us
    ppermute x5, waiting for transfers between devices, swap_chip(): lax.ppermute(block, 'rep', [(i, i ^ 2 * step) for i in range(rep_count)])  13.9 us
    ppermute x9, waiting for transfers between devices, swap_exp(): return lax.ppermute(block, 'exp', [(i, i ^ step) for i in range(exp_count)])  13.8 us
    ppermute x5, starting transfers between devices, swap_chip(): lax.ppermute(block, 'rep', [(i, i ^ 2 * step) for i in range(rep_count)])  6.61 us
    all_to_all x1, starting transfers between devices, between_chips(): lax.all_to_all(blocks, 'rep', 0, 0, axis_index_groups=cores, tiled=True)  5.09 us
    all_to_all x1, starting transfers between devices, body(): first_blocks = lax.all_to_all(sent, 'exp', 0, 0, tiled=True)  4.23 us
    all_to_all x1, waiting for transfers between devices, body(): first_blocks = lax.all_to_all(sent, 'exp', 0, 0, tiled=True)  4.09 us
  transfers between devices with their start and end apart: 19, of which 10 were waited for; matrix products, arithmetic and copies ran while one was open for 0% of the time, Pallas kernels for 10%

profile of v3, /device:TPU:0, one launch (start us, length us, event | category | flops | bytes accessed | tf_op | source)
XLA Modules:
  0.0 87.5 jit_solution(9812800608063765546)
XLA Ops:
  0.6 0.5 collective-permute-start.1
  1.1 0.1 collective-permute-start
  1.2 2.1 %begin.1 = (bf16[4,32,1792]{2,1,0:T(8,128)(2,1)S(1)}, bf16[56,1024]{1,0:T(8,128)(2,1)S(1)}, bf16[56,1024]{1,0:T(8,128)(2,1)S(1)}, bf16[56,1024]{1,0:T(8,128)(2,1)S(1)}, bf16[56,1024]{1,0:T(8,128)(2,1)S(1)}) custom-call(s32[1,8,32]{2,1,0:T(8,128)} %refs_0_.7, bf16[128,3584]{1,0:T(8,128)(2,1)} %refs_1_.5, s32[1,128]{1,0:T(1,128)} %bitcast.8, ...), custom_call_target="tpu_custom_call" | custom-call | flops 67108864 | bytes 223696 | tf_op jit(solution)/shard_map/begin/pallas_call | solution.py:63
  3.3 0.1 collective-permute-done.refs_0_.refs_2_
  3.5 0.0 collective-permute-done.1.refs_1_.refs_3_
  3.5 1.3 %serve_first.1 = bf16[4,64,1792]{2,1,0:T(8,128)(2,1)} custom-call(s32[1,8,32]{2,1,0:T(8,128)S(1)} %collective-permute-done.refs_0_.refs_2_, bf16[128,3584]{1,0:T(8,128)(2,1)S(1)} %collective-permute-done.1.refs_1_.refs_3_, bf16[4,32,1792]{2,1,0:T(8,128)(2,1)S(1)} %get-tuple-element.45.refs_2_), custom_call_target="tpu_custom_call" | custom-call | flops 117440512 | bytes 391468 | tf_op jit(solution)/shard_map/serve_first/pallas_call | solution.py:63
  4.8 0.0 copy-done.10
  4.8 0.0 copy-start.12
  4.8 0.0 copy-start.13
  4.9 5.1 %all-to-all-start = ((bf16[4,64,1792]{2,1,0:T(8,128)(2,1)}), bf16[4,64,1792]{2,1,0:T(8,128)(2,1)S(1)}, u32[]{:S(2)}, u32[]{:S(2)}) async-start(bf16[4,64,1792]{2,1,0:T(8,128)(2,1)} %serve_first.1), calls=%async_computation | async-start | bytes 1835008 | tf_op jit(solution)/shard_map/all_to_all | solution.py:100
  9.9 1.6 %collective-permute-start.2 = (bf16[56,1024]{1,0:T(8,128)(2,1)S(1)}, bf16[56,1024]{1,0:T(8,128)(2,1)S(1)}, u32[]{:S(2)}, u32[]{:S(2)}) collective-permute-start(bf16[56,1024]{1,0:T(8,128)(2,1)S(1)} %get-tuple-element.55), channel_id=1, source_target_pairs={{0,1},{1,0},{2,3},{3,2},{4,5},{5,4},{6,7},{7,6},{8,9},{9,8},{10,11... | collective-permute-start | bytes 344072 | tf_op jit(solution)/shard_map/ppermute | solution.py:85
  11.5 2.6 %collective-permute-start.3 = (bf16[56,1024]{1,0:T(8,128)(2,1)S(1)}, bf16[56,1024]{1,0:T(8,128)(2,1)S(1)}, u32[]{:S(2)}, u32[]{:S(2)}) collective-permute-start(bf16[56,1024]{1,0:T(8,128)(2,1)S(1)} %get-tuple-element.56), channel_id=1, source_target_pairs={{0,2},{1,3},{2,0},{3,1},{4,6},{5,7},{6,4},{7,5},{8,10},{9,11},{10,... | collective-permute-start | bytes 344072 | tf_op jit(solution)/shard_map/ppermute | solution.py:85
  14.1 0.2 collective-permute-start.4
  14.3 0.0 copy-done.12
  14.3 0.0 copy-done.13
  14.3 1.9 %prepare.1 = (bf16[256,256]{1,0:T(8,128)(2,1)}, bf16[256,256]{1,0:T(8,128)(2,1)}, bf16[128,256]{1,0:T(8,128)(2,1)}) custom-call(s32[1,8]{1,0:T(1,128)S(1)} %copy-done.13, s32[1,128]{1,0:T(1,128)S(1)} %bitcast.9), custom_call_target="tpu_custom_call" | custom-call | flops 33554432 | bytes 111848 | tf_op jit(solution)/shard_map/prepare/pallas_call | solution.py:63
  16.2 0.0 collective-permute-done.2.refs_3_
  16.2 7.1 %collective-permute-done.3.refs_4_ = bf16[56,1024]{1,0:T(8,128)(2,1)S(1)} collective-permute-done((bf16[56,1024]{1,0:T(8,128)(2,1)S(1)}, bf16[56,1024]{1,0:T(8,128)(2,1)S(1)}, u32[]{:S(2)}, u32[]{:S(2)}) %collective-permute-start.3) | collective-permute-done | bytes 114720 | tf_op jit(solution)/shard_map/ppermute | solution.py:85
  23.4 0.0 collective-permute-done.4.refs_5_
  23.4 0.0 all-to-all-done.refs_1_
  23.4 2.4 %pick_first.1 = (bf16[4,56,1792]{2,1,0:T(8,128)(2,1)}, bf16[256,1024]{1,0:T(8,128)(2,1)}) custom-call(bf16[256,256]{1,0:T(8,128)(2,1)} %get-tuple-element.52.refs_0_, bf16[4,64,1792]{2,1,0:T(8,128)(2,1)S(1)} %all-to-all-done.refs_1_, bf16[56,1024]{1,0:T(8,128)(2,1)S(1)} %get-tuple-element.54.refs_2_, bf16[56,1024]{1,0:T(8,128)(2,1)S(1)} %collective-permute-done.2.refs_3_, ...), custom_call_target="tpu_custom_call" | custom-call | flops 234881024 | bytes 782936 | tf_op jit(solution)/shard_map/pick_first/pallas_call | solution.py:63
  25.8 0.0 copy-start.3
  25.8 4.2 %all-to-all-start.1 = ((bf16[4,56,1792]{2,1,0:T(8,128)(2,1)}), bf16[4,56,1792]{2,1,0:T(8,128)(2,1)S(1)}, u32[]{:S(2)}, u32[]{:S(2)}) async-start(bf16[4,56,1792]{2,1,0:T(8,128)(2,1)} %get-tuple-element.60), calls=%async_computation.1 | async-start | bytes 1605632 | tf_op jit(solution)/shard_map/all_to_all | solution.py:357
  30.1 0.0 copy-done.3
  30.1 1.3 %serve_last.1 = (bf16[64,1792]{1,0:T(8,128)(2,1)S(1)}, bf16[64,1792]{1,0:T(8,128)(2,1)S(1)}, bf16[64,1792]{1,0:T(8,128)(2,1)S(1)}, bf16[64,1792]{1,0:T(8,128)(2,1)S(1)}) custom-call(s32[1,8,32]{2,1,0:T(8,128)} %refs_0_.7, bf16[128,3584]{1,0:T(8,128)(2,1)S(1)} %copy-done.3, s32[1,8,32]{2,1,0:T(8,128)} %copy-done.10, ...), custom_call_target="tpu_custom_call" | custom-call | flops 117440512 | bytes 391468 | tf_op jit(solution)/shard_map/serve_last/pallas_call | solution.py:63
  31.4 1.7 %collective-permute-start.5 = (bf16[64,1792]{1,0:T(8,128)(2,1)S(1)}, bf16[64,1792]{1,0:T(8,128)(2,1)S(1)}, u32[]{:S(2)}, u32[]{:S(2)}) collective-permute-start(bf16[64,1792]{1,0:T(8,128)(2,1)S(1)} %get-tuple-element.67), channel_id=1, source_target_pairs={{0,8},{4,12},{8,0},{12,4},{16,24},{20,28},{24,16},{28,20},{1,9},{5... | collective-permute-start | bytes 688136 | tf_op jit(solution)/shard_map/ppermute | solution.py:95
  33.1 1.5 %collective-permute-start.6 = (bf16[64,1792]{1,0:T(8,128)(2,1)S(1)}, bf16[64,1792]{1,0:T(8,128)(2,1)S(1)}, u32[]{:S(2)}, u32[]{:S(2)}) collective-permute-start(bf16[64,1792]{1,0:T(8,128)(2,1)S(1)} %get-tuple-element.68), channel_id=1, source_target_pairs={{0,16},{4,20},{8,24},{12,28},{16,0},{20,4},{24,8},{28,12},{1,17},{... | collective-permute-start | bytes 688136 | tf_op jit(solution)/shard_map/ppermute | solution.py:95
  34.6 0.4 collective-permute-start.7
  35.0 5.1 %collective-permute-done.5.refs_2_ = bf16[64,1792]{1,0:T(8,128)(2,1)S(1)} collective-permute-done((bf16[64,1792]{1,0:T(8,128)(2,1)S(1)}, bf16[64,1792]{1,0:T(8,128)(2,1)S(1)}, u32[]{:S(2)}, u32[]{:S(2)}) %collective-permute-start.5) | collective-permute-done | bytes 229408 | tf_op jit(solution)/shard_map/ppermute | solution.py:95
  40.0 3.8 %collective-permute-done.6.refs_3_ = bf16[64,1792]{1,0:T(8,128)(2,1)S(1)} collective-permute-done((bf16[64,1792]{1,0:T(8,128)(2,1)S(1)}, bf16[64,1792]{1,0:T(8,128)(2,1)S(1)}, u32[]{:S(2)}, u32[]{:S(2)}) %collective-permute-start.6) | collective-permute-done | bytes 229408 | tf_op jit(solution)/shard_map/ppermute | solution.py:95
  43.8 0.0 collective-permute-done.7.refs_4_
  43.8 0.0 copy-done.8
  43.8 1.2 %pick_last.1 = (bf16[56,1792]{1,0:T(8,128)(2,1)S(1)}, bf16[56,1792]{1,0:T(8,128)(2,1)}, bf16[56,1792]{1,0:T(8,128)(2,1)}, bf16[56,1792]{1,0:T(8,128)(2,1)}) custom-call(bf16[256,256]{1,0:T(8,128)(2,1)S(1)} %copy-done.8, bf16[64,1792]{1,0:T(8,128)(2,1)S(1)} %get-tuple-element.66.refs_1_, bf16[64,1792]{1,0:T(8,128)(2,1)S(1)} %collective-permute-done.5.refs_2_, ...), custom_call_target="tpu_custom_call" | custom-call | flops 234881024 | bytes 782936 | tf_op jit(solution)/shard_map/pick_last/pallas_call | solution.py:63
  45.0 0.7 copy-done.6
  45.7 1.7 %collective-permute-start.8 = (bf16[56,1792]{1,0:T(8,128)(2,1)}, bf16[56,1792]{1,0:T(8,128)(2,1)}, u32[]{:S(2)}, u32[]{:S(2)}) collective-permute-start(bf16[56,1792]{1,0:T(8,128)(2,1)} %get-tuple-element.71), channel_id=1, source_target_pairs={{0,1},{1,0},{2,3},{3,2},{4,5},{5,4},{6,7},{7,6},{8,9},{9,8},{10,11... | collective-permute-start | bytes 602120 | tf_op jit(solution)/shard_map/ppermute | solution.py:85
  47.4 2.4 %collective-permute-start.9 = (bf16[56,1792]{1,0:T(8,128)(2,1)}, bf16[56,1792]{1,0:T(8,128)(2,1)}, u32[]{:S(2)}, u32[]{:S(2)}) collective-permute-start(bf16[56,1792]{1,0:T(8,128)(2,1)} %get-tuple-element.72), channel_id=1, source_target_pairs={{0,2},{1,3},{2,0},{3,1},{4,6},{5,7},{6,4},{7,5},{8,10},{9,11},{10,... | collective-permute-start | bytes 602120 | tf_op jit(solution)/shard_map/ppermute | solution.py:85
  49.8 0.3 collective-permute-start.10
  50.1 4.1 %all-to-all-done.1.refs_2_ = bf16[4,56,1792]{2,1,0:T(8,128)(2,1)S(1)} async-done(((bf16[4,56,1792]{2,1,0:T(8,128)(2,1)}), bf16[4,56,1792]{2,1,0:T(8,128)(2,1)S(1)}, u32[]{:S(2)}, u32[]{:S(2)}) %all-to-all-start.1) | async-done | bytes 802848 | tf_op jit(solution)/shard_map/all_to_all | solution.py:357
  54.1 0.0 copy-done.2
  54.2 3.1 %copy-done = bf16[1,3584,1024]{2,1,0:T(8,128)(2,1)S(1)} copy-done((bf16[1,3584,1024]{2,1,0:T(8,128)(2,1)S(1)}, bf16[1,3584,1024]{2,1,0:T(8,128)(2,1)}, u32[]{:S(2)}) %copy-start) | copy-done | bytes 7340056
  57.2 1.4 %partial.1 = (bf16[256,1792]{1,0:T(8,128)(2,1)S(1)}, f32[256,1024]{1,0:T(8,128)S(1)}, f32[256,128]{1,0:T(8,128)S(1)}) custom-call(bf16[1,3584,1024]{2,1,0:T(8,128)(2,1)S(1)} %copy-done, bf16[1,3584,128]{2,1,0:T(8,128)(2,1)S(1)} %copy-done.2, bf16[4,56,1792]{2,1,0:T(8,128)(2,1)S(1)} %all-to-all-done.1.refs_2_), custom_call_target="tpu_custom_call" | custom-call | flops 1056964608 | bytes 3523215 | tf_op jit(solution)/shard_map/partial/pallas_call | solution.py:63
  58.6 0.0 collective-permute-done.8.refs_8_
  58.6 5.2 %collective-permute-done.9.refs_9_ = bf16[56,1792]{1,0:T(8,128)(2,1)} collective-permute-done((bf16[56,1792]{1,0:T(8,128)(2,1)}, bf16[56,1792]{1,0:T(8,128)(2,1)}, u32[]{:S(2)}, u32[]{:S(2)}) %collective-permute-start.9) | collective-permute-done | bytes 200736 | tf_op jit(solution)/shard_map/ppermute | solution.py:85
  63.8 0.0 collective-permute-done.10.refs_10_
  63.8 0.0 copy-done.1
  63.8 0.0 copy-done.4
  63.9 0.0 copy-done.5
  63.9 3.8 %finish.1 = (bf16[56,1024]{1,0:T(8,128)(2,1)S(1)}, bf16[56,1024]{1,0:T(8,128)(2,1)S(1)}, bf16[56,1024]{1,0:T(8,128)(2,1)S(1)}, bf16[56,1024]{1,0:T(8,128)(2,1)S(...) custom-call(bf16[256,1024]{1,0:T(8,128)(2,1)S(1)} %copy-done.4, ...), custom_call_target="tpu_custom_call" | custom-call | flops 2113929216 | bytes 7046430 | tf_op jit(solution)/shard_map/finish/pallas_call | solution.py:63
  67.6 0.1 collective-permute-start.11
  67.7 2.0 %collective-permute-done.11 = bf16[4,576,128]{2,1,0:T(8,128)(2,1)S(1)} collective-permute-done((bf16[4,576,128]{2,1,0:T(8,128)(2,1)S(1)}, bf16[4,576,128]{2,1,0:T(8,128)(2,1)S(1)}, u32[]{:S(2)}, u32[]{:S(2)}) %collective-permute-start.11) | collective-permute-done | bytes 589856 | tf_op jit(solution)/shard_map/ppermute | solution.py:89
  69.7 0.1 convert_add_fusion
  69.9 1.6 %collective-permute-start.12 = (bf16[2,576,128]{2,1,0:T(8,128)(2,1)S(1)}, bf16[2,576,128]{2,1,0:T(8,128)(2,1)S(1)}, u32[]{:S(2)}, u32[]{:S(2)}) collective-permute-start(bf16[2,576,128]{2,1,0:T(8,128)(2,1)S(1)} %slice.28), channel_id=1, source_target_pairs={{0,16},{4,20},{8,24},{12,28},{16,0},{20,4},{24,8},{28,12},{1,17},{... | collective-permute-start | bytes 884744 | tf_op jit(solution)/shard_map/ppermute | solution.py:95
  71.4 3.8 %collective-permute-start.14 = (bf16[56,1024]{1,0:T(8,128)(2,1)S(1)}, bf16[56,1024]{1,0:T(8,128)(2,1)S(1)}, u32[]{:S(2)}, u32[]{:S(2)}) collective-permute-start(bf16[56,1024]{1,0:T(8,128)(2,1)S(1)} %get-tuple-element.78), channel_id=1, source_target_pairs={{0,1},{1,0},{2,3},{3,2},{4,5},{5,4},{6,7},{7,6},{8,9},{9,8},{10,11... | collective-permute-start | bytes 344072 | tf_op jit(solution)/shard_map/ppermute | solution.py:85
  75.2 0.9 %collective-permute-start.15 = (bf16[56,1024]{1,0:T(8,128)(2,1)S(1)}, bf16[56,1024]{1,0:T(8,128)(2,1)S(1)}, u32[]{:S(2)}, u32[]{:S(2)}) collective-permute-start(bf16[56,1024]{1,0:T(8,128)(2,1)S(1)} %get-tuple-element.79), channel_id=1, source_target_pairs={{0,2},{1,3},{2,0},{3,1},{4,6},{5,7},{6,4},{7,5},{8,10},{9,11},{10,... | collective-permute-start | bytes 344072 | tf_op jit(solution)/shard_map/ppermute | solution.py:85
  76.1 1.5 %collective-permute-start.16 = (bf16[56,1024]{1,0:T(8,128)(2,1)S(1)}, bf16[56,1024]{1,0:T(8,128)(2,1)S(1)}, u32[]{:S(2)}, u32[]{:S(2)}) collective-permute-start(bf16[56,1024]{1,0:T(8,128)(2,1)S(1)} %get-tuple-element.80), channel_id=1, source_target_pairs={{0,3},{1,2},{2,1},{3,0},{4,7},{5,6},{6,5},{7,4},{8,11},{9,10},{10,... | collective-permute-start | bytes 344072 | tf_op jit(solution)/shard_map/ppermute | solution.py:85
  77.6 1.4 %collective-permute-done.12 = bf16[2,576,128]{2,1,0:T(8,128)(2,1)S(1)} collective-permute-done((bf16[2,576,128]{2,1,0:T(8,128)(2,1)S(1)}, bf16[2,576,128]{2,1,0:T(8,128)(2,1)S(1)}, u32[]{:S(2)}, u32[]{:S(2)}) %collective-permute-start.12) | collective-permute-done | bytes 294944 | tf_op jit(solution)/shard_map/ppermute | solution.py:95
  79.0 0.1 slice_add_fusion
  79.1 1.5 %collective-permute-start.13 = (bf16[576,128]{1,0:T(8,128)(2,1)S(1)}, bf16[576,128]{1,0:T(8,128)(2,1)S(1)}, u32[]{:S(2)}, u32[]{:S(2)}) collective-permute-start(bf16[576,128]{1,0:T(8,128)(2,1)S(1)} %fusion), channel_id=1, source_target_pairs={{0,8},{4,12},{8,0},{12,4},{16,24},{20,28},{24,16},{28,20},{1,9},{5... | collective-permute-start | bytes 442376 | tf_op jit(solution)/shard_map/ppermute | solution.py:95
  80.6 3.7 %collective-permute-done.13.refs_1_ = bf16[576,128]{1,0:T(8,128)(2,1)S(1)} collective-permute-done((bf16[576,128]{1,0:T(8,128)(2,1)S(1)}, bf16[576,128]{1,0:T(8,128)(2,1)S(1)}, u32[]{:S(2)}, u32[]{:S(2)}) %collective-permute-start.13) | collective-permute-done | bytes 147488 | tf_op jit(solution)/shard_map/ppermute | solution.py:95
  84.3 0.7 total.1
  85.0 0.0 collective-permute-done.14.refs_3_
  85.0 1.5 %collective-permute-done.15.refs_4_ = bf16[56,1024]{1,0:T(8,128)(2,1)S(1)} collective-permute-done((bf16[56,1024]{1,0:T(8,128)(2,1)S(1)}, bf16[56,1024]{1,0:T(8,128)(2,1)S(1)}, u32[]{:S(2)}, u32[]{:S(2)}) %collective-permute-start.15) | collective-permute-done | bytes 114720 | tf_op jit(solution)/shard_map/ppermute | solution.py:85
  86.5 0.0 collective-permute-done.16.refs_5_
  86.5 0.9 %combine.1 = bf16[128,1024]{1,0:T(8,128)(2,1)} custom-call(bf16[128,256]{1,0:T(8,128)(2,1)S(1)} %copy-done.9, f32[1,128]{1,0:T(1,128)S(1)} %bitcast.7, bf16[56,1024]{1,0:T(8,128)(2,1)S(1)} %get-tuple-element.81.refs_2_, bf16[56,1024]{1,0:T(8,128)(2,1)S(1)} %collective-permute-done.14.refs_3_, bf16[56,1024]{1,0:T(8,128)(2,1)S(1)} %collective-permute-done.15.refs_4_, ...), custom_call_target="tpu_custom_call" | custom-call | flops 67108864 | bytes 223696 | tf_op jit(solution)/shard_map/combine/pallas_call | solution.py:63
  (17 shorter events, 0.1 us)
Async XLA Ops:
  0.6 2.8 %collective-permute-start.1 = (bf16[128,3584]{1,0:T(8,128)(2,1)}, bf16[128,3584]{1,0:T(8,128)(2,1)S(1)}, u32[]{:S(2)}, u32[]{:S(2)}) collective-permute-start(bf16[128,3584]{1,0:T(8,128)(2,1)} %refs_1_.5), channel_id=1, source_target_pairs={{0,4},{4,0},{8,12},{12,8},{16,20},{20,16},{24,28},{28,24},{1,5},{5... | collective-permute-start | bytes 2752520 | tf_op jit(solution)/shard_map/ppermute | solution.py:89
  1.1 2.3 %collective-permute-start = (s32[1,8,32]{2,1,0:T(8,128)}, s32[1,8,32]{2,1,0:T(8,128)S(1)}, u32[]{:S(2)}, u32[]{:S(2)}) collective-permute-start(s32[1,8,32]{2,1,0:T(8,128)} %refs_0_.7), channel_id=1, source_target_pairs={{0,4},{4,0},{8,12},{12,8},{16,20},{20,16},{24,28},{28,24},{1,5},{5... | collective-permute-start | bytes 3080 | tf_op jit(solution)/shard_map/ppermute | solution.py:89
  3.5 1.4 %copy-start.10 = (s32[1,8,32]{2,1,0:T(8,128)}, s32[1,8,32]{2,1,0:T(8,128)S(1)}, u32[]{:S(2)}) copy-start(s32[1,8,32]{2,1,0:T(8,128)S(1)} %collective-permute-done.refs_0_.refs_2_) | copy-start | bytes 3076
  4.8 9.5 %copy-start.12 = (s32[128,1]{0,1:T(1,128)S(1)}, s32[128,1]{0,1:T(1,128)}, u32[]{:S(2)}) copy-start(s32[128,1]{0,1:T(1,128)} %param.12) | copy-start | bytes 1540
  4.8 9.5 %copy-start.13 = (s32[1,8]{1,0:T(1,128)S(1)}, s32[1,8]{1,0:T(1,128)}, u32[]{:S(2)}) copy-start(s32[1,8]{1,0:T(1,128)} %refs_0_.5) | copy-start | bytes 100
  4.9 18.5 %all-to-all-start = ((bf16[4,64,1792]{2,1,0:T(8,128)(2,1)}), bf16[4,64,1792]{2,1,0:T(8,128)(2,1)S(1)}, u32[]{:S(2)}, u32[]{:S(2)}) async-start(bf16[4,64,1792]{2,1,0:T(8,128)(2,1)} %serve_first.1), calls=%async_computation | async-start | bytes 1835008 | tf_op jit(solution)/shard_map/all_to_all | solution.py:100
  9.9 6.3 %collective-permute-start.2 = (bf16[56,1024]{1,0:T(8,128)(2,1)S(1)}, bf16[56,1024]{1,0:T(8,128)(2,1)S(1)}, u32[]{:S(2)}, u32[]{:S(2)}) collective-permute-start(bf16[56,1024]{1,0:T(8,128)(2,1)S(1)} %get-tuple-element.55), channel_id=1, source_target_pairs={{0,1},{1,0},{2,3},{3,2},{4,5},{5,4},{6,7},{7,6},{8,9},{9,8},{10,11... | collective-permute-start | bytes 344072 | tf_op jit(solution)/shard_map/ppermute | solution.py:85
  11.5 11.8 %collective-permute-start.3 = (bf16[56,1024]{1,0:T(8,128)(2,1)S(1)}, bf16[56,1024]{1,0:T(8,128)(2,1)S(1)}, u32[]{:S(2)}, u32[]{:S(2)}) collective-permute-start(bf16[56,1024]{1,0:T(8,128)(2,1)S(1)} %get-tuple-element.56), channel_id=1, source_target_pairs={{0,2},{1,3},{2,0},{3,1},{4,6},{5,7},{6,4},{7,5},{8,10},{9,11},{10,... | collective-permute-start | bytes 344072 | tf_op jit(solution)/shard_map/ppermute | solution.py:85
  14.1 9.3 %collective-permute-start.4 = (bf16[56,1024]{1,0:T(8,128)(2,1)S(1)}, bf16[56,1024]{1,0:T(8,128)(2,1)S(1)}, u32[]{:S(2)}, u32[]{:S(2)}) collective-permute-start(bf16[56,1024]{1,0:T(8,128)(2,1)S(1)} %get-tuple-element.57), channel_id=1, source_target_pairs={{0,3},{1,2},{2,1},{3,0},{4,7},{5,6},{6,5},{7,4},{8,11},{9,10},{10,... | collective-permute-start | bytes 344072 | tf_op jit(solution)/shard_map/ppermute | solution.py:85
  25.8 4.2 %copy-start.3 = (bf16[128,3584]{1,0:T(8,128)(2,1)S(1)}, bf16[128,3584]{1,0:T(8,128)(2,1)}, u32[]{:S(2)}) copy-start(bf16[128,3584]{1,0:T(8,128)(2,1)} %refs_1_.5) | copy-start | bytes 2752516
  25.8 28.3 %all-to-all-start.1 = ((bf16[4,56,1792]{2,1,0:T(8,128)(2,1)}), bf16[4,56,1792]{2,1,0:T(8,128)(2,1)S(1)}, u32[]{:S(2)}, u32[]{:S(2)}) async-start(bf16[4,56,1792]{2,1,0:T(8,128)(2,1)} %get-tuple-element.60), calls=%async_computation.1 | async-start | bytes 1605632 | tf_op jit(solution)/shard_map/all_to_all | solution.py:357
  30.1 13.7 %copy-start.8 = (bf16[256,256]{1,0:T(8,128)(2,1)S(1)}, bf16[256,256]{1,0:T(8,128)(2,1)}, u32[]{:S(2)}) copy-start(bf16[256,256]{1,0:T(8,128)(2,1)} %get-tuple-element.64.refs_0_) | copy-start | bytes 393220
  30.1 24.1 %copy-start.2 = (bf16[1,3584,128]{2,1,0:T(8,128)(2,1)S(1)}, bf16[1,3584,128]{2,1,0:T(8,128)(2,1)}, u32[]{:S(2)}) copy-start(bf16[1,3584,128]{2,1,0:T(8,128)(2,1)} %refs_5_.1) | copy-start | bytes 2752516
  31.4 8.6 %collective-permute-start.5 = (bf16[64,1792]{1,0:T(8,128)(2,1)S(1)}, bf16[64,1792]{1,0:T(8,128)(2,1)S(1)}, u32[]{:S(2)}, u32[]{:S(2)}) collective-permute-start(bf16[64,1792]{1,0:T(8,128)(2,1)S(1)} %get-tuple-element.67), channel_id=1, source_target_pairs={{0,8},{4,12},{8,0},{12,4},{16,24},{20,28},{24,16},{28,20},{1,9},{5... | collective-permute-start | bytes 688136 | tf_op jit(solution)/shard_map/ppermute | solution.py:95
  33.1 10.7 %collective-permute-start.6 = (bf16[64,1792]{1,0:T(8,128)(2,1)S(1)}, bf16[64,1792]{1,0:T(8,128)(2,1)S(1)}, u32[]{:S(2)}, u32[]{:S(2)}) collective-permute-start(bf16[64,1792]{1,0:T(8,128)(2,1)S(1)} %get-tuple-element.68), channel_id=1, source_target_pairs={{0,16},{4,20},{8,24},{12,28},{16,0},{20,4},{24,8},{28,12},{1,17},{... | collective-permute-start | bytes 688136 | tf_op jit(solution)/shard_map/ppermute | solution.py:95
  34.6 9.2 %collective-permute-start.7 = (bf16[64,1792]{1,0:T(8,128)(2,1)S(1)}, bf16[64,1792]{1,0:T(8,128)(2,1)S(1)}, u32[]{:S(2)}, u32[]{:S(2)}) collective-permute-start(bf16[64,1792]{1,0:T(8,128)(2,1)S(1)} %get-tuple-element.69), channel_id=1, source_target_pairs={{0,24},{4,28},{8,16},{12,20},{16,8},{20,12},{24,0},{28,4},{1,25},{... | collective-permute-start | bytes 688136 | tf_op jit(solution)/shard_map/ppermute | solution.py:95
  45.0 0.7 copy-start.6
  45.7 13.0 %collective-permute-start.8 = (bf16[56,1792]{1,0:T(8,128)(2,1)}, bf16[56,1792]{1,0:T(8,128)(2,1)}, u32[]{:S(2)}, u32[]{:S(2)}) collective-permute-start(bf16[56,1792]{1,0:T(8,128)(2,1)} %get-tuple-element.71), channel_id=1, source_target_pairs={{0,1},{1,0},{2,3},{3,2},{4,5},{5,4},{6,7},{7,6},{8,9},{9,8},{10,11... | collective-permute-start | bytes 602120 | tf_op jit(solution)/shard_map/ppermute | solution.py:85
  47.4 16.4 %collective-permute-start.9 = (bf16[56,1792]{1,0:T(8,128)(2,1)}, bf16[56,1792]{1,0:T(8,128)(2,1)}, u32[]{:S(2)}, u32[]{:S(2)}) collective-permute-start(bf16[56,1792]{1,0:T(8,128)(2,1)} %get-tuple-element.72), channel_id=1, source_target_pairs={{0,2},{1,3},{2,0},{3,1},{4,6},{5,7},{6,4},{7,5},{8,10},{9,11},{10,... | collective-permute-start | bytes 602120 | tf_op jit(solution)/shard_map/ppermute | solution.py:85
  49.8 14.1 %collective-permute-start.10 = (bf16[56,1792]{1,0:T(8,128)(2,1)}, bf16[56,1792]{1,0:T(8,128)(2,1)}, u32[]{:S(2)}, u32[]{:S(2)}) collective-permute-start(bf16[56,1792]{1,0:T(8,128)(2,1)} %get-tuple-element.73), channel_id=1, source_target_pairs={{0,3},{1,2},{2,1},{3,0},{4,7},{5,6},{6,5},{7,4},{8,11},{9,10},{10,... | collective-permute-start | bytes 602120 | tf_op jit(solution)/shard_map/ppermute | solution.py:85
  54.2 3.1 %copy-start = (bf16[1,3584,1024]{2,1,0:T(8,128)(2,1)S(1)}, bf16[1,3584,1024]{2,1,0:T(8,128)(2,1)}, u32[]{:S(2)}) copy-start(bf16[1,3584,1024]{2,1,0:T(8,128)(2,1)} %refs_4_.3) | copy-start | bytes 22020100
  57.2 6.6 %copy-start.1 = (bf16[1,3584,1024]{2,1,0:T(8,128)(2,1)S(1)}, bf16[1,3584,1024]{2,1,0:T(8,128)(2,1)}, u32[]{:S(2)}) copy-start(bf16[1,3584,1024]{2,1,0:T(8,128)(2,1)} %refs_4_.3) | copy-start | bytes 22020100
  57.2 6.6 %copy-start.4 = (bf16[256,1024]{1,0:T(8,128)(2,1)S(1)}, bf16[256,1024]{1,0:T(8,128)(2,1)}, u32[]{:S(2)}) copy-start(bf16[256,1024]{1,0:T(8,128)(2,1)} %get-tuple-element.58.refs_0_) | copy-start | bytes 1572868
  57.2 6.6 %copy-start.5 = (bf16[1,128,1024]{2,1,0:T(8,128)(2,1)S(1)}, bf16[1,128,1024]{2,1,0:T(8,128)(2,1)}, u32[]{:S(2)}) copy-start(bf16[1,128,1024]{2,1,0:T(8,128)(2,1)} %refs_6_.1) | copy-start | bytes 786436
  57.2 6.6 %copy-start.7 = (bf16[56,1792]{1,0:T(8,128)(2,1)S(1)}, bf16[56,1792]{1,0:T(8,128)(2,1)}, u32[]{:S(2)}) copy-start(bf16[56,1792]{1,0:T(8,128)(2,1)} %copy-done.6) | copy-start | bytes 602116
  67.6 2.1 %collective-permute-start.11 = (bf16[4,576,128]{2,1,0:T(8,128)(2,1)S(1)}, bf16[4,576,128]{2,1,0:T(8,128)(2,1)S(1)}, u32[]{:S(2)}, u32[]{:S(2)}) collective-permute-start(bf16[4,576,128]{2,1,0:T(8,128)(2,1)S(1)} %get-tuple-element.75), channel_id=1, source_target_pairs={{0,4},{4,0},{8,12},{12,8},{16,20},{20,16},{24,28},{28,24},{1,5},{5... | collective-permute-start | bytes 1769480 | tf_op jit(solution)/shard_map/ppermute | solution.py:89
  69.9 9.1 %collective-permute-start.12 = (bf16[2,576,128]{2,1,0:T(8,128)(2,1)S(1)}, bf16[2,576,128]{2,1,0:T(8,128)(2,1)S(1)}, u32[]{:S(2)}, u32[]{:S(2)}) collective-permute-start(bf16[2,576,128]{2,1,0:T(8,128)(2,1)S(1)} %slice.28), channel_id=1, source_target_pairs={{0,16},{4,20},{8,24},{12,28},{16,0},{20,4},{24,8},{28,12},{1,17},{... | collective-permute-start | bytes 884744 | tf_op jit(solution)/shard_map/ppermute | solution.py:95
  71.4 13.6 %collective-permute-start.14 = (bf16[56,1024]{1,0:T(8,128)(2,1)S(1)}, bf16[56,1024]{1,0:T(8,128)(2,1)S(1)}, u32[]{:S(2)}, u32[]{:S(2)}) collective-permute-start(bf16[56,1024]{1,0:T(8,128)(2,1)S(1)} %get-tuple-element.78), channel_id=1, source_target_pairs={{0,1},{1,0},{2,3},{3,2},{4,5},{5,4},{6,7},{7,6},{8,9},{9,8},{10,11... | collective-permute-start | bytes 344072 | tf_op jit(solution)/shard_map/ppermute | solution.py:85
  75.2 11.3 %collective-permute-start.15 = (bf16[56,1024]{1,0:T(8,128)(2,1)S(1)}, bf16[56,1024]{1,0:T(8,128)(2,1)S(1)}, u32[]{:S(2)}, u32[]{:S(2)}) collective-permute-start(bf16[56,1024]{1,0:T(8,128)(2,1)S(1)} %get-tuple-element.79), channel_id=1, source_target_pairs={{0,2},{1,3},{2,0},{3,1},{4,6},{5,7},{6,4},{7,5},{8,10},{9,11},{10,... | collective-permute-start | bytes 344072 | tf_op jit(solution)/shard_map/ppermute | solution.py:85
  76.1 10.4 %copy-start.9 = (bf16[128,256]{1,0:T(8,128)(2,1)S(1)}, bf16[128,256]{1,0:T(8,128)(2,1)}, u32[]{:S(2)}) copy-start(bf16[128,256]{1,0:T(8,128)(2,1)} %get-tuple-element.51.refs_0_) | copy-start | bytes 196612
  76.1 10.4 %copy-start.11 = (f32[128,1]{0,1:T(1,128)S(1)}, f32[128,1]{0,1:T(1,128)}, u32[]{:S(2)}) copy-start(f32[128,1]{0,1:T(1,128)} %param.13) | copy-start | bytes 1540
  76.1 10.4 %collective-permute-start.16 = (bf16[56,1024]{1,0:T(8,128)(2,1)S(1)}, bf16[56,1024]{1,0:T(8,128)(2,1)S(1)}, u32[]{:S(2)}, u32[]{:S(2)}) collective-permute-start(bf16[56,1024]{1,0:T(8,128)(2,1)S(1)} %get-tuple-element.80), channel_id=1, source_target_pairs={{0,3},{1,2},{2,1},{3,0},{4,7},{5,6},{6,5},{7,4},{8,11},{9,10},{10,... | collective-permute-start | bytes 344072 | tf_op jit(solution)/shard_map/ppermute | solution.py:85
  79.1 5.2 %collective-permute-start.13 = (bf16[576,128]{1,0:T(8,128)(2,1)S(1)}, bf16[576,128]{1,0:T(8,128)(2,1)S(1)}, u32[]{:S(2)}, u32[]{:S(2)}) collective-permute-start(bf16[576,128]{1,0:T(8,128)(2,1)S(1)} %fusion), channel_id=1, source_target_pairs={{0,8},{4,12},{8,0},{12,4},{16,24},{20,28},{24,16},{28,20},{1,9},{5... | collective-permute-start | bytes 442376 | tf_op jit(solution)/shard_map/ppermute | solution.py:95

commit v4 on v3

v4 whole, which is shorter than its diff:
```python
import functools

import jax
import jax.numpy as jnp
from jax import lax
from jax.experimental import pallas as pl
from jax.experimental.pallas import tpu as pltpu
from jax.sharding import PartitionSpec as P

FIRST_PART = 1
PARTS = 2
bf16 = jnp.bfloat16
f32 = jnp.float32
i32 = jnp.int32


def dot(a, b, contract=((1,), (0,))):
    return lax.dot_general(a, b, (contract, ((), ())), preferred_element_type=f32)


def call(kernel, out_shape, operands, counts=None, resident=(), far=(), stored=(), scratch=(), flops=0, vmem=16, name=None):
    first_out = len(operands)
    away = [number for number, array in enumerate(operands) if any(array is other for other in far)]
    moved = [*away, *(first_out + number for number in stored)]
    arrays = [*operands, *out_shape]

    def moving(*refs):
        inner = list(refs)
        copies = {}
        if moved:
            *inner, sems = inner
            near = inner[len(inner) - len(moved) :]
            inner = inner[: len(inner) - len(moved)]
            for place, number in enumerate(moved):
                ends = (inner[number], near[place]) if number < first_out else (near[place], inner[number])
                copies[number] = pltpu.make_async_copy(*ends, sems.at[place])
                inner[number] = near[place]
        for number in away:
            copies[number].start()
        for number in away:
            copies[number].wait()
        kernel(*inner)
        for number in moved[len(away) :]:
            copies[number].start()
        for number in moved[len(away) :]:
            copies[number].wait()

    def space(number):
        array = arrays[number]
        zeros = (0,) * len(array.shape)
        if number in moved:
            return pl.BlockSpec(memory_space=pltpu.HBM)
        if any(array is other for other in resident):
            return pl.BlockSpec(memory_space=pltpu.VMEM)
        if array is counts:
            return pl.BlockSpec(memory_space=pltpu.SMEM)
        return pl.BlockSpec(array.shape, lambda i: zeros)

    near = [pltpu.VMEM(arrays[number].shape, arrays[number].dtype) for number in moved]
    operands = [
        pltpu.with_memory_space_constraint(array, pltpu.HBM) if number in away else array
        for number, array in enumerate(operands)
    ]
    return pl.pallas_call(
        moving,
        out_shape=[
            pltpu.HBM(out.shape, out.dtype) if number in stored else out for number, out in enumerate(out_shape)
        ],
        grid=(1,),
        in_specs=[space(number) for number in range(first_out)],
        out_specs=[space(first_out + number) for number in range(len(out_shape))],
        scratch_shapes=[*scratch, *near] + ([pltpu.SemaphoreType.DMA((len(moved),))] if moved else []),
        cost_estimate=pl.CostEstimate(flops=flops, bytes_accessed=flops // 300, transcendentals=0),
        compiler_params=pltpu.CompilerParams(vmem_limit_bytes=vmem * 1024 * 1024),
        name=name,
    )(*operands)


def shape(dims, kind):
    return jax.ShapeDtypeStruct(dims, kind)


def swap_exp(block, step, exp_count):
    if step == 0:
        return block
    return lax.ppermute(block, "exp", [(i, i ^ step) for i in range(exp_count)])


def swap_core(block, rep_count):
    return lax.ppermute(block, "rep", [(i, i ^ 1) for i in range(rep_count)])


def swap_chip(block, step, rep_count):
    if step == 0:
        return block
    return lax.ppermute(block, "rep", [(i, i ^ (2 * step)) for i in range(rep_count)])


def upright(row):
    count = row.shape[1]
    same = lax.broadcasted_iota(i32, (count, count), 0) == lax.broadcasted_iota(i32, (count, count), 1)
    return jnp.sum(jnp.where(same, row, jnp.zeros_like(row)), axis=1, keepdims=True)


def one_hot(spots):
    return spots.astype(f32).astype(bf16)


def slot_spots(capacity, padded, exp_count, routes):
    tokens = routes.shape[1]
    block = jnp.bitwise_xor(upright(routes[...]), lax.axis_index("exp"))
    chosen = block == lax.broadcasted_iota(i32, (tokens, exp_count), 1)
    above = lax.broadcasted_iota(i32, (tokens, tokens), 1) < lax.broadcasted_iota(i32, (tokens, tokens), 0)
    ranks = dot(one_hot(above), one_hot(chosen))
    rank = jnp.sum(jnp.where(chosen, ranks, 0.0), axis=1, keepdims=True).astype(i32)
    target = block * padded + rank
    return one_hot(target == lax.broadcasted_iota(i32, (tokens, exp_count * padded), 1))


def prepare_kernel(fetch_slots, capacity, padded, exp_count, counts, routes, pick, pick_swapped, home):
    tokens = routes.shape[1]
    rep_count = counts.shape[1]
    replica = lax.axis_index("rep")
    position = lax.broadcasted_iota(i32, (tokens, 1), 0)
    source = jnp.zeros((tokens, 1), i32)
    start = jnp.zeros((tokens, 1), i32)
    end = jnp.int32(0)
    for shard in range(rep_count):
        end = end + counts[0, shard]
        passed = position >= end
        source = source + passed.astype(i32)
        start = jnp.where(passed, end, start)
    home_of = slot_spots(capacity, padded, exp_count, routes)
    home[...] = home_of

    places = lax.broadcasted_iota(i32, (tokens, rep_count * fetch_slots), 1)
    for shard, matrix in ((source, pick), (jnp.bitwise_xor(source, replica), pick_swapped)):
        place = shard * fetch_slots + position - start
        matrix[...] = dot(home_of, one_hot(place == places), ((0,), (0,))).astype(bf16)


def part_of(chunk, width):
    return slice(chunk * width, (chunk + 1) * width)


def serve(table, rows, asking):
    fetch_slots = table.shape[2]
    asked = jnp.concatenate([table[0, pl.ds(replica, 1), :] for replica in asking], axis=1)
    chosen = asked == lax.broadcasted_iota(i32, (rows.shape[0], asked.shape[1]), 0)
    found = dot(one_hot(chosen), rows, ((0,), (0,))).astype(bf16)
    return [found[number * fetch_slots : (number + 1) * fetch_slots] for number in range(len(asking))]


def begin_kernel(capacity, padded, table_far, rows_far, routes_far, weight_far, grads_far, *refs):
    served_far, *sent = refs[:-7]
    table, rows, routes, weight, grads, served, sems = refs[-7:]
    width = served.shape[2]
    fetches = [
        pltpu.make_async_copy(far, near, sems.at[number])
        for number, (far, near) in enumerate(
            (
                (table_far, table),
                (rows_far.at[:, :width], rows),
                (routes_far, routes),
                (weight_far, weight),
                (grads_far, grads),
            )
        )
    ]
    store = pltpu.make_async_copy(served, served_far, sems.at[5])
    for copy in fetches:
        copy.start()
    for copy in fetches[:2]:
        copy.wait()
    for replica, found in enumerate(serve(table, rows[...], range(served.shape[0]))):
        served[replica] = found
    store.start()
    for copy in fetches[2:]:
        copy.wait()
    home = slot_spots(capacity, padded, len(sent), routes)
    scaled = (upright(weight[...]) * grads[...].astype(f32)).astype(bf16)
    by_slot = dot(home, scaled, ((0,), (0,))).astype(bf16)
    for step in range(len(sent)):
        sent[step][...] = by_slot[step * padded : step * padded + capacity]
    store.wait()


def serve_last_kernel(own_table, own_rows, pair_table, pair_rows, *served):
    fetch_slots = own_table.shape[2]
    width = served[0].shape[1]
    asking = [jnp.bitwise_xor(lax.axis_index("rep"), 2 * step) for step in range(len(served))]
    for table, rows, base in ((own_table, own_rows, 0), (pair_table, pair_rows, fetch_slots)):
        for block, found in zip(served, serve(table, rows[:, rows.shape[1] - width :], asking)):
            block[base : base + fetch_slots] = found


def pick_first_kernel(capacity, padded, pick, arrived, *refs):
    exp_count = (len(refs) - 3) // 2
    grads, refs = refs[:exp_count], refs[exp_count:]
    sent_far, grads_far, (sent, sems) = refs[0], refs[1 : exp_count + 1], refs[exp_count + 1 :]
    put_away = [
        pltpu.make_async_copy(block, place, sems.at[exp_count + step])
        for step, (block, place) in enumerate(zip(grads, grads_far))
    ]
    for copy in put_away:
        copy.start()
    shards, rows, width = arrived.shape
    by_slot = dot(pick[...], arrived[...].reshape(shards * rows, width)).astype(bf16)
    column = lax.axis_index("exp")
    for step in range(exp_count):
        sent[step] = by_slot[step * padded : step * padded + capacity]
        copy = pltpu.make_async_copy(sent.at[step], sent_far.at[jnp.bitwise_xor(column, step)], sems.at[step])
        copy.start()
        put_away.append(copy)
    for copy in put_away:
        copy.wait()


def pick_last_kernel(capacity, padded, chips, pick, *refs):
    arrived, sent = refs[:chips], refs[chips:]
    rows = jnp.concatenate([block[...] for block in arrived], axis=0)
    by_slot = dot(pick[...], rows).astype(bf16)
    for step in range(len(sent)):
        sent[step][...] = by_slot[step * padded : step * padded + capacity]


def fill(tile, blocks, capacity, padded):
    tile[...] = jnp.zeros(tile.shape, tile.dtype)
    for step, block in enumerate(blocks):
        tile[step * padded : step * padded + capacity, :] = block[...]


def partial_kernel(capacity, padded, gate, down, arrived, turned, pre_act, adapted, tile):
    column = lax.axis_index("exp")
    tile[...] = jnp.zeros(tile.shape, tile.dtype)
    for step in range(arrived.shape[0]):
        tile[step * padded : step * padded + capacity, :] = arrived[jnp.bitwise_xor(column, step)]
    width = tile.shape[1]
    pre_act[...] = dot(tile[...], gate[0, :width])
    adapted[...] = dot(tile[...], down[0, :width])
    turned[...] = tile[...].T


def fetch_kernel(*refs):
    count = (len(refs) - 1) // 2
    sems = refs[-1]
    copies = [pltpu.make_async_copy(refs[i], refs[count + i], sems.at[i]) for i in range(count)]
    for copy in copies:
        copy.start()
    for copy in copies:
        copy.wait()


def forward(rows, pre_first, adapted_first, grads, gate, down, up):
    width = gate.shape[1] - rows.shape[1]
    adapted = (adapted_first + dot(rows, down[0, width:])).astype(bf16)
    pre_act = pre_first + dot(rows, gate[0, width:]) + dot(adapted, up[0])
    gate_value = jax.nn.sigmoid(pre_act)
    activated = (pre_act * gate_value).astype(bf16)
    slope = gate_value * (1.0 + pre_act * (1.0 - gate_value))
    grad_pre = (grads.astype(f32) * slope).astype(bf16)
    back = dot(grad_pre, up[0], ((1,), (1,))).astype(bf16)
    return activated, adapted, grad_pre, back


def early_kernel(capacity, padded, steps, pre_first, adapted_first, gate, down, up, *refs):
    blocks, refs = refs[:steps], refs[steps:]
    grads, refs = refs[:steps], refs[steps:]
    activated, refs = refs[:steps], refs[steps:]
    turned, adapted, grad_pre, back, tile, grad_tile = refs
    fill(tile, blocks, capacity, padded)
    fill(grad_tile, grads, capacity, padded)
    count = tile.shape[0]
    rows, adapted[...], grad_pre[...], back[...] = forward(
        tile[...], pre_first[:count], adapted_first[:count], grad_tile[...], gate, down, up
    )
    for step in range(steps):
        activated[step][...] = rows[step * padded : step * padded + capacity]
    turned[...] = tile[...].T


def late_kernel(
    capacity,
    padded,
    steps,
    turned_first,
    turned_early,
    adapted_early,
    grad_early,
    back_early,
    pre_first,
    adapted_first,
    gate,
    down,
    up,
    *refs,
):
    blocks, refs = refs[:steps], refs[steps:]
    grads, refs = refs[:steps], refs[steps:]
    activated, refs = refs[:steps], refs[steps:]
    keep, give, tile, grad_tile, down_term, up_term = refs
    fill(tile, blocks, capacity, padded)
    fill(grad_tile, grads, capacity, padded)
    count = pre_first.shape[0] - tile.shape[0]
    rows, adapted, grad_pre, back = forward(
        tile[...], pre_first[count:], adapted_first[count:], grad_tile[...], gate, down, up
    )
    for step in range(steps):
        activated[step][...] = rows[step * padded : step * padded + capacity]
    width = turned_first.shape[0]
    down_term[:width] = dot(turned_first[...], jnp.concatenate([back_early[...], back], axis=0))
    down_term[width:] = dot(turned_early[...], back_early[...]) + dot(tile[...], back, ((0,), (0,)))
    owners, up_rows, hidden_units = up_term.shape
    part = dot(
        jnp.concatenate([adapted_early[...], adapted], axis=0),
        jnp.concatenate([grad_early[...], grad_pre], axis=0),
        ((0,), (0,)),
    )
    for owner in range(owners):
        up_term[owner] = part[owner * up_rows : (owner + 1) * up_rows]

    pairs, _, lanes = keep.shape
    down_rows = down_term.shape[0] // owners
    replica = lax.axis_index("rep")
    for chip in range(pairs):
        for flip, target in ((0, keep), (1, give)):
            owner = jnp.bitwise_xor(replica, 2 * chip + flip)
            mine = down_term[pl.ds(pl.multiple_of(owner * down_rows, 8), down_rows)]
            target[chip, :down_rows] = mine.astype(target.dtype)
            mine = up_term[owner].astype(target.dtype)
            for part in range(hidden_units // lanes):
                base = down_rows + part * up_rows
                target[chip, base : base + up_rows] = mine[:, part * lanes : (part + 1) * lanes]


def end_kernel(capacity, padded, home, weight, kept, came, *refs):
    *blocks, down_grad, up_grad, out, tile = refs
    total = kept[...].astype(f32) + came[...].astype(f32)
    down_rows = down_grad.shape[1]
    up_rows, hidden_units = up_grad.shape[1:]
    lanes = total.shape[1]
    down_grad[0] = total[:down_rows]
    for part in range(hidden_units // lanes):
        base = down_rows + part * up_rows
        up_grad[0, :, part * lanes : (part + 1) * lanes] = total[base : base + up_rows]
    fill(tile, blocks, capacity, padded)
    out[...] = (upright(weight[...]) * dot(home[...], tile[...])).astype(bf16)


def body(
    replay_buffer_rows,
    shard_request_index,
    replica_fetch_count,
    routes,
    router_route_weight,
    output_gradient,
    frozen_gate_weight,
    adapter_down_weight,
    adapter_up_weight,
):
    rep_count = lax.axis_size("rep")
    exp_count = lax.axis_size("exp")
    pairs = rep_count // 2
    token_count = routes.shape[0]
    shard_rows, model_width = replay_buffer_rows.shape
    fetch_slots = shard_request_index.shape[2]
    hidden_units = frozen_gate_weight.shape[2]
    rank_width = adapter_down_weight.shape[2]
    capacity = 7 * token_count // (4 * exp_count)
    padded = -(-capacity // 16) * 16
    slots = exp_count * padded
    fetched_rows = rep_count * fetch_slots
    first_width = model_width // 128 * FIRST_PART // PARTS * 128
    last_width = model_width - first_width

    routes_row = routes.reshape(1, token_count)
    weight_row = router_route_weight.reshape(1, token_count)

    pair_rows = swap_core(replay_buffer_rows, rep_count)
    pair_table = swap_core(shard_request_index, rep_count)
    operands = [shard_request_index, replay_buffer_rows, routes_row, weight_row, output_gradient]
    far = pl.BlockSpec(memory_space=pltpu.HBM)
    near = pl.BlockSpec(memory_space=pltpu.VMEM)
    served, *grads = pl.pallas_call(
        functools.partial(begin_kernel, capacity, padded),
        out_shape=[pltpu.HBM((rep_count, fetch_slots, first_width), bf16)]
        + [shape((capacity, hidden_units), bf16)] * exp_count,
        in_specs=[far] * len(operands),
        out_specs=[far] + [near] * exp_count,
        scratch_shapes=[
            pltpu.VMEM(shard_request_index.shape, i32),
            pltpu.VMEM((shard_rows, first_width), bf16),
            pltpu.VMEM(routes_row.shape, i32),
            pltpu.VMEM(weight_row.shape, f32),
            pltpu.VMEM(output_gradient.shape, bf16),
            pltpu.VMEM((rep_count, fetch_slots, first_width), bf16),
            pltpu.SemaphoreType.DMA((6,)),
        ],
        compiler_params=pltpu.CompilerParams(vmem_limit_bytes=16 * 1024 * 1024),
        name="begin",
    )(*[pltpu.with_memory_space_constraint(array, pltpu.HBM) for array in operands])
    served, routes_row, pair_rows, pair_table = lax.optimization_barrier((served, routes_row, pair_rows, pair_table))
    arrived = lax.all_to_all(served, "rep", 0, 0, tiled=True)
    grads = [swap_exp(block, step, exp_count) for step, block in enumerate(grads)]
    routes_row, grads[1] = lax.optimization_barrier((routes_row, grads[1]))
    pick, pick_swapped, home = call(
        functools.partial(prepare_kernel, fetch_slots, capacity, padded, exp_count),
        [shape((slots, fetched_rows), bf16)] * 2 + [shape((token_count, slots), bf16)],
        [replica_fetch_count, routes_row],
        counts=replica_fetch_count,
        stored=[1, 2],
        flops=4 * token_count * slots * fetched_rows,
        name="prepare",
    )
    sent, *grads = pl.pallas_call(
        functools.partial(pick_first_kernel, capacity, padded),
        out_shape=[pltpu.HBM((exp_count, capacity, first_width), bf16)]
        + [pltpu.HBM((capacity, hidden_units), bf16)] * exp_count,
        in_specs=[near] * (2 + exp_count),
        out_specs=[far] * (1 + exp_count),
        scratch_shapes=[
            pltpu.VMEM((exp_count, capacity, first_width), bf16),
            pltpu.SemaphoreType.DMA((2 * exp_count,)),
        ],
        compiler_params=pltpu.CompilerParams(vmem_limit_bytes=16 * 1024 * 1024),
        name="pick_first",
    )(pick, arrived, *grads)

    pair_rows, sent = lax.optimization_barrier((pair_rows, sent))
    first_blocks = lax.all_to_all(sent, "exp", 0, 0, tiled=True)
    served = call(
        serve_last_kernel,
        [shape((2 * fetch_slots, last_width), bf16)] * pairs,
        [shard_request_index, replay_buffer_rows, pair_table, pair_rows],
        far=[shard_request_index, pair_table],
        flops=2 * fetched_rows * shard_rows * last_width,
        name="serve_last",
    )
    arrived = [swap_chip(block, step, rep_count) for step, block in enumerate(served)]
    first_sent, *sent = call(
        functools.partial(pick_last_kernel, capacity, padded, pairs),
        [shape((capacity, last_width), bf16)] * exp_count,
        [pick_swapped, *arrived],
        flops=2 * slots * fetched_rows * last_width,
        name="pick_last",
    )
    weights = [frozen_gate_weight, adapter_down_weight, adapter_up_weight]
    first_sent, *weights = lax.optimization_barrier((first_sent, *weights))
    weights = pl.pallas_call(
        fetch_kernel,
        out_shape=[pltpu.VMEM(array.shape, array.dtype) for array in weights],
        in_specs=[far] * len(weights),
        out_specs=[near] * len(weights),
        scratch_shapes=[pltpu.SemaphoreType.DMA((len(weights),))],
        compiler_params=pltpu.CompilerParams(vmem_limit_bytes=16 * 1024 * 1024),
        name="fetch",
    )(*[pltpu.with_memory_space_constraint(array, pltpu.HBM) for array in weights])
    weights = [pltpu.with_memory_space_constraint(array, pltpu.VMEM) for array in weights]
    last_blocks = [swap_exp(block, step, exp_count) for step, block in enumerate((first_sent, *sent))]

    turned, pre_first, adapted_first = call(
        functools.partial(partial_kernel, capacity, padded),
        [shape((first_width, slots), bf16), shape((slots, hidden_units), f32), shape((slots, rank_width), f32)],
        [*weights[:2], first_blocks],
        resident=weights,
        scratch=[pltpu.VMEM((slots, first_width), bf16)],
        flops=2 * slots * first_width * (hidden_units + rank_width),
        name="partial",
    )

    term_rows = (model_width + rank_width * hidden_units // rank_width) // rep_count
    steps = exp_count // 2
    count = steps * padded
    *activated, turned_early, adapted_early, grad_early, back_early = call(
        functools.partial(early_kernel, capacity, padded, steps),
        [shape((capacity, hidden_units), bf16)] * steps
        + [
            shape((last_width, count), bf16),
            shape((count, rank_width), bf16),
            shape((count, hidden_units), bf16),
            shape((count, rank_width), bf16),
        ],
        [pre_first, adapted_first, *weights, *last_blocks[:steps], *grads[:steps]],
        resident=weights,
        scratch=[pltpu.VMEM((count, last_width), bf16), pltpu.VMEM((count, hidden_units), bf16)],
        flops=2 * count * last_width * (hidden_units + rank_width),
        name="early",
    )
    count = slots - count
    *late, keep, give = call(
        functools.partial(late_kernel, capacity, padded, exp_count - steps),
        [shape((capacity, hidden_units), bf16)] * (exp_count - steps)
        + [shape((pairs, term_rows, rank_width), kind) for kind in (f32, bf16)],
        [
            turned,
            turned_early,
            adapted_early,
            grad_early,
            back_early,
            pre_first,
            adapted_first,
            *weights,
            *last_blocks[steps:],
            *grads[steps:],
        ],
        resident=weights,
        scratch=[
            pltpu.VMEM((count, last_width), bf16),
            pltpu.VMEM((count, hidden_units), bf16),
            pltpu.VMEM((model_width, rank_width), f32),
            pltpu.VMEM((rep_count, rank_width // rep_count, hidden_units), f32),
        ],
        flops=2 * count * last_width * (hidden_units + rank_width) + 4 * slots * model_width * rank_width,
        name="late",
    )
    activated += late

    pair_terms = swap_core(give, rep_count)
    results = [swap_exp(block, step, exp_count) for step, block in enumerate(activated)]
    terms = keep + pair_terms.astype(f32)
    while terms.shape[0] > 2:
        half = terms.shape[0] // 2
        terms = terms[:half] + swap_chip(terms[half:].astype(bf16), half, rep_count).astype(f32)
    down_grad, up_grad, out_rows = call(
        functools.partial(end_kernel, capacity, padded),
        [
            shape((1, model_width // rep_count, rank_width), f32),
            shape((1, rank_width // rep_count, hidden_units), f32),
            shape((token_count, hidden_units), bf16),
        ],
        [home, weight_row, terms[0], swap_chip(terms[1].astype(bf16), 1, rep_count), *results],
        scratch=[pltpu.VMEM((slots, hidden_units), bf16)],
        flops=2 * token_count * slots * hidden_units,
        name="end",
    )
    return (out_rows, down_grad, up_grad)


def solution(mesh):
    placed = (
        P(("rep", "exp"), None),
        P(("rep", "exp"), None, None),
        P(("rep", "exp"), None),
        P(("rep", "exp"), None),
        P(("rep", "exp"), None),
        P(("rep", "exp"), None),
        P("exp", None, None),
        P("exp", None, None),
        P("exp", None, None),
    )
    return jax.shard_map(
        body,
        mesh=mesh,
        in_specs=placed,
        out_specs=(P(("rep", "exp"), None), P("exp", "rep", None), P("exp", "rep", None)),
        check_vma=False,
    )
```

time: 87.8 us -> 84.1 us (0.958)
  waiting for transfers between devices: 33.9 us -> 27.2 us
  local copies, waits for them, and re-layouts: 3.9 us -> 6.11 us
  starting transfers between devices: 31.5 us -> 33.3 us
  Pallas kernels: 17.1 us -> 16.1 us
    pallas_call x10 -> x7, Pallas kernels: 17.1 us -> 8.96 us  [call(): pl.pallas_call(moving, out_shape=[pltpu.HBM(out.shape, out.dtype) if numb...]
    pallas_call x0 -> x3, Pallas kernels: none -> 7.17 us  [the longest x1 3.32 us: body(): pl.pallas_call(fetch_kernel, out_shape=[pltpu.VMEM(array.shape, array.dty...]
    all_to_all x1, waiting for transfers between devices: 4.09 us -> 0.01 us  [body(): first_blocks = lax.all_to_all(sent, 'exp', 0, 0, tiled=True)]
    ppermute x5, starting transfers between devices: 6.61 us -> 8.88 us  [swap_chip(): lax.ppermute(block, 'rep', [(i, i ^ 2 * step) for i in range(rep_count)])]
    unnamed x28 -> x26, local copies, waits for them, and re-layouts: 3.82 us -> 6.03 us
    ppermute x9, waiting for transfers between devices: 13.8 us -> 12.2 us  [swap_exp(): return lax.ppermute(block, 'exp', [(i, i ^ step) for i in range(exp_count)])]
    ppermute x5, waiting for transfers between devices: 13.9 us -> 12.4 us  [swap_chip(): lax.ppermute(block, 'rep', [(i, i ^ 2 * step) for i in range(rep_count)])]
    ppermute x9, starting transfers between devices: 14.9 us -> 13.6 us  [swap_exp(): return lax.ppermute(block, 'exp', [(i, i ^ step) for i in range(exp_count)])]
  transfers between devices with their start and end apart: 19 -> 19, of which waited for: 10 -> 11; matrix products, arithmetic and copies ran while one was open for 0% -> 0% of each run, Pallas kernels for 10% -> 14%
where the time goes in v4:
time: 84.1 us; the launch traced here: 83.8 us
  starting transfers between devices  33.3 us (40%)
  waiting for transfers between devices  27.2 us (32%)
  Pallas kernels  16.1 us (19%)
  local copies, waits for them, and re-layouts  6.11 us (7%)
  between operations  0.86 us (1%)
    ppermute x9, starting transfers between devices, swap_exp(): return lax.ppermute(block, 'exp', [(i, i ^ step) for i in range(exp_count)])  13.6 us
    ppermute x5, waiting for transfers between devices, swap_chip(): lax.ppermute(block, 'rep', [(i, i ^ 2 * step) for i in range(rep_count)])  12.4 us
    ppermute x9, waiting for transfers between devices, swap_exp(): return lax.ppermute(block, 'exp', [(i, i ^ step) for i in range(exp_count)])  12.2 us
    pallas_call x7, Pallas kernels, call(): pl.pallas_call(moving, out_shape=[pltpu.HBM(out.shape, out.dtype) if numb...  8.96 us
    ppermute x5, starting transfers between devices, swap_chip(): lax.ppermute(block, 'rep', [(i, i ^ 2 * step) for i in range(rep_count)])  8.88 us
    unnamed x26, local copies, waits for them, and re-layouts  6.03 us
    all_to_all x1, starting transfers between devices, body(): arrived = lax.all_to_all(served, 'rep', 0, 0, tiled=True)  5.15 us
    all_to_all x1, starting transfers between devices, body(): first_blocks = lax.all_to_all(sent, 'exp', 0, 0, tiled=True)  5.02 us
  transfers between devices with their start and end apart: 19, of which 11 were waited for; matrix products, arithmetic and copies ran while one was open for 0% of the time, Pallas kernels for 14%

profile of v4, /device:TPU:0, one launch (start us, length us, event | category | flops | bytes accessed | tf_op | source)
XLA Modules:
  0.0 83.8 jit_solution(2727336072555728537)
XLA Ops:
  0.6 0.5 collective-permute-start
  1.1 0.1 collective-permute-start.1
  1.2 2.5 %begin.1 = (bf16[8,32,1792]{2,1,0:T(8,128)(2,1)}, bf16[56,1024]{1,0:T(8,128)(2,1)S(1)}, bf16[56,1024]{1,0:T(8,128)(2,1)S(1)}, bf16[56,1024]{1,0:T(8,128)(2,1)S(1)}, bf16[56,1024]{1,0:T(8,128)(2,1)S(1)}) custom-call(s32[1,8,32]{2,1,0:T(8,128)} %refs_0_.3, bf16[128,3584]{1,0:T(8,128)(2,1)} %refs_1_.1, s32[1,128]{1,0:T(1,128)} %bitcast.8, f32[1,128]{1,0:T(1,128)} %bitcast.6, ...), custom_call_target="tpu_custom_call" | custom-call | tf_op jit(solution)/shard_map/begin/pallas_call | solution.py:384
  3.8 0.0 copy-start.10
  3.8 0.0 copy-start.11
  3.8 0.0 collective-permute-done.1.refs_2_
  3.8 0.0 copy-start.12
  3.8 0.0 collective-permute-done.refs_3_
  3.8 5.2 %all-to-all-start = ((bf16[8,32,1792]{2,1,0:T(8,128)(2,1)}), bf16[8,32,1792]{2,1,0:T(8,128)(2,1)S(1)}, u32[]{:S(2)}, u32[]{:S(2)}) async-start(bf16[8,32,1792]{2,1,0:T(8,128)(2,1)} %get-tuple-element.64), calls=%async_computation | async-start | bytes 1835008 | tf_op jit(solution)/shard_map/all_to_all | solution.py:403
  9.0 1.6 %collective-permute-start.2 = (bf16[56,1024]{1,0:T(8,128)(2,1)S(1)}, bf16[56,1024]{1,0:T(8,128)(2,1)S(1)}, u32[]{:S(2)}, u32[]{:S(2)}) collective-permute-start(bf16[56,1024]{1,0:T(8,128)(2,1)S(1)} %get-tuple-element.57), channel_id=1, source_target_pairs={{0,1},{1,0},{2,3},{3,2},{4,5},{5,4},{6,7},{7,6},{8,9},{9,8},{10,11... | collective-permute-start | bytes 344072 | tf_op jit(solution)/shard_map/ppermute | solution.py:86
  10.6 2.6 %collective-permute-start.3 = (bf16[56,1024]{1,0:T(8,128)(2,1)S(1)}, bf16[56,1024]{1,0:T(8,128)(2,1)S(1)}, u32[]{:S(2)}, u32[]{:S(2)}) collective-permute-start(bf16[56,1024]{1,0:T(8,128)(2,1)S(1)} %get-tuple-element.67), channel_id=1, source_target_pairs={{0,2},{1,3},{2,0},{3,1},{4,6},{5,7},{6,4},{7,5},{8,10},{9,11},{10,... | collective-permute-start | bytes 344072 | tf_op jit(solution)/shard_map/ppermute | solution.py:86
  13.2 0.2 collective-permute-start.4
  13.4 3.0 %collective-permute-done.2.refs_1_ = bf16[56,1024]{1,0:T(8,128)(2,1)S(1)} collective-permute-done((bf16[56,1024]{1,0:T(8,128)(2,1)S(1)}, bf16[56,1024]{1,0:T(8,128)(2,1)S(1)}, u32[]{:S(2)}, u32[]{:S(2)}) %collective-permute-start.2) | collective-permute-done | bytes 114720 | tf_op jit(solution)/shard_map/ppermute | solution.py:86
  16.4 0.0 copy-done.10
  16.4 0.0 copy-done.11
  16.4 1.8 %prepare.1 = (bf16[256,256]{1,0:T(8,128)(2,1)S(1)}, bf16[256,256]{1,0:T(8,128)(2,1)}, bf16[128,256]{1,0:T(8,128)(2,1)}) custom-call(s32[1,8]{1,0:T(1,128)S(1)} %copy-done.11, s32[1,128]{1,0:T(1,128)S(1)} %bitcast.9), custom_call_target="tpu_custom_call" | custom-call | flops 33554432 | bytes 111848 | tf_op jit(solution)/shard_map/prepare/pallas_call | solution.py:64
  18.2 4.2 %collective-permute-done.3.refs_2_ = bf16[56,1024]{1,0:T(8,128)(2,1)S(1)} collective-permute-done((bf16[56,1024]{1,0:T(8,128)(2,1)S(1)}, bf16[56,1024]{1,0:T(8,128)(2,1)S(1)}, u32[]{:S(2)}, u32[]{:S(2)}) %collective-permute-start.3) | collective-permute-done | bytes 114720 | tf_op jit(solution)/shard_map/ppermute | solution.py:86
  22.4 0.0 collective-permute-done.4.refs_3_
  22.4 0.6 all-to-all-done.arrived
  23.0 1.3 %pick_first.1 = (bf16[4,56,1792]{2,1,0:T(8,128)(2,1)}, bf16[56,1024]{1,0:T(8,128)(2,1)}, bf16[56,1024]{1,0:T(8,128)(2,1)}, bf16[56,1024]{1,0:T(8,128)(2,1)}, bf16[56,1024]{1,0:T(8,128)(2,1)}) custom-call(bf16[256,256]{1,0:T(8,128)(2,1)S(1)} %get-tuple-element.63.pick, bf16[8,32,1792]{2,1,0:T(8,128)(2,1)S(1)} %all-to-all-done.arrived, ...), custom_call_target="tpu_custom_call" | custom-call | tf_op jit(solution)/shard_map/pick_first/pallas_call | solution.py:415
  24.3 0.0 copy-start.2
  24.3 5.0 %all-to-all-start.1 = ((bf16[4,56,1792]{2,1,0:T(8,128)(2,1)}), bf16[4,56,1792]{2,1,0:T(8,128)(2,1)S(1)}, u32[]{:S(2)}, u32[]{:S(2)}) async-start(bf16[4,56,1792]{2,1,0:T(8,128)(2,1)} %get-tuple-element.81), calls=%async_computation.1 | async-start | bytes 1605632 | tf_op jit(solution)/shard_map/all_to_all | solution.py:430
  29.4 0.0 copy-done.2
  29.4 1.3 %serve_last.1 = (bf16[64,1792]{1,0:T(8,128)(2,1)S(1)}, bf16[64,1792]{1,0:T(8,128)(2,1)S(1)}, bf16[64,1792]{1,0:T(8,128)(2,1)S(1)}, bf16[64,1792]{1,0:T(8,128)(2,1)S(1)}) custom-call(s32[1,8,32]{2,1,0:T(8,128)} %refs_0_.3, bf16[128,3584]{1,0:T(8,128)(2,1)S(1)} %copy-done.2, s32[1,8,32]{2,1,0:T(8,128)} %copy-done.12, ...), custom_call_target="tpu_custom_call" | custom-call | flops 117440512 | bytes 391468 | tf_op jit(solution)/shard_map/serve_last/pallas_call | solution.py:64
  30.6 0.9 %collective-permute-start.5 = (bf16[64,1792]{1,0:T(8,128)(2,1)S(1)}, bf16[64,1792]{1,0:T(8,128)(2,1)S(1)}, u32[]{:S(2)}, u32[]{:S(2)}) collective-permute-start(bf16[64,1792]{1,0:T(8,128)(2,1)S(1)} %get-tuple-element.72), channel_id=1, source_target_pairs={{0,8},{4,12},{8,0},{12,4},{16,24},{20,28},{24,16},{28,20},{1,9},{5... | collective-permute-start | bytes 688136 | tf_op jit(solution)/shard_map/ppermute | solution.py:96
  31.5 1.5 %collective-permute-start.6 = (bf16[64,1792]{1,0:T(8,128)(2,1)S(1)}, bf16[64,1792]{1,0:T(8,128)(2,1)S(1)}, u32[]{:S(2)}, u32[]{:S(2)}) collective-permute-start(bf16[64,1792]{1,0:T(8,128)(2,1)S(1)} %get-tuple-element.73), channel_id=1, source_target_pairs={{0,16},{4,20},{8,24},{12,28},{16,0},{20,4},{24,8},{28,12},{1,17},{... | collective-permute-start | bytes 688136 | tf_op jit(solution)/shard_map/ppermute | solution.py:96
  33.0 1.2 %collective-permute-start.7 = (bf16[64,1792]{1,0:T(8,128)(2,1)S(1)}, bf16[64,1792]{1,0:T(8,128)(2,1)S(1)}, u32[]{:S(2)}, u32[]{:S(2)}) collective-permute-start(bf16[64,1792]{1,0:T(8,128)(2,1)S(1)} %get-tuple-element.74), channel_id=1, source_target_pairs={{0,24},{4,28},{8,16},{12,20},{16,8},{20,12},{24,0},{28,4},{1,25},{... | collective-permute-start | bytes 688136 | tf_op jit(solution)/shard_map/ppermute | solution.py:96
  34.2 4.9 %collective-permute-done.5.refs_2_ = bf16[64,1792]{1,0:T(8,128)(2,1)S(1)} collective-permute-done((bf16[64,1792]{1,0:T(8,128)(2,1)S(1)}, bf16[64,1792]{1,0:T(8,128)(2,1)S(1)}, u32[]{:S(2)}, u32[]{:S(2)}) %collective-permute-start.5) | collective-permute-done | bytes 229408 | tf_op jit(solution)/shard_map/ppermute | solution.py:96
  39.0 4.1 %collective-permute-done.6.refs_3_ = bf16[64,1792]{1,0:T(8,128)(2,1)S(1)} collective-permute-done((bf16[64,1792]{1,0:T(8,128)(2,1)S(1)}, bf16[64,1792]{1,0:T(8,128)(2,1)S(1)}, u32[]{:S(2)}, u32[]{:S(2)}) %collective-permute-start.6) | collective-permute-done | bytes 229408 | tf_op jit(solution)/shard_map/ppermute | solution.py:96
  43.1 0.0 collective-permute-done.7.refs_4_
  43.1 0.4 pick_last.1
  43.5 1.8 %collective-permute-start.8 = (bf16[56,1792]{1,0:T(8,128)(2,1)S(1)}, bf16[56,1792]{1,0:T(8,128)(2,1)S(1)}, u32[]{:S(2)}, u32[]{:S(2)}) collective-permute-start(bf16[56,1792]{1,0:T(8,128)(2,1)S(1)} %get-tuple-element.87), channel_id=1, source_target_pairs={{0,1},{1,0},{2,3},{3,2},{4,5},{5,4},{6,7},{7,6},{8,9},{9,8},{10,11... | collective-permute-start | bytes 602120 | tf_op jit(solution)/shard_map/ppermute | solution.py:86
  45.4 2.4 %collective-permute-start.9 = (bf16[56,1792]{1,0:T(8,128)(2,1)S(1)}, bf16[56,1792]{1,0:T(8,128)(2,1)S(1)}, u32[]{:S(2)}, u32[]{:S(2)}) collective-permute-start(bf16[56,1792]{1,0:T(8,128)(2,1)S(1)} %get-tuple-element.94), channel_id=1, source_target_pairs={{0,2},{1,3},{2,0},{3,1},{4,6},{5,7},{6,4},{7,5},{8,10},{9,11},{10,... | collective-permute-start | bytes 602120 | tf_op jit(solution)/shard_map/ppermute | solution.py:86
  47.7 0.3 collective-permute-start.10
  48.0 3.3 %fetch.1 = (bf16[1,3584,1024]{2,1,0:T(8,128)(2,1)S(1)}, bf16[1,3584,128]{2,1,0:T(8,128)(2,1)S(1)}, bf16[1,128,1024]{2,1,0:T(8,128)(2,1)S(1)}) custom-call(bf16[1,3584,1024]{2,1,0:T(8,128)(2,1)} %refs_0_.4, bf16[1,3584,128]{2,1,0:T(8,128)(2,1)} %refs_1_.2, bf16[1,128,1024]{2,1,0:T(8,128)(2,1)} %refs_2_), custom_call_target="tpu_custom_call" | custom-call | tf_op jit(solution)/shard_map/fetch/pallas_call | solution.py:449
  51.3 2.9 %copy-done = bf16[1,3584,1024]{2,1,0:T(8,128)(2,1)} copy-done((bf16[1,3584,1024]{2,1,0:T(8,128)(2,1)}, bf16[1,3584,1024]{2,1,0:T(8,128)(2,1)S(1)}, u32[]{:S(2)}) %copy-start) | copy-done | bytes 7340056
  54.2 0.0 all-to-all-done.1.refs_2_
  54.2 3.1 %copy-done.1 = bf16[1,3584,1024]{2,1,0:T(8,128)(2,1)S(1)} copy-done((bf16[1,3584,1024]{2,1,0:T(8,128)(2,1)S(1)}, bf16[1,3584,1024]{2,1,0:T(8,128)(2,1)}, u32[]{:S(2)}) %copy-start.1) | copy-done | bytes 7340056
  57.3 1.4 %partial.1 = (bf16[1792,256]{1,0:T(8,128)(2,1)S(1)}, f32[256,1024]{1,0:T(8,128)S(1)}, f32[256,128]{1,0:T(8,128)S(1)}) custom-call(bf16[1,3584,1024]{2,1,0:T(8,128)(2,1)S(1)} %copy-done.1, bf16[1,3584,128]{2,1,0:T(8,128)(2,1)S(1)} %get-tuple-element.80.refs_1_.refs_3_.refs_8_, bf16[4,56,1792]{2,1,0:T(8,128)(2,1)S(1)} %all-to-all-done.1.refs_2_), custom_call_target="tpu_custom_call" | custom-call | flops 1056964608 | bytes 3523215 | tf_op jit(solution)/shard_map/partial/pallas_call | solution.py:64
  58.7 0.0 collective-permute-done.8.refs_6_
  58.7 0.0 copy-done.6
  58.8 0.0 copy-done.7
  58.8 0.0 copy-start.4
  58.8 0.0 copy-start.5
  58.8 1.1 %early.1 = (bf16[56,1024]{1,0:T(8,128)(2,1)S(1)}, bf16[56,1024]{1,0:T(8,128)(2,1)S(1)}, bf16[1792,128]{1,0:T(8,128)(2,1)S(1)}, bf16[128,128]{1,0:T(8,128)(2,1)S(...) custom-call(f32[256,1024]{1,0:T(8,128)S(1)} %get-tuple-element.83.refs_0_.refs_5_, ...), custom_call_target="tpu_custom_call" | custom-call | flops 528482304 | bytes 1761607 | tf_op jit(solution)/shard_map/early/pallas_call | solution.py:64
  59.9 2.6 %collective-permute-done.9.refs_10_ = bf16[56,1792]{1,0:T(8,128)(2,1)S(1)} collective-permute-done((bf16[56,1792]{1,0:T(8,128)(2,1)S(1)}, bf16[56,1792]{1,0:T(8,128)(2,1)S(1)}, u32[]{:S(2)}, u32[]{:S(2)}) %collective-permute-start.9) | collective-permute-done | bytes 200736 | tf_op jit(solution)/shard_map/ppermute | solution.py:86
  62.5 0.0 collective-permute-done.10.refs_11_
  62.5 1.9 %late.1 = (bf16[56,1024]{1,0:T(8,128)(2,1)S(1)}, bf16[56,1024]{1,0:T(8,128)(2,1)S(1)}, f32[4,576,128]{2,1,0:T(8,128)S(1)}, bf16[4,576,128]{2,1,0:T(8,128)(2,1)S(1)}) custom-call(bf16[1792,256]{1,0:T(8,128)(2,1)S(1)} %get-tuple-element.82.refs_0_, bf16[1792,128]{1,0:T(8,128)(2,1)S(1)} %get-tuple-element.90.refs_1_, ...), custom_call_target="tpu_custom_call" | custom-call | flops 998244352 | bytes 3327481 | tf_op jit(solution)/shard_map/late/pallas_call | solution.py:64
  64.5 0.1 collective-permute-start.11
  64.6 2.0 %collective-permute-done.11 = bf16[4,576,128]{2,1,0:T(8,128)(2,1)S(1)} collective-permute-done((bf16[4,576,128]{2,1,0:T(8,128)(2,1)S(1)}, bf16[4,576,128]{2,1,0:T(8,128)(2,1)S(1)}, u32[]{:S(2)}, u32[]{:S(2)}) %collective-permute-start.11) | collective-permute-done | bytes 589856 | tf_op jit(solution)/shard_map/ppermute | solution.py:90
  66.6 0.1 convert_add_fusion
  66.7 2.8 %collective-permute-start.12 = (bf16[2,576,128]{2,1,0:T(8,128)(2,1)S(1)}, bf16[2,576,128]{2,1,0:T(8,128)(2,1)S(1)}, u32[]{:S(2)}, u32[]{:S(2)}) collective-permute-start(bf16[2,576,128]{2,1,0:T(8,128)(2,1)S(1)} %slice.28), channel_id=1, source_target_pairs={{0,16},{4,20},{8,24},{12,28},{16,0},{20,4},{24,8},{28,12},{1,17},{... | collective-permute-start | bytes 884744 | tf_op jit(solution)/shard_map/ppermute | solution.py:96
  69.5 2.4 %collective-permute-start.15 = (bf16[56,1024]{1,0:T(8,128)(2,1)S(1)}, bf16[56,1024]{1,0:T(8,128)(2,1)S(1)}, u32[]{:S(2)}, u32[]{:S(2)}) collective-permute-start(bf16[56,1024]{1,0:T(8,128)(2,1)S(1)} %get-tuple-element.102), channel_id=1, source_target_pairs={{0,2},{1,3},{2,0},{3,1},{4,6},{5,7},{6,4},{7,5},{8,10},{9,11},{10,... | collective-permute-start | bytes 344072 | tf_op jit(solution)/shard_map/ppermute | solution.py:86
  71.9 2.3 %collective-permute-start.16 = (bf16[56,1024]{1,0:T(8,128)(2,1)S(1)}, bf16[56,1024]{1,0:T(8,128)(2,1)S(1)}, u32[]{:S(2)}, u32[]{:S(2)}) collective-permute-start(bf16[56,1024]{1,0:T(8,128)(2,1)S(1)} %get-tuple-element.103), channel_id=1, source_target_pairs={{0,3},{1,2},{2,1},{3,0},{4,7},{5,6},{6,5},{7,4},{8,11},{9,10},{10,... | collective-permute-start | bytes 344072 | tf_op jit(solution)/shard_map/ppermute | solution.py:86
  74.3 0.0 collective-permute-start.14
  74.3 2.6 %collective-permute-done.12 = bf16[2,576,128]{2,1,0:T(8,128)(2,1)S(1)} collective-permute-done((bf16[2,576,128]{2,1,0:T(8,128)(2,1)S(1)}, bf16[2,576,128]{2,1,0:T(8,128)(2,1)S(1)}, u32[]{:S(2)}, u32[]{:S(2)}) %collective-permute-start.12) | collective-permute-done | bytes 294944 | tf_op jit(solution)/shard_map/ppermute | solution.py:96
  76.8 0.1 slice_add_fusion
  76.9 2.5 %collective-permute-start.13 = (bf16[576,128]{1,0:T(8,128)(2,1)S(1)}, bf16[576,128]{1,0:T(8,128)(2,1)S(1)}, u32[]{:S(2)}, u32[]{:S(2)}) collective-permute-start(bf16[576,128]{1,0:T(8,128)(2,1)S(1)} %fusion), channel_id=1, source_target_pairs={{0,8},{4,12},{8,0},{12,4},{16,24},{20,28},{24,16},{28,20},{1,9},{5... | collective-permute-start | bytes 442376 | tf_op jit(solution)/shard_map/ppermute | solution.py:96
  79.5 1.8 %collective-permute-done.15.refs_6_ = bf16[56,1024]{1,0:T(8,128)(2,1)S(1)} collective-permute-done((bf16[56,1024]{1,0:T(8,128)(2,1)S(1)}, bf16[56,1024]{1,0:T(8,128)(2,1)S(1)}, u32[]{:S(2)}, u32[]{:S(2)}) %collective-permute-start.15) | collective-permute-done | bytes 114720 | tf_op jit(solution)/shard_map/ppermute | solution.py:86
  81.2 0.0 collective-permute-done.16.refs_7_
  81.2 0.6 collective-permute-done.14.refs_5_
  81.8 0.9 %collective-permute-done.13.refs_3_ = bf16[576,128]{1,0:T(8,128)(2,1)S(1)} collective-permute-done((bf16[576,128]{1,0:T(8,128)(2,1)S(1)}, bf16[576,128]{1,0:T(8,128)(2,1)S(1)}, u32[]{:S(2)}, u32[]{:S(2)}) %collective-permute-start.13) | collective-permute-done | bytes 147488 | tf_op jit(solution)/shard_map/ppermute | solution.py:96
  82.8 0.0 copy-done.8
  82.8 1.0 %end.1 = (f32[1,448,128]{2,1,0:T(8,128)}, f32[1,16,1024]{2,1,0:T(8,128)}, bf16[128,1024]{1,0:T(8,128)(2,1)}) custom-call(bf16[128,256]{1,0:T(8,128)(2,1)S(1)} %copy-done.8, f32[1,128]{1,0:T(1,128)S(1)} %bitcast.7, f32[576,128]{1,0:T(8,128)S(1)} %slice_bitcast_fusion.refs_2_, bf16[576,128]{1,0:T(8,128)(2,1)S(1)} %collective-permute-done.13.refs_3_, ...), custom_call_target="tpu_custom_call" | custom-call | flops 67108864 | bytes 223696 | tf_op jit(solution)/shard_map/end/pallas_call | solution.py:64
  (15 shorter events, 0.1 us)
Async XLA Ops:
  0.6 3.2 %collective-permute-start = (bf16[128,3584]{1,0:T(8,128)(2,1)}, bf16[128,3584]{1,0:T(8,128)(2,1)S(1)}, u32[]{:S(2)}, u32[]{:S(2)}) collective-permute-start(bf16[128,3584]{1,0:T(8,128)(2,1)} %refs_1_.1), channel_id=1, source_target_pairs={{0,4},{4,0},{8,12},{12,8},{16,20},{20,16},{24,28},{28,24},{1,5},{5... | collective-permute-start | bytes 2752520 | tf_op jit(solution)/shard_map/ppermute | solution.py:90
  1.1 2.6 %collective-permute-start.1 = (s32[1,8,32]{2,1,0:T(8,128)}, s32[1,8,32]{2,1,0:T(8,128)S(1)}, u32[]{:S(2)}, u32[]{:S(2)}) collective-permute-start(s32[1,8,32]{2,1,0:T(8,128)} %refs_0_.3), channel_id=1, source_target_pairs={{0,4},{4,0},{8,12},{12,8},{16,20},{20,16},{24,28},{28,24},{1,5},{5... | collective-permute-start | bytes 3080 | tf_op jit(solution)/shard_map/ppermute | solution.py:90
  3.8 12.6 %copy-start.10 = (s32[128,1]{0,1:T(1,128)S(1)}, s32[128,1]{0,1:T(1,128)}, u32[]{:S(2)}) copy-start(s32[128,1]{0,1:T(1,128)} %param.12) | copy-start | bytes 1540
  3.8 12.6 %copy-start.11 = (s32[1,8]{1,0:T(1,128)S(1)}, s32[1,8]{1,0:T(1,128)}, u32[]{:S(2)}) copy-start(s32[1,8]{1,0:T(1,128)} %refs_0_.2) | copy-start | bytes 100
  3.8 20.5 %copy-start.12 = (s32[1,8,32]{2,1,0:T(8,128)}, s32[1,8,32]{2,1,0:T(8,128)S(1)}, u32[]{:S(2)}) copy-start(s32[1,8,32]{2,1,0:T(8,128)S(1)} %collective-permute-done.1.refs_2_) | copy-start | bytes 3076
  3.8 19.2 %all-to-all-start = ((bf16[8,32,1792]{2,1,0:T(8,128)(2,1)}), bf16[8,32,1792]{2,1,0:T(8,128)(2,1)S(1)}, u32[]{:S(2)}, u32[]{:S(2)}) async-start(bf16[8,32,1792]{2,1,0:T(8,128)(2,1)} %get-tuple-element.64), calls=%async_computation | async-start | bytes 1835008 | tf_op jit(solution)/shard_map/all_to_all | solution.py:403
  9.0 7.4 %collective-permute-start.2 = (bf16[56,1024]{1,0:T(8,128)(2,1)S(1)}, bf16[56,1024]{1,0:T(8,128)(2,1)S(1)}, u32[]{:S(2)}, u32[]{:S(2)}) collective-permute-start(bf16[56,1024]{1,0:T(8,128)(2,1)S(1)} %get-tuple-element.57), channel_id=1, source_target_pairs={{0,1},{1,0},{2,3},{3,2},{4,5},{5,4},{6,7},{7,6},{8,9},{9,8},{10,11... | collective-permute-start | bytes 344072 | tf_op jit(solution)/shard_map/ppermute | solution.py:86
  10.6 11.8 %collective-permute-start.3 = (bf16[56,1024]{1,0:T(8,128)(2,1)S(1)}, bf16[56,1024]{1,0:T(8,128)(2,1)S(1)}, u32[]{:S(2)}, u32[]{:S(2)}) collective-permute-start(bf16[56,1024]{1,0:T(8,128)(2,1)S(1)} %get-tuple-element.67), channel_id=1, source_target_pairs={{0,2},{1,3},{2,0},{3,1},{4,6},{5,7},{6,4},{7,5},{8,10},{9,11},{10,... | collective-permute-start | bytes 344072 | tf_op jit(solution)/shard_map/ppermute | solution.py:86
  13.2 9.2 %collective-permute-start.4 = (bf16[56,1024]{1,0:T(8,128)(2,1)S(1)}, bf16[56,1024]{1,0:T(8,128)(2,1)S(1)}, u32[]{:S(2)}, u32[]{:S(2)}) collective-permute-start(bf16[56,1024]{1,0:T(8,128)(2,1)S(1)} %get-tuple-element.68), channel_id=1, source_target_pairs={{0,3},{1,2},{2,1},{3,0},{4,7},{5,6},{6,5},{7,4},{8,11},{9,10},{10,... | collective-permute-start | bytes 344072 | tf_op jit(solution)/shard_map/ppermute | solution.py:86
  24.3 5.0 %copy-start.2 = (bf16[128,3584]{1,0:T(8,128)(2,1)S(1)}, bf16[128,3584]{1,0:T(8,128)(2,1)}, u32[]{:S(2)}) copy-start(bf16[128,3584]{1,0:T(8,128)(2,1)} %refs_1_.1) | copy-start | bytes 2752516
  24.3 29.9 %all-to-all-start.1 = ((bf16[4,56,1792]{2,1,0:T(8,128)(2,1)}), bf16[4,56,1792]{2,1,0:T(8,128)(2,1)S(1)}, u32[]{:S(2)}, u32[]{:S(2)}) async-start(bf16[4,56,1792]{2,1,0:T(8,128)(2,1)} %get-tuple-element.81), calls=%async_computation.1 | async-start | bytes 1605632 | tf_op jit(solution)/shard_map/all_to_all | solution.py:430
  29.4 13.8 %copy-start.3 = (bf16[256,256]{1,0:T(8,128)(2,1)S(1)}, bf16[256,256]{1,0:T(8,128)(2,1)}, u32[]{:S(2)}) copy-start(bf16[256,256]{1,0:T(8,128)(2,1)} %get-tuple-element.60.refs_0_) | copy-start | bytes 393220
  30.6 8.4 %collective-permute-start.5 = (bf16[64,1792]{1,0:T(8,128)(2,1)S(1)}, bf16[64,1792]{1,0:T(8,128)(2,1)S(1)}, u32[]{:S(2)}, u32[]{:S(2)}) collective-permute-start(bf16[64,1792]{1,0:T(8,128)(2,1)S(1)} %get-tuple-element.72), channel_id=1, source_target_pairs={{0,8},{4,12},{8,0},{12,4},{16,24},{20,28},{24,16},{28,20},{1,9},{5... | collective-permute-start | bytes 688136 | tf_op jit(solution)/shard_map/ppermute | solution.py:96
  31.5 11.6 %collective-permute-start.6 = (bf16[64,1792]{1,0:T(8,128)(2,1)S(1)}, bf16[64,1792]{1,0:T(8,128)(2,1)S(1)}, u32[]{:S(2)}, u32[]{:S(2)}) collective-permute-start(bf16[64,1792]{1,0:T(8,128)(2,1)S(1)} %get-tuple-element.73), channel_id=1, source_target_pairs={{0,16},{4,20},{8,24},{12,28},{16,0},{20,4},{24,8},{28,12},{1,17},{... | collective-permute-start | bytes 688136 | tf_op jit(solution)/shard_map/ppermute | solution.py:96
  33.0 10.1 %collective-permute-start.7 = (bf16[64,1792]{1,0:T(8,128)(2,1)S(1)}, bf16[64,1792]{1,0:T(8,128)(2,1)S(1)}, u32[]{:S(2)}, u32[]{:S(2)}) collective-permute-start(bf16[64,1792]{1,0:T(8,128)(2,1)S(1)} %get-tuple-element.74), channel_id=1, source_target_pairs={{0,24},{4,28},{8,16},{12,20},{16,8},{20,12},{24,0},{28,4},{1,25},{... | collective-permute-start | bytes 688136 | tf_op jit(solution)/shard_map/ppermute | solution.py:96
  43.5 15.2 %collective-permute-start.8 = (bf16[56,1792]{1,0:T(8,128)(2,1)S(1)}, bf16[56,1792]{1,0:T(8,128)(2,1)S(1)}, u32[]{:S(2)}, u32[]{:S(2)}) collective-permute-start(bf16[56,1792]{1,0:T(8,128)(2,1)S(1)} %get-tuple-element.87), channel_id=1, source_target_pairs={{0,1},{1,0},{2,3},{3,2},{4,5},{5,4},{6,7},{7,6},{8,9},{9,8},{10,11... | collective-permute-start | bytes 602120 | tf_op jit(solution)/shard_map/ppermute | solution.py:86
  45.4 17.2 %collective-permute-start.9 = (bf16[56,1792]{1,0:T(8,128)(2,1)S(1)}, bf16[56,1792]{1,0:T(8,128)(2,1)S(1)}, u32[]{:S(2)}, u32[]{:S(2)}) collective-permute-start(bf16[56,1792]{1,0:T(8,128)(2,1)S(1)} %get-tuple-element.94), channel_id=1, source_target_pairs={{0,2},{1,3},{2,0},{3,1},{4,6},{5,7},{6,4},{7,5},{8,10},{9,11},{10,... | collective-permute-start | bytes 602120 | tf_op jit(solution)/shard_map/ppermute | solution.py:86
  47.7 14.8 %collective-permute-start.10 = (bf16[56,1792]{1,0:T(8,128)(2,1)S(1)}, bf16[56,1792]{1,0:T(8,128)(2,1)S(1)}, u32[]{:S(2)}, u32[]{:S(2)}) collective-permute-start(bf16[56,1792]{1,0:T(8,128)(2,1)S(1)} %get-tuple-element.95), channel_id=1, source_target_pairs={{0,3},{1,2},{2,1},{3,0},{4,7},{5,6},{6,5},{7,4},{8,11},{9,10},{10,... | collective-permute-start | bytes 602120 | tf_op jit(solution)/shard_map/ppermute | solution.py:86
  51.3 2.9 %copy-start = (bf16[1,3584,1024]{2,1,0:T(8,128)(2,1)}, bf16[1,3584,1024]{2,1,0:T(8,128)(2,1)S(1)}, u32[]{:S(2)}) copy-start(bf16[1,3584,1024]{2,1,0:T(8,128)(2,1)S(1)} %get-tuple-element.79.refs_0_.refs_2_.refs_7_) | copy-start | bytes 22020100
  54.2 3.1 %copy-start.1 = (bf16[1,3584,1024]{2,1,0:T(8,128)(2,1)S(1)}, bf16[1,3584,1024]{2,1,0:T(8,128)(2,1)}, u32[]{:S(2)}) copy-start(bf16[1,3584,1024]{2,1,0:T(8,128)(2,1)} %copy-done) | copy-start | bytes 22020100
  57.3 1.4 %copy-start.6 = (bf16[56,1024]{1,0:T(8,128)(2,1)S(1)}, bf16[56,1024]{1,0:T(8,128)(2,1)}, u32[]{:S(2)}) copy-start(bf16[56,1024]{1,0:T(8,128)(2,1)} %get-tuple-element.88.refs_7_) | copy-start | bytes 344068
  57.3 1.4 %copy-start.7 = (bf16[56,1024]{1,0:T(8,128)(2,1)S(1)}, bf16[56,1024]{1,0:T(8,128)(2,1)}, u32[]{:S(2)}) copy-start(bf16[56,1024]{1,0:T(8,128)(2,1)} %get-tuple-element.89.refs_8_) | copy-start | bytes 344068
  58.8 3.8 %copy-start.4 = (bf16[56,1024]{1,0:T(8,128)(2,1)S(1)}, bf16[56,1024]{1,0:T(8,128)(2,1)}, u32[]{:S(2)}) copy-start(bf16[56,1024]{1,0:T(8,128)(2,1)} %get-tuple-element.96.refs_12_) | copy-start | bytes 344068
  58.8 3.8 %copy-start.5 = (bf16[56,1024]{1,0:T(8,128)(2,1)S(1)}, bf16[56,1024]{1,0:T(8,128)(2,1)}, u32[]{:S(2)}) copy-start(bf16[56,1024]{1,0:T(8,128)(2,1)} %get-tuple-element.97.refs_13_) | copy-start | bytes 344068
  64.5 2.1 %collective-permute-start.11 = (bf16[4,576,128]{2,1,0:T(8,128)(2,1)S(1)}, bf16[4,576,128]{2,1,0:T(8,128)(2,1)S(1)}, u32[]{:S(2)}, u32[]{:S(2)}) collective-permute-start(bf16[4,576,128]{2,1,0:T(8,128)(2,1)S(1)} %get-tuple-element.99), channel_id=1, source_target_pairs={{0,4},{4,0},{8,12},{12,8},{16,20},{20,16},{24,28},{28,24},{1,5},{5... | collective-permute-start | bytes 1769480 | tf_op jit(solution)/shard_map/ppermute | solution.py:90
  66.7 10.1 %collective-permute-start.12 = (bf16[2,576,128]{2,1,0:T(8,128)(2,1)S(1)}, bf16[2,576,128]{2,1,0:T(8,128)(2,1)S(1)}, u32[]{:S(2)}, u32[]{:S(2)}) collective-permute-start(bf16[2,576,128]{2,1,0:T(8,128)(2,1)S(1)} %slice.28), channel_id=1, source_target_pairs={{0,16},{4,20},{8,24},{12,28},{16,0},{20,4},{24,8},{28,12},{1,17},{... | collective-permute-start | bytes 884744 | tf_op jit(solution)/shard_map/ppermute | solution.py:96
  69.5 11.7 %collective-permute-start.15 = (bf16[56,1024]{1,0:T(8,128)(2,1)S(1)}, bf16[56,1024]{1,0:T(8,128)(2,1)S(1)}, u32[]{:S(2)}, u32[]{:S(2)}) collective-permute-start(bf16[56,1024]{1,0:T(8,128)(2,1)S(1)} %get-tuple-element.102), channel_id=1, source_target_pairs={{0,2},{1,3},{2,0},{3,1},{4,6},{5,7},{6,4},{7,5},{8,10},{9,11},{10,... | collective-permute-start | bytes 344072 | tf_op jit(solution)/shard_map/ppermute | solution.py:86
  71.9 9.3 %collective-permute-start.16 = (bf16[56,1024]{1,0:T(8,128)(2,1)S(1)}, bf16[56,1024]{1,0:T(8,128)(2,1)S(1)}, u32[]{:S(2)}, u32[]{:S(2)}) collective-permute-start(bf16[56,1024]{1,0:T(8,128)(2,1)S(1)} %get-tuple-element.103), channel_id=1, source_target_pairs={{0,3},{1,2},{2,1},{3,0},{4,7},{5,6},{6,5},{7,4},{8,11},{9,10},{10,... | collective-permute-start | bytes 344072 | tf_op jit(solution)/shard_map/ppermute | solution.py:86
  74.3 8.5 %copy-start.8 = (bf16[128,256]{1,0:T(8,128)(2,1)S(1)}, bf16[128,256]{1,0:T(8,128)(2,1)}, u32[]{:S(2)}) copy-start(bf16[128,256]{1,0:T(8,128)(2,1)} %get-tuple-element.59.refs_0_) | copy-start | bytes 196612
  74.3 8.5 %copy-start.9 = (f32[128,1]{0,1:T(1,128)S(1)}, f32[128,1]{0,1:T(1,128)}, u32[]{:S(2)}) copy-start(f32[128,1]{0,1:T(1,128)} %param.13) | copy-start | bytes 1540
  74.3 7.6 %collective-permute-start.14 = (bf16[56,1024]{1,0:T(8,128)(2,1)S(1)}, bf16[56,1024]{1,0:T(8,128)(2,1)S(1)}, u32[]{:S(2)}, u32[]{:S(2)}) collective-permute-start(bf16[56,1024]{1,0:T(8,128)(2,1)S(1)} %get-tuple-element.101), channel_id=1, source_target_pairs={{0,1},{1,0},{2,3},{3,2},{4,5},{5,4},{6,7},{7,6},{8,9},{9,8},{10,11... | collective-permute-start | bytes 344072 | tf_op jit(solution)/shard_map/ppermute | solution.py:86
  76.9 5.8 %collective-permute-start.13 = (bf16[576,128]{1,0:T(8,128)(2,1)S(1)}, bf16[576,128]{1,0:T(8,128)(2,1)S(1)}, u32[]{:S(2)}, u32[]{:S(2)}) collective-permute-start(bf16[576,128]{1,0:T(8,128)(2,1)S(1)} %fusion), channel_id=1, source_target_pairs={{0,8},{4,12},{8,0},{12,4},{16,24},{20,28},{24,16},{28,20},{1,9},{5... | collective-permute-start | bytes 442376 | tf_op jit(solution)/shard_map/ppermute | solution.py:96

commit v5 on v4

--- a/solution.py
+++ b/solution.py
@@ -7,8 +7,8 @@
 from jax.experimental.pallas import tpu as pltpu
 from jax.sharding import PartitionSpec as P
 
-FIRST_PART = 1
-PARTS = 2
+FIRST_PART = 13
+PARTS = 28
 bf16 = jnp.bfloat16
 f32 = jnp.float32
 i32 = jnp.int32
@@ -86,6 +86,13 @@
     return lax.ppermute(block, "exp", [(i, i ^ step) for i in range(exp_count)])
 
 
+def swap_all(blocks, exp_count):
+    came = list(blocks)
+    for step in [*range(exp_count // 2, exp_count), *range(1, exp_count // 2)]:
+        came[step] = swap_exp(blocks[step], step, exp_count)
+    return came
+
+
 def swap_core(block, rep_count):
     return lax.ppermute(block, "rep", [(i, i ^ 1) for i in range(rep_count)])
 
@@ -117,7 +124,7 @@
     return one_hot(target == lax.broadcasted_iota(i32, (tokens, exp_count * padded), 1))
 
 
-def prepare_kernel(fetch_slots, capacity, padded, exp_count, counts, routes, pick, pick_swapped, home):
+def prepare_kernel(fetch_slots, capacity, padded, exp_count, counts, routes, pick, home):
     tokens = routes.shape[1]
     rep_count = counts.shape[1]
     replica = lax.axis_index("rep")
@@ -134,9 +141,8 @@
     home[...] = home_of
 
     places = lax.broadcasted_iota(i32, (tokens, rep_count * fetch_slots), 1)
-    for shard, matrix in ((source, pick), (jnp.bitwise_xor(source, replica), pick_swapped)):
-        place = shard * fetch_slots + position - start
-        matrix[...] = dot(home_of, one_hot(place == places), ((0,), (0,))).astype(bf16)
+    place = jnp.bitwise_xor(source, replica) * fetch_slots + position - start
+    pick[...] = dot(home_of, one_hot(place == places), ((0,), (0,))).astype(bf16)
 
 
 def part_of(chunk, width):
@@ -151,50 +157,60 @@
     return [found[number * fetch_slots : (number + 1) * fetch_slots] for number in range(len(asking))]
 
 
+def asking_chips(pairs):
+    return [jnp.bitwise_xor(lax.axis_index("rep"), 2 * step) for step in range(pairs)]
+
+
 def begin_kernel(capacity, padded, table_far, rows_far, routes_far, weight_far, grads_far, *refs):
-    served_far, *sent = refs[:-7]
-    table, rows, routes, weight, grads, served, sems = refs[-7:]
-    width = served.shape[2]
+    served, *sent = refs[:-6]
+    table, rows, routes, weight, grads, sems = refs[-6:]
+    width = rows.shape[1]
     fetches = [
         pltpu.make_async_copy(far, near, sems.at[number])
         for number, (far, near) in enumerate(
             (
-                (table_far, table),
-                (rows_far.at[:, :width], rows),
                 (routes_far, routes),
                 (weight_far, weight),
                 (grads_far, grads),
+                (table_far, table),
+                (rows_far.at[:, :width], rows),
             )
         )
     ]
-    store = pltpu.make_async_copy(served, served_far, sems.at[5])
     for copy in fetches:
         copy.start()
-    for copy in fetches[:2]:
-        copy.wait()
-    for replica, found in enumerate(serve(table, rows[...], range(served.shape[0]))):
-        served[replica] = found
-    store.start()
-    for copy in fetches[2:]:
+    for copy in fetches[:3]:
         copy.wait()
     home = slot_spots(capacity, padded, len(sent), routes)
     scaled = (upright(weight[...]) * grads[...].astype(f32)).astype(bf16)
     by_slot = dot(home, scaled, ((0,), (0,))).astype(bf16)
     for step in range(len(sent)):
         sent[step][...] = by_slot[step * padded : step * padded + capacity]
-    store.wait()
+    for copy in fetches[3:]:
+        copy.wait()
+    for step, found in enumerate(serve(table, rows[...], asking_chips(served.shape[0]))):
+        served[step] = found
+
+
+def serve_first_kernel(table, rows, own, *served):
+    fetch_slots = own.shape[1]
+    width = own.shape[2]
+    for step, found in enumerate(serve(table, rows[:, :width], asking_chips(len(served)))):
+        served[step][:fetch_slots] = own[step]
+        served[step][fetch_slots:] = found
 
 
 def serve_last_kernel(own_table, own_rows, pair_table, pair_rows, *served):
     fetch_slots = own_table.shape[2]
     width = served[0].shape[1]
-    asking = [jnp.bitwise_xor(lax.axis_index("rep"), 2 * step) for step in range(len(served))]
+    asking = asking_chips(len(served))
     for table, rows, base in ((own_table, own_rows, 0), (pair_table, pair_rows, fetch_slots)):
         for block, found in zip(served, serve(table, rows[:, rows.shape[1] - width :], asking)):
             block[base : base + fetch_slots] = found
 
 
-def pick_first_kernel(capacity, padded, pick, arrived, *refs):
+def pick_first_kernel(capacity, padded, chips, pick, *refs):
+    arrived, refs = refs[:chips], refs[chips:]
     exp_count = (len(refs) - 3) // 2
     grads, refs = refs[:exp_count], refs[exp_count:]
     sent_far, grads_far, (sent, sems) = refs[0], refs[1 : exp_count + 1], refs[exp_count + 1 :]
@@ -204,8 +220,8 @@
     ]
     for copy in put_away:
         copy.start()
-    shards, rows, width = arrived.shape
-    by_slot = dot(pick[...], arrived[...].reshape(shards * rows, width)).astype(bf16)
+    rows = jnp.concatenate([block[...] for block in arrived], axis=0)
+    by_slot = dot(pick[...], rows).astype(bf16)
     column = lax.axis_index("exp")
     for step in range(exp_count):
         sent[step] = by_slot[step * padded : step * padded + capacity]
@@ -383,40 +399,46 @@
     near = pl.BlockSpec(memory_space=pltpu.VMEM)
     served, *grads = pl.pallas_call(
         functools.partial(begin_kernel, capacity, padded),
-        out_shape=[pltpu.HBM((rep_count, fetch_slots, first_width), bf16)]
+        out_shape=[shape((pairs, fetch_slots, first_width), bf16)]
         + [shape((capacity, hidden_units), bf16)] * exp_count,
         in_specs=[far] * len(operands),
-        out_specs=[far] + [near] * exp_count,
+        out_specs=[near] * (1 + exp_count),
         scratch_shapes=[
             pltpu.VMEM(shard_request_index.shape, i32),
             pltpu.VMEM((shard_rows, first_width), bf16),
             pltpu.VMEM(routes_row.shape, i32),
             pltpu.VMEM(weight_row.shape, f32),
             pltpu.VMEM(output_gradient.shape, bf16),
-            pltpu.VMEM((rep_count, fetch_slots, first_width), bf16),
-            pltpu.SemaphoreType.DMA((6,)),
+            pltpu.SemaphoreType.DMA((5,)),
         ],
         compiler_params=pltpu.CompilerParams(vmem_limit_bytes=16 * 1024 * 1024),
         name="begin",
     )(*[pltpu.with_memory_space_constraint(array, pltpu.HBM) for array in operands])
-    served, routes_row, pair_rows, pair_table = lax.optimization_barrier((served, routes_row, pair_rows, pair_table))
-    arrived = lax.all_to_all(served, "rep", 0, 0, tiled=True)
-    grads = [swap_exp(block, step, exp_count) for step, block in enumerate(grads)]
-    routes_row, grads[1] = lax.optimization_barrier((routes_row, grads[1]))
-    pick, pick_swapped, home = call(
+    *grads, pair_table, pair_rows = lax.optimization_barrier((*grads, pair_table, pair_rows))
+    served = call(
+        serve_first_kernel,
+        [shape((2 * fetch_slots, first_width), bf16)] * pairs,
+        [pair_table, pair_rows, served],
+        flops=2 * fetched_rows * shard_rows * first_width,
+        name="serve_first",
+    )
+    *served, routes_row, pair_rows = lax.optimization_barrier((*served, routes_row, pair_rows))
+    arrived = [swap_chip(block, step, rep_count) for step, block in enumerate(served)]
+    grads = swap_all(grads, exp_count)
+    pick, home = call(
         functools.partial(prepare_kernel, fetch_slots, capacity, padded, exp_count),
-        [shape((slots, fetched_rows), bf16)] * 2 + [shape((token_count, slots), bf16)],
+        [shape((slots, fetched_rows), bf16), shape((token_count, slots), bf16)],
         [replica_fetch_count, routes_row],
         counts=replica_fetch_count,
-        stored=[1, 2],
-        flops=4 * token_count * slots * fetched_rows,
+        stored=[1],
+        flops=2 * token_count * slots * fetched_rows,
         name="prepare",
     )
     sent, *grads = pl.pallas_call(
-        functools.partial(pick_first_kernel, capacity, padded),
+        functools.partial(pick_first_kernel, capacity, padded, pairs),
         out_shape=[pltpu.HBM((exp_count, capacity, first_width), bf16)]
         + [pltpu.HBM((capacity, hidden_units), bf16)] * exp_count,
-        in_specs=[near] * (2 + exp_count),
+        in_specs=[near] * (1 + pairs + exp_count),
         out_specs=[far] * (1 + exp_count),
         scratch_shapes=[
             pltpu.VMEM((exp_count, capacity, first_width), bf16),
@@ -424,7 +446,8 @@
         ],
         compiler_params=pltpu.CompilerParams(vmem_limit_bytes=16 * 1024 * 1024),
         name="pick_first",
-    )(pick, arrived, *grads)
+    )(pick, *arrived, *grads[exp_count // 2 :], *grads[: exp_count // 2])
+    grads = [*grads[exp_count // 2 :], *grads[: exp_count // 2]]
 
     pair_rows, sent = lax.optimization_barrier((pair_rows, sent))
     first_blocks = lax.all_to_all(sent, "exp", 0, 0, tiled=True)
@@ -440,7 +463,7 @@
     first_sent, *sent = call(
         functools.partial(pick_last_kernel, capacity, padded, pairs),
         [shape((capacity, last_width), bf16)] * exp_count,
-        [pick_swapped, *arrived],
+        [pick, *arrived],
         flops=2 * slots * fetched_rows * last_width,
         name="pick_last",
     )
@@ -456,7 +479,7 @@
         name="fetch",
     )(*[pltpu.with_memory_space_constraint(array, pltpu.HBM) for array in weights])
     weights = [pltpu.with_memory_space_constraint(array, pltpu.VMEM) for array in weights]
-    last_blocks = [swap_exp(block, step, exp_count) for step, block in enumerate((first_sent, *sent))]
+    last_blocks = swap_all([first_sent, *sent], exp_count)
 
     turned, pre_first, adapted_first = call(
         functools.partial(partial_kernel, capacity, padded),
@@ -516,7 +539,7 @@
     activated += late
 
     pair_terms = swap_core(give, rep_count)
-    results = [swap_exp(block, step, exp_count) for step, block in enumerate(activated)]
+    results = swap_all(activated, exp_count)
     terms = keep + pair_terms.astype(f32)
     while terms.shape[0] > 2:
         half = terms.shape[0] // 2

time: 84.1 us -> 80.2 us (0.954)
  waiting for transfers between devices: 27.2 us -> 24 us
    all_to_all x1 -> x0, starting transfers between devices: 5.15 us -> none  [body(): arrived = lax.all_to_all(served, 'rep', 0, 0, tiled=True)]
    ppermute x9, starting transfers between devices: 13.6 us -> 18.4 us  [swap_exp(): return lax.ppermute(block, 'exp', [(i, i ^ step) for i in range(exp_count)])]
    ppermute x9, waiting for transfers between devices: 12.2 us -> 10.2 us  [swap_exp(): return lax.ppermute(block, 'exp', [(i, i ^ step) for i in range(exp_count)])]
    ppermute x5 -> x8, starting transfers between devices: 8.88 us -> 10.2 us  [swap_chip(): lax.ppermute(block, 'rep', [(i, i ^ 2 * step) for i in range(rep_count)])]
    all_to_all x1, starting transfers between devices: 5.02 us -> 3.81 us  [body(): first_blocks = lax.all_to_all(sent, 'exp', 0, 0, tiled=True)]
    ppermute x5 -> x8, waiting for transfers between devices: 12.4 us -> 11.7 us  [swap_chip(): lax.ppermute(block, 'rep', [(i, i ^ 2 * step) for i in range(rep_count)])]
    pallas_call x7 -> x8, Pallas kernels: 8.96 us -> 9.04 us  [call(): pl.pallas_call(moving, out_shape=[pltpu.HBM(out.shape, out.dtype) if numb...]
    unnamed x26 -> x24, local copies, waits for them, and re-layouts: 6.03 us -> 6.02 us
  transfers between devices with their start and end apart: 19 -> 21, of which waited for: 11 -> 12; matrix products, arithmetic and copies ran while one was open for 0% -> 0% of each run, Pallas kernels for 14% -> 14%
where the time goes in v5:
time: 80.2 us; the launch traced here: 79.9 us
  starting transfers between devices  33 us (41%)
  waiting for transfers between devices  24 us (30%)
  Pallas kernels  15.7 us (20%)
  local copies, waits for them, and re-layouts  6.09 us (8%)
  between operations  0.83 us (1%)
    ppermute x9, starting transfers between devices, swap_exp(): return lax.ppermute(block, 'exp', [(i, i ^ step) for i in range(exp_count)])  18.4 us
    ppermute x8, waiting for transfers between devices, swap_chip(): lax.ppermute(block, 'rep', [(i, i ^ 2 * step) for i in range(rep_count)])  11.7 us
    ppermute x9, waiting for transfers between devices, swap_exp(): return lax.ppermute(block, 'exp', [(i, i ^ step) for i in range(exp_count)])  10.2 us
    ppermute x8, starting transfers between devices, swap_chip(): lax.ppermute(block, 'rep', [(i, i ^ 2 * step) for i in range(rep_count)])  10.2 us
    pallas_call x8, Pallas kernels, call(): pl.pallas_call(moving, out_shape=[pltpu.HBM(out.shape, out.dtype) if numb...  9.04 us
    unnamed x24, local copies, waits for them, and re-layouts  6.02 us
    all_to_all x1, starting transfers between devices, body(): first_blocks = lax.all_to_all(sent, 'exp', 0, 0, tiled=True)  3.81 us
    pallas_call x1, Pallas kernels, body(): pl.pallas_call(fetch_kernel, out_shape=[pltpu.VMEM(array.shape, array.dty...  3.32 us
  transfers between devices with their start and end apart: 21, of which 12 were waited for; matrix products, arithmetic and copies ran while one was open for 0% of the time, Pallas kernels for 14%

profile of v5, /device:TPU:0, one launch (start us, length us, event | category | flops | bytes accessed | tf_op | source)
XLA Modules:
  0.0 79.9 jit_solution(10307822545817280469)
XLA Ops:
  0.6 0.5 collective-permute-start.1
  1.1 0.1 collective-permute-start
  1.2 2.1 %begin.1 = (bf16[4,32,1664]{2,1,0:T(8,128)(2,1)S(1)}, bf16[56,1024]{1,0:T(8,128)(2,1)S(1)}, bf16[56,1024]{1,0:T(8,128)(2,1)S(1)}, bf16[56,1024]{1,0:T(8,128)(2,1)S(1)}, bf16[56,1024]{1,0:T(8,128)(2,1)S(1)}) custom-call(s32[1,8,32]{2,1,0:T(8,128)} %refs_0_.3, bf16[128,3584]{1,0:T(8,128)(2,1)} %refs_1_.1, s32[1,128]{1,0:T(1,128)} %bitcast.8, ...), custom_call_target="tpu_custom_call" | custom-call | tf_op jit(solution)/shard_map/begin/pallas_call | solution.py:400
  3.3 0.1 collective-permute-done.refs_0_.refs_2_
  3.5 0.0 collective-permute-done.1.refs_1_.refs_3_
  3.5 4.0 %collective-permute-start.5 = (bf16[56,1024]{1,0:T(8,128)(2,1)S(1)}, bf16[56,1024]{1,0:T(8,128)(2,1)S(1)}, u32[]{:S(2)}, u32[]{:S(2)}) collective-permute-start(bf16[56,1024]{1,0:T(8,128)(2,1)S(1)} %get-tuple-element.83), channel_id=1, source_target_pairs={{0,2},{1,3},{2,0},{3,1},{4,6},{5,7},{6,4},{7,5},{8,10},{9,11},{10,... | collective-permute-start | bytes 344072 | tf_op jit(solution)/shard_map/ppermute | solution.py:86
  7.4 0.4 serve_first.1
  7.8 1.6 %collective-permute-start.2 = (bf16[64,1664]{1,0:T(8,128)(2,1)S(1)}, bf16[64,1664]{1,0:T(8,128)(2,1)S(1)}, u32[]{:S(2)}, u32[]{:S(2)}) collective-permute-start(bf16[64,1664]{1,0:T(8,128)(2,1)S(1)} %get-tuple-element.80), channel_id=1, source_target_pairs={{0,8},{4,12},{8,0},{12,4},{16,24},{20,28},{24,16},{28,20},{1,9},{5... | collective-permute-start | bytes 638984 | tf_op jit(solution)/shard_map/ppermute | solution.py:103
  9.4 1.5 %collective-permute-start.3 = (bf16[64,1664]{1,0:T(8,128)(2,1)S(1)}, bf16[64,1664]{1,0:T(8,128)(2,1)S(1)}, u32[]{:S(2)}, u32[]{:S(2)}) collective-permute-start(bf16[64,1664]{1,0:T(8,128)(2,1)S(1)} %get-tuple-element.81), channel_id=1, source_target_pairs={{0,16},{4,20},{8,24},{12,28},{16,0},{20,4},{24,8},{28,12},{1,17},{... | collective-permute-start | bytes 638984 | tf_op jit(solution)/shard_map/ppermute | solution.py:103
  10.9 0.5 collective-permute-start.4
  11.4 1.3 %collective-permute-start.6 = (bf16[56,1024]{1,0:T(8,128)(2,1)S(1)}, bf16[56,1024]{1,0:T(8,128)(2,1)S(1)}, u32[]{:S(2)}, u32[]{:S(2)}) collective-permute-start(bf16[56,1024]{1,0:T(8,128)(2,1)S(1)} %get-tuple-element.84), channel_id=1, source_target_pairs={{0,3},{1,2},{2,1},{3,0},{4,7},{5,6},{6,5},{7,4},{8,11},{9,10},{10,... | collective-permute-start | bytes 344072 | tf_op jit(solution)/shard_map/ppermute | solution.py:86
  12.7 0.6 collective-permute-done.5.refs_4_
  13.3 2.1 %collective-permute-start.7 = (bf16[56,1024]{1,0:T(8,128)(2,1)S(1)}, bf16[56,1024]{1,0:T(8,128)(2,1)S(1)}, u32[]{:S(2)}, u32[]{:S(2)}) collective-permute-start(bf16[56,1024]{1,0:T(8,128)(2,1)S(1)} %get-tuple-element.86), channel_id=1, source_target_pairs={{0,1},{1,0},{2,3},{3,2},{4,5},{5,4},{6,7},{7,6},{8,9},{9,8},{10,11... | collective-permute-start | bytes 344072 | tf_op jit(solution)/shard_map/ppermute | solution.py:86
  15.5 0.0 copy-done.10
  15.5 0.0 copy-done.11
  15.5 1.5 %prepare.1 = (bf16[256,256]{1,0:T(8,128)(2,1)S(1)}, bf16[128,256]{1,0:T(8,128)(2,1)}) custom-call(s32[1,8]{1,0:T(1,128)S(1)} %copy-done.11, s32[1,128]{1,0:T(1,128)S(1)} %bitcast.9), custom_call_target="tpu_custom_call" | custom-call | flops 16777216 | bytes 55924 | tf_op jit(solution)/shard_map/prepare/pallas_call | solution.py:64
  17.0 1.1 %collective-permute-done.6.refs_5_ = bf16[56,1024]{1,0:T(8,128)(2,1)S(1)} collective-permute-done((bf16[56,1024]{1,0:T(8,128)(2,1)S(1)}, bf16[56,1024]{1,0:T(8,128)(2,1)S(1)}, u32[]{:S(2)}, u32[]{:S(2)}) %collective-permute-start.6) | collective-permute-done | bytes 114720 | tf_op jit(solution)/shard_map/ppermute | solution.py:86
  18.1 1.7 %collective-permute-done.7.refs_7_ = bf16[56,1024]{1,0:T(8,128)(2,1)S(1)} collective-permute-done((bf16[56,1024]{1,0:T(8,128)(2,1)S(1)}, bf16[56,1024]{1,0:T(8,128)(2,1)S(1)}, u32[]{:S(2)}, u32[]{:S(2)}) %collective-permute-start.7) | collective-permute-done | bytes 114720 | tf_op jit(solution)/shard_map/ppermute | solution.py:86
  19.8 0.0 collective-permute-done.2.refs_1_
  19.8 0.9 %collective-permute-done.3.refs_2_ = bf16[64,1664]{1,0:T(8,128)(2,1)S(1)} collective-permute-done((bf16[64,1664]{1,0:T(8,128)(2,1)S(1)}, bf16[64,1664]{1,0:T(8,128)(2,1)S(1)}, u32[]{:S(2)}, u32[]{:S(2)}) %collective-permute-start.3) | collective-permute-done | bytes 213024 | tf_op jit(solution)/shard_map/ppermute | solution.py:103
  20.7 0.0 collective-permute-done.4.refs_3_
  20.7 1.3 %pick_first.1 = (bf16[4,56,1664]{2,1,0:T(8,128)(2,1)}, bf16[56,1024]{1,0:T(8,128)(2,1)}, bf16[56,1024]{1,0:T(8,128)(2,1)}, bf16[56,1024]{1,0:T(8,128)(2,1)}, bf16[56,1024]{1,0:T(8,128)(2,1)}) custom-call(bf16[256,256]{1,0:T(8,128)(2,1)S(1)} %get-tuple-element.77.pick.refs_0_, bf16[64,1664]{1,0:T(8,128)(2,1)S(1)} %get-tuple-element.79.refs_0_, ...), custom_call_target="tpu_custom_call" | custom-call | tf_op jit(solution)/shard_map/pick_first/pallas_call | solution.py:437
  22.0 0.0 copy-done.8
  22.0 3.8 %all-to-all-start = ((bf16[4,56,1664]{2,1,0:T(8,128)(2,1)}), bf16[4,56,1664]{2,1,0:T(8,128)(2,1)S(1)}, u32[]{:S(2)}, u32[]{:S(2)}) async-start(bf16[4,56,1664]{2,1,0:T(8,128)(2,1)} %get-tuple-element.99), calls=%async_computation | async-start | bytes 1490944 | tf_op jit(solution)/shard_map/all_to_all | solution.py:453
  25.8 1.2 %serve_last.1 = (bf16[64,1920]{1,0:T(8,128)(2,1)S(1)}, bf16[64,1920]{1,0:T(8,128)(2,1)S(1)}, bf16[64,1920]{1,0:T(8,128)(2,1)S(1)}, bf16[64,1920]{1,0:T(8,128)(2,1)S(1)}) custom-call(s32[1,8,32]{2,1,0:T(8,128)} %refs_0_.3, bf16[128,3584]{1,0:T(8,128)(2,1)S(1)} %copy-done.2, s32[1,8,32]{2,1,0:T(8,128)} %copy-done.8, ...), custom_call_target="tpu_custom_call" | custom-call | flops 125829120 | bytes 419430 | tf_op jit(solution)/shard_map/serve_last/pallas_call | solution.py:64
  27.1 1.6 %collective-permute-start.8 = (bf16[64,1920]{1,0:T(8,128)(2,1)S(1)}, bf16[64,1920]{1,0:T(8,128)(2,1)S(1)}, u32[]{:S(2)}, u32[]{:S(2)}) collective-permute-start(bf16[64,1920]{1,0:T(8,128)(2,1)S(1)} %get-tuple-element.90), channel_id=1, source_target_pairs={{0,8},{4,12},{8,0},{12,4},{16,24},{20,28},{24,16},{28,20},{1,9},{5... | collective-permute-start | bytes 737288 | tf_op jit(solution)/shard_map/ppermute | solution.py:103
  28.6 1.5 %collective-permute-start.9 = (bf16[64,1920]{1,0:T(8,128)(2,1)S(1)}, bf16[64,1920]{1,0:T(8,128)(2,1)S(1)}, u32[]{:S(2)}, u32[]{:S(2)}) collective-permute-start(bf16[64,1920]{1,0:T(8,128)(2,1)S(1)} %get-tuple-element.91), channel_id=1, source_target_pairs={{0,16},{4,20},{8,24},{12,28},{16,0},{20,4},{24,8},{28,12},{1,17},{... | collective-permute-start | bytes 737288 | tf_op jit(solution)/shard_map/ppermute | solution.py:103
  30.1 0.5 collective-permute-start.10
  30.6 5.4 %collective-permute-done.8.refs_2_ = bf16[64,1920]{1,0:T(8,128)(2,1)S(1)} collective-permute-done((bf16[64,1920]{1,0:T(8,128)(2,1)S(1)}, bf16[64,1920]{1,0:T(8,128)(2,1)S(1)}, u32[]{:S(2)}, u32[]{:S(2)}) %collective-permute-start.8) | collective-permute-done | bytes 245792 | tf_op jit(solution)/shard_map/ppermute | solution.py:103
  36.0 4.2 %collective-permute-done.9.refs_3_ = bf16[64,1920]{1,0:T(8,128)(2,1)S(1)} collective-permute-done((bf16[64,1920]{1,0:T(8,128)(2,1)S(1)}, bf16[64,1920]{1,0:T(8,128)(2,1)S(1)}, u32[]{:S(2)}, u32[]{:S(2)}) %collective-permute-start.9) | collective-permute-done | bytes 245792 | tf_op jit(solution)/shard_map/ppermute | solution.py:103
  40.3 0.0 collective-permute-done.10.refs_4_
  40.3 0.4 pick_last.1
  40.7 1.8 %collective-permute-start.11 = (bf16[56,1920]{1,0:T(8,128)(2,1)S(1)}, bf16[56,1920]{1,0:T(8,128)(2,1)S(1)}, u32[]{:S(2)}, u32[]{:S(2)}) collective-permute-start(bf16[56,1920]{1,0:T(8,128)(2,1)S(1)} %get-tuple-element.105), channel_id=1, source_target_pairs={{0,1},{1,0},{2,3},{3,2},{4,5},{5,4},{6,7},{7,6},{8,9},{9,8},{10,11... | collective-permute-start | bytes 645128 | tf_op jit(solution)/shard_map/ppermute | solution.py:86
  42.5 2.4 %collective-permute-start.12 = (bf16[56,1920]{1,0:T(8,128)(2,1)S(1)}, bf16[56,1920]{1,0:T(8,128)(2,1)S(1)}, u32[]{:S(2)}, u32[]{:S(2)}) collective-permute-start(bf16[56,1920]{1,0:T(8,128)(2,1)S(1)} %get-tuple-element.112), channel_id=1, source_target_pairs={{0,2},{1,3},{2,0},{3,1},{4,6},{5,7},{6,4},{7,5},{8,10},{9,11},{10,... | collective-permute-start | bytes 645128 | tf_op jit(solution)/shard_map/ppermute | solution.py:86
  44.9 0.3 collective-permute-start.13
  45.2 3.3 %fetch.1 = (bf16[1,3584,1024]{2,1,0:T(8,128)(2,1)S(1)}, bf16[1,3584,128]{2,1,0:T(8,128)(2,1)S(1)}, bf16[1,128,1024]{2,1,0:T(8,128)(2,1)S(1)}) custom-call(bf16[1,3584,1024]{2,1,0:T(8,128)(2,1)} %refs_0_.4, bf16[1,3584,128]{2,1,0:T(8,128)(2,1)} %refs_1_.2, bf16[1,128,1024]{2,1,0:T(8,128)(2,1)} %refs_2_), custom_call_target="tpu_custom_call" | custom-call | tf_op jit(solution)/shard_map/fetch/pallas_call | solution.py:472
  48.5 2.9 %copy-done = bf16[1,3584,1024]{2,1,0:T(8,128)(2,1)} copy-done((bf16[1,3584,1024]{2,1,0:T(8,128)(2,1)}, bf16[1,3584,1024]{2,1,0:T(8,128)(2,1)S(1)}, u32[]{:S(2)}) %copy-start) | copy-done | bytes 7340056
  51.4 0.0 all-to-all-done.refs_2_
  51.4 3.1 %copy-done.1 = bf16[1,3584,1024]{2,1,0:T(8,128)(2,1)S(1)} copy-done((bf16[1,3584,1024]{2,1,0:T(8,128)(2,1)S(1)}, bf16[1,3584,1024]{2,1,0:T(8,128)(2,1)}, u32[]{:S(2)}) %copy-start.1) | copy-done | bytes 7340056
  54.5 1.3 %partial.1 = (bf16[1664,256]{1,0:T(8,128)(2,1)S(1)}, f32[256,1024]{1,0:T(8,128)S(1)}, f32[256,128]{1,0:T(8,128)S(1)}) custom-call(bf16[1,3584,1024]{2,1,0:T(8,128)(2,1)S(1)} %copy-done.1, bf16[1,3584,128]{2,1,0:T(8,128)(2,1)S(1)} %get-tuple-element.98.refs_1_.refs_3_.refs_8_, bf16[4,56,1664]{2,1,0:T(8,128)(2,1)S(1)} %all-to-all-done.refs_2_), custom_call_target="tpu_custom_call" | custom-call | flops 981467136 | bytes 3271557 | tf_op jit(solution)/shard_map/partial/pallas_call | solution.py:64
  55.8 0.0 collective-permute-done.11.refs_6_
  55.9 0.0 copy-start.3
  55.9 0.0 copy-start.4
  55.9 1.2 %early.1 = (bf16[56,1024]{1,0:T(8,128)(2,1)S(1)}, bf16[56,1024]{1,0:T(8,128)(2,1)S(1)}, bf16[1920,128]{1,0:T(8,128)(2,1)S(1)}, bf16[128,128]{1,0:T(8,128)(2,1)S(...) custom-call(f32[256,1024]{1,0:T(8,128)S(1)} %get-tuple-element.101.refs_0_.refs_5_, ...), custom_call_target="tpu_custom_call" | custom-call | flops 566231040 | bytes 1887436 | tf_op jit(solution)/shard_map/early/pallas_call | solution.py:64
  57.1 2.3 %collective-permute-done.12.refs_10_ = bf16[56,1920]{1,0:T(8,128)(2,1)S(1)} collective-permute-done((bf16[56,1920]{1,0:T(8,128)(2,1)S(1)}, bf16[56,1920]{1,0:T(8,128)(2,1)S(1)}, u32[]{:S(2)}, u32[]{:S(2)}) %collective-permute-start.12) | collective-permute-done | bytes 215072 | tf_op jit(solution)/shard_map/ppermute | solution.py:86
  59.3 0.0 collective-permute-done.13.refs_11_
  59.3 0.0 copy-done.4
  59.3 2.0 %late.1 = (bf16[56,1024]{1,0:T(8,128)(2,1)S(1)}, bf16[56,1024]{1,0:T(8,128)(2,1)S(1)}, f32[4,576,128]{2,1,0:T(8,128)S(1)}, bf16[4,576,128]{2,1,0:T(8,128)(2,1)S(1)}) custom-call(bf16[1664,256]{1,0:T(8,128)(2,1)S(1)} %get-tuple-element.100.refs_0_, bf16[1920,128]{1,0:T(8,128)(2,1)S(1)} %get-tuple-element.108.refs_1_, ...), custom_call_target="tpu_custom_call" | custom-call | flops 1035993088 | bytes 3453310 | tf_op jit(solution)/shard_map/late/pallas_call | solution.py:64
  61.3 0.1 collective-permute-start.14
  61.4 2.0 %collective-permute-done.14 = bf16[4,576,128]{2,1,0:T(8,128)(2,1)S(1)} collective-permute-done((bf16[4,576,128]{2,1,0:T(8,128)(2,1)S(1)}, bf16[4,576,128]{2,1,0:T(8,128)(2,1)S(1)}, u32[]{:S(2)}, u32[]{:S(2)}) %collective-permute-start.14) | collective-permute-done | bytes 589856 | tf_op jit(solution)/shard_map/ppermute | solution.py:97
  63.4 0.1 convert_add_fusion
  63.5 1.5 %collective-permute-start.15 = (bf16[2,576,128]{2,1,0:T(8,128)(2,1)S(1)}, bf16[2,576,128]{2,1,0:T(8,128)(2,1)S(1)}, u32[]{:S(2)}, u32[]{:S(2)}) collective-permute-start(bf16[2,576,128]{2,1,0:T(8,128)(2,1)S(1)} %slice.28), channel_id=1, source_target_pairs={{0,16},{4,20},{8,24},{12,28},{16,0},{20,4},{24,8},{28,12},{1,17},{... | collective-permute-start | bytes 884744 | tf_op jit(solution)/shard_map/ppermute | solution.py:103
  65.0 4.1 %collective-permute-start.18 = (bf16[56,1024]{1,0:T(8,128)(2,1)S(1)}, bf16[56,1024]{1,0:T(8,128)(2,1)S(1)}, u32[]{:S(2)}, u32[]{:S(2)}) collective-permute-start(bf16[56,1024]{1,0:T(8,128)(2,1)S(1)} %get-tuple-element.120), channel_id=1, source_target_pairs={{0,2},{1,3},{2,0},{3,1},{4,6},{5,7},{6,4},{7,5},{8,10},{9,11},{10,... | collective-permute-start | bytes 344072 | tf_op jit(solution)/shard_map/ppermute | solution.py:86
  69.2 2.4 %collective-permute-start.19 = (bf16[56,1024]{1,0:T(8,128)(2,1)S(1)}, bf16[56,1024]{1,0:T(8,128)(2,1)S(1)}, u32[]{:S(2)}, u32[]{:S(2)}) collective-permute-start(bf16[56,1024]{1,0:T(8,128)(2,1)S(1)} %get-tuple-element.121), channel_id=1, source_target_pairs={{0,3},{1,2},{2,1},{3,0},{4,7},{5,6},{6,5},{7,4},{8,11},{9,10},{10,... | collective-permute-start | bytes 344072 | tf_op jit(solution)/shard_map/ppermute | solution.py:86
  71.5 0.0 collective-permute-start.17
  71.5 1.1 %collective-permute-done.15 = bf16[2,576,128]{2,1,0:T(8,128)(2,1)S(1)} collective-permute-done((bf16[2,576,128]{2,1,0:T(8,128)(2,1)S(1)}, bf16[2,576,128]{2,1,0:T(8,128)(2,1)S(1)}, u32[]{:S(2)}, u32[]{:S(2)}) %collective-permute-start.15) | collective-permute-done | bytes 294944 | tf_op jit(solution)/shard_map/ppermute | solution.py:103
  72.6 0.1 slice_add_fusion
  72.7 1.6 %collective-permute-start.16 = (bf16[576,128]{1,0:T(8,128)(2,1)S(1)}, bf16[576,128]{1,0:T(8,128)(2,1)S(1)}, u32[]{:S(2)}, u32[]{:S(2)}) collective-permute-start(bf16[576,128]{1,0:T(8,128)(2,1)S(1)} %fusion), channel_id=1, source_target_pairs={{0,8},{4,12},{8,0},{12,4},{16,24},{20,28},{24,16},{28,20},{1,9},{5... | collective-permute-start | bytes 442376 | tf_op jit(solution)/shard_map/ppermute | solution.py:103
  74.3 3.7 %collective-permute-done.18.refs_6_ = bf16[56,1024]{1,0:T(8,128)(2,1)S(1)} collective-permute-done((bf16[56,1024]{1,0:T(8,128)(2,1)S(1)}, bf16[56,1024]{1,0:T(8,128)(2,1)S(1)}, u32[]{:S(2)}, u32[]{:S(2)}) %collective-permute-start.18) | collective-permute-done | bytes 114720 | tf_op jit(solution)/shard_map/ppermute | solution.py:86
  78.0 0.0 collective-permute-done.19.refs_7_
  78.0 0.8 %collective-permute-done.17.refs_5_ = bf16[56,1024]{1,0:T(8,128)(2,1)S(1)} collective-permute-done((bf16[56,1024]{1,0:T(8,128)(2,1)S(1)}, bf16[56,1024]{1,0:T(8,128)(2,1)S(1)}, u32[]{:S(2)}, u32[]{:S(2)}) %collective-permute-start.17) | collective-permute-done | bytes 114720 | tf_op jit(solution)/shard_map/ppermute | solution.py:86
  78.9 0.0 collective-permute-done.16.refs_3_
  78.9 0.0 copy-done.9
  78.9 1.0 %end.1 = (f32[1,448,128]{2,1,0:T(8,128)}, f32[1,16,1024]{2,1,0:T(8,128)}, bf16[128,1024]{1,0:T(8,128)(2,1)}) custom-call(bf16[128,256]{1,0:T(8,128)(2,1)S(1)} %copy-done.7, f32[1,128]{1,0:T(1,128)S(1)} %bitcast.7, f32[576,128]{1,0:T(8,128)S(1)} %slice_bitcast_fusion.refs_2_, bf16[576,128]{1,0:T(8,128)(2,1)S(1)} %collective-permute-done.16.refs_3_, ...), custom_call_target="tpu_custom_call" | custom-call | flops 67108864 | bytes 223696 | tf_op jit(solution)/shard_map/end/pallas_call | solution.py:64
  (18 shorter events, 0.1 us)
Async XLA Ops:
  0.6 2.8 %collective-permute-start.1 = (bf16[128,3584]{1,0:T(8,128)(2,1)}, bf16[128,3584]{1,0:T(8,128)(2,1)S(1)}, u32[]{:S(2)}, u32[]{:S(2)}) collective-permute-start(bf16[128,3584]{1,0:T(8,128)(2,1)} %refs_1_.1), channel_id=1, source_target_pairs={{0,4},{4,0},{8,12},{12,8},{16,20},{20,16},{24,28},{28,24},{1,5},{5... | collective-permute-start | bytes 2752520 | tf_op jit(solution)/shard_map/ppermute | solution.py:97
  1.1 2.3 %collective-permute-start = (s32[1,8,32]{2,1,0:T(8,128)}, s32[1,8,32]{2,1,0:T(8,128)S(1)}, u32[]{:S(2)}, u32[]{:S(2)}) collective-permute-start(s32[1,8,32]{2,1,0:T(8,128)} %refs_0_.3), channel_id=1, source_target_pairs={{0,4},{4,0},{8,12},{12,8},{16,20},{20,16},{24,28},{28,24},{1,5},{5... | collective-permute-start | bytes 3080 | tf_op jit(solution)/shard_map/ppermute | solution.py:97
  1.2 14.2 %copy-start.10 = (s32[128,1]{0,1:T(1,128)S(1)}, s32[128,1]{0,1:T(1,128)}, u32[]{:S(2)}) copy-start(s32[128,1]{0,1:T(1,128)} %param.12) | copy-start | bytes 1540
  1.2 14.2 %copy-start.11 = (s32[1,8]{1,0:T(1,128)S(1)}, s32[1,8]{1,0:T(1,128)}, u32[]{:S(2)}) copy-start(s32[1,8]{1,0:T(1,128)} %refs_0_.2) | copy-start | bytes 100
  3.5 18.5 %copy-start.8 = (s32[1,8,32]{2,1,0:T(8,128)}, s32[1,8,32]{2,1,0:T(8,128)S(1)}, u32[]{:S(2)}) copy-start(s32[1,8,32]{2,1,0:T(8,128)S(1)} %collective-permute-done.refs_0_.refs_2_) | copy-start | bytes 3076
  3.5 9.9 %collective-permute-start.5 = (bf16[56,1024]{1,0:T(8,128)(2,1)S(1)}, bf16[56,1024]{1,0:T(8,128)(2,1)S(1)}, u32[]{:S(2)}, u32[]{:S(2)}) collective-permute-start(bf16[56,1024]{1,0:T(8,128)(2,1)S(1)} %get-tuple-element.83), channel_id=1, source_target_pairs={{0,2},{1,3},{2,0},{3,1},{4,6},{5,7},{6,4},{7,5},{8,10},{9,11},{10,... | collective-permute-start | bytes 344072 | tf_op jit(solution)/shard_map/ppermute | solution.py:86
  7.8 12.0 %collective-permute-start.2 = (bf16[64,1664]{1,0:T(8,128)(2,1)S(1)}, bf16[64,1664]{1,0:T(8,128)(2,1)S(1)}, u32[]{:S(2)}, u32[]{:S(2)}) collective-permute-start(bf16[64,1664]{1,0:T(8,128)(2,1)S(1)} %get-tuple-element.80), channel_id=1, source_target_pairs={{0,8},{4,12},{8,0},{12,4},{16,24},{20,28},{24,16},{28,20},{1,9},{5... | collective-permute-start | bytes 638984 | tf_op jit(solution)/shard_map/ppermute | solution.py:103
  9.4 11.3 %collective-permute-start.3 = (bf16[64,1664]{1,0:T(8,128)(2,1)S(1)}, bf16[64,1664]{1,0:T(8,128)(2,1)S(1)}, u32[]{:S(2)}, u32[]{:S(2)}) collective-permute-start(bf16[64,1664]{1,0:T(8,128)(2,1)S(1)} %get-tuple-element.81), channel_id=1, source_target_pairs={{0,16},{4,20},{8,24},{12,28},{16,0},{20,4},{24,8},{28,12},{1,17},{... | collective-permute-start | bytes 638984 | tf_op jit(solution)/shard_map/ppermute | solution.py:103
  10.9 9.8 %collective-permute-start.4 = (bf16[64,1664]{1,0:T(8,128)(2,1)S(1)}, bf16[64,1664]{1,0:T(8,128)(2,1)S(1)}, u32[]{:S(2)}, u32[]{:S(2)}) collective-permute-start(bf16[64,1664]{1,0:T(8,128)(2,1)S(1)} %get-tuple-element.82), channel_id=1, source_target_pairs={{0,24},{4,28},{8,16},{12,20},{16,8},{20,12},{24,0},{28,4},{1,25},{... | collective-permute-start | bytes 638984 | tf_op jit(solution)/shard_map/ppermute | solution.py:103
  11.4 6.8 %collective-permute-start.6 = (bf16[56,1024]{1,0:T(8,128)(2,1)S(1)}, bf16[56,1024]{1,0:T(8,128)(2,1)S(1)}, u32[]{:S(2)}, u32[]{:S(2)}) collective-permute-start(bf16[56,1024]{1,0:T(8,128)(2,1)S(1)} %get-tuple-element.84), channel_id=1, source_target_pairs={{0,3},{1,2},{2,1},{3,0},{4,7},{5,6},{6,5},{7,4},{8,11},{9,10},{10,... | collective-permute-start | bytes 344072 | tf_op jit(solution)/shard_map/ppermute | solution.py:86
  13.3 6.5 %collective-permute-start.7 = (bf16[56,1024]{1,0:T(8,128)(2,1)S(1)}, bf16[56,1024]{1,0:T(8,128)(2,1)S(1)}, u32[]{:S(2)}, u32[]{:S(2)}) collective-permute-start(bf16[56,1024]{1,0:T(8,128)(2,1)S(1)} %get-tuple-element.86), channel_id=1, source_target_pairs={{0,1},{1,0},{2,3},{3,2},{4,5},{5,4},{6,7},{7,6},{8,9},{9,8},{10,11... | collective-permute-start | bytes 344072 | tf_op jit(solution)/shard_map/ppermute | solution.py:86
  20.7 5.1 %copy-start.2 = (bf16[128,3584]{1,0:T(8,128)(2,1)S(1)}, bf16[128,3584]{1,0:T(8,128)(2,1)}, u32[]{:S(2)}) copy-start(bf16[128,3584]{1,0:T(8,128)(2,1)} %refs_1_.1) | copy-start | bytes 2752516
  22.0 29.4 %all-to-all-start = ((bf16[4,56,1664]{2,1,0:T(8,128)(2,1)}), bf16[4,56,1664]{2,1,0:T(8,128)(2,1)S(1)}, u32[]{:S(2)}, u32[]{:S(2)}) async-start(bf16[4,56,1664]{2,1,0:T(8,128)(2,1)} %get-tuple-element.99), calls=%async_computation | async-start | bytes 1490944 | tf_op jit(solution)/shard_map/all_to_all | solution.py:453
  27.1 9.0 %collective-permute-start.8 = (bf16[64,1920]{1,0:T(8,128)(2,1)S(1)}, bf16[64,1920]{1,0:T(8,128)(2,1)S(1)}, u32[]{:S(2)}, u32[]{:S(2)}) collective-permute-start(bf16[64,1920]{1,0:T(8,128)(2,1)S(1)} %get-tuple-element.90), channel_id=1, source_target_pairs={{0,8},{4,12},{8,0},{12,4},{16,24},{20,28},{24,16},{28,20},{1,9},{5... | collective-permute-start | bytes 737288 | tf_op jit(solution)/shard_map/ppermute | solution.py:103
  28.6 11.7 %collective-permute-start.9 = (bf16[64,1920]{1,0:T(8,128)(2,1)S(1)}, bf16[64,1920]{1,0:T(8,128)(2,1)S(1)}, u32[]{:S(2)}, u32[]{:S(2)}) collective-permute-start(bf16[64,1920]{1,0:T(8,128)(2,1)S(1)} %get-tuple-element.91), channel_id=1, source_target_pairs={{0,16},{4,20},{8,24},{12,28},{16,0},{20,4},{24,8},{28,12},{1,17},{... | collective-permute-start | bytes 737288 | tf_op jit(solution)/shard_map/ppermute | solution.py:103
  30.1 10.1 %collective-permute-start.10 = (bf16[64,1920]{1,0:T(8,128)(2,1)S(1)}, bf16[64,1920]{1,0:T(8,128)(2,1)S(1)}, u32[]{:S(2)}, u32[]{:S(2)}) collective-permute-start(bf16[64,1920]{1,0:T(8,128)(2,1)S(1)} %get-tuple-element.92), channel_id=1, source_target_pairs={{0,24},{4,28},{8,16},{12,20},{16,8},{20,12},{24,0},{28,4},{1,25},{... | collective-permute-start | bytes 737288 | tf_op jit(solution)/shard_map/ppermute | solution.py:103
  40.7 15.1 %collective-permute-start.11 = (bf16[56,1920]{1,0:T(8,128)(2,1)S(1)}, bf16[56,1920]{1,0:T(8,128)(2,1)S(1)}, u32[]{:S(2)}, u32[]{:S(2)}) collective-permute-start(bf16[56,1920]{1,0:T(8,128)(2,1)S(1)} %get-tuple-element.105), channel_id=1, source_target_pairs={{0,1},{1,0},{2,3},{3,2},{4,5},{5,4},{6,7},{7,6},{8,9},{9,8},{10,11... | collective-permute-start | bytes 645128 | tf_op jit(solution)/shard_map/ppermute | solution.py:86
  42.5 16.8 %collective-permute-start.12 = (bf16[56,1920]{1,0:T(8,128)(2,1)S(1)}, bf16[56,1920]{1,0:T(8,128)(2,1)S(1)}, u32[]{:S(2)}, u32[]{:S(2)}) collective-permute-start(bf16[56,1920]{1,0:T(8,128)(2,1)S(1)} %get-tuple-element.112), channel_id=1, source_target_pairs={{0,2},{1,3},{2,0},{3,1},{4,6},{5,7},{6,4},{7,5},{8,10},{9,11},{10,... | collective-permute-start | bytes 645128 | tf_op jit(solution)/shard_map/ppermute | solution.py:86
  44.9 14.4 %collective-permute-start.13 = (bf16[56,1920]{1,0:T(8,128)(2,1)S(1)}, bf16[56,1920]{1,0:T(8,128)(2,1)S(1)}, u32[]{:S(2)}, u32[]{:S(2)}) collective-permute-start(bf16[56,1920]{1,0:T(8,128)(2,1)S(1)} %get-tuple-element.113), channel_id=1, source_target_pairs={{0,3},{1,2},{2,1},{3,0},{4,7},{5,6},{6,5},{7,4},{8,11},{9,10},{10,... | collective-permute-start | bytes 645128 | tf_op jit(solution)/shard_map/ppermute | solution.py:86
  48.5 2.9 %copy-start = (bf16[1,3584,1024]{2,1,0:T(8,128)(2,1)}, bf16[1,3584,1024]{2,1,0:T(8,128)(2,1)S(1)}, u32[]{:S(2)}) copy-start(bf16[1,3584,1024]{2,1,0:T(8,128)(2,1)S(1)} %get-tuple-element.97.refs_0_.refs_2_.refs_7_) | copy-start | bytes 22020100
  51.4 3.1 %copy-start.1 = (bf16[1,3584,1024]{2,1,0:T(8,128)(2,1)S(1)}, bf16[1,3584,1024]{2,1,0:T(8,128)(2,1)}, u32[]{:S(2)}) copy-start(bf16[1,3584,1024]{2,1,0:T(8,128)(2,1)} %copy-done) | copy-start | bytes 22020100
  54.5 1.4 %copy-start.5 = (bf16[56,1024]{1,0:T(8,128)(2,1)S(1)}, bf16[56,1024]{1,0:T(8,128)(2,1)}, u32[]{:S(2)}) copy-start(bf16[56,1024]{1,0:T(8,128)(2,1)} %get-tuple-element.106.refs_7_) | copy-start | bytes 344068
  54.5 1.4 %copy-start.6 = (bf16[56,1024]{1,0:T(8,128)(2,1)S(1)}, bf16[56,1024]{1,0:T(8,128)(2,1)}, u32[]{:S(2)}) copy-start(bf16[56,1024]{1,0:T(8,128)(2,1)} %get-tuple-element.107.refs_8_) | copy-start | bytes 344068
  55.9 3.5 %copy-start.3 = (bf16[56,1024]{1,0:T(8,128)(2,1)S(1)}, bf16[56,1024]{1,0:T(8,128)(2,1)}, u32[]{:S(2)}) copy-start(bf16[56,1024]{1,0:T(8,128)(2,1)} %get-tuple-element.114.refs_12_) | copy-start | bytes 344068
  55.9 3.5 %copy-start.4 = (bf16[56,1024]{1,0:T(8,128)(2,1)S(1)}, bf16[56,1024]{1,0:T(8,128)(2,1)}, u32[]{:S(2)}) copy-start(bf16[56,1024]{1,0:T(8,128)(2,1)} %get-tuple-element.115.refs_13_) | copy-start | bytes 344068
  61.3 2.1 %collective-permute-start.14 = (bf16[4,576,128]{2,1,0:T(8,128)(2,1)S(1)}, bf16[4,576,128]{2,1,0:T(8,128)(2,1)S(1)}, u32[]{:S(2)}, u32[]{:S(2)}) collective-permute-start(bf16[4,576,128]{2,1,0:T(8,128)(2,1)S(1)} %get-tuple-element.117), channel_id=1, source_target_pairs={{0,4},{4,0},{8,12},{12,8},{16,20},{20,16},{24,28},{28,24},{1,5},{5... | collective-permute-start | bytes 1769480 | tf_op jit(solution)/shard_map/ppermute | solution.py:97
  63.5 9.1 %collective-permute-start.15 = (bf16[2,576,128]{2,1,0:T(8,128)(2,1)S(1)}, bf16[2,576,128]{2,1,0:T(8,128)(2,1)S(1)}, u32[]{:S(2)}, u32[]{:S(2)}) collective-permute-start(bf16[2,576,128]{2,1,0:T(8,128)(2,1)S(1)} %slice.28), channel_id=1, source_target_pairs={{0,16},{4,20},{8,24},{12,28},{16,0},{20,4},{24,8},{28,12},{1,17},{... | collective-permute-start | bytes 884744 | tf_op jit(solution)/shard_map/ppermute | solution.py:103
  65.0 13.0 %collective-permute-start.18 = (bf16[56,1024]{1,0:T(8,128)(2,1)S(1)}, bf16[56,1024]{1,0:T(8,128)(2,1)S(1)}, u32[]{:S(2)}, u32[]{:S(2)}) collective-permute-start(bf16[56,1024]{1,0:T(8,128)(2,1)S(1)} %get-tuple-element.120), channel_id=1, source_target_pairs={{0,2},{1,3},{2,0},{3,1},{4,6},{5,7},{6,4},{7,5},{8,10},{9,11},{10,... | collective-permute-start | bytes 344072 | tf_op jit(solution)/shard_map/ppermute | solution.py:86
  69.2 8.9 %collective-permute-start.19 = (bf16[56,1024]{1,0:T(8,128)(2,1)S(1)}, bf16[56,1024]{1,0:T(8,128)(2,1)S(1)}, u32[]{:S(2)}, u32[]{:S(2)}) collective-permute-start(bf16[56,1024]{1,0:T(8,128)(2,1)S(1)} %get-tuple-element.121), channel_id=1, source_target_pairs={{0,3},{1,2},{2,1},{3,0},{4,7},{5,6},{6,5},{7,4},{8,11},{9,10},{10,... | collective-permute-start | bytes 344072 | tf_op jit(solution)/shard_map/ppermute | solution.py:86
  71.5 7.4 %copy-start.7 = (bf16[128,256]{1,0:T(8,128)(2,1)S(1)}, bf16[128,256]{1,0:T(8,128)(2,1)}, u32[]{:S(2)}) copy-start(bf16[128,256]{1,0:T(8,128)(2,1)} %get-tuple-element.76.refs_0_) | copy-start | bytes 196612
  71.5 7.4 %copy-start.9 = (f32[128,1]{0,1:T(1,128)S(1)}, f32[128,1]{0,1:T(1,128)}, u32[]{:S(2)}) copy-start(f32[128,1]{0,1:T(1,128)} %param.13) | copy-start | bytes 1540
  71.5 7.3 %collective-permute-start.17 = (bf16[56,1024]{1,0:T(8,128)(2,1)S(1)}, bf16[56,1024]{1,0:T(8,128)(2,1)S(1)}, u32[]{:S(2)}, u32[]{:S(2)}) collective-permute-start(bf16[56,1024]{1,0:T(8,128)(2,1)S(1)} %get-tuple-element.119), channel_id=1, source_target_pairs={{0,1},{1,0},{2,3},{3,2},{4,5},{5,4},{6,7},{7,6},{8,9},{9,8},{10,11... | collective-permute-start | bytes 344072 | tf_op jit(solution)/shard_map/ppermute | solution.py:86
  72.7 6.1 %collective-permute-start.16 = (bf16[576,128]{1,0:T(8,128)(2,1)S(1)}, bf16[576,128]{1,0:T(8,128)(2,1)S(1)}, u32[]{:S(2)}, u32[]{:S(2)}) collective-permute-start(bf16[576,128]{1,0:T(8,128)(2,1)S(1)} %fusion), channel_id=1, source_target_pairs={{0,8},{4,12},{8,0},{12,4},{16,24},{20,28},{24,16},{28,20},{1,9},{5... | collective-permute-start | bytes 442376 | tf_op jit(solution)/shard_map/ppermute | solution.py:103

commit v6 on v5

--- a/solution.py
+++ b/solution.py
@@ -349,9 +349,12 @@
                 target[chip, base : base + up_rows] = mine[:, part * lanes : (part + 1) * lanes]
 
 
-def end_kernel(capacity, padded, home, weight, kept, came, *refs):
-    *blocks, down_grad, up_grad, out, tile = refs
-    total = kept[...].astype(f32) + came[...].astype(f32)
+def end_kernel(capacity, padded, chips, home, weight, *refs):
+    *refs, down_grad, up_grad, out, tile = refs
+    blocks, terms = refs[:-chips], refs[-chips:]
+    total = terms[0][...]
+    for term in terms[1:]:
+        total = total + term[...].astype(f32)
     down_rows = down_grad.shape[1]
     up_rows, hidden_units = up_grad.shape[1:]
     lanes = total.shape[1]
@@ -539,19 +542,19 @@
     activated += late
 
     pair_terms = swap_core(give, rep_count)
+    terms = keep + pair_terms.astype(f32)
+    sent_terms = terms[1:].astype(bf16)
+    came = [swap_chip(sent_terms[step - 1], step, rep_count) for step in range(1, pairs)]
     results = swap_all(activated, exp_count)
-    terms = keep + pair_terms.astype(f32)
-    while terms.shape[0] > 2:
-        half = terms.shape[0] // 2
-        terms = terms[:half] + swap_chip(terms[half:].astype(bf16), half, rep_count).astype(f32)
+
     down_grad, up_grad, out_rows = call(
-        functools.partial(end_kernel, capacity, padded),
+        functools.partial(end_kernel, capacity, padded, pairs),
         [
             shape((1, model_width // rep_count, rank_width), f32),
             shape((1, rank_width // rep_count, hidden_units), f32),
             shape((token_count, hidden_units), bf16),
         ],
-        [home, weight_row, terms[0], swap_chip(terms[1].astype(bf16), 1, rep_count), *results],
+        [home, weight_row, *results, terms[0], *came[::-1]],
         scratch=[pltpu.VMEM((slots, hidden_units), bf16)],
         flops=2 * token_count * slots * hidden_units,
         name="end",

time: 80.2 us -> 79.3 us (0.989)
  waiting for transfers between devices: 24 us -> 22.4 us
    ppermute x3, waiting for transfers between devices: 2.14 us -> 0.15 us  [swap_core(): return lax.ppermute(block, 'rep', [(i, i ^ 1) for i in range(rep_count)])]
    ppermute x9, waiting for transfers between devices: 10.2 us -> 11.1 us  [swap_exp(): return lax.ppermute(block, 'exp', [(i, i ^ step) for i in range(exp_count)])]
    ppermute x8 -> x9, waiting for transfers between devices: 11.7 us -> 11.1 us  [swap_chip(): lax.ppermute(block, 'rep', [(i, i ^ 2 * step) for i in range(rep_count)])]
    ppermute x8 -> x9, starting transfers between devices: 10.2 us -> 10.7 us  [swap_chip(): lax.ppermute(block, 'rep', [(i, i ^ 2 * step) for i in range(rep_count)])]
  transfers between devices with their start and end apart: 21 -> 22, of which waited for: 12 -> 11; matrix products, arithmetic and copies ran while one was open for 0% -> 0% of each run, Pallas kernels for 14% -> 15%
where the time goes in v6:
time: 79.3 us; the launch traced here: 79 us
  starting transfers between devices  33.7 us (42%)
  waiting for transfers between devices  22.4 us (28%)
  Pallas kernels  15.9 us (20%)
  local copies, waits for them, and re-layouts  6.07 us (8%)
  between operations  0.83 us (1%)
    ppermute x9, starting transfers between devices, swap_exp(): return lax.ppermute(block, 'exp', [(i, i ^ step) for i in range(exp_count)])  18.5 us
    ppermute x9, waiting for transfers between devices, swap_chip(): lax.ppermute(block, 'rep', [(i, i ^ 2 * step) for i in range(rep_count)])  11.1 us
    ppermute x9, waiting for transfers between devices, swap_exp(): return lax.ppermute(block, 'exp', [(i, i ^ step) for i in range(exp_count)])  11.1 us
    ppermute x9, starting transfers between devices, swap_chip(): lax.ppermute(block, 'rep', [(i, i ^ 2 * step) for i in range(rep_count)])  10.7 us
    pallas_call x8, Pallas kernels, call(): pl.pallas_call(moving, out_shape=[pltpu.HBM(out.shape, out.dtype) if numb...  9.17 us
    unnamed x24, local copies, waits for them, and re-layouts  6.02 us
    all_to_all x1, starting transfers between devices, body(): first_blocks = lax.all_to_all(sent, 'exp', 0, 0, tiled=True)  3.83 us
    pallas_call x1, Pallas kernels, body(): pl.pallas_call(fetch_kernel, out_shape=[pltpu.VMEM(array.shape, array.dty...  3.32 us
  transfers between devices with their start and end apart: 22, of which 11 were waited for; matrix products, arithmetic and copies ran while one was open for 0% of the time, Pallas kernels for 15%

profile of v6, /device:TPU:0, one launch (start us, length us, event | category | flops | bytes accessed | tf_op | source)
XLA Modules:
  0.0 79.0 jit_solution(17310890596791996136)
XLA Ops:
  0.6 0.5 collective-permute-start.1
  1.1 0.1 collective-permute-start
  1.2 2.1 %begin.1 = (bf16[4,32,1664]{2,1,0:T(8,128)(2,1)S(1)}, bf16[56,1024]{1,0:T(8,128)(2,1)S(1)}, bf16[56,1024]{1,0:T(8,128)(2,1)S(1)}, bf16[56,1024]{1,0:T(8,128)(2,1)S(1)}, bf16[56,1024]{1,0:T(8,128)(2,1)S(1)}) custom-call(s32[1,8,32]{2,1,0:T(8,128)} %refs_0_.3, bf16[128,3584]{1,0:T(8,128)(2,1)} %refs_1_.1, s32[1,128]{1,0:T(1,128)} %bitcast.12, ...), custom_call_target="tpu_custom_call" | custom-call | tf_op jit(solution)/shard_map/begin/pallas_call | solution.py:403
  3.3 0.1 collective-permute-done.refs_0_.refs_2_
  3.5 0.0 collective-permute-done.1.refs_1_.refs_3_
  3.5 4.0 %collective-permute-start.5 = (bf16[56,1024]{1,0:T(8,128)(2,1)S(1)}, bf16[56,1024]{1,0:T(8,128)(2,1)S(1)}, u32[]{:S(2)}, u32[]{:S(2)}) collective-permute-start(bf16[56,1024]{1,0:T(8,128)(2,1)S(1)} %get-tuple-element.83), channel_id=1, source_target_pairs={{0,2},{1,3},{2,0},{3,1},{4,6},{5,7},{6,4},{7,5},{8,10},{9,11},{10,... | collective-permute-start | bytes 344072 | tf_op jit(solution)/shard_map/ppermute | solution.py:86
  7.4 0.4 serve_first.1
  7.8 1.6 %collective-permute-start.2 = (bf16[64,1664]{1,0:T(8,128)(2,1)S(1)}, bf16[64,1664]{1,0:T(8,128)(2,1)S(1)}, u32[]{:S(2)}, u32[]{:S(2)}) collective-permute-start(bf16[64,1664]{1,0:T(8,128)(2,1)S(1)} %get-tuple-element.80), channel_id=1, source_target_pairs={{0,8},{4,12},{8,0},{12,4},{16,24},{20,28},{24,16},{28,20},{1,9},{5... | collective-permute-start | bytes 638984 | tf_op jit(solution)/shard_map/ppermute | solution.py:103
  9.4 1.5 %collective-permute-start.3 = (bf16[64,1664]{1,0:T(8,128)(2,1)S(1)}, bf16[64,1664]{1,0:T(8,128)(2,1)S(1)}, u32[]{:S(2)}, u32[]{:S(2)}) collective-permute-start(bf16[64,1664]{1,0:T(8,128)(2,1)S(1)} %get-tuple-element.81), channel_id=1, source_target_pairs={{0,16},{4,20},{8,24},{12,28},{16,0},{20,4},{24,8},{28,12},{1,17},{... | collective-permute-start | bytes 638984 | tf_op jit(solution)/shard_map/ppermute | solution.py:103
  10.9 0.5 collective-permute-start.4
  11.4 1.3 %collective-permute-start.6 = (bf16[56,1024]{1,0:T(8,128)(2,1)S(1)}, bf16[56,1024]{1,0:T(8,128)(2,1)S(1)}, u32[]{:S(2)}, u32[]{:S(2)}) collective-permute-start(bf16[56,1024]{1,0:T(8,128)(2,1)S(1)} %get-tuple-element.84), channel_id=1, source_target_pairs={{0,3},{1,2},{2,1},{3,0},{4,7},{5,6},{6,5},{7,4},{8,11},{9,10},{10,... | collective-permute-start | bytes 344072 | tf_op jit(solution)/shard_map/ppermute | solution.py:86
  12.7 0.6 collective-permute-done.5.refs_4_
  13.3 2.1 %collective-permute-start.7 = (bf16[56,1024]{1,0:T(8,128)(2,1)S(1)}, bf16[56,1024]{1,0:T(8,128)(2,1)S(1)}, u32[]{:S(2)}, u32[]{:S(2)}) collective-permute-start(bf16[56,1024]{1,0:T(8,128)(2,1)S(1)} %get-tuple-element.86), channel_id=1, source_target_pairs={{0,1},{1,0},{2,3},{3,2},{4,5},{5,4},{6,7},{7,6},{8,9},{9,8},{10,11... | collective-permute-start | bytes 344072 | tf_op jit(solution)/shard_map/ppermute | solution.py:86
  15.5 1.5 %prepare.1 = (bf16[256,256]{1,0:T(8,128)(2,1)S(1)}, bf16[128,256]{1,0:T(8,128)(2,1)}) custom-call(s32[1,8]{1,0:T(1,128)S(1)} %copy-done.11, s32[1,128]{1,0:T(1,128)S(1)} %bitcast.13), custom_call_target="tpu_custom_call" | custom-call | flops 16777216 | bytes 55924 | tf_op jit(solution)/shard_map/prepare/pallas_call | solution.py:64
  17.0 1.1 %collective-permute-done.6.refs_5_ = bf16[56,1024]{1,0:T(8,128)(2,1)S(1)} collective-permute-done((bf16[56,1024]{1,0:T(8,128)(2,1)S(1)}, bf16[56,1024]{1,0:T(8,128)(2,1)S(1)}, u32[]{:S(2)}, u32[]{:S(2)}) %collective-permute-start.6) | collective-permute-done | bytes 114720 | tf_op jit(solution)/shard_map/ppermute | solution.py:86
  18.1 1.7 %collective-permute-done.7.refs_7_ = bf16[56,1024]{1,0:T(8,128)(2,1)S(1)} collective-permute-done((bf16[56,1024]{1,0:T(8,128)(2,1)S(1)}, bf16[56,1024]{1,0:T(8,128)(2,1)S(1)}, u32[]{:S(2)}, u32[]{:S(2)}) %collective-permute-start.7) | collective-permute-done | bytes 114720 | tf_op jit(solution)/shard_map/ppermute | solution.py:86
  19.8 0.0 collective-permute-done.2.refs_1_
  19.8 0.9 %collective-permute-done.3.refs_2_ = bf16[64,1664]{1,0:T(8,128)(2,1)S(1)} collective-permute-done((bf16[64,1664]{1,0:T(8,128)(2,1)S(1)}, bf16[64,1664]{1,0:T(8,128)(2,1)S(1)}, u32[]{:S(2)}, u32[]{:S(2)}) %collective-permute-start.3) | collective-permute-done | bytes 213024 | tf_op jit(solution)/shard_map/ppermute | solution.py:103
  20.7 0.0 collective-permute-done.4.refs_3_
  20.7 1.3 %pick_first.1 = (bf16[4,56,1664]{2,1,0:T(8,128)(2,1)}, bf16[56,1024]{1,0:T(8,128)(2,1)}, bf16[56,1024]{1,0:T(8,128)(2,1)}, bf16[56,1024]{1,0:T(8,128)(2,1)}, bf16[56,1024]{1,0:T(8,128)(2,1)}) custom-call(bf16[256,256]{1,0:T(8,128)(2,1)S(1)} %get-tuple-element.77.pick.refs_0_, bf16[64,1664]{1,0:T(8,128)(2,1)S(1)} %get-tuple-element.79.refs_0_, ...), custom_call_target="tpu_custom_call" | custom-call | tf_op jit(solution)/shard_map/pick_first/pallas_call | solution.py:440
  22.0 0.0 copy-done.8
  22.0 3.8 %all-to-all-start = ((bf16[4,56,1664]{2,1,0:T(8,128)(2,1)}), bf16[4,56,1664]{2,1,0:T(8,128)(2,1)S(1)}, u32[]{:S(2)}, u32[]{:S(2)}) async-start(bf16[4,56,1664]{2,1,0:T(8,128)(2,1)} %get-tuple-element.99), calls=%async_computation | async-start | bytes 1490944 | tf_op jit(solution)/shard_map/all_to_all | solution.py:456
  25.8 0.0 copy-done.2
  25.8 1.2 %serve_last.1 = (bf16[64,1920]{1,0:T(8,128)(2,1)S(1)}, bf16[64,1920]{1,0:T(8,128)(2,1)S(1)}, bf16[64,1920]{1,0:T(8,128)(2,1)S(1)}, bf16[64,1920]{1,0:T(8,128)(2,1)S(1)}) custom-call(s32[1,8,32]{2,1,0:T(8,128)} %refs_0_.3, bf16[128,3584]{1,0:T(8,128)(2,1)S(1)} %copy-done.2, s32[1,8,32]{2,1,0:T(8,128)} %copy-done.8, ...), custom_call_target="tpu_custom_call" | custom-call | flops 125829120 | bytes 419430 | tf_op jit(solution)/shard_map/serve_last/pallas_call | solution.py:64
  27.1 1.6 %collective-permute-start.8 = (bf16[64,1920]{1,0:T(8,128)(2,1)S(1)}, bf16[64,1920]{1,0:T(8,128)(2,1)S(1)}, u32[]{:S(2)}, u32[]{:S(2)}) collective-permute-start(bf16[64,1920]{1,0:T(8,128)(2,1)S(1)} %get-tuple-element.90), channel_id=1, source_target_pairs={{0,8},{4,12},{8,0},{12,4},{16,24},{20,28},{24,16},{28,20},{1,9},{5... | collective-permute-start | bytes 737288 | tf_op jit(solution)/shard_map/ppermute | solution.py:103
  28.6 1.5 %collective-permute-start.9 = (bf16[64,1920]{1,0:T(8,128)(2,1)S(1)}, bf16[64,1920]{1,0:T(8,128)(2,1)S(1)}, u32[]{:S(2)}, u32[]{:S(2)}) collective-permute-start(bf16[64,1920]{1,0:T(8,128)(2,1)S(1)} %get-tuple-element.91), channel_id=1, source_target_pairs={{0,16},{4,20},{8,24},{12,28},{16,0},{20,4},{24,8},{28,12},{1,17},{... | collective-permute-start | bytes 737288 | tf_op jit(solution)/shard_map/ppermute | solution.py:103
  30.1 0.5 collective-permute-start.10
  30.6 5.4 %collective-permute-done.8.refs_2_ = bf16[64,1920]{1,0:T(8,128)(2,1)S(1)} collective-permute-done((bf16[64,1920]{1,0:T(8,128)(2,1)S(1)}, bf16[64,1920]{1,0:T(8,128)(2,1)S(1)}, u32[]{:S(2)}, u32[]{:S(2)}) %collective-permute-start.8) | collective-permute-done | bytes 245792 | tf_op jit(solution)/shard_map/ppermute | solution.py:103
  36.0 4.2 %collective-permute-done.9.refs_3_ = bf16[64,1920]{1,0:T(8,128)(2,1)S(1)} collective-permute-done((bf16[64,1920]{1,0:T(8,128)(2,1)S(1)}, bf16[64,1920]{1,0:T(8,128)(2,1)S(1)}, u32[]{:S(2)}, u32[]{:S(2)}) %collective-permute-start.9) | collective-permute-done | bytes 245792 | tf_op jit(solution)/shard_map/ppermute | solution.py:103
  40.3 0.0 collective-permute-done.10.refs_4_
  40.3 0.4 pick_last.1
  40.7 1.8 %collective-permute-start.11 = (bf16[56,1920]{1,0:T(8,128)(2,1)S(1)}, bf16[56,1920]{1,0:T(8,128)(2,1)S(1)}, u32[]{:S(2)}, u32[]{:S(2)}) collective-permute-start(bf16[56,1920]{1,0:T(8,128)(2,1)S(1)} %get-tuple-element.104), channel_id=1, source_target_pairs={{0,1},{1,0},{2,3},{3,2},{4,5},{5,4},{6,7},{7,6},{8,9},{9,8},{10,11... | collective-permute-start | bytes 645128 | tf_op jit(solution)/shard_map/ppermute | solution.py:86
  42.5 2.4 %collective-permute-start.13 = (bf16[56,1920]{1,0:T(8,128)(2,1)S(1)}, bf16[56,1920]{1,0:T(8,128)(2,1)S(1)}, u32[]{:S(2)}, u32[]{:S(2)}) collective-permute-start(bf16[56,1920]{1,0:T(8,128)(2,1)S(1)} %get-tuple-element.114), channel_id=1, source_target_pairs={{0,2},{1,3},{2,0},{3,1},{4,6},{5,7},{6,4},{7,5},{8,10},{9,11},{10,... | collective-permute-start | bytes 645128 | tf_op jit(solution)/shard_map/ppermute | solution.py:86
  44.9 0.3 collective-permute-start.14
  45.2 3.3 %fetch.1 = (bf16[1,3584,1024]{2,1,0:T(8,128)(2,1)S(1)}, bf16[1,3584,128]{2,1,0:T(8,128)(2,1)S(1)}, bf16[1,128,1024]{2,1,0:T(8,128)(2,1)S(1)}) custom-call(bf16[1,3584,1024]{2,1,0:T(8,128)(2,1)} %refs_0_.4, bf16[1,3584,128]{2,1,0:T(8,128)(2,1)} %refs_1_.2, bf16[1,128,1024]{2,1,0:T(8,128)(2,1)} %refs_2_), custom_call_target="tpu_custom_call" | custom-call | tf_op jit(solution)/shard_map/fetch/pallas_call | solution.py:475
  48.5 2.9 %copy-done = bf16[1,3584,1024]{2,1,0:T(8,128)(2,1)} copy-done((bf16[1,3584,1024]{2,1,0:T(8,128)(2,1)}, bf16[1,3584,1024]{2,1,0:T(8,128)(2,1)S(1)}, u32[]{:S(2)}) %copy-start) | copy-done | bytes 7340056
  51.4 0.0 all-to-all-done.refs_2_
  51.4 3.1 %copy-done.1 = bf16[1,3584,1024]{2,1,0:T(8,128)(2,1)S(1)} copy-done((bf16[1,3584,1024]{2,1,0:T(8,128)(2,1)S(1)}, bf16[1,3584,1024]{2,1,0:T(8,128)(2,1)}, u32[]{:S(2)}) %copy-start.1) | copy-done | bytes 7340056
  54.5 1.4 %partial.1 = (bf16[1664,256]{1,0:T(8,128)(2,1)S(1)}, f32[256,1024]{1,0:T(8,128)S(1)}, f32[256,128]{1,0:T(8,128)S(1)}) custom-call(bf16[1,3584,1024]{2,1,0:T(8,128)(2,1)S(1)} %copy-done.1, bf16[1,3584,128]{2,1,0:T(8,128)(2,1)S(1)} %get-tuple-element.98.refs_1_.refs_3_.refs_8_, bf16[4,56,1664]{2,1,0:T(8,128)(2,1)S(1)} %all-to-all-done.refs_2_), custom_call_target="tpu_custom_call" | custom-call | flops 981467136 | bytes 3271557 | tf_op jit(solution)/shard_map/partial/pallas_call | solution.py:64
  55.9 0.0 collective-permute-done.11.refs_6_
  55.9 0.0 copy-start.3
  55.9 0.0 copy-start.4
  55.9 1.2 %early.1 = (bf16[56,1024]{1,0:T(8,128)(2,1)S(1)}, bf16[56,1024]{1,0:T(8,128)(2,1)S(1)}, bf16[1920,128]{1,0:T(8,128)(2,1)S(1)}, bf16[128,128]{1,0:T(8,128)(2,1)S(...) custom-call(f32[256,1024]{1,0:T(8,128)S(1)} %get-tuple-element.100.refs_0_.refs_5_, ...), custom_call_target="tpu_custom_call" | custom-call | flops 566231040 | bytes 1887436 | tf_op jit(solution)/shard_map/early/pallas_call | solution.py:64
  57.1 2.1 %collective-permute-done.13.refs_10_ = bf16[56,1920]{1,0:T(8,128)(2,1)S(1)} collective-permute-done((bf16[56,1920]{1,0:T(8,128)(2,1)S(1)}, bf16[56,1920]{1,0:T(8,128)(2,1)S(1)}, u32[]{:S(2)}, u32[]{:S(2)}) %collective-permute-start.13) | collective-permute-done | bytes 215072 | tf_op jit(solution)/shard_map/ppermute | solution.py:86
  59.3 0.0 collective-permute-done.14.refs_11_
  59.3 2.0 %late.1 = (bf16[56,1024]{1,0:T(8,128)(2,1)S(1)}, bf16[56,1024]{1,0:T(8,128)(2,1)S(1)}, f32[4,576,128]{2,1,0:T(8,128)S(1)}, bf16[4,576,128]{2,1,0:T(8,128)(2,1)S(1)}) custom-call(bf16[1664,256]{1,0:T(8,128)(2,1)S(1)} %get-tuple-element.109.refs_0_, bf16[1920,128]{1,0:T(8,128)(2,1)S(1)} %get-tuple-element.110.refs_1_, ...), custom_call_target="tpu_custom_call" | custom-call | flops 1035993088 | bytes 3453310 | tf_op jit(solution)/shard_map/late/pallas_call | solution.py:64
  61.3 0.1 collective-permute-start.17
  61.4 4.2 %collective-permute-start.12 = (bf16[56,1024]{1,0:T(8,128)(2,1)S(1)}, bf16[56,1024]{1,0:T(8,128)(2,1)S(1)}, u32[]{:S(2)}, u32[]{:S(2)}) collective-permute-start(bf16[56,1024]{1,0:T(8,128)(2,1)S(1)} %get-tuple-element.108), channel_id=1, source_target_pairs={{0,1},{1,0},{2,3},{3,2},{4,5},{5,4},{6,7},{7,6},{8,9},{9,8},{10,11... | collective-permute-start | bytes 344072 | tf_op jit(solution)/shard_map/ppermute | solution.py:86
  65.6 0.1 collective-permute-start.15
  65.6 2.4 %collective-permute-start.16 = (bf16[56,1024]{1,0:T(8,128)(2,1)S(1)}, bf16[56,1024]{1,0:T(8,128)(2,1)S(1)}, u32[]{:S(2)}, u32[]{:S(2)}) collective-permute-start(bf16[56,1024]{1,0:T(8,128)(2,1)S(1)} %get-tuple-element.119), channel_id=1, source_target_pairs={{0,3},{1,2},{2,1},{3,0},{4,7},{5,6},{6,5},{7,4},{8,11},{9,10},{10,... | collective-permute-start | bytes 344072 | tf_op jit(solution)/shard_map/ppermute | solution.py:86
  68.0 0.0 collective-permute-done.17
  68.0 0.2 fusion
  68.2 0.0 copy-start.7
  68.2 0.0 copy-start.9
  68.2 2.5 %collective-permute-start.18 = (bf16[576,128]{1,0:T(8,128)(2,1)S(1)}, bf16[576,128]{1,0:T(8,128)(2,1)S(1)}, u32[]{:S(2)}, u32[]{:S(2)}) collective-permute-start(bf16[576,128]{1,0:T(8,128)(2,1)S(1)} %get-tuple-element.129), channel_id=1, source_target_pairs={{0,24},{4,28},{8,16},{12,20},{16,8},{20,12},{24,0},{28,4},{1,25},{... | collective-permute-start | bytes 442376 | tf_op jit(solution)/shard_map/ppermute | solution.py:103
  70.7 0.5 collective-permute-start.19
  71.2 0.0 collective-permute-done.12.refs_3_
  71.2 0.5 collective-permute-start.20
  71.8 5.6 %collective-permute-done.15.refs_4_ = bf16[56,1024]{1,0:T(8,128)(2,1)S(1)} collective-permute-done((bf16[56,1024]{1,0:T(8,128)(2,1)S(1)}, bf16[56,1024]{1,0:T(8,128)(2,1)S(1)}, u32[]{:S(2)}, u32[]{:S(2)}) %collective-permute-start.15) | collective-permute-done | bytes 114720 | tf_op jit(solution)/shard_map/ppermute | solution.py:86
  77.4 0.0 collective-permute-done.16.refs_5_
  77.4 0.0 collective-permute-done.18.refs_7_
  77.4 0.5 collective-permute-done.19.refs_8_
  77.9 0.1 collective-permute-done.20.refs_9_
  78.0 1.0 %end.1 = (f32[1,448,128]{2,1,0:T(8,128)}, f32[1,16,1024]{2,1,0:T(8,128)}, bf16[128,1024]{1,0:T(8,128)(2,1)}) custom-call(bf16[128,256]{1,0:T(8,128)(2,1)S(1)} %copy-done.7, f32[1,128]{1,0:T(1,128)S(1)} %bitcast.11, bf16[56,1024]{1,0:T(8,128)(2,1)S(1)} %get-tuple-element.107.refs_2_, bf16[56,1024]{1,0:T(8,128)(2,1)S(1)} %collective-permute-done.12.refs_3_, ...), custom_call_target="tpu_custom_call" | custom-call | flops 67108864 | bytes 223696 | tf_op jit(solution)/shard_map/end/pallas_call | solution.py:64
  (18 shorter events, 0.1 us)
Async XLA Ops:
  0.6 2.8 %collective-permute-start.1 = (bf16[128,3584]{1,0:T(8,128)(2,1)}, bf16[128,3584]{1,0:T(8,128)(2,1)S(1)}, u32[]{:S(2)}, u32[]{:S(2)}) collective-permute-start(bf16[128,3584]{1,0:T(8,128)(2,1)} %refs_1_.1), channel_id=1, source_target_pairs={{0,4},{4,0},{8,12},{12,8},{16,20},{20,16},{24,28},{28,24},{1,5},{5... | collective-permute-start | bytes 2752520 | tf_op jit(solution)/shard_map/ppermute | solution.py:97
  1.1 2.3 %collective-permute-start = (s32[1,8,32]{2,1,0:T(8,128)}, s32[1,8,32]{2,1,0:T(8,128)S(1)}, u32[]{:S(2)}, u32[]{:S(2)}) collective-permute-start(s32[1,8,32]{2,1,0:T(8,128)} %refs_0_.3), channel_id=1, source_target_pairs={{0,4},{4,0},{8,12},{12,8},{16,20},{20,16},{24,28},{28,24},{1,5},{5... | collective-permute-start | bytes 3080 | tf_op jit(solution)/shard_map/ppermute | solution.py:97
  1.2 14.2 %copy-start.10 = (s32[128,1]{0,1:T(1,128)S(1)}, s32[128,1]{0,1:T(1,128)}, u32[]{:S(2)}) copy-start(s32[128,1]{0,1:T(1,128)} %param.12) | copy-start | bytes 1540
  1.2 14.2 %copy-start.11 = (s32[1,8]{1,0:T(1,128)S(1)}, s32[1,8]{1,0:T(1,128)}, u32[]{:S(2)}) copy-start(s32[1,8]{1,0:T(1,128)} %refs_0_.2) | copy-start | bytes 100
  3.5 18.5 %copy-start.8 = (s32[1,8,32]{2,1,0:T(8,128)}, s32[1,8,32]{2,1,0:T(8,128)S(1)}, u32[]{:S(2)}) copy-start(s32[1,8,32]{2,1,0:T(8,128)S(1)} %collective-permute-done.refs_0_.refs_2_) | copy-start | bytes 3076
  3.5 9.9 %collective-permute-start.5 = (bf16[56,1024]{1,0:T(8,128)(2,1)S(1)}, bf16[56,1024]{1,0:T(8,128)(2,1)S(1)}, u32[]{:S(2)}, u32[]{:S(2)}) collective-permute-start(bf16[56,1024]{1,0:T(8,128)(2,1)S(1)} %get-tuple-element.83), channel_id=1, source_target_pairs={{0,2},{1,3},{2,0},{3,1},{4,6},{5,7},{6,4},{7,5},{8,10},{9,11},{10,... | collective-permute-start | bytes 344072 | tf_op jit(solution)/shard_map/ppermute | solution.py:86
  7.8 12.0 %collective-permute-start.2 = (bf16[64,1664]{1,0:T(8,128)(2,1)S(1)}, bf16[64,1664]{1,0:T(8,128)(2,1)S(1)}, u32[]{:S(2)}, u32[]{:S(2)}) collective-permute-start(bf16[64,1664]{1,0:T(8,128)(2,1)S(1)} %get-tuple-element.80), channel_id=1, source_target_pairs={{0,8},{4,12},{8,0},{12,4},{16,24},{20,28},{24,16},{28,20},{1,9},{5... | collective-permute-start | bytes 638984 | tf_op jit(solution)/shard_map/ppermute | solution.py:103
  9.4 11.3 %collective-permute-start.3 = (bf16[64,1664]{1,0:T(8,128)(2,1)S(1)}, bf16[64,1664]{1,0:T(8,128)(2,1)S(1)}, u32[]{:S(2)}, u32[]{:S(2)}) collective-permute-start(bf16[64,1664]{1,0:T(8,128)(2,1)S(1)} %get-tuple-element.81), channel_id=1, source_target_pairs={{0,16},{4,20},{8,24},{12,28},{16,0},{20,4},{24,8},{28,12},{1,17},{... | collective-permute-start | bytes 638984 | tf_op jit(solution)/shard_map/ppermute | solution.py:103
  10.9 9.8 %collective-permute-start.4 = (bf16[64,1664]{1,0:T(8,128)(2,1)S(1)}, bf16[64,1664]{1,0:T(8,128)(2,1)S(1)}, u32[]{:S(2)}, u32[]{:S(2)}) collective-permute-start(bf16[64,1664]{1,0:T(8,128)(2,1)S(1)} %get-tuple-element.82), channel_id=1, source_target_pairs={{0,24},{4,28},{8,16},{12,20},{16,8},{20,12},{24,0},{28,4},{1,25},{... | collective-permute-start | bytes 638984 | tf_op jit(solution)/shard_map/ppermute | solution.py:103
  11.4 6.8 %collective-permute-start.6 = (bf16[56,1024]{1,0:T(8,128)(2,1)S(1)}, bf16[56,1024]{1,0:T(8,128)(2,1)S(1)}, u32[]{:S(2)}, u32[]{:S(2)}) collective-permute-start(bf16[56,1024]{1,0:T(8,128)(2,1)S(1)} %get-tuple-element.84), channel_id=1, source_target_pairs={{0,3},{1,2},{2,1},{3,0},{4,7},{5,6},{6,5},{7,4},{8,11},{9,10},{10,... | collective-permute-start | bytes 344072 | tf_op jit(solution)/shard_map/ppermute | solution.py:86
  13.3 6.5 %collective-permute-start.7 = (bf16[56,1024]{1,0:T(8,128)(2,1)S(1)}, bf16[56,1024]{1,0:T(8,128)(2,1)S(1)}, u32[]{:S(2)}, u32[]{:S(2)}) collective-permute-start(bf16[56,1024]{1,0:T(8,128)(2,1)S(1)} %get-tuple-element.86), channel_id=1, source_target_pairs={{0,1},{1,0},{2,3},{3,2},{4,5},{5,4},{6,7},{7,6},{8,9},{9,8},{10,11... | collective-permute-start | bytes 344072 | tf_op jit(solution)/shard_map/ppermute | solution.py:86
  20.7 5.1 %copy-start.2 = (bf16[128,3584]{1,0:T(8,128)(2,1)S(1)}, bf16[128,3584]{1,0:T(8,128)(2,1)}, u32[]{:S(2)}) copy-start(bf16[128,3584]{1,0:T(8,128)(2,1)} %refs_1_.1) | copy-start | bytes 2752516
  22.0 29.4 %all-to-all-start = ((bf16[4,56,1664]{2,1,0:T(8,128)(2,1)}), bf16[4,56,1664]{2,1,0:T(8,128)(2,1)S(1)}, u32[]{:S(2)}, u32[]{:S(2)}) async-start(bf16[4,56,1664]{2,1,0:T(8,128)(2,1)} %get-tuple-element.99), calls=%async_computation | async-start | bytes 1490944 | tf_op jit(solution)/shard_map/all_to_all | solution.py:456
  27.1 9.0 %collective-permute-start.8 = (bf16[64,1920]{1,0:T(8,128)(2,1)S(1)}, bf16[64,1920]{1,0:T(8,128)(2,1)S(1)}, u32[]{:S(2)}, u32[]{:S(2)}) collective-permute-start(bf16[64,1920]{1,0:T(8,128)(2,1)S(1)} %get-tuple-element.90), channel_id=1, source_target_pairs={{0,8},{4,12},{8,0},{12,4},{16,24},{20,28},{24,16},{28,20},{1,9},{5... | collective-permute-start | bytes 737288 | tf_op jit(solution)/shard_map/ppermute | solution.py:103
  28.6 11.7 %collective-permute-start.9 = (bf16[64,1920]{1,0:T(8,128)(2,1)S(1)}, bf16[64,1920]{1,0:T(8,128)(2,1)S(1)}, u32[]{:S(2)}, u32[]{:S(2)}) collective-permute-start(bf16[64,1920]{1,0:T(8,128)(2,1)S(1)} %get-tuple-element.91), channel_id=1, source_target_pairs={{0,16},{4,20},{8,24},{12,28},{16,0},{20,4},{24,8},{28,12},{1,17},{... | collective-permute-start | bytes 737288 | tf_op jit(solution)/shard_map/ppermute | solution.py:103
  30.1 10.1 %collective-permute-start.10 = (bf16[64,1920]{1,0:T(8,128)(2,1)S(1)}, bf16[64,1920]{1,0:T(8,128)(2,1)S(1)}, u32[]{:S(2)}, u32[]{:S(2)}) collective-permute-start(bf16[64,1920]{1,0:T(8,128)(2,1)S(1)} %get-tuple-element.92), channel_id=1, source_target_pairs={{0,24},{4,28},{8,16},{12,20},{16,8},{20,12},{24,0},{28,4},{1,25},{... | collective-permute-start | bytes 737288 | tf_op jit(solution)/shard_map/ppermute | solution.py:103
  40.7 15.1 %collective-permute-start.11 = (bf16[56,1920]{1,0:T(8,128)(2,1)S(1)}, bf16[56,1920]{1,0:T(8,128)(2,1)S(1)}, u32[]{:S(2)}, u32[]{:S(2)}) collective-permute-start(bf16[56,1920]{1,0:T(8,128)(2,1)S(1)} %get-tuple-element.104), channel_id=1, source_target_pairs={{0,1},{1,0},{2,3},{3,2},{4,5},{5,4},{6,7},{7,6},{8,9},{9,8},{10,11... | collective-permute-start | bytes 645128 | tf_op jit(solution)/shard_map/ppermute | solution.py:86
  42.5 16.7 %collective-permute-start.13 = (bf16[56,1920]{1,0:T(8,128)(2,1)S(1)}, bf16[56,1920]{1,0:T(8,128)(2,1)S(1)}, u32[]{:S(2)}, u32[]{:S(2)}) collective-permute-start(bf16[56,1920]{1,0:T(8,128)(2,1)S(1)} %get-tuple-element.114), channel_id=1, source_target_pairs={{0,2},{1,3},{2,0},{3,1},{4,6},{5,7},{6,4},{7,5},{8,10},{9,11},{10,... | collective-permute-start | bytes 645128 | tf_op jit(solution)/shard_map/ppermute | solution.py:86
  44.9 14.4 %collective-permute-start.14 = (bf16[56,1920]{1,0:T(8,128)(2,1)S(1)}, bf16[56,1920]{1,0:T(8,128)(2,1)S(1)}, u32[]{:S(2)}, u32[]{:S(2)}) collective-permute-start(bf16[56,1920]{1,0:T(8,128)(2,1)S(1)} %get-tuple-element.115), channel_id=1, source_target_pairs={{0,3},{1,2},{2,1},{3,0},{4,7},{5,6},{6,5},{7,4},{8,11},{9,10},{10,... | collective-permute-start | bytes 645128 | tf_op jit(solution)/shard_map/ppermute | solution.py:86
  48.5 2.9 %copy-start = (bf16[1,3584,1024]{2,1,0:T(8,128)(2,1)}, bf16[1,3584,1024]{2,1,0:T(8,128)(2,1)S(1)}, u32[]{:S(2)}) copy-start(bf16[1,3584,1024]{2,1,0:T(8,128)(2,1)S(1)} %get-tuple-element.97.refs_0_.refs_2_.refs_7_) | copy-start | bytes 22020100
  51.4 3.1 %copy-start.1 = (bf16[1,3584,1024]{2,1,0:T(8,128)(2,1)S(1)}, bf16[1,3584,1024]{2,1,0:T(8,128)(2,1)}, u32[]{:S(2)}) copy-start(bf16[1,3584,1024]{2,1,0:T(8,128)(2,1)} %copy-done) | copy-start | bytes 22020100
  54.5 1.4 %copy-start.5 = (bf16[56,1024]{1,0:T(8,128)(2,1)S(1)}, bf16[56,1024]{1,0:T(8,128)(2,1)}, u32[]{:S(2)}) copy-start(bf16[56,1024]{1,0:T(8,128)(2,1)} %get-tuple-element.105.refs_7_) | copy-start | bytes 344068
  54.5 1.4 %copy-start.6 = (bf16[56,1024]{1,0:T(8,128)(2,1)S(1)}, bf16[56,1024]{1,0:T(8,128)(2,1)}, u32[]{:S(2)}) copy-start(bf16[56,1024]{1,0:T(8,128)(2,1)} %get-tuple-element.106.refs_8_) | copy-start | bytes 344068
  55.9 3.4 %copy-start.3 = (bf16[56,1024]{1,0:T(8,128)(2,1)S(1)}, bf16[56,1024]{1,0:T(8,128)(2,1)}, u32[]{:S(2)}) copy-start(bf16[56,1024]{1,0:T(8,128)(2,1)} %get-tuple-element.116.refs_12_) | copy-start | bytes 344068
  55.9 3.4 %copy-start.4 = (bf16[56,1024]{1,0:T(8,128)(2,1)S(1)}, bf16[56,1024]{1,0:T(8,128)(2,1)}, u32[]{:S(2)}) copy-start(bf16[56,1024]{1,0:T(8,128)(2,1)} %get-tuple-element.117.refs_13_) | copy-start | bytes 344068
  61.3 6.7 %collective-permute-start.17 = (bf16[4,576,128]{2,1,0:T(8,128)(2,1)S(1)}, bf16[4,576,128]{2,1,0:T(8,128)(2,1)S(1)}, u32[]{:S(2)}, u32[]{:S(2)}) collective-permute-start(bf16[4,576,128]{2,1,0:T(8,128)(2,1)S(1)} %get-tuple-element.121), channel_id=1, source_target_pairs={{0,4},{4,0},{8,12},{12,8},{16,20},{20,16},{24,28},{28,24},{1,5},{5... | collective-permute-start | bytes 1769480 | tf_op jit(solution)/shard_map/ppermute | solution.py:97
  61.4 9.9 %collective-permute-start.12 = (bf16[56,1024]{1,0:T(8,128)(2,1)S(1)}, bf16[56,1024]{1,0:T(8,128)(2,1)S(1)}, u32[]{:S(2)}, u32[]{:S(2)}) collective-permute-start(bf16[56,1024]{1,0:T(8,128)(2,1)S(1)} %get-tuple-element.108), channel_id=1, source_target_pairs={{0,1},{1,0},{2,3},{3,2},{4,5},{5,4},{6,7},{7,6},{8,9},{9,8},{10,11... | collective-permute-start | bytes 344072 | tf_op jit(solution)/shard_map/ppermute | solution.py:86
  65.6 11.8 %collective-permute-start.15 = (bf16[56,1024]{1,0:T(8,128)(2,1)S(1)}, bf16[56,1024]{1,0:T(8,128)(2,1)S(1)}, u32[]{:S(2)}, u32[]{:S(2)}) collective-permute-start(bf16[56,1024]{1,0:T(8,128)(2,1)S(1)} %get-tuple-element.118), channel_id=1, source_target_pairs={{0,2},{1,3},{2,0},{3,1},{4,6},{5,7},{6,4},{7,5},{8,10},{9,11},{10,... | collective-permute-start | bytes 344072 | tf_op jit(solution)/shard_map/ppermute | solution.py:86
  65.6 11.7 %collective-permute-start.16 = (bf16[56,1024]{1,0:T(8,128)(2,1)S(1)}, bf16[56,1024]{1,0:T(8,128)(2,1)S(1)}, u32[]{:S(2)}, u32[]{:S(2)}) collective-permute-start(bf16[56,1024]{1,0:T(8,128)(2,1)S(1)} %get-tuple-element.119), channel_id=1, source_target_pairs={{0,3},{1,2},{2,1},{3,0},{4,7},{5,6},{6,5},{7,4},{8,11},{9,10},{10,... | collective-permute-start | bytes 344072 | tf_op jit(solution)/shard_map/ppermute | solution.py:86
  68.2 9.8 %copy-start.7 = (bf16[128,256]{1,0:T(8,128)(2,1)S(1)}, bf16[128,256]{1,0:T(8,128)(2,1)}, u32[]{:S(2)}) copy-start(bf16[128,256]{1,0:T(8,128)(2,1)} %get-tuple-element.76.refs_0_) | copy-start | bytes 196612
  68.2 9.8 %copy-start.9 = (f32[128,1]{0,1:T(1,128)S(1)}, f32[128,1]{0,1:T(1,128)}, u32[]{:S(2)}) copy-start(f32[128,1]{0,1:T(1,128)} %param.13) | copy-start | bytes 1540
  68.2 9.1 %collective-permute-start.18 = (bf16[576,128]{1,0:T(8,128)(2,1)S(1)}, bf16[576,128]{1,0:T(8,128)(2,1)S(1)}, u32[]{:S(2)}, u32[]{:S(2)}) collective-permute-start(bf16[576,128]{1,0:T(8,128)(2,1)S(1)} %get-tuple-element.129), channel_id=1, source_target_pairs={{0,24},{4,28},{8,16},{12,20},{16,8},{20,12},{24,0},{28,4},{1,25},{... | collective-permute-start | bytes 442376 | tf_op jit(solution)/shard_map/ppermute | solution.py:103
  70.7 7.2 %collective-permute-start.19 = (bf16[576,128]{1,0:T(8,128)(2,1)S(1)}, bf16[576,128]{1,0:T(8,128)(2,1)S(1)}, u32[]{:S(2)}, u32[]{:S(2)}) collective-permute-start(bf16[576,128]{1,0:T(8,128)(2,1)S(1)} %get-tuple-element.128), channel_id=1, source_target_pairs={{0,16},{4,20},{8,24},{12,28},{16,0},{20,4},{24,8},{28,12},{1,17},{... | collective-permute-start | bytes 442376 | tf_op jit(solution)/shard_map/ppermute | solution.py:103
  71.2 6.7 %collective-permute-start.20 = (bf16[576,128]{1,0:T(8,128)(2,1)S(1)}, bf16[576,128]{1,0:T(8,128)(2,1)S(1)}, u32[]{:S(2)}, u32[]{:S(2)}) collective-permute-start(bf16[576,128]{1,0:T(8,128)(2,1)S(1)} %get-tuple-element.127), channel_id=1, source_target_pairs={{0,8},{4,12},{8,0},{12,4},{16,24},{20,28},{24,16},{28,20},{1,9},{5... | collective-permute-start | bytes 442376 | tf_op jit(solution)/shard_map/ppermute | solution.py:103

commit v7 on v6

--- a/solution.py
+++ b/solution.py
@@ -7,7 +7,7 @@
 from jax.experimental.pallas import tpu as pltpu
 from jax.sharding import PartitionSpec as P
 
-FIRST_PART = 13
+FIRST_PART = 17
 PARTS = 28
 bf16 = jnp.bfloat16
 f32 = jnp.float32
@@ -211,23 +211,19 @@
 
 def pick_first_kernel(capacity, padded, chips, pick, *refs):
     arrived, refs = refs[:chips], refs[chips:]
-    exp_count = (len(refs) - 3) // 2
-    grads, refs = refs[:exp_count], refs[exp_count:]
-    sent_far, grads_far, (sent, sems) = refs[0], refs[1 : exp_count + 1], refs[exp_count + 1 :]
+    *refs, sems = refs
+    kept = sems.shape[0]
+    grads, sent, grads_far = refs[:kept], refs[kept : len(refs) - kept], refs[len(refs) - kept :]
+    exp_count = len(sent)
     put_away = [
-        pltpu.make_async_copy(block, place, sems.at[exp_count + step])
-        for step, (block, place) in enumerate(zip(grads, grads_far))
+        pltpu.make_async_copy(block, place, sems.at[step]) for step, (block, place) in enumerate(zip(grads, grads_far))
     ]
     for copy in put_away:
         copy.start()
     rows = jnp.concatenate([block[...] for block in arrived], axis=0)
     by_slot = dot(pick[...], rows).astype(bf16)
-    column = lax.axis_index("exp")
     for step in range(exp_count):
-        sent[step] = by_slot[step * padded : step * padded + capacity]
-        copy = pltpu.make_async_copy(sent.at[step], sent_far.at[jnp.bitwise_xor(column, step)], sems.at[step])
-        copy.start()
-        put_away.append(copy)
+        sent[step][...] = by_slot[step * padded : step * padded + capacity]
     for copy in put_away:
         copy.wait()
 
@@ -246,11 +242,10 @@
         tile[step * padded : step * padded + capacity, :] = block[...]
 
 
-def partial_kernel(capacity, padded, gate, down, arrived, turned, pre_act, adapted, tile):
-    column = lax.axis_index("exp")
-    tile[...] = jnp.zeros(tile.shape, tile.dtype)
-    for step in range(arrived.shape[0]):
-        tile[step * padded : step * padded + capacity, :] = arrived[jnp.bitwise_xor(column, step)]
+def partial_kernel(capacity, padded, gate, down, *refs):
+    *blocks, turned, pre_act, adapted, tile = refs
+    half = len(blocks) // 2
+    fill(tile, [*blocks[half:], *blocks[:half]], capacity, padded)
     width = tile.shape[1]
     pre_act[...] = dot(tile[...], gate[0, :width])
     adapted[...] = dot(tile[...], down[0, :width])
@@ -437,24 +432,10 @@
         flops=2 * token_count * slots * fetched_rows,
         name="prepare",
     )
-    sent, *grads = pl.pallas_call(
-        functools.partial(pick_first_kernel, capacity, padded, pairs),
-        out_shape=[pltpu.HBM((exp_count, capacity, first_width), bf16)]
-        + [pltpu.HBM((capacity, hidden_units), bf16)] * exp_count,
-        in_specs=[near] * (1 + pairs + exp_count),
-        out_specs=[far] * (1 + exp_count),
-        scratch_shapes=[
-            pltpu.VMEM((exp_count, capacity, first_width), bf16),
-            pltpu.SemaphoreType.DMA((2 * exp_count,)),
-        ],
-        compiler_params=pltpu.CompilerParams(vmem_limit_bytes=16 * 1024 * 1024),
-        name="pick_first",
-    )(pick, *arrived, *grads[exp_count // 2 :], *grads[: exp_count // 2])
-    grads = [*grads[exp_count // 2 :], *grads[: exp_count // 2]]
-
-    pair_rows, sent = lax.optimization_barrier((pair_rows, sent))
-    first_blocks = lax.all_to_all(sent, "exp", 0, 0, tiled=True)
-    served = call(
+    half = exp_count // 2
+    kept = [*grads[half:], grads[0]]
+    pair_rows, pick = lax.optimization_barrier((pair_rows, pick))
+    served_last = call(
         serve_last_kernel,
         [shape((2 * fetch_slots, last_width), bf16)] * pairs,
         [shard_request_index, replay_buffer_rows, pair_table, pair_rows],
@@ -462,6 +443,22 @@
         flops=2 * fetched_rows * shard_rows * last_width,
         name="serve_last",
     )
+    blocks = pl.pallas_call(
+        functools.partial(pick_first_kernel, capacity, padded, pairs),
+        out_shape=[shape((capacity, first_width), bf16)] * exp_count
+        + [pltpu.HBM((capacity, hidden_units), bf16)] * len(kept),
+        in_specs=[near] * (1 + pairs + len(kept)),
+        out_specs=[near] * exp_count + [far] * len(kept),
+        scratch_shapes=[pltpu.SemaphoreType.DMA((len(kept),))],
+        compiler_params=pltpu.CompilerParams(vmem_limit_bytes=16 * 1024 * 1024),
+        name="pick_first",
+    )(pick, *arrived, *kept)
+    sent, kept = blocks[:exp_count], blocks[exp_count:]
+    grads = [kept[half], *grads[1:half], *kept[:half]]
+
+    joined = lax.optimization_barrier((*served_last, *sent))
+    served, sent = joined[:pairs], joined[pairs:]
+    first_blocks = swap_all(sent, exp_count)
     arrived = [swap_chip(block, step, rep_count) for step, block in enumerate(served)]
     first_sent, *sent = call(
         functools.partial(pick_last_kernel, capacity, padded, pairs),
@@ -487,7 +484,7 @@
     turned, pre_first, adapted_first = call(
         functools.partial(partial_kernel, capacity, padded),
         [shape((first_width, slots), bf16), shape((slots, hidden_units), f32), shape((slots, rank_width), f32)],
-        [*weights[:2], first_blocks],
+        [*weights[:2], *first_blocks[exp_count // 2 :], *first_blocks[: exp_count // 2]],
         resident=weights,
         scratch=[pltpu.VMEM((slots, first_width), bf16)],
         flops=2 * slots * first_width * (hidden_units + rank_width),

time: 79.3 us -> 77.8 us (0.981)
  waiting for transfers between devices: 22.4 us -> 28.4 us
  local copies, waits for them, and re-layouts: 6.07 us -> 0.09 us
  starting transfers between devices: 33.7 us -> 32.7 us
    ppermute x9 -> x12, waiting for transfers between devices: 11.1 us -> 19.7 us  [swap_exp(): return lax.ppermute(block, 'exp', [(i, i ^ step) for i in range(exp_count)])]
    unnamed x24 -> x18, local copies, waits for them, and re-layouts: 6.02 us -> 0.04 us
    all_to_all x1 -> x0, starting transfers between devices: 3.83 us -> none  [body(): first_blocks = lax.all_to_all(sent, 'exp', 0, 0, tiled=True)]
    ppermute x9, waiting for transfers between devices: 11.1 us -> 8.63 us  [swap_chip(): lax.ppermute(block, 'rep', [(i, i ^ 2 * step) for i in range(rep_count)])]
    ppermute x9 -> x12, starting transfers between devices: 18.5 us -> 20.4 us  [swap_exp(): return lax.ppermute(block, 'exp', [(i, i ^ step) for i in range(exp_count)])]
    ppermute x9, starting transfers between devices: 10.7 us -> 11.6 us  [swap_chip(): lax.ppermute(block, 'rep', [(i, i ^ 2 * step) for i in range(rep_count)])]
  transfers between devices with their start and end apart: 22 -> 24, of which waited for: 11 -> 8; matrix products, arithmetic and copies ran while one was open for 0% -> 0% of each run, Pallas kernels for 15% -> 15%
where the time goes in v7:
time: 77.8 us; the launch traced here: 77.6 us
  starting transfers between devices  32.7 us (42%)
  waiting for transfers between devices  28.4 us (37%)
  Pallas kernels  15.4 us (20%)
  between operations  0.8 us (1%)
    ppermute x12, starting transfers between devices, swap_exp(): return lax.ppermute(block, 'exp', [(i, i ^ step) for i in range(exp_count)])  20.4 us
    ppermute x12, waiting for transfers between devices, swap_exp(): return lax.ppermute(block, 'exp', [(i, i ^ step) for i in range(exp_count)])  19.7 us
    ppermute x9, starting transfers between devices, swap_chip(): lax.ppermute(block, 'rep', [(i, i ^ 2 * step) for i in range(rep_count)])  11.6 us
    pallas_call x8, Pallas kernels, call(): pl.pallas_call(moving, out_shape=[pltpu.HBM(out.shape, out.dtype) if numb...  9.16 us
    ppermute x9, waiting for transfers between devices, swap_chip(): lax.ppermute(block, 'rep', [(i, i ^ 2 * step) for i in range(rep_count)])  8.63 us
    pallas_call x1, Pallas kernels, body(): pl.pallas_call(fetch_kernel, out_shape=[pltpu.VMEM(array.shape, array.dty...  3.32 us
    pallas_call x1, Pallas kernels, body(): pl.pallas_call(functools.partial(begin_kernel, capacity, padded), out_sha...  2.18 us
  transfers between devices with their start and end apart: 24, of which 8 were waited for; matrix products, arithmetic and copies ran while one was open for 0% of the time, Pallas kernels for 15%

profile of v7, /device:TPU:0, one launch (start us, length us, event | category | flops | bytes accessed | tf_op | source)
XLA Modules:
  0.0 77.6 jit_solution(8114207111974850875)
XLA Ops:
  0.6 0.5 collective-permute-start.1
  1.1 0.1 collective-permute-start
  1.2 2.2 %begin.1 = (bf16[4,32,2176]{2,1,0:T(8,128)(2,1)S(1)}, bf16[56,1024]{1,0:T(8,128)(2,1)S(1)}, bf16[56,1024]{1,0:T(8,128)(2,1)S(1)}, bf16[56,1024]{1,0:T(8,128)(2,1)S(1)}, bf16[56,1024]{1,0:T(8,128)(2,1)S(1)}) custom-call(s32[1,8,32]{2,1,0:T(8,128)} %refs_0_.3, bf16[128,3584]{1,0:T(8,128)(2,1)} %refs_1_.1, s32[1,128]{1,0:T(1,128)} %bitcast.12, ...), custom_call_target="tpu_custom_call" | custom-call | tf_op jit(solution)/shard_map/begin/pallas_call | solution.py:398
  3.4 0.0 collective-permute-done.refs_0_.refs_2_
  3.5 0.0 collective-permute-done.1.refs_1_.refs_3_
  3.5 0.4 serve_first.1
  3.9 3.0 %collective-permute-start.2 = (bf16[64,2176]{1,0:T(8,128)(2,1)S(1)}, bf16[64,2176]{1,0:T(8,128)(2,1)S(1)}, u32[]{:S(2)}, u32[]{:S(2)}) collective-permute-start(bf16[64,2176]{1,0:T(8,128)(2,1)S(1)} %get-tuple-element.96), channel_id=1, source_target_pairs={{0,8},{4,12},{8,0},{12,4},{16,24},{20,28},{24,16},{28,20},{1,9},{5... | collective-permute-start | bytes 835592 | tf_op jit(solution)/shard_map/ppermute | solution.py:103
  6.9 1.5 %collective-permute-start.3 = (bf16[64,2176]{1,0:T(8,128)(2,1)S(1)}, bf16[64,2176]{1,0:T(8,128)(2,1)S(1)}, u32[]{:S(2)}, u32[]{:S(2)}) collective-permute-start(bf16[64,2176]{1,0:T(8,128)(2,1)S(1)} %get-tuple-element.97), channel_id=1, source_target_pairs={{0,16},{4,20},{8,24},{12,28},{16,0},{20,4},{24,8},{28,12},{1,17},{... | collective-permute-start | bytes 835592 | tf_op jit(solution)/shard_map/ppermute | solution.py:103
  8.4 0.0 collective-permute-start.4
  8.4 3.0 %collective-permute-start.5 = (bf16[56,1024]{1,0:T(8,128)(2,1)S(1)}, bf16[56,1024]{1,0:T(8,128)(2,1)S(1)}, u32[]{:S(2)}, u32[]{:S(2)}) collective-permute-start(bf16[56,1024]{1,0:T(8,128)(2,1)S(1)} %get-tuple-element.99), channel_id=1, source_target_pairs={{0,2},{1,3},{2,0},{3,1},{4,6},{5,7},{6,4},{7,5},{8,10},{9,11},{10,... | collective-permute-start | bytes 344072 | tf_op jit(solution)/shard_map/ppermute | solution.py:86
  11.4 1.3 %collective-permute-start.6 = (bf16[56,1024]{1,0:T(8,128)(2,1)S(1)}, bf16[56,1024]{1,0:T(8,128)(2,1)S(1)}, u32[]{:S(2)}, u32[]{:S(2)}) collective-permute-start(bf16[56,1024]{1,0:T(8,128)(2,1)S(1)} %get-tuple-element.100), channel_id=1, source_target_pairs={{0,3},{1,2},{2,1},{3,0},{4,7},{5,6},{6,5},{7,4},{8,11},{9,10},{10,... | collective-permute-start | bytes 344072 | tf_op jit(solution)/shard_map/ppermute | solution.py:86
  12.8 1.5 %prepare.1 = (bf16[256,256]{1,0:T(8,128)(2,1)S(1)}, bf16[128,256]{1,0:T(8,128)(2,1)}) custom-call(s32[1,8]{1,0:T(1,128)S(1)} %copy-done.8, s32[1,128]{1,0:T(1,128)S(1)} %bitcast.13), custom_call_target="tpu_custom_call" | custom-call | flops 16777216 | bytes 55924 | tf_op jit(solution)/shard_map/prepare/pallas_call | solution.py:64
  14.3 1.2 %serve_last.1 = (bf16[64,1408]{1,0:T(8,128)(2,1)S(1)}, bf16[64,1408]{1,0:T(8,128)(2,1)S(1)}, bf16[64,1408]{1,0:T(8,128)(2,1)S(1)}, bf16[64,1408]{1,0:T(8,128)(2,1)S(1)}) custom-call(s32[1,8,32]{2,1,0:T(8,128)} %refs_0_.3, bf16[128,3584]{1,0:T(8,128)(2,1)S(1)} %copy-done, s32[1,8,32]{2,1,0:T(8,128)} %copy-done.5, ...), custom_call_target="tpu_custom_call" | custom-call | flops 92274688 | bytes 307582 | tf_op jit(solution)/shard_map/serve_last/pallas_call | solution.py:64
  15.5 4.6 %collective-permute-done.5.refs_4_ = bf16[56,1024]{1,0:T(8,128)(2,1)S(1)} collective-permute-done((bf16[56,1024]{1,0:T(8,128)(2,1)S(1)}, bf16[56,1024]{1,0:T(8,128)(2,1)S(1)}, u32[]{:S(2)}, u32[]{:S(2)}) %collective-permute-start.5) | collective-permute-done | bytes 114720 | tf_op jit(solution)/shard_map/ppermute | solution.py:86
  20.1 0.0 collective-permute-done.6.refs_5_
  20.1 0.0 collective-permute-done.2.refs_1_
  20.1 1.1 %collective-permute-done.3.refs_2_ = bf16[64,2176]{1,0:T(8,128)(2,1)S(1)} collective-permute-done((bf16[64,2176]{1,0:T(8,128)(2,1)S(1)}, bf16[64,2176]{1,0:T(8,128)(2,1)S(1)}, u32[]{:S(2)}, u32[]{:S(2)}) %collective-permute-start.3) | collective-permute-done | bytes 278560 | tf_op jit(solution)/shard_map/ppermute | solution.py:103
  21.2 0.0 collective-permute-done.4.refs_3_
  21.2 0.8 pick_first.1
  22.0 1.3 %collective-permute-start.7 = (bf16[64,1408]{1,0:T(8,128)(2,1)S(1)}, bf16[64,1408]{1,0:T(8,128)(2,1)S(1)}, u32[]{:S(2)}, u32[]{:S(2)}) collective-permute-start(bf16[64,1408]{1,0:T(8,128)(2,1)S(1)} %get-tuple-element.107), channel_id=1, source_target_pairs={{0,8},{4,12},{8,0},{12,4},{16,24},{20,28},{24,16},{28,20},{1,9},{5... | collective-permute-start | bytes 540680 | tf_op jit(solution)/shard_map/ppermute | solution.py:103
  23.3 3.1 %collective-permute-start.10 = (bf16[56,2176]{1,0:T(8,128)(2,1)S(1)}, bf16[56,2176]{1,0:T(8,128)(2,1)S(1)}, u32[]{:S(2)}, u32[]{:S(2)}) collective-permute-start(bf16[56,2176]{1,0:T(8,128)(2,1)S(1)} %get-tuple-element.116), channel_id=1, source_target_pairs={{0,2},{1,3},{2,0},{3,1},{4,6},{5,7},{6,4},{7,5},{8,10},{9,11},{10,... | collective-permute-start | bytes 731144 | tf_op jit(solution)/shard_map/ppermute | solution.py:86
  26.4 0.8 %collective-permute-start.11 = (bf16[56,2176]{1,0:T(8,128)(2,1)S(1)}, bf16[56,2176]{1,0:T(8,128)(2,1)S(1)}, u32[]{:S(2)}, u32[]{:S(2)}) collective-permute-start(bf16[56,2176]{1,0:T(8,128)(2,1)S(1)} %get-tuple-element.117), channel_id=1, source_target_pairs={{0,3},{1,2},{2,1},{3,0},{4,7},{5,6},{6,5},{7,4},{8,11},{9,10},{10,... | collective-permute-start | bytes 731144 | tf_op jit(solution)/shard_map/ppermute | solution.py:86
  27.2 0.2 collective-permute-start.12
  27.4 1.0 %collective-permute-start.8 = (bf16[64,1408]{1,0:T(8,128)(2,1)S(1)}, bf16[64,1408]{1,0:T(8,128)(2,1)S(1)}, u32[]{:S(2)}, u32[]{:S(2)}) collective-permute-start(bf16[64,1408]{1,0:T(8,128)(2,1)S(1)} %get-tuple-element.108), channel_id=1, source_target_pairs={{0,16},{4,20},{8,24},{12,28},{16,0},{20,4},{24,8},{28,12},{1,17},{... | collective-permute-start | bytes 540680 | tf_op jit(solution)/shard_map/ppermute | solution.py:103
  28.5 0.0 collective-permute-done.7.refs_2_
  28.5 1.2 %collective-permute-start.9 = (bf16[64,1408]{1,0:T(8,128)(2,1)S(1)}, bf16[64,1408]{1,0:T(8,128)(2,1)S(1)}, u32[]{:S(2)}, u32[]{:S(2)}) collective-permute-start(bf16[64,1408]{1,0:T(8,128)(2,1)S(1)} %get-tuple-element.109), channel_id=1, source_target_pairs={{0,24},{4,28},{8,16},{12,20},{16,8},{20,12},{24,0},{28,4},{1,25},{... | collective-permute-start | bytes 540680 | tf_op jit(solution)/shard_map/ppermute | solution.py:103
  29.7 6.9 %collective-permute-done.8.refs_3_ = bf16[64,1408]{1,0:T(8,128)(2,1)S(1)} collective-permute-done((bf16[64,1408]{1,0:T(8,128)(2,1)S(1)}, bf16[64,1408]{1,0:T(8,128)(2,1)S(1)}, u32[]{:S(2)}, u32[]{:S(2)}) %collective-permute-start.8) | collective-permute-done | bytes 180256 | tf_op jit(solution)/shard_map/ppermute | solution.py:103
  36.6 0.0 collective-permute-done.9.refs_4_
  36.6 0.4 pick_last.1
  37.0 1.7 %collective-permute-start.13 = (bf16[56,1408]{1,0:T(8,128)(2,1)S(1)}, bf16[56,1408]{1,0:T(8,128)(2,1)S(1)}, u32[]{:S(2)}, u32[]{:S(2)}) collective-permute-start(bf16[56,1408]{1,0:T(8,128)(2,1)S(1)} %get-tuple-element.124), channel_id=1, source_target_pairs={{0,1},{1,0},{2,3},{3,2},{4,5},{5,4},{6,7},{7,6},{8,9},{9,8},{10,11... | collective-permute-start | bytes 473096 | tf_op jit(solution)/shard_map/ppermute | solution.py:86
  38.7 0.4 collective-permute-start.14
  39.1 3.3 %fetch.1 = (bf16[1,3584,1024]{2,1,0:T(8,128)(2,1)S(1)}, bf16[1,3584,128]{2,1,0:T(8,128)(2,1)S(1)}, bf16[1,128,1024]{2,1,0:T(8,128)(2,1)S(1)}) custom-call(bf16[1,3584,1024]{2,1,0:T(8,128)(2,1)} %refs_0_.4, bf16[1,3584,128]{2,1,0:T(8,128)(2,1)} %refs_1_.2, bf16[1,128,1024]{2,1,0:T(8,128)(2,1)} %refs_2_), custom_call_target="tpu_custom_call" | custom-call | tf_op jit(solution)/shard_map/fetch/pallas_call | solution.py:472
  42.4 0.5 collective-permute-done.10.refs_2_
  42.9 3.1 %collective-permute-start.16 = (bf16[56,1408]{1,0:T(8,128)(2,1)S(1)}, bf16[56,1408]{1,0:T(8,128)(2,1)S(1)}, u32[]{:S(2)}, u32[]{:S(2)}) collective-permute-start(bf16[56,1408]{1,0:T(8,128)(2,1)S(1)} %get-tuple-element.134), channel_id=1, source_target_pairs={{0,2},{1,3},{2,0},{3,1},{4,6},{5,7},{6,4},{7,5},{8,10},{9,11},{10,... | collective-permute-start | bytes 473096 | tf_op jit(solution)/shard_map/ppermute | solution.py:86
  46.0 0.0 collective-permute-done.11.refs_3_
  46.0 0.5 collective-permute-start.17
  46.5 0.0 collective-permute-done.12.refs_5_
  46.5 1.7 %partial.1 = (bf16[2176,256]{1,0:T(8,128)(2,1)S(1)}, f32[256,1024]{1,0:T(8,128)S(1)}, f32[256,128]{1,0:T(8,128)S(1)}) custom-call(bf16[1,3584,1024]{2,1,0:T(8,128)(2,1)S(1)} %get-tuple-element.114.refs_0_.refs_2_.refs_7_, bf16[1,3584,128]{2,1,0:T(8,128)(2,1)S(1)} %get-tuple-element.115.refs_1_.refs_3_.refs_8_, ...), custom_call_target="tpu_custom_call" | custom-call | flops 1283457024 | bytes 4278190 | tf_op jit(solution)/shard_map/partial/pallas_call | solution.py:64
  48.2 2.7 %collective-permute-done.14.refs_8_ = bf16[56,1024]{1,0:T(8,128)(2,1)S(1)} collective-permute-done((bf16[56,1024]{1,0:T(8,128)(2,1)S(1)}, bf16[56,1024]{1,0:T(8,128)(2,1)S(1)}, u32[]{:S(2)}, u32[]{:S(2)}) %collective-permute-start.14) | collective-permute-done | bytes 114720 | tf_op jit(solution)/shard_map/ppermute | solution.py:86
  50.9 0.0 collective-permute-done.13.refs_6_
  51.0 0.0 copy-start.2
  51.0 1.0 %early.1 = (bf16[56,1024]{1,0:T(8,128)(2,1)S(1)}, bf16[56,1024]{1,0:T(8,128)(2,1)S(1)}, bf16[1408,128]{1,0:T(8,128)(2,1)S(1)}, bf16[128,128]{1,0:T(8,128)(2,1)S(...) custom-call(f32[256,1024]{1,0:T(8,128)S(1)} %get-tuple-element.120.refs_0_.refs_5_, ...), custom_call_target="tpu_custom_call" | custom-call | flops 415236096 | bytes 1384120 | tf_op jit(solution)/shard_map/early/pallas_call | solution.py:64
  52.0 6.3 %collective-permute-done.16.refs_10_ = bf16[56,1408]{1,0:T(8,128)(2,1)S(1)} collective-permute-done((bf16[56,1408]{1,0:T(8,128)(2,1)S(1)}, bf16[56,1408]{1,0:T(8,128)(2,1)S(1)}, u32[]{:S(2)}, u32[]{:S(2)}) %collective-permute-start.16) | collective-permute-done | bytes 157728 | tf_op jit(solution)/shard_map/ppermute | solution.py:86
  58.3 0.0 collective-permute-done.17.refs_11_
  58.3 0.0 copy-done.2
  58.3 1.9 %late.1 = (bf16[56,1024]{1,0:T(8,128)(2,1)S(1)}, bf16[56,1024]{1,0:T(8,128)(2,1)S(1)}, f32[4,576,128]{2,1,0:T(8,128)S(1)}, bf16[4,576,128]{2,1,0:T(8,128)(2,1)S(1)}) custom-call(bf16[2176,256]{1,0:T(8,128)(2,1)S(1)} %get-tuple-element.129.refs_0_, bf16[1408,128]{1,0:T(8,128)(2,1)S(1)} %get-tuple-element.130.refs_1_, ...), custom_call_target="tpu_custom_call" | custom-call | flops 884998144 | bytes 2949993 | tf_op jit(solution)/shard_map/late/pallas_call | solution.py:64
  60.3 0.1 collective-permute-start.20
  60.3 3.7 %collective-permute-start.15 = (bf16[56,1024]{1,0:T(8,128)(2,1)S(1)}, bf16[56,1024]{1,0:T(8,128)(2,1)S(1)}, u32[]{:S(2)}, u32[]{:S(2)}) collective-permute-start(bf16[56,1024]{1,0:T(8,128)(2,1)S(1)} %get-tuple-element.128), channel_id=1, source_target_pairs={{0,1},{1,0},{2,3},{3,2},{4,5},{5,4},{6,7},{7,6},{8,9},{9,8},{10,11... | collective-permute-start | bytes 344072 | tf_op jit(solution)/shard_map/ppermute | solution.py:86
  64.1 1.0 %collective-permute-start.18 = (bf16[56,1024]{1,0:T(8,128)(2,1)S(1)}, bf16[56,1024]{1,0:T(8,128)(2,1)S(1)}, u32[]{:S(2)}, u32[]{:S(2)}) collective-permute-start(bf16[56,1024]{1,0:T(8,128)(2,1)S(1)} %get-tuple-element.138), channel_id=1, source_target_pairs={{0,2},{1,3},{2,0},{3,1},{4,6},{5,7},{6,4},{7,5},{8,10},{9,11},{10,... | collective-permute-start | bytes 344072 | tf_op jit(solution)/shard_map/ppermute | solution.py:86
  65.1 1.4 %collective-permute-start.19 = (bf16[56,1024]{1,0:T(8,128)(2,1)S(1)}, bf16[56,1024]{1,0:T(8,128)(2,1)S(1)}, u32[]{:S(2)}, u32[]{:S(2)}) collective-permute-start(bf16[56,1024]{1,0:T(8,128)(2,1)S(1)} %get-tuple-element.139), channel_id=1, source_target_pairs={{0,3},{1,2},{2,1},{3,0},{4,7},{5,6},{6,5},{7,4},{8,11},{9,10},{10,... | collective-permute-start | bytes 344072 | tf_op jit(solution)/shard_map/ppermute | solution.py:86
  66.5 0.0 collective-permute-done.20
  66.5 0.2 fusion
  66.7 0.0 copy-start.4
  66.7 0.0 copy-start.6
  66.8 1.6 %collective-permute-start.21 = (bf16[576,128]{1,0:T(8,128)(2,1)S(1)}, bf16[576,128]{1,0:T(8,128)(2,1)S(1)}, u32[]{:S(2)}, u32[]{:S(2)}) collective-permute-start(bf16[576,128]{1,0:T(8,128)(2,1)S(1)} %get-tuple-element.149), channel_id=1, source_target_pairs={{0,24},{4,28},{8,16},{12,20},{16,8},{20,12},{24,0},{28,4},{1,25},{... | collective-permute-start | bytes 442376 | tf_op jit(solution)/shard_map/ppermute | solution.py:103
  68.3 0.5 collective-permute-start.22
  68.8 0.0 collective-permute-done.15.refs_3_
  68.9 1.5 %collective-permute-start.23 = (bf16[576,128]{1,0:T(8,128)(2,1)S(1)}, bf16[576,128]{1,0:T(8,128)(2,1)S(1)}, u32[]{:S(2)}, u32[]{:S(2)}) collective-permute-start(bf16[576,128]{1,0:T(8,128)(2,1)S(1)} %get-tuple-element.147), channel_id=1, source_target_pairs={{0,8},{4,12},{8,0},{12,4},{16,24},{20,28},{24,16},{28,20},{1,9},{5... | collective-permute-start | bytes 442376 | tf_op jit(solution)/shard_map/ppermute | solution.py:103
  70.3 5.6 %collective-permute-done.18.refs_4_ = bf16[56,1024]{1,0:T(8,128)(2,1)S(1)} collective-permute-done((bf16[56,1024]{1,0:T(8,128)(2,1)S(1)}, bf16[56,1024]{1,0:T(8,128)(2,1)S(1)}, u32[]{:S(2)}, u32[]{:S(2)}) %collective-permute-start.18) | collective-permute-done | bytes 114720 | tf_op jit(solution)/shard_map/ppermute | solution.py:86
  75.9 0.0 collective-permute-done.19.refs_5_
  75.9 0.0 collective-permute-done.21.refs_7_
  75.9 0.6 collective-permute-done.22.refs_8_
  76.5 0.0 collective-permute-done.23.refs_9_
  76.5 1.0 %end.1 = (f32[1,448,128]{2,1,0:T(8,128)}, f32[1,16,1024]{2,1,0:T(8,128)}, bf16[128,1024]{1,0:T(8,128)(2,1)}) custom-call(bf16[128,256]{1,0:T(8,128)(2,1)S(1)} %copy-done.4, f32[1,128]{1,0:T(1,128)S(1)} %bitcast.11, bf16[56,1024]{1,0:T(8,128)(2,1)S(1)} %get-tuple-element.127.refs_2_, bf16[56,1024]{1,0:T(8,128)(2,1)S(1)} %collective-permute-done.15.refs_3_, ...), custom_call_target="tpu_custom_call" | custom-call | flops 67108864 | bytes 223696 | tf_op jit(solution)/shard_map/end/pallas_call | solution.py:64
  (16 shorter events, 0.1 us)
Async XLA Ops:
  0.6 2.8 %collective-permute-start.1 = (bf16[128,3584]{1,0:T(8,128)(2,1)}, bf16[128,3584]{1,0:T(8,128)(2,1)S(1)}, u32[]{:S(2)}, u32[]{:S(2)}) collective-permute-start(bf16[128,3584]{1,0:T(8,128)(2,1)} %refs_1_.1), channel_id=1, source_target_pairs={{0,4},{4,0},{8,12},{12,8},{16,20},{20,16},{24,28},{28,24},{1,5},{5... | collective-permute-start | bytes 2752520 | tf_op jit(solution)/shard_map/ppermute | solution.py:97
  1.1 2.3 %collective-permute-start = (s32[1,8,32]{2,1,0:T(8,128)}, s32[1,8,32]{2,1,0:T(8,128)S(1)}, u32[]{:S(2)}, u32[]{:S(2)}) collective-permute-start(s32[1,8,32]{2,1,0:T(8,128)} %refs_0_.3), channel_id=1, source_target_pairs={{0,4},{4,0},{8,12},{12,8},{16,20},{20,16},{24,28},{28,24},{1,5},{5... | collective-permute-start | bytes 3080 | tf_op jit(solution)/shard_map/ppermute | solution.py:97
  1.2 11.6 %copy-start.7 = (s32[128,1]{0,1:T(1,128)S(1)}, s32[128,1]{0,1:T(1,128)}, u32[]{:S(2)}) copy-start(s32[128,1]{0,1:T(1,128)} %param.12) | copy-start | bytes 1540
  1.2 11.6 %copy-start.8 = (s32[1,8]{1,0:T(1,128)S(1)}, s32[1,8]{1,0:T(1,128)}, u32[]{:S(2)}) copy-start(s32[1,8]{1,0:T(1,128)} %refs_0_.2) | copy-start | bytes 100
  1.2 13.1 %copy-start = (bf16[128,3584]{1,0:T(8,128)(2,1)S(1)}, bf16[128,3584]{1,0:T(8,128)(2,1)}, u32[]{:S(2)}) copy-start(bf16[128,3584]{1,0:T(8,128)(2,1)} %refs_1_.1) | copy-start | bytes 2752516
  3.5 10.8 %copy-start.5 = (s32[1,8,32]{2,1,0:T(8,128)}, s32[1,8,32]{2,1,0:T(8,128)S(1)}, u32[]{:S(2)}) copy-start(s32[1,8,32]{2,1,0:T(8,128)S(1)} %collective-permute-done.refs_0_.refs_2_) | copy-start | bytes 3076
  3.9 16.3 %collective-permute-start.2 = (bf16[64,2176]{1,0:T(8,128)(2,1)S(1)}, bf16[64,2176]{1,0:T(8,128)(2,1)S(1)}, u32[]{:S(2)}, u32[]{:S(2)}) collective-permute-start(bf16[64,2176]{1,0:T(8,128)(2,1)S(1)} %get-tuple-element.96), channel_id=1, source_target_pairs={{0,8},{4,12},{8,0},{12,4},{16,24},{20,28},{24,16},{28,20},{1,9},{5... | collective-permute-start | bytes 835592 | tf_op jit(solution)/shard_map/ppermute | solution.py:103
  6.9 14.3 %collective-permute-start.3 = (bf16[64,2176]{1,0:T(8,128)(2,1)S(1)}, bf16[64,2176]{1,0:T(8,128)(2,1)S(1)}, u32[]{:S(2)}, u32[]{:S(2)}) collective-permute-start(bf16[64,2176]{1,0:T(8,128)(2,1)S(1)} %get-tuple-element.97), channel_id=1, source_target_pairs={{0,16},{4,20},{8,24},{12,28},{16,0},{20,4},{24,8},{28,12},{1,17},{... | collective-permute-start | bytes 835592 | tf_op jit(solution)/shard_map/ppermute | solution.py:103
  8.4 12.8 %collective-permute-start.4 = (bf16[64,2176]{1,0:T(8,128)(2,1)S(1)}, bf16[64,2176]{1,0:T(8,128)(2,1)S(1)}, u32[]{:S(2)}, u32[]{:S(2)}) collective-permute-start(bf16[64,2176]{1,0:T(8,128)(2,1)S(1)} %get-tuple-element.98), channel_id=1, source_target_pairs={{0,24},{4,28},{8,16},{12,20},{16,8},{20,12},{24,0},{28,4},{1,25},{... | collective-permute-start | bytes 835592 | tf_op jit(solution)/shard_map/ppermute | solution.py:103
  8.4 11.7 %collective-permute-start.5 = (bf16[56,1024]{1,0:T(8,128)(2,1)S(1)}, bf16[56,1024]{1,0:T(8,128)(2,1)S(1)}, u32[]{:S(2)}, u32[]{:S(2)}) collective-permute-start(bf16[56,1024]{1,0:T(8,128)(2,1)S(1)} %get-tuple-element.99), channel_id=1, source_target_pairs={{0,2},{1,3},{2,0},{3,1},{4,6},{5,7},{6,4},{7,5},{8,10},{9,11},{10,... | collective-permute-start | bytes 344072 | tf_op jit(solution)/shard_map/ppermute | solution.py:86
  11.4 8.7 %collective-permute-start.6 = (bf16[56,1024]{1,0:T(8,128)(2,1)S(1)}, bf16[56,1024]{1,0:T(8,128)(2,1)S(1)}, u32[]{:S(2)}, u32[]{:S(2)}) collective-permute-start(bf16[56,1024]{1,0:T(8,128)(2,1)S(1)} %get-tuple-element.100), channel_id=1, source_target_pairs={{0,3},{1,2},{2,1},{3,0},{4,7},{5,6},{6,5},{7,4},{8,11},{9,10},{10,... | collective-permute-start | bytes 344072 | tf_op jit(solution)/shard_map/ppermute | solution.py:86
  22.0 6.5 %collective-permute-start.7 = (bf16[64,1408]{1,0:T(8,128)(2,1)S(1)}, bf16[64,1408]{1,0:T(8,128)(2,1)S(1)}, u32[]{:S(2)}, u32[]{:S(2)}) collective-permute-start(bf16[64,1408]{1,0:T(8,128)(2,1)S(1)} %get-tuple-element.107), channel_id=1, source_target_pairs={{0,8},{4,12},{8,0},{12,4},{16,24},{20,28},{24,16},{28,20},{1,9},{5... | collective-permute-start | bytes 540680 | tf_op jit(solution)/shard_map/ppermute | solution.py:103
  23.3 19.7 %collective-permute-start.10 = (bf16[56,2176]{1,0:T(8,128)(2,1)S(1)}, bf16[56,2176]{1,0:T(8,128)(2,1)S(1)}, u32[]{:S(2)}, u32[]{:S(2)}) collective-permute-start(bf16[56,2176]{1,0:T(8,128)(2,1)S(1)} %get-tuple-element.116), channel_id=1, source_target_pairs={{0,2},{1,3},{2,0},{3,1},{4,6},{5,7},{6,4},{7,5},{8,10},{9,11},{10,... | collective-permute-start | bytes 731144 | tf_op jit(solution)/shard_map/ppermute | solution.py:86
  26.4 19.6 %collective-permute-start.11 = (bf16[56,2176]{1,0:T(8,128)(2,1)S(1)}, bf16[56,2176]{1,0:T(8,128)(2,1)S(1)}, u32[]{:S(2)}, u32[]{:S(2)}) collective-permute-start(bf16[56,2176]{1,0:T(8,128)(2,1)S(1)} %get-tuple-element.117), channel_id=1, source_target_pairs={{0,3},{1,2},{2,1},{3,0},{4,7},{5,6},{6,5},{7,4},{8,11},{9,10},{10,... | collective-permute-start | bytes 731144 | tf_op jit(solution)/shard_map/ppermute | solution.py:86
  27.2 19.3 %collective-permute-start.12 = (bf16[56,2176]{1,0:T(8,128)(2,1)S(1)}, bf16[56,2176]{1,0:T(8,128)(2,1)S(1)}, u32[]{:S(2)}, u32[]{:S(2)}) collective-permute-start(bf16[56,2176]{1,0:T(8,128)(2,1)S(1)} %get-tuple-element.119), channel_id=1, source_target_pairs={{0,1},{1,0},{2,3},{3,2},{4,5},{5,4},{6,7},{7,6},{8,9},{9,8},{10,11... | collective-permute-start | bytes 731144 | tf_op jit(solution)/shard_map/ppermute | solution.py:86
  27.4 9.2 %collective-permute-start.8 = (bf16[64,1408]{1,0:T(8,128)(2,1)S(1)}, bf16[64,1408]{1,0:T(8,128)(2,1)S(1)}, u32[]{:S(2)}, u32[]{:S(2)}) collective-permute-start(bf16[64,1408]{1,0:T(8,128)(2,1)S(1)} %get-tuple-element.108), channel_id=1, source_target_pairs={{0,16},{4,20},{8,24},{12,28},{16,0},{20,4},{24,8},{28,12},{1,17},{... | collective-permute-start | bytes 540680 | tf_op jit(solution)/shard_map/ppermute | solution.py:103
  28.5 8.2 %collective-permute-start.9 = (bf16[64,1408]{1,0:T(8,128)(2,1)S(1)}, bf16[64,1408]{1,0:T(8,128)(2,1)S(1)}, u32[]{:S(2)}, u32[]{:S(2)}) collective-permute-start(bf16[64,1408]{1,0:T(8,128)(2,1)S(1)} %get-tuple-element.109), channel_id=1, source_target_pairs={{0,24},{4,28},{8,16},{12,20},{16,8},{20,12},{24,0},{28,4},{1,25},{... | collective-permute-start | bytes 540680 | tf_op jit(solution)/shard_map/ppermute | solution.py:103
  37.0 13.9 %collective-permute-start.13 = (bf16[56,1408]{1,0:T(8,128)(2,1)S(1)}, bf16[56,1408]{1,0:T(8,128)(2,1)S(1)}, u32[]{:S(2)}, u32[]{:S(2)}) collective-permute-start(bf16[56,1408]{1,0:T(8,128)(2,1)S(1)} %get-tuple-element.124), channel_id=1, source_target_pairs={{0,1},{1,0},{2,3},{3,2},{4,5},{5,4},{6,7},{7,6},{8,9},{9,8},{10,11... | collective-permute-start | bytes 473096 | tf_op jit(solution)/shard_map/ppermute | solution.py:86
  38.7 12.2 %collective-permute-start.14 = (bf16[56,1024]{1,0:T(8,128)(2,1)S(1)}, bf16[56,1024]{1,0:T(8,128)(2,1)S(1)}, u32[]{:S(2)}, u32[]{:S(2)}) collective-permute-start(bf16[56,1024]{1,0:T(8,128)(2,1)S(1)} %get-tuple-element.126), channel_id=1, source_target_pairs={{0,1},{1,0},{2,3},{3,2},{4,5},{5,4},{6,7},{7,6},{8,9},{9,8},{10,11... | collective-permute-start | bytes 344072 | tf_op jit(solution)/shard_map/ppermute | solution.py:86
  42.9 15.4 %collective-permute-start.16 = (bf16[56,1408]{1,0:T(8,128)(2,1)S(1)}, bf16[56,1408]{1,0:T(8,128)(2,1)S(1)}, u32[]{:S(2)}, u32[]{:S(2)}) collective-permute-start(bf16[56,1408]{1,0:T(8,128)(2,1)S(1)} %get-tuple-element.134), channel_id=1, source_target_pairs={{0,2},{1,3},{2,0},{3,1},{4,6},{5,7},{6,4},{7,5},{8,10},{9,11},{10,... | collective-permute-start | bytes 473096 | tf_op jit(solution)/shard_map/ppermute | solution.py:86
  46.0 12.3 %collective-permute-start.17 = (bf16[56,1408]{1,0:T(8,128)(2,1)S(1)}, bf16[56,1408]{1,0:T(8,128)(2,1)S(1)}, u32[]{:S(2)}, u32[]{:S(2)}) collective-permute-start(bf16[56,1408]{1,0:T(8,128)(2,1)S(1)} %get-tuple-element.135), channel_id=1, source_target_pairs={{0,3},{1,2},{2,1},{3,0},{4,7},{5,6},{6,5},{7,4},{8,11},{9,10},{10,... | collective-permute-start | bytes 473096 | tf_op jit(solution)/shard_map/ppermute | solution.py:86
  46.5 4.4 %copy-start.3 = (bf16[56,1024]{1,0:T(8,128)(2,1)S(1)}, bf16[56,1024]{1,0:T(8,128)(2,1)}, u32[]{:S(2)}) copy-start(bf16[56,1024]{1,0:T(8,128)(2,1)} %get-tuple-element.125.refs_7_) | copy-start | bytes 344068
  51.0 7.3 %copy-start.1 = (bf16[56,1024]{1,0:T(8,128)(2,1)S(1)}, bf16[56,1024]{1,0:T(8,128)(2,1)}, u32[]{:S(2)}) copy-start(bf16[56,1024]{1,0:T(8,128)(2,1)} %get-tuple-element.136.refs_12_) | copy-start | bytes 344068
  51.0 7.3 %copy-start.2 = (bf16[56,1024]{1,0:T(8,128)(2,1)S(1)}, bf16[56,1024]{1,0:T(8,128)(2,1)}, u32[]{:S(2)}) copy-start(bf16[56,1024]{1,0:T(8,128)(2,1)} %get-tuple-element.137.refs_13_) | copy-start | bytes 344068
  60.3 6.3 %collective-permute-start.20 = (bf16[4,576,128]{2,1,0:T(8,128)(2,1)S(1)}, bf16[4,576,128]{2,1,0:T(8,128)(2,1)S(1)}, u32[]{:S(2)}, u32[]{:S(2)}) collective-permute-start(bf16[4,576,128]{2,1,0:T(8,128)(2,1)S(1)} %get-tuple-element.141), channel_id=1, source_target_pairs={{0,4},{4,0},{8,12},{12,8},{16,20},{20,16},{24,28},{28,24},{1,5},{5... | collective-permute-start | bytes 1769480 | tf_op jit(solution)/shard_map/ppermute | solution.py:97
  60.3 8.5 %collective-permute-start.15 = (bf16[56,1024]{1,0:T(8,128)(2,1)S(1)}, bf16[56,1024]{1,0:T(8,128)(2,1)S(1)}, u32[]{:S(2)}, u32[]{:S(2)}) collective-permute-start(bf16[56,1024]{1,0:T(8,128)(2,1)S(1)} %get-tuple-element.128), channel_id=1, source_target_pairs={{0,1},{1,0},{2,3},{3,2},{4,5},{5,4},{6,7},{7,6},{8,9},{9,8},{10,11... | collective-permute-start | bytes 344072 | tf_op jit(solution)/shard_map/ppermute | solution.py:86
  64.1 11.8 %collective-permute-start.18 = (bf16[56,1024]{1,0:T(8,128)(2,1)S(1)}, bf16[56,1024]{1,0:T(8,128)(2,1)S(1)}, u32[]{:S(2)}, u32[]{:S(2)}) collective-permute-start(bf16[56,1024]{1,0:T(8,128)(2,1)S(1)} %get-tuple-element.138), channel_id=1, source_target_pairs={{0,2},{1,3},{2,0},{3,1},{4,6},{5,7},{6,4},{7,5},{8,10},{9,11},{10,... | collective-permute-start | bytes 344072 | tf_op jit(solution)/shard_map/ppermute | solution.py:86
  65.1 10.8 %collective-permute-start.19 = (bf16[56,1024]{1,0:T(8,128)(2,1)S(1)}, bf16[56,1024]{1,0:T(8,128)(2,1)S(1)}, u32[]{:S(2)}, u32[]{:S(2)}) collective-permute-start(bf16[56,1024]{1,0:T(8,128)(2,1)S(1)} %get-tuple-element.139), channel_id=1, source_target_pairs={{0,3},{1,2},{2,1},{3,0},{4,7},{5,6},{6,5},{7,4},{8,11},{9,10},{10,... | collective-permute-start | bytes 344072 | tf_op jit(solution)/shard_map/ppermute | solution.py:86
  66.7 9.8 %copy-start.4 = (bf16[128,256]{1,0:T(8,128)(2,1)S(1)}, bf16[128,256]{1,0:T(8,128)(2,1)}, u32[]{:S(2)}) copy-start(bf16[128,256]{1,0:T(8,128)(2,1)} %get-tuple-element.86.refs_0_) | copy-start | bytes 196612
  66.7 9.8 %copy-start.6 = (f32[128,1]{0,1:T(1,128)S(1)}, f32[128,1]{0,1:T(1,128)}, u32[]{:S(2)}) copy-start(f32[128,1]{0,1:T(1,128)} %param.13) | copy-start | bytes 1540
  66.8 9.1 %collective-permute-start.21 = (bf16[576,128]{1,0:T(8,128)(2,1)S(1)}, bf16[576,128]{1,0:T(8,128)(2,1)S(1)}, u32[]{:S(2)}, u32[]{:S(2)}) collective-permute-start(bf16[576,128]{1,0:T(8,128)(2,1)S(1)} %get-tuple-element.149), channel_id=1, source_target_pairs={{0,24},{4,28},{8,16},{12,20},{16,8},{20,12},{24,0},{28,4},{1,25},{... | collective-permute-start | bytes 442376 | tf_op jit(solution)/shard_map/ppermute | solution.py:103
  68.3 8.2 %collective-permute-start.22 = (bf16[576,128]{1,0:T(8,128)(2,1)S(1)}, bf16[576,128]{1,0:T(8,128)(2,1)S(1)}, u32[]{:S(2)}, u32[]{:S(2)}) collective-permute-start(bf16[576,128]{1,0:T(8,128)(2,1)S(1)} %get-tuple-element.148), channel_id=1, source_target_pairs={{0,16},{4,20},{8,24},{12,28},{16,0},{20,4},{24,8},{28,12},{1,17},{... | collective-permute-start | bytes 442376 | tf_op jit(solution)/shard_map/ppermute | solution.py:103
  68.9 7.7 %collective-permute-start.23 = (bf16[576,128]{1,0:T(8,128)(2,1)S(1)}, bf16[576,128]{1,0:T(8,128)(2,1)S(1)}, u32[]{:S(2)}, u32[]{:S(2)}) collective-permute-start(bf16[576,128]{1,0:T(8,128)(2,1)S(1)} %get-tuple-element.147), channel_id=1, source_target_pairs={{0,8},{4,12},{8,0},{12,4},{16,24},{20,28},{24,16},{28,20},{1,9},{5... | collective-permute-start | bytes 442376 | tf_op jit(solution)/shard_map/ppermute | solution.py:103

commit v8 on v7

--- a/solution.py
+++ b/solution.py
@@ -211,21 +211,17 @@
 
 def pick_first_kernel(capacity, padded, chips, pick, *refs):
     arrived, refs = refs[:chips], refs[chips:]
-    *refs, sems = refs
-    kept = sems.shape[0]
-    grads, sent, grads_far = refs[:kept], refs[kept : len(refs) - kept], refs[len(refs) - kept :]
-    exp_count = len(sent)
-    put_away = [
-        pltpu.make_async_copy(block, place, sems.at[step]) for step, (block, place) in enumerate(zip(grads, grads_far))
-    ]
-    for copy in put_away:
-        copy.start()
+    *refs, kept_far, kept, sem = refs
+    count = kept.shape[0] // padded
+    grads, sent = refs[:count], refs[count:]
+    fill(kept, grads, capacity, padded)
+    put_away = pltpu.make_async_copy(kept, kept_far, sem)
+    put_away.start()
     rows = jnp.concatenate([block[...] for block in arrived], axis=0)
     by_slot = dot(pick[...], rows).astype(bf16)
-    for step in range(exp_count):
+    for step in range(len(sent)):
         sent[step][...] = by_slot[step * padded : step * padded + capacity]
-    for copy in put_away:
-        copy.wait()
+    put_away.wait()
 
 
 def pick_last_kernel(capacity, padded, chips, pick, *refs):
@@ -276,11 +272,13 @@
 
 def early_kernel(capacity, padded, steps, pre_first, adapted_first, gate, down, up, *refs):
     blocks, refs = refs[:steps], refs[steps:]
-    grads, refs = refs[:steps], refs[steps:]
+    kept, grads, refs = refs[0], refs[1:steps], refs[steps:]
     activated, refs = refs[:steps], refs[steps:]
     turned, adapted, grad_pre, back, tile, grad_tile = refs
     fill(tile, blocks, capacity, padded)
-    fill(grad_tile, grads, capacity, padded)
+    grad_tile[:padded] = kept[kept.shape[0] - padded :]
+    if grads:
+        fill(grad_tile.at[padded:], grads, capacity, padded)
     count = tile.shape[0]
     rows, adapted[...], grad_pre[...], back[...] = forward(
         tile[...], pre_first[:count], adapted_first[:count], grad_tile[...], gate, down, up
@@ -307,14 +305,13 @@
     *refs,
 ):
     blocks, refs = refs[:steps], refs[steps:]
-    grads, refs = refs[:steps], refs[steps:]
+    kept, refs = refs[0], refs[1:]
     activated, refs = refs[:steps], refs[steps:]
-    keep, give, tile, grad_tile, down_term, up_term = refs
+    keep, give, tile, down_term, up_term = refs
     fill(tile, blocks, capacity, padded)
-    fill(grad_tile, grads, capacity, padded)
     count = pre_first.shape[0] - tile.shape[0]
     rows, adapted, grad_pre, back = forward(
-        tile[...], pre_first[count:], adapted_first[count:], grad_tile[...], gate, down, up
+        tile[...], pre_first[count:], adapted_first[count:], kept[: tile.shape[0]], gate, down, up
     )
     for step in range(steps):
         activated[step][...] = rows[step * padded : step * padded + capacity]
@@ -446,15 +443,14 @@
     blocks = pl.pallas_call(
         functools.partial(pick_first_kernel, capacity, padded, pairs),
         out_shape=[shape((capacity, first_width), bf16)] * exp_count
-        + [pltpu.HBM((capacity, hidden_units), bf16)] * len(kept),
+        + [pltpu.HBM((len(kept) * padded, hidden_units), bf16)],
         in_specs=[near] * (1 + pairs + len(kept)),
-        out_specs=[near] * exp_count + [far] * len(kept),
-        scratch_shapes=[pltpu.SemaphoreType.DMA((len(kept),))],
+        out_specs=[near] * exp_count + [far],
+        scratch_shapes=[pltpu.VMEM((len(kept) * padded, hidden_units), bf16), pltpu.SemaphoreType.DMA],
         compiler_params=pltpu.CompilerParams(vmem_limit_bytes=16 * 1024 * 1024),
         name="pick_first",
     )(pick, *arrived, *kept)
-    sent, kept = blocks[:exp_count], blocks[exp_count:]
-    grads = [kept[half], *grads[1:half], *kept[:half]]
+    *sent, kept = blocks
 
     joined = lax.optimization_barrier((*served_last, *sent))
     served, sent = joined[:pairs], joined[pairs:]
@@ -503,7 +499,7 @@
             shape((count, hidden_units), bf16),
             shape((count, rank_width), bf16),
         ],
-        [pre_first, adapted_first, *weights, *last_blocks[:steps], *grads[:steps]],
+        [pre_first, adapted_first, *weights, *last_blocks[:steps], kept, *grads[1:steps]],
         resident=weights,
         scratch=[pltpu.VMEM((count, last_width), bf16), pltpu.VMEM((count, hidden_units), bf16)],
         flops=2 * count * last_width * (hidden_units + rank_width),
@@ -524,12 +520,11 @@
             adapted_first,
             *weights,
             *last_blocks[steps:],
-            *grads[steps:],
+            kept,
         ],
         resident=weights,
         scratch=[
             pltpu.VMEM((count, last_width), bf16),
-            pltpu.VMEM((count, hidden_units), bf16),
             pltpu.VMEM((model_width, rank_width), f32),
             pltpu.VMEM((rep_count, rank_width // rep_count, hidden_units), f32),
         ],

time: 77.8 us -> 78.2 us (level)
  transfers between devices with their start and end apart: 24 -> 24, of which waited for: 8 -> 8; matrix products, arithmetic and copies ran while one was open for 0% -> 0% of each run, Pallas kernels for 15% -> 14%
where the time goes in v8:
time: 78.2 us; the launch traced here: 78 us
  starting transfers between devices  32.7 us (42%)
  waiting for transfers between devices  28.4 us (36%)
  Pallas kernels  15.8 us (20%)
    ppermute x12, starting transfers between devices, swap_exp(): return lax.ppermute(block, 'exp', [(i, i ^ step) for i in range(exp_count)])  20.4 us
    ppermute x12, waiting for transfers between devices, swap_exp(): return lax.ppermute(block, 'exp', [(i, i ^ step) for i in range(exp_count)])  19.7 us
    ppermute x9, starting transfers between devices, swap_chip(): lax.ppermute(block, 'rep', [(i, i ^ 2 * step) for i in range(rep_count)])  11.6 us
    pallas_call x8, Pallas kernels, call(): pl.pallas_call(moving, out_shape=[pltpu.HBM(out.shape, out.dtype) if numb...  9.14 us
    ppermute x9, waiting for transfers between devices, swap_chip(): lax.ppermute(block, 'rep', [(i, i ^ 2 * step) for i in range(rep_count)])  8.63 us
    pallas_call x1, Pallas kernels, body(): pl.pallas_call(fetch_kernel, out_shape=[pltpu.VMEM(array.shape, array.dty...  3.32 us
    pallas_call x1, Pallas kernels, body(): pl.pallas_call(functools.partial(begin_kernel, capacity, padded), out_sha...  2.18 us
  transfers between devices with their start and end apart: 24, of which 8 were waited for; matrix products, arithmetic and copies ran while one was open for 0% of the time, Pallas kernels for 14%

profile of v8, /device:TPU:0, one launch (start us, length us, event | category | flops | bytes accessed | tf_op | source)
XLA Modules:
  0.0 78.0 jit_solution(12812504142986090082)
XLA Ops:
  0.6 0.5 collective-permute-start.1
  1.1 0.1 collective-permute-start
  1.2 2.2 %begin.1 = (bf16[4,32,2176]{2,1,0:T(8,128)(2,1)S(1)}, bf16[56,1024]{1,0:T(8,128)(2,1)S(1)}, bf16[56,1024]{1,0:T(8,128)(2,1)S(1)}, bf16[56,1024]{1,0:T(8,128)(2,1)S(1)}, bf16[56,1024]{1,0:T(8,128)(2,1)S(1)}) custom-call(s32[1,8,32]{2,1,0:T(8,128)} %refs_0_.3, bf16[128,3584]{1,0:T(8,128)(2,1)} %refs_1_.1, s32[1,128]{1,0:T(1,128)} %bitcast.12, ...), custom_call_target="tpu_custom_call" | custom-call | tf_op jit(solution)/shard_map/begin/pallas_call | solution.py:395
  3.4 0.0 collective-permute-done.refs_0_.refs_2_
  3.5 0.0 collective-permute-done.1.refs_1_.refs_3_
  3.5 0.4 serve_first.1
  3.9 3.0 %collective-permute-start.2 = (bf16[64,2176]{1,0:T(8,128)(2,1)S(1)}, bf16[64,2176]{1,0:T(8,128)(2,1)S(1)}, u32[]{:S(2)}, u32[]{:S(2)}) collective-permute-start(bf16[64,2176]{1,0:T(8,128)(2,1)S(1)} %get-tuple-element.94), channel_id=1, source_target_pairs={{0,8},{4,12},{8,0},{12,4},{16,24},{20,28},{24,16},{28,20},{1,9},{5... | collective-permute-start | bytes 835592 | tf_op jit(solution)/shard_map/ppermute | solution.py:103
  6.9 1.5 %collective-permute-start.3 = (bf16[64,2176]{1,0:T(8,128)(2,1)S(1)}, bf16[64,2176]{1,0:T(8,128)(2,1)S(1)}, u32[]{:S(2)}, u32[]{:S(2)}) collective-permute-start(bf16[64,2176]{1,0:T(8,128)(2,1)S(1)} %get-tuple-element.95), channel_id=1, source_target_pairs={{0,16},{4,20},{8,24},{12,28},{16,0},{20,4},{24,8},{28,12},{1,17},{... | collective-permute-start | bytes 835592 | tf_op jit(solution)/shard_map/ppermute | solution.py:103
  8.4 0.0 collective-permute-start.4
  8.4 3.0 %collective-permute-start.5 = (bf16[56,1024]{1,0:T(8,128)(2,1)S(1)}, bf16[56,1024]{1,0:T(8,128)(2,1)S(1)}, u32[]{:S(2)}, u32[]{:S(2)}) collective-permute-start(bf16[56,1024]{1,0:T(8,128)(2,1)S(1)} %get-tuple-element.97), channel_id=1, source_target_pairs={{0,2},{1,3},{2,0},{3,1},{4,6},{5,7},{6,4},{7,5},{8,10},{9,11},{10,... | collective-permute-start | bytes 344072 | tf_op jit(solution)/shard_map/ppermute | solution.py:86
  11.4 1.3 %collective-permute-start.6 = (bf16[56,1024]{1,0:T(8,128)(2,1)S(1)}, bf16[56,1024]{1,0:T(8,128)(2,1)S(1)}, u32[]{:S(2)}, u32[]{:S(2)}) collective-permute-start(bf16[56,1024]{1,0:T(8,128)(2,1)S(1)} %get-tuple-element.98), channel_id=1, source_target_pairs={{0,3},{1,2},{2,1},{3,0},{4,7},{5,6},{6,5},{7,4},{8,11},{9,10},{10,... | collective-permute-start | bytes 344072 | tf_op jit(solution)/shard_map/ppermute | solution.py:86
  12.8 0.0 copy-done.6
  12.8 1.5 %prepare.1 = (bf16[256,256]{1,0:T(8,128)(2,1)S(1)}, bf16[128,256]{1,0:T(8,128)(2,1)}) custom-call(s32[1,8]{1,0:T(1,128)S(1)} %copy-done.6, s32[1,128]{1,0:T(1,128)S(1)} %bitcast.13), custom_call_target="tpu_custom_call" | custom-call | flops 16777216 | bytes 55924 | tf_op jit(solution)/shard_map/prepare/pallas_call | solution.py:64
  14.3 0.0 copy-done.3
  14.3 1.2 %serve_last.1 = (bf16[64,1408]{1,0:T(8,128)(2,1)S(1)}, bf16[64,1408]{1,0:T(8,128)(2,1)S(1)}, bf16[64,1408]{1,0:T(8,128)(2,1)S(1)}, bf16[64,1408]{1,0:T(8,128)(2,1)S(1)}) custom-call(s32[1,8,32]{2,1,0:T(8,128)} %refs_0_.3, bf16[128,3584]{1,0:T(8,128)(2,1)S(1)} %copy-done, s32[1,8,32]{2,1,0:T(8,128)} %copy-done.3, ...), custom_call_target="tpu_custom_call" | custom-call | flops 92274688 | bytes 307582 | tf_op jit(solution)/shard_map/serve_last/pallas_call | solution.py:64
  15.5 4.6 %collective-permute-done.5.refs_4_ = bf16[56,1024]{1,0:T(8,128)(2,1)S(1)} collective-permute-done((bf16[56,1024]{1,0:T(8,128)(2,1)S(1)}, bf16[56,1024]{1,0:T(8,128)(2,1)S(1)}, u32[]{:S(2)}, u32[]{:S(2)}) %collective-permute-start.5) | collective-permute-done | bytes 114720 | tf_op jit(solution)/shard_map/ppermute | solution.py:86
  20.1 0.0 collective-permute-done.6.refs_5_
  20.1 0.0 collective-permute-done.2.refs_1_
  20.1 1.1 %collective-permute-done.3.refs_2_ = bf16[64,2176]{1,0:T(8,128)(2,1)S(1)} collective-permute-done((bf16[64,2176]{1,0:T(8,128)(2,1)S(1)}, bf16[64,2176]{1,0:T(8,128)(2,1)S(1)}, u32[]{:S(2)}, u32[]{:S(2)}) %collective-permute-start.3) | collective-permute-done | bytes 278560 | tf_op jit(solution)/shard_map/ppermute | solution.py:103
  21.2 0.0 collective-permute-done.4.refs_3_
  21.2 1.2 %pick_first.1 = (bf16[56,2176]{1,0:T(8,128)(2,1)S(1)}, bf16[56,2176]{1,0:T(8,128)(2,1)S(1)}, bf16[56,2176]{1,0:T(8,128)(2,1)S(1)}, bf16[56,2176]{1,0:T(8,128)(2,1)S(1)}, bf16[192,1024]{1,0:T(8,128)(2,1)}) custom-call(bf16[256,256]{1,0:T(8,128)(2,1)S(1)} %get-tuple-element.87.pick.refs_0_, bf16[64,2176]{1,0:T(8,128)(2,1)S(1)} %get-tuple-element.93.refs_0_, ...), custom_call_target="tpu_custom_call" | custom-call | tf_op jit(solution)/shard_map/pick_first/pallas_call | solution.py:443
  22.4 1.3 %collective-permute-start.7 = (bf16[64,1408]{1,0:T(8,128)(2,1)S(1)}, bf16[64,1408]{1,0:T(8,128)(2,1)S(1)}, u32[]{:S(2)}, u32[]{:S(2)}) collective-permute-start(bf16[64,1408]{1,0:T(8,128)(2,1)S(1)} %get-tuple-element.105), channel_id=1, source_target_pairs={{0,8},{4,12},{8,0},{12,4},{16,24},{20,28},{24,16},{28,20},{1,9},{5... | collective-permute-start | bytes 540680 | tf_op jit(solution)/shard_map/ppermute | solution.py:103
  23.7 3.1 %collective-permute-start.10 = (bf16[56,2176]{1,0:T(8,128)(2,1)S(1)}, bf16[56,2176]{1,0:T(8,128)(2,1)S(1)}, u32[]{:S(2)}, u32[]{:S(2)}) collective-permute-start(bf16[56,2176]{1,0:T(8,128)(2,1)S(1)} %get-tuple-element.114), channel_id=1, source_target_pairs={{0,2},{1,3},{2,0},{3,1},{4,6},{5,7},{6,4},{7,5},{8,10},{9,11},{10,... | collective-permute-start | bytes 731144 | tf_op jit(solution)/shard_map/ppermute | solution.py:86
  26.8 0.8 %collective-permute-start.11 = (bf16[56,2176]{1,0:T(8,128)(2,1)S(1)}, bf16[56,2176]{1,0:T(8,128)(2,1)S(1)}, u32[]{:S(2)}, u32[]{:S(2)}) collective-permute-start(bf16[56,2176]{1,0:T(8,128)(2,1)S(1)} %get-tuple-element.115), channel_id=1, source_target_pairs={{0,3},{1,2},{2,1},{3,0},{4,7},{5,6},{6,5},{7,4},{8,11},{9,10},{10,... | collective-permute-start | bytes 731144 | tf_op jit(solution)/shard_map/ppermute | solution.py:86
  27.6 0.2 collective-permute-start.12
  27.9 1.0 %collective-permute-start.8 = (bf16[64,1408]{1,0:T(8,128)(2,1)S(1)}, bf16[64,1408]{1,0:T(8,128)(2,1)S(1)}, u32[]{:S(2)}, u32[]{:S(2)}) collective-permute-start(bf16[64,1408]{1,0:T(8,128)(2,1)S(1)} %get-tuple-element.106), channel_id=1, source_target_pairs={{0,16},{4,20},{8,24},{12,28},{16,0},{20,4},{24,8},{28,12},{1,17},{... | collective-permute-start | bytes 540680 | tf_op jit(solution)/shard_map/ppermute | solution.py:103
  28.9 0.0 collective-permute-done.7.refs_2_
  28.9 1.2 %collective-permute-start.9 = (bf16[64,1408]{1,0:T(8,128)(2,1)S(1)}, bf16[64,1408]{1,0:T(8,128)(2,1)S(1)}, u32[]{:S(2)}, u32[]{:S(2)}) collective-permute-start(bf16[64,1408]{1,0:T(8,128)(2,1)S(1)} %get-tuple-element.107), channel_id=1, source_target_pairs={{0,24},{4,28},{8,16},{12,20},{16,8},{20,12},{24,0},{28,4},{1,25},{... | collective-permute-start | bytes 540680 | tf_op jit(solution)/shard_map/ppermute | solution.py:103
  30.1 6.9 %collective-permute-done.8.refs_3_ = bf16[64,1408]{1,0:T(8,128)(2,1)S(1)} collective-permute-done((bf16[64,1408]{1,0:T(8,128)(2,1)S(1)}, bf16[64,1408]{1,0:T(8,128)(2,1)S(1)}, u32[]{:S(2)}, u32[]{:S(2)}) %collective-permute-start.8) | collective-permute-done | bytes 180256 | tf_op jit(solution)/shard_map/ppermute | solution.py:103
  37.0 0.0 collective-permute-done.9.refs_4_
  37.1 0.4 pick_last.1
  37.4 1.7 %collective-permute-start.13 = (bf16[56,1408]{1,0:T(8,128)(2,1)S(1)}, bf16[56,1408]{1,0:T(8,128)(2,1)S(1)}, u32[]{:S(2)}, u32[]{:S(2)}) collective-permute-start(bf16[56,1408]{1,0:T(8,128)(2,1)S(1)} %get-tuple-element.122), channel_id=1, source_target_pairs={{0,1},{1,0},{2,3},{3,2},{4,5},{5,4},{6,7},{7,6},{8,9},{9,8},{10,11... | collective-permute-start | bytes 473096 | tf_op jit(solution)/shard_map/ppermute | solution.py:86
  39.1 0.4 collective-permute-start.14
  39.5 3.3 %fetch.1 = (bf16[1,3584,1024]{2,1,0:T(8,128)(2,1)S(1)}, bf16[1,3584,128]{2,1,0:T(8,128)(2,1)S(1)}, bf16[1,128,1024]{2,1,0:T(8,128)(2,1)S(1)}) custom-call(bf16[1,3584,1024]{2,1,0:T(8,128)(2,1)} %refs_0_.4, bf16[1,3584,128]{2,1,0:T(8,128)(2,1)} %refs_1_.2, bf16[1,128,1024]{2,1,0:T(8,128)(2,1)} %refs_2_), custom_call_target="tpu_custom_call" | custom-call | tf_op jit(solution)/shard_map/fetch/pallas_call | solution.py:468
  42.9 0.5 collective-permute-done.10.refs_2_
  43.3 3.1 %collective-permute-start.16 = (bf16[56,1408]{1,0:T(8,128)(2,1)S(1)}, bf16[56,1408]{1,0:T(8,128)(2,1)S(1)}, u32[]{:S(2)}, u32[]{:S(2)}) collective-permute-start(bf16[56,1408]{1,0:T(8,128)(2,1)S(1)} %get-tuple-element.132), channel_id=1, source_target_pairs={{0,2},{1,3},{2,0},{3,1},{4,6},{5,7},{6,4},{7,5},{8,10},{9,11},{10,... | collective-permute-start | bytes 473096 | tf_op jit(solution)/shard_map/ppermute | solution.py:86
  46.4 0.0 collective-permute-done.11.refs_3_
  46.4 0.5 collective-permute-start.17
  46.9 0.0 collective-permute-done.12.refs_5_
  46.9 1.7 %partial.1 = (bf16[2176,256]{1,0:T(8,128)(2,1)S(1)}, f32[256,1024]{1,0:T(8,128)S(1)}, f32[256,128]{1,0:T(8,128)S(1)}) custom-call(bf16[1,3584,1024]{2,1,0:T(8,128)(2,1)S(1)} %get-tuple-element.112.refs_0_.refs_2_.refs_7_, bf16[1,3584,128]{2,1,0:T(8,128)(2,1)S(1)} %get-tuple-element.113.refs_1_.refs_3_.refs_8_, ...), custom_call_target="tpu_custom_call" | custom-call | flops 1283457024 | bytes 4278190 | tf_op jit(solution)/shard_map/partial/pallas_call | solution.py:64
  48.6 2.7 %collective-permute-done.14.refs_8_ = bf16[56,1024]{1,0:T(8,128)(2,1)S(1)} collective-permute-done((bf16[56,1024]{1,0:T(8,128)(2,1)S(1)}, bf16[56,1024]{1,0:T(8,128)(2,1)S(1)}, u32[]{:S(2)}, u32[]{:S(2)}) %collective-permute-start.14) | collective-permute-done | bytes 114720 | tf_op jit(solution)/shard_map/ppermute | solution.py:86
  51.4 0.0 collective-permute-done.13.refs_6_
  51.4 1.0 %early.1 = (bf16[56,1024]{1,0:T(8,128)(2,1)S(1)}, bf16[56,1024]{1,0:T(8,128)(2,1)S(1)}, bf16[1408,128]{1,0:T(8,128)(2,1)S(1)}, bf16[128,128]{1,0:T(8,128)(2,1)S(...) custom-call(f32[256,1024]{1,0:T(8,128)S(1)} %get-tuple-element.118.refs_0_.refs_5_, ...), custom_call_target="tpu_custom_call" | custom-call | flops 415236096 | bytes 1384120 | tf_op jit(solution)/shard_map/early/pallas_call | solution.py:64
  52.4 6.3 %collective-permute-done.16.refs_10_ = bf16[56,1408]{1,0:T(8,128)(2,1)S(1)} collective-permute-done((bf16[56,1408]{1,0:T(8,128)(2,1)S(1)}, bf16[56,1408]{1,0:T(8,128)(2,1)S(1)}, u32[]{:S(2)}, u32[]{:S(2)}) %collective-permute-start.16) | collective-permute-done | bytes 157728 | tf_op jit(solution)/shard_map/ppermute | solution.py:86
  58.7 0.0 collective-permute-done.17.refs_11_
  58.7 1.9 %late.1 = (bf16[56,1024]{1,0:T(8,128)(2,1)S(1)}, bf16[56,1024]{1,0:T(8,128)(2,1)S(1)}, f32[4,576,128]{2,1,0:T(8,128)S(1)}, bf16[4,576,128]{2,1,0:T(8,128)(2,1)S(1)}) custom-call(bf16[2176,256]{1,0:T(8,128)(2,1)S(1)} %get-tuple-element.127.refs_0_, bf16[1408,128]{1,0:T(8,128)(2,1)S(1)} %get-tuple-element.128.refs_1_, ...), custom_call_target="tpu_custom_call" | custom-call | flops 884998144 | bytes 2949993 | tf_op jit(solution)/shard_map/late/pallas_call | solution.py:64
  60.6 0.1 collective-permute-start.20
  60.7 3.7 %collective-permute-start.15 = (bf16[56,1024]{1,0:T(8,128)(2,1)S(1)}, bf16[56,1024]{1,0:T(8,128)(2,1)S(1)}, u32[]{:S(2)}, u32[]{:S(2)}) collective-permute-start(bf16[56,1024]{1,0:T(8,128)(2,1)S(1)} %get-tuple-element.126), channel_id=1, source_target_pairs={{0,1},{1,0},{2,3},{3,2},{4,5},{5,4},{6,7},{7,6},{8,9},{9,8},{10,11... | collective-permute-start | bytes 344072 | tf_op jit(solution)/shard_map/ppermute | solution.py:86
  64.5 1.0 %collective-permute-start.18 = (bf16[56,1024]{1,0:T(8,128)(2,1)S(1)}, bf16[56,1024]{1,0:T(8,128)(2,1)S(1)}, u32[]{:S(2)}, u32[]{:S(2)}) collective-permute-start(bf16[56,1024]{1,0:T(8,128)(2,1)S(1)} %get-tuple-element.134), channel_id=1, source_target_pairs={{0,2},{1,3},{2,0},{3,1},{4,6},{5,7},{6,4},{7,5},{8,10},{9,11},{10,... | collective-permute-start | bytes 344072 | tf_op jit(solution)/shard_map/ppermute | solution.py:86
  65.5 1.4 %collective-permute-start.19 = (bf16[56,1024]{1,0:T(8,128)(2,1)S(1)}, bf16[56,1024]{1,0:T(8,128)(2,1)S(1)}, u32[]{:S(2)}, u32[]{:S(2)}) collective-permute-start(bf16[56,1024]{1,0:T(8,128)(2,1)S(1)} %get-tuple-element.135), channel_id=1, source_target_pairs={{0,3},{1,2},{2,1},{3,0},{4,7},{5,6},{6,5},{7,4},{8,11},{9,10},{10,... | collective-permute-start | bytes 344072 | tf_op jit(solution)/shard_map/ppermute | solution.py:86
  66.9 0.0 collective-permute-done.20
  66.9 0.2 fusion
  67.1 0.0 copy-start.2
  67.1 0.0 copy-start.4
  67.2 1.6 %collective-permute-start.21 = (bf16[576,128]{1,0:T(8,128)(2,1)S(1)}, bf16[576,128]{1,0:T(8,128)(2,1)S(1)}, u32[]{:S(2)}, u32[]{:S(2)}) collective-permute-start(bf16[576,128]{1,0:T(8,128)(2,1)S(1)} %get-tuple-element.145), channel_id=1, source_target_pairs={{0,24},{4,28},{8,16},{12,20},{16,8},{20,12},{24,0},{28,4},{1,25},{... | collective-permute-start | bytes 442376 | tf_op jit(solution)/shard_map/ppermute | solution.py:103
  68.7 0.5 collective-permute-start.22
  69.2 0.0 collective-permute-done.15.refs_3_
  69.2 1.5 %collective-permute-start.23 = (bf16[576,128]{1,0:T(8,128)(2,1)S(1)}, bf16[576,128]{1,0:T(8,128)(2,1)S(1)}, u32[]{:S(2)}, u32[]{:S(2)}) collective-permute-start(bf16[576,128]{1,0:T(8,128)(2,1)S(1)} %get-tuple-element.143), channel_id=1, source_target_pairs={{0,8},{4,12},{8,0},{12,4},{16,24},{20,28},{24,16},{28,20},{1,9},{5... | collective-permute-start | bytes 442376 | tf_op jit(solution)/shard_map/ppermute | solution.py:103
  70.7 5.6 %collective-permute-done.18.refs_4_ = bf16[56,1024]{1,0:T(8,128)(2,1)S(1)} collective-permute-done((bf16[56,1024]{1,0:T(8,128)(2,1)S(1)}, bf16[56,1024]{1,0:T(8,128)(2,1)S(1)}, u32[]{:S(2)}, u32[]{:S(2)}) %collective-permute-start.18) | collective-permute-done | bytes 114720 | tf_op jit(solution)/shard_map/ppermute | solution.py:86
  76.3 0.0 collective-permute-done.19.refs_5_
  76.3 0.0 collective-permute-done.21.refs_7_
  76.3 0.6 collective-permute-done.22.refs_8_
  76.9 0.0 collective-permute-done.23.refs_9_
  76.9 1.0 %end.1 = (f32[1,448,128]{2,1,0:T(8,128)}, f32[1,16,1024]{2,1,0:T(8,128)}, bf16[128,1024]{1,0:T(8,128)(2,1)}) custom-call(bf16[128,256]{1,0:T(8,128)(2,1)S(1)} %copy-done.2, f32[1,128]{1,0:T(1,128)S(1)} %bitcast.11, bf16[56,1024]{1,0:T(8,128)(2,1)S(1)} %get-tuple-element.125.refs_2_, bf16[56,1024]{1,0:T(8,128)(2,1)S(1)} %collective-permute-done.15.refs_3_, ...), custom_call_target="tpu_custom_call" | custom-call | flops 67108864 | bytes 223696 | tf_op jit(solution)/shard_map/end/pallas_call | solution.py:64
  (12 shorter events, 0.1 us)
Async XLA Ops:
  0.6 2.8 %collective-permute-start.1 = (bf16[128,3584]{1,0:T(8,128)(2,1)}, bf16[128,3584]{1,0:T(8,128)(2,1)S(1)}, u32[]{:S(2)}, u32[]{:S(2)}) collective-permute-start(bf16[128,3584]{1,0:T(8,128)(2,1)} %refs_1_.1), channel_id=1, source_target_pairs={{0,4},{4,0},{8,12},{12,8},{16,20},{20,16},{24,28},{28,24},{1,5},{5... | collective-permute-start | bytes 2752520 | tf_op jit(solution)/shard_map/ppermute | solution.py:97
  1.1 2.3 %collective-permute-start = (s32[1,8,32]{2,1,0:T(8,128)}, s32[1,8,32]{2,1,0:T(8,128)S(1)}, u32[]{:S(2)}, u32[]{:S(2)}) collective-permute-start(s32[1,8,32]{2,1,0:T(8,128)} %refs_0_.3), channel_id=1, source_target_pairs={{0,4},{4,0},{8,12},{12,8},{16,20},{20,16},{24,28},{28,24},{1,5},{5... | collective-permute-start | bytes 3080 | tf_op jit(solution)/shard_map/ppermute | solution.py:97
  1.2 11.6 %copy-start.5 = (s32[128,1]{0,1:T(1,128)S(1)}, s32[128,1]{0,1:T(1,128)}, u32[]{:S(2)}) copy-start(s32[128,1]{0,1:T(1,128)} %param.12) | copy-start | bytes 1540
  1.2 11.6 %copy-start.6 = (s32[1,8]{1,0:T(1,128)S(1)}, s32[1,8]{1,0:T(1,128)}, u32[]{:S(2)}) copy-start(s32[1,8]{1,0:T(1,128)} %refs_0_.2) | copy-start | bytes 100
  1.2 13.1 %copy-start = (bf16[128,3584]{1,0:T(8,128)(2,1)S(1)}, bf16[128,3584]{1,0:T(8,128)(2,1)}, u32[]{:S(2)}) copy-start(bf16[128,3584]{1,0:T(8,128)(2,1)} %refs_1_.1) | copy-start | bytes 2752516
  3.5 10.8 %copy-start.3 = (s32[1,8,32]{2,1,0:T(8,128)}, s32[1,8,32]{2,1,0:T(8,128)S(1)}, u32[]{:S(2)}) copy-start(s32[1,8,32]{2,1,0:T(8,128)S(1)} %collective-permute-done.refs_0_.refs_2_) | copy-start | bytes 3076
  3.9 16.3 %collective-permute-start.2 = (bf16[64,2176]{1,0:T(8,128)(2,1)S(1)}, bf16[64,2176]{1,0:T(8,128)(2,1)S(1)}, u32[]{:S(2)}, u32[]{:S(2)}) collective-permute-start(bf16[64,2176]{1,0:T(8,128)(2,1)S(1)} %get-tuple-element.94), channel_id=1, source_target_pairs={{0,8},{4,12},{8,0},{12,4},{16,24},{20,28},{24,16},{28,20},{1,9},{5... | collective-permute-start | bytes 835592 | tf_op jit(solution)/shard_map/ppermute | solution.py:103
  6.9 14.3 %collective-permute-start.3 = (bf16[64,2176]{1,0:T(8,128)(2,1)S(1)}, bf16[64,2176]{1,0:T(8,128)(2,1)S(1)}, u32[]{:S(2)}, u32[]{:S(2)}) collective-permute-start(bf16[64,2176]{1,0:T(8,128)(2,1)S(1)} %get-tuple-element.95), channel_id=1, source_target_pairs={{0,16},{4,20},{8,24},{12,28},{16,0},{20,4},{24,8},{28,12},{1,17},{... | collective-permute-start | bytes 835592 | tf_op jit(solution)/shard_map/ppermute | solution.py:103
  8.4 12.8 %collective-permute-start.4 = (bf16[64,2176]{1,0:T(8,128)(2,1)S(1)}, bf16[64,2176]{1,0:T(8,128)(2,1)S(1)}, u32[]{:S(2)}, u32[]{:S(2)}) collective-permute-start(bf16[64,2176]{1,0:T(8,128)(2,1)S(1)} %get-tuple-element.96), channel_id=1, source_target_pairs={{0,24},{4,28},{8,16},{12,20},{16,8},{20,12},{24,0},{28,4},{1,25},{... | collective-permute-start | bytes 835592 | tf_op jit(solution)/shard_map/ppermute | solution.py:103
  8.4 11.7 %collective-permute-start.5 = (bf16[56,1024]{1,0:T(8,128)(2,1)S(1)}, bf16[56,1024]{1,0:T(8,128)(2,1)S(1)}, u32[]{:S(2)}, u32[]{:S(2)}) collective-permute-start(bf16[56,1024]{1,0:T(8,128)(2,1)S(1)} %get-tuple-element.97), channel_id=1, source_target_pairs={{0,2},{1,3},{2,0},{3,1},{4,6},{5,7},{6,4},{7,5},{8,10},{9,11},{10,... | collective-permute-start | bytes 344072 | tf_op jit(solution)/shard_map/ppermute | solution.py:86
  11.4 8.7 %collective-permute-start.6 = (bf16[56,1024]{1,0:T(8,128)(2,1)S(1)}, bf16[56,1024]{1,0:T(8,128)(2,1)S(1)}, u32[]{:S(2)}, u32[]{:S(2)}) collective-permute-start(bf16[56,1024]{1,0:T(8,128)(2,1)S(1)} %get-tuple-element.98), channel_id=1, source_target_pairs={{0,3},{1,2},{2,1},{3,0},{4,7},{5,6},{6,5},{7,4},{8,11},{9,10},{10,... | collective-permute-start | bytes 344072 | tf_op jit(solution)/shard_map/ppermute | solution.py:86
  22.4 6.5 %collective-permute-start.7 = (bf16[64,1408]{1,0:T(8,128)(2,1)S(1)}, bf16[64,1408]{1,0:T(8,128)(2,1)S(1)}, u32[]{:S(2)}, u32[]{:S(2)}) collective-permute-start(bf16[64,1408]{1,0:T(8,128)(2,1)S(1)} %get-tuple-element.105), channel_id=1, source_target_pairs={{0,8},{4,12},{8,0},{12,4},{16,24},{20,28},{24,16},{28,20},{1,9},{5... | collective-permute-start | bytes 540680 | tf_op jit(solution)/shard_map/ppermute | solution.py:103
  23.7 19.7 %collective-permute-start.10 = (bf16[56,2176]{1,0:T(8,128)(2,1)S(1)}, bf16[56,2176]{1,0:T(8,128)(2,1)S(1)}, u32[]{:S(2)}, u32[]{:S(2)}) collective-permute-start(bf16[56,2176]{1,0:T(8,128)(2,1)S(1)} %get-tuple-element.114), channel_id=1, source_target_pairs={{0,2},{1,3},{2,0},{3,1},{4,6},{5,7},{6,4},{7,5},{8,10},{9,11},{10,... | collective-permute-start | bytes 731144 | tf_op jit(solution)/shard_map/ppermute | solution.py:86
  26.8 19.6 %collective-permute-start.11 = (bf16[56,2176]{1,0:T(8,128)(2,1)S(1)}, bf16[56,2176]{1,0:T(8,128)(2,1)S(1)}, u32[]{:S(2)}, u32[]{:S(2)}) collective-permute-start(bf16[56,2176]{1,0:T(8,128)(2,1)S(1)} %get-tuple-element.115), channel_id=1, source_target_pairs={{0,3},{1,2},{2,1},{3,0},{4,7},{5,6},{6,5},{7,4},{8,11},{9,10},{10,... | collective-permute-start | bytes 731144 | tf_op jit(solution)/shard_map/ppermute | solution.py:86
  27.6 19.3 %collective-permute-start.12 = (bf16[56,2176]{1,0:T(8,128)(2,1)S(1)}, bf16[56,2176]{1,0:T(8,128)(2,1)S(1)}, u32[]{:S(2)}, u32[]{:S(2)}) collective-permute-start(bf16[56,2176]{1,0:T(8,128)(2,1)S(1)} %get-tuple-element.117), channel_id=1, source_target_pairs={{0,1},{1,0},{2,3},{3,2},{4,5},{5,4},{6,7},{7,6},{8,9},{9,8},{10,11... | collective-permute-start | bytes 731144 | tf_op jit(solution)/shard_map/ppermute | solution.py:86
  27.9 9.2 %collective-permute-start.8 = (bf16[64,1408]{1,0:T(8,128)(2,1)S(1)}, bf16[64,1408]{1,0:T(8,128)(2,1)S(1)}, u32[]{:S(2)}, u32[]{:S(2)}) collective-permute-start(bf16[64,1408]{1,0:T(8,128)(2,1)S(1)} %get-tuple-element.106), channel_id=1, source_target_pairs={{0,16},{4,20},{8,24},{12,28},{16,0},{20,4},{24,8},{28,12},{1,17},{... | collective-permute-start | bytes 540680 | tf_op jit(solution)/shard_map/ppermute | solution.py:103
  28.9 8.2 %collective-permute-start.9 = (bf16[64,1408]{1,0:T(8,128)(2,1)S(1)}, bf16[64,1408]{1,0:T(8,128)(2,1)S(1)}, u32[]{:S(2)}, u32[]{:S(2)}) collective-permute-start(bf16[64,1408]{1,0:T(8,128)(2,1)S(1)} %get-tuple-element.107), channel_id=1, source_target_pairs={{0,24},{4,28},{8,16},{12,20},{16,8},{20,12},{24,0},{28,4},{1,25},{... | collective-permute-start | bytes 540680 | tf_op jit(solution)/shard_map/ppermute | solution.py:103
  37.4 13.9 %collective-permute-start.13 = (bf16[56,1408]{1,0:T(8,128)(2,1)S(1)}, bf16[56,1408]{1,0:T(8,128)(2,1)S(1)}, u32[]{:S(2)}, u32[]{:S(2)}) collective-permute-start(bf16[56,1408]{1,0:T(8,128)(2,1)S(1)} %get-tuple-element.122), channel_id=1, source_target_pairs={{0,1},{1,0},{2,3},{3,2},{4,5},{5,4},{6,7},{7,6},{8,9},{9,8},{10,11... | collective-permute-start | bytes 473096 | tf_op jit(solution)/shard_map/ppermute | solution.py:86
  39.1 12.2 %collective-permute-start.14 = (bf16[56,1024]{1,0:T(8,128)(2,1)S(1)}, bf16[56,1024]{1,0:T(8,128)(2,1)S(1)}, u32[]{:S(2)}, u32[]{:S(2)}) collective-permute-start(bf16[56,1024]{1,0:T(8,128)(2,1)S(1)} %get-tuple-element.124), channel_id=1, source_target_pairs={{0,1},{1,0},{2,3},{3,2},{4,5},{5,4},{6,7},{7,6},{8,9},{9,8},{10,11... | collective-permute-start | bytes 344072 | tf_op jit(solution)/shard_map/ppermute | solution.py:86
  43.3 15.4 %collective-permute-start.16 = (bf16[56,1408]{1,0:T(8,128)(2,1)S(1)}, bf16[56,1408]{1,0:T(8,128)(2,1)S(1)}, u32[]{:S(2)}, u32[]{:S(2)}) collective-permute-start(bf16[56,1408]{1,0:T(8,128)(2,1)S(1)} %get-tuple-element.132), channel_id=1, source_target_pairs={{0,2},{1,3},{2,0},{3,1},{4,6},{5,7},{6,4},{7,5},{8,10},{9,11},{10,... | collective-permute-start | bytes 473096 | tf_op jit(solution)/shard_map/ppermute | solution.py:86
  46.4 12.3 %collective-permute-start.17 = (bf16[56,1408]{1,0:T(8,128)(2,1)S(1)}, bf16[56,1408]{1,0:T(8,128)(2,1)S(1)}, u32[]{:S(2)}, u32[]{:S(2)}) collective-permute-start(bf16[56,1408]{1,0:T(8,128)(2,1)S(1)} %get-tuple-element.133), channel_id=1, source_target_pairs={{0,3},{1,2},{2,1},{3,0},{4,7},{5,6},{6,5},{7,4},{8,11},{9,10},{10,... | collective-permute-start | bytes 473096 | tf_op jit(solution)/shard_map/ppermute | solution.py:86
  46.9 4.4 %copy-start.1 = (bf16[192,1024]{1,0:T(8,128)(2,1)S(1)}, bf16[192,1024]{1,0:T(8,128)(2,1)}, u32[]{:S(2)}) copy-start(bf16[192,1024]{1,0:T(8,128)(2,1)} %get-tuple-element.123.refs_7_.refs_12_) | copy-start | bytes 1179652
  60.6 6.3 %collective-permute-start.20 = (bf16[4,576,128]{2,1,0:T(8,128)(2,1)S(1)}, bf16[4,576,128]{2,1,0:T(8,128)(2,1)S(1)}, u32[]{:S(2)}, u32[]{:S(2)}) collective-permute-start(bf16[4,576,128]{2,1,0:T(8,128)(2,1)S(1)} %get-tuple-element.137), channel_id=1, source_target_pairs={{0,4},{4,0},{8,12},{12,8},{16,20},{20,16},{24,28},{28,24},{1,5},{5... | collective-permute-start | bytes 1769480 | tf_op jit(solution)/shard_map/ppermute | solution.py:97
  60.7 8.5 %collective-permute-start.15 = (bf16[56,1024]{1,0:T(8,128)(2,1)S(1)}, bf16[56,1024]{1,0:T(8,128)(2,1)S(1)}, u32[]{:S(2)}, u32[]{:S(2)}) collective-permute-start(bf16[56,1024]{1,0:T(8,128)(2,1)S(1)} %get-tuple-element.126), channel_id=1, source_target_pairs={{0,1},{1,0},{2,3},{3,2},{4,5},{5,4},{6,7},{7,6},{8,9},{9,8},{10,11... | collective-permute-start | bytes 344072 | tf_op jit(solution)/shard_map/ppermute | solution.py:86
  64.5 11.8 %collective-permute-start.18 = (bf16[56,1024]{1,0:T(8,128)(2,1)S(1)}, bf16[56,1024]{1,0:T(8,128)(2,1)S(1)}, u32[]{:S(2)}, u32[]{:S(2)}) collective-permute-start(bf16[56,1024]{1,0:T(8,128)(2,1)S(1)} %get-tuple-element.134), channel_id=1, source_target_pairs={{0,2},{1,3},{2,0},{3,1},{4,6},{5,7},{6,4},{7,5},{8,10},{9,11},{10,... | collective-permute-start | bytes 344072 | tf_op jit(solution)/shard_map/ppermute | solution.py:86
  65.5 10.8 %collective-permute-start.19 = (bf16[56,1024]{1,0:T(8,128)(2,1)S(1)}, bf16[56,1024]{1,0:T(8,128)(2,1)S(1)}, u32[]{:S(2)}, u32[]{:S(2)}) collective-permute-start(bf16[56,1024]{1,0:T(8,128)(2,1)S(1)} %get-tuple-element.135), channel_id=1, source_target_pairs={{0,3},{1,2},{2,1},{3,0},{4,7},{5,6},{6,5},{7,4},{8,11},{9,10},{10,... | collective-permute-start | bytes 344072 | tf_op jit(solution)/shard_map/ppermute | solution.py:86
  67.1 9.8 %copy-start.2 = (bf16[128,256]{1,0:T(8,128)(2,1)S(1)}, bf16[128,256]{1,0:T(8,128)(2,1)}, u32[]{:S(2)}) copy-start(bf16[128,256]{1,0:T(8,128)(2,1)} %get-tuple-element.84.refs_0_) | copy-start | bytes 196612
  67.1 9.8 %copy-start.4 = (f32[128,1]{0,1:T(1,128)S(1)}, f32[128,1]{0,1:T(1,128)}, u32[]{:S(2)}) copy-start(f32[128,1]{0,1:T(1,128)} %param.13) | copy-start | bytes 1540
  67.2 9.1 %collective-permute-start.21 = (bf16[576,128]{1,0:T(8,128)(2,1)S(1)}, bf16[576,128]{1,0:T(8,128)(2,1)S(1)}, u32[]{:S(2)}, u32[]{:S(2)}) collective-permute-start(bf16[576,128]{1,0:T(8,128)(2,1)S(1)} %get-tuple-element.145), channel_id=1, source_target_pairs={{0,24},{4,28},{8,16},{12,20},{16,8},{20,12},{24,0},{28,4},{1,25},{... | collective-permute-start | bytes 442376 | tf_op jit(solution)/shard_map/ppermute | solution.py:103
  68.7 8.2 %collective-permute-start.22 = (bf16[576,128]{1,0:T(8,128)(2,1)S(1)}, bf16[576,128]{1,0:T(8,128)(2,1)S(1)}, u32[]{:S(2)}, u32[]{:S(2)}) collective-permute-start(bf16[576,128]{1,0:T(8,128)(2,1)S(1)} %get-tuple-element.144), channel_id=1, source_target_pairs={{0,16},{4,20},{8,24},{12,28},{16,0},{20,4},{24,8},{28,12},{1,17},{... | collective-permute-start | bytes 442376 | tf_op jit(solution)/shard_map/ppermute | solution.py:103
  69.2 7.7 %collective-permute-start.23 = (bf16[576,128]{1,0:T(8,128)(2,1)S(1)}, bf16[576,128]{1,0:T(8,128)(2,1)S(1)}, u32[]{:S(2)}, u32[]{:S(2)}) collective-permute-start(bf16[576,128]{1,0:T(8,128)(2,1)S(1)} %get-tuple-element.143), channel_id=1, source_target_pairs={{0,8},{4,12},{8,0},{12,4},{16,24},{20,28},{24,16},{28,20},{1,9},{5... | collective-permute-start | bytes 442376 | tf_op jit(solution)/shard_map/ppermute | solution.py:103

commit v9 on v7

--- a/solution.py
+++ b/solution.py
@@ -149,6 +149,11 @@
     return slice(chunk * width, (chunk + 1) * width)
 
 
+def asked_spots(table, count, asking):
+    asked = jnp.concatenate([table[0, pl.ds(replica, 1), :] for replica in asking], axis=1)
+    return one_hot(asked == lax.broadcasted_iota(i32, (count, asked.shape[1]), 0))
+
+
 def serve(table, rows, asking):
     fetch_slots = table.shape[2]
     asked = jnp.concatenate([table[0, pl.ds(replica, 1), :] for replica in asking], axis=1)
@@ -165,31 +170,31 @@
     served, *sent = refs[:-6]
     table, rows, routes, weight, grads, sems = refs[-6:]
     width = rows.shape[1]
-    fetches = [
-        pltpu.make_async_copy(far, near, sems.at[number])
-        for number, (far, near) in enumerate(
-            (
-                (routes_far, routes),
-                (weight_far, weight),
-                (grads_far, grads),
-                (table_far, table),
-                (rows_far.at[:, :width], rows),
-            )
-        )
-    ]
+    ends = (
+        (routes_far, routes),
+        (weight_far, weight),
+        (table_far, table),
+        (grads_far, grads),
+        (rows_far.at[:, :width], rows),
+    )
+    fetches = [pltpu.make_async_copy(far, near, sems.at[number]) for number, (far, near) in enumerate(ends)]
     for copy in fetches:
         copy.start()
-    for copy in fetches[:3]:
-        copy.wait()
+    fetches[0].wait()
     home = slot_spots(capacity, padded, len(sent), routes)
-    scaled = (upright(weight[...]) * grads[...].astype(f32)).astype(bf16)
-    by_slot = dot(home, scaled, ((0,), (0,))).astype(bf16)
+    fetches[1].wait()
+    scale = upright(weight[...])
+    fetches[2].wait()
+    asked = asked_spots(table, rows.shape[0], asking_chips(served.shape[0]))
+    fetches[3].wait()
+    by_slot = dot(home, (scale * grads[...].astype(f32)).astype(bf16), ((0,), (0,))).astype(bf16)
     for step in range(len(sent)):
         sent[step][...] = by_slot[step * padded : step * padded + capacity]
-    for copy in fetches[3:]:
-        copy.wait()
-    for step, found in enumerate(serve(table, rows[...], asking_chips(served.shape[0]))):
-        served[step] = found
+    fetches[4].wait()
+    found = dot(asked, rows[...], ((0,), (0,))).astype(bf16)
+    fetch_slots = served.shape[1]
+    for step in range(served.shape[0]):
+        served[step] = found[step * fetch_slots : (step + 1) * fetch_slots]
 
 
 def serve_first_kernel(table, rows, own, *served):
@@ -309,7 +314,7 @@
     blocks, refs = refs[:steps], refs[steps:]
     grads, refs = refs[:steps], refs[steps:]
     activated, refs = refs[:steps], refs[steps:]
-    keep, give, tile, grad_tile, down_term, up_term = refs
+    keep, give, tile, grad_tile, turned_last, down_term, up_term = refs
     fill(tile, blocks, capacity, padded)
     fill(grad_tile, grads, capacity, padded)
     count = pre_first.shape[0] - tile.shape[0]
@@ -319,8 +324,11 @@
     for step in range(steps):
         activated[step][...] = rows[step * padded : step * padded + capacity]
     width = turned_first.shape[0]
-    down_term[:width] = dot(turned_first[...], jnp.concatenate([back_early[...], back], axis=0))
-    down_term[width:] = dot(turned_early[...], back_early[...]) + dot(tile[...], back, ((0,), (0,)))
+    turned_last[:, :count] = turned_early[...]
+    turned_last[:, count:] = tile[...].T
+    back = jnp.concatenate([back_early[...], back], axis=0)
+    down_term[:width] = dot(turned_first[...], back)
+    down_term[width:] = dot(turned_last[...], back)
     owners, up_rows, hidden_units = up_term.shape
     part = dot(
         jnp.concatenate([adapted_early[...], adapted], axis=0),
@@ -530,6 +538,7 @@
         scratch=[
             pltpu.VMEM((count, last_width), bf16),
             pltpu.VMEM((count, hidden_units), bf16),
+            pltpu.VMEM((last_width, slots), bf16),
             pltpu.VMEM((model_width, rank_width), f32),
             pltpu.VMEM((rep_count, rank_width // rep_count, hidden_units), f32),
         ],

time: 77.8 us -> 77.8 us (level)
  transfers between devices with their start and end apart: 24 -> 24, of which waited for: 8 -> 9; matrix products, arithmetic and copies ran while one was open for 0% -> 0% of each run, Pallas kernels for 15% -> 14%
where the time goes in v9:
time: 77.8 us; the launch traced here: 77.6 us
  starting transfers between devices  32.7 us (42%)
  waiting for transfers between devices  28.7 us (37%)
  Pallas kernels  15.2 us (20%)
  between operations  0.8 us (1%)
    ppermute x12, starting transfers between devices, swap_exp(): return lax.ppermute(block, 'exp', [(i, i ^ step) for i in range(exp_count)])  20.4 us
    ppermute x12, waiting for transfers between devices, swap_exp(): return lax.ppermute(block, 'exp', [(i, i ^ step) for i in range(exp_count)])  19.7 us
    ppermute x9, starting transfers between devices, swap_chip(): lax.ppermute(block, 'rep', [(i, i ^ 2 * step) for i in range(rep_count)])  11.6 us
    pallas_call x8, Pallas kernels, call(): pl.pallas_call(moving, out_shape=[pltpu.HBM(out.shape, out.dtype) if numb...  9.16 us
    ppermute x9, waiting for transfers between devices, swap_chip(): lax.ppermute(block, 'rep', [(i, i ^ 2 * step) for i in range(rep_count)])  8.64 us
    pallas_call x1, Pallas kernels, body(): pl.pallas_call(fetch_kernel, out_shape=[pltpu.VMEM(array.shape, array.dty...  3.32 us
    pallas_call x1, Pallas kernels, body(): pl.pallas_call(functools.partial(begin_kernel, capacity, padded), out_sha...  1.93 us
  transfers between devices with their start and end apart: 24, of which 9 were waited for; matrix products, arithmetic and copies ran while one was open for 0% of the time, Pallas kernels for 14%

profile of v9, /device:TPU:0, one launch (start us, length us, event | category | flops | bytes accessed | tf_op | source)
XLA Modules:
  0.0 77.6 jit_solution(5636438449249464647)
XLA Ops:
  0.6 0.5 collective-permute-start.1
  1.1 0.1 collective-permute-start
  1.2 1.9 %begin.1 = (bf16[4,32,2176]{2,1,0:T(8,128)(2,1)S(1)}, bf16[56,1024]{1,0:T(8,128)(2,1)S(1)}, bf16[56,1024]{1,0:T(8,128)(2,1)S(1)}, bf16[56,1024]{1,0:T(8,128)(2,1)S(1)}, bf16[56,1024]{1,0:T(8,128)(2,1)S(1)}) custom-call(s32[1,8,32]{2,1,0:T(8,128)} %refs_0_.3, bf16[128,3584]{1,0:T(8,128)(2,1)} %refs_1_.1, s32[1,128]{1,0:T(1,128)} %bitcast.12, ...), custom_call_target="tpu_custom_call" | custom-call | tf_op jit(solution)/shard_map/begin/pallas_call | solution.py:406
  3.2 0.3 collective-permute-done.refs_0_.refs_2_
  3.5 0.0 collective-permute-done.1.refs_1_.refs_3_
  3.5 0.4 serve_first.1
  3.9 2.9 %collective-permute-start.2 = (bf16[64,2176]{1,0:T(8,128)(2,1)S(1)}, bf16[64,2176]{1,0:T(8,128)(2,1)S(1)}, u32[]{:S(2)}, u32[]{:S(2)}) collective-permute-start(bf16[64,2176]{1,0:T(8,128)(2,1)S(1)} %get-tuple-element.96), channel_id=1, source_target_pairs={{0,8},{4,12},{8,0},{12,4},{16,24},{20,28},{24,16},{28,20},{1,9},{5... | collective-permute-start | bytes 835592 | tf_op jit(solution)/shard_map/ppermute | solution.py:103
  6.8 1.5 %collective-permute-start.3 = (bf16[64,2176]{1,0:T(8,128)(2,1)S(1)}, bf16[64,2176]{1,0:T(8,128)(2,1)S(1)}, u32[]{:S(2)}, u32[]{:S(2)}) collective-permute-start(bf16[64,2176]{1,0:T(8,128)(2,1)S(1)} %get-tuple-element.97), channel_id=1, source_target_pairs={{0,16},{4,20},{8,24},{12,28},{16,0},{20,4},{24,8},{28,12},{1,17},{... | collective-permute-start | bytes 835592 | tf_op jit(solution)/shard_map/ppermute | solution.py:103
  8.3 0.0 collective-permute-start.4
  8.4 3.0 %collective-permute-start.5 = (bf16[56,1024]{1,0:T(8,128)(2,1)S(1)}, bf16[56,1024]{1,0:T(8,128)(2,1)S(1)}, u32[]{:S(2)}, u32[]{:S(2)}) collective-permute-start(bf16[56,1024]{1,0:T(8,128)(2,1)S(1)} %get-tuple-element.99), channel_id=1, source_target_pairs={{0,2},{1,3},{2,0},{3,1},{4,6},{5,7},{6,4},{7,5},{8,10},{9,11},{10,... | collective-permute-start | bytes 344072 | tf_op jit(solution)/shard_map/ppermute | solution.py:86
  11.4 1.3 %collective-permute-start.6 = (bf16[56,1024]{1,0:T(8,128)(2,1)S(1)}, bf16[56,1024]{1,0:T(8,128)(2,1)S(1)}, u32[]{:S(2)}, u32[]{:S(2)}) collective-permute-start(bf16[56,1024]{1,0:T(8,128)(2,1)S(1)} %get-tuple-element.100), channel_id=1, source_target_pairs={{0,3},{1,2},{2,1},{3,0},{4,7},{5,6},{6,5},{7,4},{8,11},{9,10},{10,... | collective-permute-start | bytes 344072 | tf_op jit(solution)/shard_map/ppermute | solution.py:86
  12.8 1.5 %prepare.1 = (bf16[256,256]{1,0:T(8,128)(2,1)S(1)}, bf16[128,256]{1,0:T(8,128)(2,1)}) custom-call(s32[1,8]{1,0:T(1,128)S(1)} %copy-done.8, s32[1,128]{1,0:T(1,128)S(1)} %bitcast.13), custom_call_target="tpu_custom_call" | custom-call | flops 16777216 | bytes 55924 | tf_op jit(solution)/shard_map/prepare/pallas_call | solution.py:64
  14.3 1.2 %serve_last.1 = (bf16[64,1408]{1,0:T(8,128)(2,1)S(1)}, bf16[64,1408]{1,0:T(8,128)(2,1)S(1)}, bf16[64,1408]{1,0:T(8,128)(2,1)S(1)}, bf16[64,1408]{1,0:T(8,128)(2,1)S(1)}) custom-call(s32[1,8,32]{2,1,0:T(8,128)} %refs_0_.3, bf16[128,3584]{1,0:T(8,128)(2,1)S(1)} %copy-done, s32[1,8,32]{2,1,0:T(8,128)} %copy-done.5, ...), custom_call_target="tpu_custom_call" | custom-call | flops 92274688 | bytes 307582 | tf_op jit(solution)/shard_map/serve_last/pallas_call | solution.py:64
  15.5 4.7 %collective-permute-done.5.refs_4_ = bf16[56,1024]{1,0:T(8,128)(2,1)S(1)} collective-permute-done((bf16[56,1024]{1,0:T(8,128)(2,1)S(1)}, bf16[56,1024]{1,0:T(8,128)(2,1)S(1)}, u32[]{:S(2)}, u32[]{:S(2)}) %collective-permute-start.5) | collective-permute-done | bytes 114720 | tf_op jit(solution)/shard_map/ppermute | solution.py:86
  20.1 0.0 collective-permute-done.6.refs_5_
  20.1 0.0 collective-permute-done.2.refs_1_
  20.1 1.1 %collective-permute-done.3.refs_2_ = bf16[64,2176]{1,0:T(8,128)(2,1)S(1)} collective-permute-done((bf16[64,2176]{1,0:T(8,128)(2,1)S(1)}, bf16[64,2176]{1,0:T(8,128)(2,1)S(1)}, u32[]{:S(2)}, u32[]{:S(2)}) %collective-permute-start.3) | collective-permute-done | bytes 278560 | tf_op jit(solution)/shard_map/ppermute | solution.py:103
  21.2 0.0 collective-permute-done.4.refs_3_
  21.2 0.8 pick_first.1
  22.0 1.3 %collective-permute-start.7 = (bf16[64,1408]{1,0:T(8,128)(2,1)S(1)}, bf16[64,1408]{1,0:T(8,128)(2,1)S(1)}, u32[]{:S(2)}, u32[]{:S(2)}) collective-permute-start(bf16[64,1408]{1,0:T(8,128)(2,1)S(1)} %get-tuple-element.107), channel_id=1, source_target_pairs={{0,8},{4,12},{8,0},{12,4},{16,24},{20,28},{24,16},{28,20},{1,9},{5... | collective-permute-start | bytes 540680 | tf_op jit(solution)/shard_map/ppermute | solution.py:103
  23.3 3.1 %collective-permute-start.10 = (bf16[56,2176]{1,0:T(8,128)(2,1)S(1)}, bf16[56,2176]{1,0:T(8,128)(2,1)S(1)}, u32[]{:S(2)}, u32[]{:S(2)}) collective-permute-start(bf16[56,2176]{1,0:T(8,128)(2,1)S(1)} %get-tuple-element.116), channel_id=1, source_target_pairs={{0,2},{1,3},{2,0},{3,1},{4,6},{5,7},{6,4},{7,5},{8,10},{9,11},{10,... | collective-permute-start | bytes 731144 | tf_op jit(solution)/shard_map/ppermute | solution.py:86
  26.4 0.8 %collective-permute-start.11 = (bf16[56,2176]{1,0:T(8,128)(2,1)S(1)}, bf16[56,2176]{1,0:T(8,128)(2,1)S(1)}, u32[]{:S(2)}, u32[]{:S(2)}) collective-permute-start(bf16[56,2176]{1,0:T(8,128)(2,1)S(1)} %get-tuple-element.117), channel_id=1, source_target_pairs={{0,3},{1,2},{2,1},{3,0},{4,7},{5,6},{6,5},{7,4},{8,11},{9,10},{10,... | collective-permute-start | bytes 731144 | tf_op jit(solution)/shard_map/ppermute | solution.py:86
  27.2 0.2 collective-permute-start.12
  27.4 1.0 %collective-permute-start.8 = (bf16[64,1408]{1,0:T(8,128)(2,1)S(1)}, bf16[64,1408]{1,0:T(8,128)(2,1)S(1)}, u32[]{:S(2)}, u32[]{:S(2)}) collective-permute-start(bf16[64,1408]{1,0:T(8,128)(2,1)S(1)} %get-tuple-element.108), channel_id=1, source_target_pairs={{0,16},{4,20},{8,24},{12,28},{16,0},{20,4},{24,8},{28,12},{1,17},{... | collective-permute-start | bytes 540680 | tf_op jit(solution)/shard_map/ppermute | solution.py:103
  28.5 0.0 collective-permute-done.7.refs_2_
  28.5 1.2 %collective-permute-start.9 = (bf16[64,1408]{1,0:T(8,128)(2,1)S(1)}, bf16[64,1408]{1,0:T(8,128)(2,1)S(1)}, u32[]{:S(2)}, u32[]{:S(2)}) collective-permute-start(bf16[64,1408]{1,0:T(8,128)(2,1)S(1)} %get-tuple-element.109), channel_id=1, source_target_pairs={{0,24},{4,28},{8,16},{12,20},{16,8},{20,12},{24,0},{28,4},{1,25},{... | collective-permute-start | bytes 540680 | tf_op jit(solution)/shard_map/ppermute | solution.py:103
  29.7 6.9 %collective-permute-done.8.refs_3_ = bf16[64,1408]{1,0:T(8,128)(2,1)S(1)} collective-permute-done((bf16[64,1408]{1,0:T(8,128)(2,1)S(1)}, bf16[64,1408]{1,0:T(8,128)(2,1)S(1)}, u32[]{:S(2)}, u32[]{:S(2)}) %collective-permute-start.8) | collective-permute-done | bytes 180256 | tf_op jit(solution)/shard_map/ppermute | solution.py:103
  36.6 0.0 collective-permute-done.9.refs_4_
  36.6 0.4 pick_last.1
  37.0 1.7 %collective-permute-start.13 = (bf16[56,1408]{1,0:T(8,128)(2,1)S(1)}, bf16[56,1408]{1,0:T(8,128)(2,1)S(1)}, u32[]{:S(2)}, u32[]{:S(2)}) collective-permute-start(bf16[56,1408]{1,0:T(8,128)(2,1)S(1)} %get-tuple-element.124), channel_id=1, source_target_pairs={{0,1},{1,0},{2,3},{3,2},{4,5},{5,4},{6,7},{7,6},{8,9},{9,8},{10,11... | collective-permute-start | bytes 473096 | tf_op jit(solution)/shard_map/ppermute | solution.py:86
  38.7 0.4 collective-permute-start.14
  39.1 3.3 %fetch.1 = (bf16[1,3584,1024]{2,1,0:T(8,128)(2,1)S(1)}, bf16[1,3584,128]{2,1,0:T(8,128)(2,1)S(1)}, bf16[1,128,1024]{2,1,0:T(8,128)(2,1)S(1)}) custom-call(bf16[1,3584,1024]{2,1,0:T(8,128)(2,1)} %refs_0_.4, bf16[1,3584,128]{2,1,0:T(8,128)(2,1)} %refs_1_.2, bf16[1,128,1024]{2,1,0:T(8,128)(2,1)} %refs_2_), custom_call_target="tpu_custom_call" | custom-call | tf_op jit(solution)/shard_map/fetch/pallas_call | solution.py:480
  42.4 0.5 collective-permute-done.10.refs_2_
  42.9 3.1 %collective-permute-start.16 = (bf16[56,1408]{1,0:T(8,128)(2,1)S(1)}, bf16[56,1408]{1,0:T(8,128)(2,1)S(1)}, u32[]{:S(2)}, u32[]{:S(2)}) collective-permute-start(bf16[56,1408]{1,0:T(8,128)(2,1)S(1)} %get-tuple-element.134), channel_id=1, source_target_pairs={{0,2},{1,3},{2,0},{3,1},{4,6},{5,7},{6,4},{7,5},{8,10},{9,11},{10,... | collective-permute-start | bytes 473096 | tf_op jit(solution)/shard_map/ppermute | solution.py:86
  46.0 0.0 collective-permute-done.11.refs_3_
  46.0 0.5 collective-permute-start.17
  46.5 0.0 collective-permute-done.12.refs_5_
  46.5 1.7 %partial.1 = (bf16[2176,256]{1,0:T(8,128)(2,1)S(1)}, f32[256,1024]{1,0:T(8,128)S(1)}, f32[256,128]{1,0:T(8,128)S(1)}) custom-call(bf16[1,3584,1024]{2,1,0:T(8,128)(2,1)S(1)} %get-tuple-element.114.refs_0_.refs_2_.refs_7_, bf16[1,3584,128]{2,1,0:T(8,128)(2,1)S(1)} %get-tuple-element.115.refs_1_.refs_3_.refs_8_, ...), custom_call_target="tpu_custom_call" | custom-call | flops 1283457024 | bytes 4278190 | tf_op jit(solution)/shard_map/partial/pallas_call | solution.py:64
  48.2 2.7 %collective-permute-done.14.refs_8_ = bf16[56,1024]{1,0:T(8,128)(2,1)S(1)} collective-permute-done((bf16[56,1024]{1,0:T(8,128)(2,1)S(1)}, bf16[56,1024]{1,0:T(8,128)(2,1)S(1)}, u32[]{:S(2)}, u32[]{:S(2)}) %collective-permute-start.14) | collective-permute-done | bytes 114720 | tf_op jit(solution)/shard_map/ppermute | solution.py:86
  50.9 0.0 collective-permute-done.13.refs_6_
  51.0 0.0 copy-start.2
  51.0 1.0 %early.1 = (bf16[56,1024]{1,0:T(8,128)(2,1)S(1)}, bf16[56,1024]{1,0:T(8,128)(2,1)S(1)}, bf16[1408,128]{1,0:T(8,128)(2,1)S(1)}, bf16[128,128]{1,0:T(8,128)(2,1)S(...) custom-call(f32[256,1024]{1,0:T(8,128)S(1)} %get-tuple-element.120.refs_0_.refs_5_, ...), custom_call_target="tpu_custom_call" | custom-call | flops 415236096 | bytes 1384120 | tf_op jit(solution)/shard_map/early/pallas_call | solution.py:64
  52.0 6.3 %collective-permute-done.16.refs_10_ = bf16[56,1408]{1,0:T(8,128)(2,1)S(1)} collective-permute-done((bf16[56,1408]{1,0:T(8,128)(2,1)S(1)}, bf16[56,1408]{1,0:T(8,128)(2,1)S(1)}, u32[]{:S(2)}, u32[]{:S(2)}) %collective-permute-start.16) | collective-permute-done | bytes 157728 | tf_op jit(solution)/shard_map/ppermute | solution.py:86
  58.3 0.0 collective-permute-done.17.refs_11_
  58.3 0.0 copy-done.1
  58.3 1.9 %late.1 = (bf16[56,1024]{1,0:T(8,128)(2,1)S(1)}, bf16[56,1024]{1,0:T(8,128)(2,1)S(1)}, f32[4,576,128]{2,1,0:T(8,128)S(1)}, bf16[4,576,128]{2,1,0:T(8,128)(2,1)S(1)}) custom-call(bf16[2176,256]{1,0:T(8,128)(2,1)S(1)} %get-tuple-element.129.refs_0_, bf16[1408,128]{1,0:T(8,128)(2,1)S(1)} %get-tuple-element.130.refs_1_, ...), custom_call_target="tpu_custom_call" | custom-call | flops 884998144 | bytes 2949993 | tf_op jit(solution)/shard_map/late/pallas_call | solution.py:64
  60.3 0.1 collective-permute-start.20
  60.3 3.7 %collective-permute-start.15 = (bf16[56,1024]{1,0:T(8,128)(2,1)S(1)}, bf16[56,1024]{1,0:T(8,128)(2,1)S(1)}, u32[]{:S(2)}, u32[]{:S(2)}) collective-permute-start(bf16[56,1024]{1,0:T(8,128)(2,1)S(1)} %get-tuple-element.128), channel_id=1, source_target_pairs={{0,1},{1,0},{2,3},{3,2},{4,5},{5,4},{6,7},{7,6},{8,9},{9,8},{10,11... | collective-permute-start | bytes 344072 | tf_op jit(solution)/shard_map/ppermute | solution.py:86
  64.1 1.1 %collective-permute-start.18 = (bf16[56,1024]{1,0:T(8,128)(2,1)S(1)}, bf16[56,1024]{1,0:T(8,128)(2,1)S(1)}, u32[]{:S(2)}, u32[]{:S(2)}) collective-permute-start(bf16[56,1024]{1,0:T(8,128)(2,1)S(1)} %get-tuple-element.138), channel_id=1, source_target_pairs={{0,2},{1,3},{2,0},{3,1},{4,6},{5,7},{6,4},{7,5},{8,10},{9,11},{10,... | collective-permute-start | bytes 344072 | tf_op jit(solution)/shard_map/ppermute | solution.py:86
  65.1 1.4 %collective-permute-start.19 = (bf16[56,1024]{1,0:T(8,128)(2,1)S(1)}, bf16[56,1024]{1,0:T(8,128)(2,1)S(1)}, u32[]{:S(2)}, u32[]{:S(2)}) collective-permute-start(bf16[56,1024]{1,0:T(8,128)(2,1)S(1)} %get-tuple-element.139), channel_id=1, source_target_pairs={{0,3},{1,2},{2,1},{3,0},{4,7},{5,6},{6,5},{7,4},{8,11},{9,10},{10,... | collective-permute-start | bytes 344072 | tf_op jit(solution)/shard_map/ppermute | solution.py:86
  66.5 0.0 collective-permute-done.20
  66.5 0.2 fusion
  66.7 0.0 copy-start.4
  66.7 0.0 copy-start.6
  66.8 1.5 %collective-permute-start.21 = (bf16[576,128]{1,0:T(8,128)(2,1)S(1)}, bf16[576,128]{1,0:T(8,128)(2,1)S(1)}, u32[]{:S(2)}, u32[]{:S(2)}) collective-permute-start(bf16[576,128]{1,0:T(8,128)(2,1)S(1)} %get-tuple-element.149), channel_id=1, source_target_pairs={{0,24},{4,28},{8,16},{12,20},{16,8},{20,12},{24,0},{28,4},{1,25},{... | collective-permute-start | bytes 442376 | tf_op jit(solution)/shard_map/ppermute | solution.py:103
  68.3 0.6 collective-permute-start.22
  68.9 0.0 collective-permute-done.15.refs_3_
  68.9 1.5 %collective-permute-start.23 = (bf16[576,128]{1,0:T(8,128)(2,1)S(1)}, bf16[576,128]{1,0:T(8,128)(2,1)S(1)}, u32[]{:S(2)}, u32[]{:S(2)}) collective-permute-start(bf16[576,128]{1,0:T(8,128)(2,1)S(1)} %get-tuple-element.147), channel_id=1, source_target_pairs={{0,8},{4,12},{8,0},{12,4},{16,24},{20,28},{24,16},{28,20},{1,9},{5... | collective-permute-start | bytes 442376 | tf_op jit(solution)/shard_map/ppermute | solution.py:103
  70.4 5.5 %collective-permute-done.18.refs_4_ = bf16[56,1024]{1,0:T(8,128)(2,1)S(1)} collective-permute-done((bf16[56,1024]{1,0:T(8,128)(2,1)S(1)}, bf16[56,1024]{1,0:T(8,128)(2,1)S(1)}, u32[]{:S(2)}, u32[]{:S(2)}) %collective-permute-start.18) | collective-permute-done | bytes 114720 | tf_op jit(solution)/shard_map/ppermute | solution.py:86
  75.9 0.0 collective-permute-done.19.refs_5_
  75.9 0.0 collective-permute-done.21.refs_7_
  75.9 0.6 collective-permute-done.22.refs_8_
  76.5 0.0 collective-permute-done.23.refs_9_
  76.5 1.0 %end.1 = (f32[1,448,128]{2,1,0:T(8,128)}, f32[1,16,1024]{2,1,0:T(8,128)}, bf16[128,1024]{1,0:T(8,128)(2,1)}) custom-call(bf16[128,256]{1,0:T(8,128)(2,1)S(1)} %copy-done.4, f32[1,128]{1,0:T(1,128)S(1)} %bitcast.11, bf16[56,1024]{1,0:T(8,128)(2,1)S(1)} %get-tuple-element.127.refs_2_, bf16[56,1024]{1,0:T(8,128)(2,1)S(1)} %collective-permute-done.15.refs_3_, ...), custom_call_target="tpu_custom_call" | custom-call | flops 67108864 | bytes 223696 | tf_op jit(solution)/shard_map/end/pallas_call | solution.py:64
  (16 shorter events, 0.1 us)
Async XLA Ops:
  0.6 2.8 %collective-permute-start.1 = (bf16[128,3584]{1,0:T(8,128)(2,1)}, bf16[128,3584]{1,0:T(8,128)(2,1)S(1)}, u32[]{:S(2)}, u32[]{:S(2)}) collective-permute-start(bf16[128,3584]{1,0:T(8,128)(2,1)} %refs_1_.1), channel_id=1, source_target_pairs={{0,4},{4,0},{8,12},{12,8},{16,20},{20,16},{24,28},{28,24},{1,5},{5... | collective-permute-start | bytes 2752520 | tf_op jit(solution)/shard_map/ppermute | solution.py:97
  1.1 2.3 %collective-permute-start = (s32[1,8,32]{2,1,0:T(8,128)}, s32[1,8,32]{2,1,0:T(8,128)S(1)}, u32[]{:S(2)}, u32[]{:S(2)}) collective-permute-start(s32[1,8,32]{2,1,0:T(8,128)} %refs_0_.3), channel_id=1, source_target_pairs={{0,4},{4,0},{8,12},{12,8},{16,20},{20,16},{24,28},{28,24},{1,5},{5... | collective-permute-start | bytes 3080 | tf_op jit(solution)/shard_map/ppermute | solution.py:97
  1.2 11.5 %copy-start.7 = (s32[128,1]{0,1:T(1,128)S(1)}, s32[128,1]{0,1:T(1,128)}, u32[]{:S(2)}) copy-start(s32[128,1]{0,1:T(1,128)} %param.12) | copy-start | bytes 1540
  1.2 11.5 %copy-start.8 = (s32[1,8]{1,0:T(1,128)S(1)}, s32[1,8]{1,0:T(1,128)}, u32[]{:S(2)}) copy-start(s32[1,8]{1,0:T(1,128)} %refs_0_.2) | copy-start | bytes 100
  1.2 13.1 %copy-start = (bf16[128,3584]{1,0:T(8,128)(2,1)S(1)}, bf16[128,3584]{1,0:T(8,128)(2,1)}, u32[]{:S(2)}) copy-start(bf16[128,3584]{1,0:T(8,128)(2,1)} %refs_1_.1) | copy-start | bytes 2752516
  3.5 10.8 %copy-start.5 = (s32[1,8,32]{2,1,0:T(8,128)}, s32[1,8,32]{2,1,0:T(8,128)S(1)}, u32[]{:S(2)}) copy-start(s32[1,8,32]{2,1,0:T(8,128)S(1)} %collective-permute-done.refs_0_.refs_2_) | copy-start | bytes 3076
  3.9 16.3 %collective-permute-start.2 = (bf16[64,2176]{1,0:T(8,128)(2,1)S(1)}, bf16[64,2176]{1,0:T(8,128)(2,1)S(1)}, u32[]{:S(2)}, u32[]{:S(2)}) collective-permute-start(bf16[64,2176]{1,0:T(8,128)(2,1)S(1)} %get-tuple-element.96), channel_id=1, source_target_pairs={{0,8},{4,12},{8,0},{12,4},{16,24},{20,28},{24,16},{28,20},{1,9},{5... | collective-permute-start | bytes 835592 | tf_op jit(solution)/shard_map/ppermute | solution.py:103
  6.8 14.4 %collective-permute-start.3 = (bf16[64,2176]{1,0:T(8,128)(2,1)S(1)}, bf16[64,2176]{1,0:T(8,128)(2,1)S(1)}, u32[]{:S(2)}, u32[]{:S(2)}) collective-permute-start(bf16[64,2176]{1,0:T(8,128)(2,1)S(1)} %get-tuple-element.97), channel_id=1, source_target_pairs={{0,16},{4,20},{8,24},{12,28},{16,0},{20,4},{24,8},{28,12},{1,17},{... | collective-permute-start | bytes 835592 | tf_op jit(solution)/shard_map/ppermute | solution.py:103
  8.3 12.9 %collective-permute-start.4 = (bf16[64,2176]{1,0:T(8,128)(2,1)S(1)}, bf16[64,2176]{1,0:T(8,128)(2,1)S(1)}, u32[]{:S(2)}, u32[]{:S(2)}) collective-permute-start(bf16[64,2176]{1,0:T(8,128)(2,1)S(1)} %get-tuple-element.98), channel_id=1, source_target_pairs={{0,24},{4,28},{8,16},{12,20},{16,8},{20,12},{24,0},{28,4},{1,25},{... | collective-permute-start | bytes 835592 | tf_op jit(solution)/shard_map/ppermute | solution.py:103
  8.4 11.8 %collective-permute-start.5 = (bf16[56,1024]{1,0:T(8,128)(2,1)S(1)}, bf16[56,1024]{1,0:T(8,128)(2,1)S(1)}, u32[]{:S(2)}, u32[]{:S(2)}) collective-permute-start(bf16[56,1024]{1,0:T(8,128)(2,1)S(1)} %get-tuple-element.99), channel_id=1, source_target_pairs={{0,2},{1,3},{2,0},{3,1},{4,6},{5,7},{6,4},{7,5},{8,10},{9,11},{10,... | collective-permute-start | bytes 344072 | tf_op jit(solution)/shard_map/ppermute | solution.py:86
  11.4 8.7 %collective-permute-start.6 = (bf16[56,1024]{1,0:T(8,128)(2,1)S(1)}, bf16[56,1024]{1,0:T(8,128)(2,1)S(1)}, u32[]{:S(2)}, u32[]{:S(2)}) collective-permute-start(bf16[56,1024]{1,0:T(8,128)(2,1)S(1)} %get-tuple-element.100), channel_id=1, source_target_pairs={{0,3},{1,2},{2,1},{3,0},{4,7},{5,6},{6,5},{7,4},{8,11},{9,10},{10,... | collective-permute-start | bytes 344072 | tf_op jit(solution)/shard_map/ppermute | solution.py:86
  22.0 6.5 %collective-permute-start.7 = (bf16[64,1408]{1,0:T(8,128)(2,1)S(1)}, bf16[64,1408]{1,0:T(8,128)(2,1)S(1)}, u32[]{:S(2)}, u32[]{:S(2)}) collective-permute-start(bf16[64,1408]{1,0:T(8,128)(2,1)S(1)} %get-tuple-element.107), channel_id=1, source_target_pairs={{0,8},{4,12},{8,0},{12,4},{16,24},{20,28},{24,16},{28,20},{1,9},{5... | collective-permute-start | bytes 540680 | tf_op jit(solution)/shard_map/ppermute | solution.py:103
  23.3 19.7 %collective-permute-start.10 = (bf16[56,2176]{1,0:T(8,128)(2,1)S(1)}, bf16[56,2176]{1,0:T(8,128)(2,1)S(1)}, u32[]{:S(2)}, u32[]{:S(2)}) collective-permute-start(bf16[56,2176]{1,0:T(8,128)(2,1)S(1)} %get-tuple-element.116), channel_id=1, source_target_pairs={{0,2},{1,3},{2,0},{3,1},{4,6},{5,7},{6,4},{7,5},{8,10},{9,11},{10,... | collective-permute-start | bytes 731144 | tf_op jit(solution)/shard_map/ppermute | solution.py:86
  26.4 19.6 %collective-permute-start.11 = (bf16[56,2176]{1,0:T(8,128)(2,1)S(1)}, bf16[56,2176]{1,0:T(8,128)(2,1)S(1)}, u32[]{:S(2)}, u32[]{:S(2)}) collective-permute-start(bf16[56,2176]{1,0:T(8,128)(2,1)S(1)} %get-tuple-element.117), channel_id=1, source_target_pairs={{0,3},{1,2},{2,1},{3,0},{4,7},{5,6},{6,5},{7,4},{8,11},{9,10},{10,... | collective-permute-start | bytes 731144 | tf_op jit(solution)/shard_map/ppermute | solution.py:86
  27.2 19.3 %collective-permute-start.12 = (bf16[56,2176]{1,0:T(8,128)(2,1)S(1)}, bf16[56,2176]{1,0:T(8,128)(2,1)S(1)}, u32[]{:S(2)}, u32[]{:S(2)}) collective-permute-start(bf16[56,2176]{1,0:T(8,128)(2,1)S(1)} %get-tuple-element.119), channel_id=1, source_target_pairs={{0,1},{1,0},{2,3},{3,2},{4,5},{5,4},{6,7},{7,6},{8,9},{9,8},{10,11... | collective-permute-start | bytes 731144 | tf_op jit(solution)/shard_map/ppermute | solution.py:86
  27.4 9.2 %collective-permute-start.8 = (bf16[64,1408]{1,0:T(8,128)(2,1)S(1)}, bf16[64,1408]{1,0:T(8,128)(2,1)S(1)}, u32[]{:S(2)}, u32[]{:S(2)}) collective-permute-start(bf16[64,1408]{1,0:T(8,128)(2,1)S(1)} %get-tuple-element.108), channel_id=1, source_target_pairs={{0,16},{4,20},{8,24},{12,28},{16,0},{20,4},{24,8},{28,12},{1,17},{... | collective-permute-start | bytes 540680 | tf_op jit(solution)/shard_map/ppermute | solution.py:103
  28.5 8.2 %collective-permute-start.9 = (bf16[64,1408]{1,0:T(8,128)(2,1)S(1)}, bf16[64,1408]{1,0:T(8,128)(2,1)S(1)}, u32[]{:S(2)}, u32[]{:S(2)}) collective-permute-start(bf16[64,1408]{1,0:T(8,128)(2,1)S(1)} %get-tuple-element.109), channel_id=1, source_target_pairs={{0,24},{4,28},{8,16},{12,20},{16,8},{20,12},{24,0},{28,4},{1,25},{... | collective-permute-start | bytes 540680 | tf_op jit(solution)/shard_map/ppermute | solution.py:103
  37.0 13.9 %collective-permute-start.13 = (bf16[56,1408]{1,0:T(8,128)(2,1)S(1)}, bf16[56,1408]{1,0:T(8,128)(2,1)S(1)}, u32[]{:S(2)}, u32[]{:S(2)}) collective-permute-start(bf16[56,1408]{1,0:T(8,128)(2,1)S(1)} %get-tuple-element.124), channel_id=1, source_target_pairs={{0,1},{1,0},{2,3},{3,2},{4,5},{5,4},{6,7},{7,6},{8,9},{9,8},{10,11... | collective-permute-start | bytes 473096 | tf_op jit(solution)/shard_map/ppermute | solution.py:86
  38.7 12.2 %collective-permute-start.14 = (bf16[56,1024]{1,0:T(8,128)(2,1)S(1)}, bf16[56,1024]{1,0:T(8,128)(2,1)S(1)}, u32[]{:S(2)}, u32[]{:S(2)}) collective-permute-start(bf16[56,1024]{1,0:T(8,128)(2,1)S(1)} %get-tuple-element.126), channel_id=1, source_target_pairs={{0,1},{1,0},{2,3},{3,2},{4,5},{5,4},{6,7},{7,6},{8,9},{9,8},{10,11... | collective-permute-start | bytes 344072 | tf_op jit(solution)/shard_map/ppermute | solution.py:86
  42.9 15.4 %collective-permute-start.16 = (bf16[56,1408]{1,0:T(8,128)(2,1)S(1)}, bf16[56,1408]{1,0:T(8,128)(2,1)S(1)}, u32[]{:S(2)}, u32[]{:S(2)}) collective-permute-start(bf16[56,1408]{1,0:T(8,128)(2,1)S(1)} %get-tuple-element.134), channel_id=1, source_target_pairs={{0,2},{1,3},{2,0},{3,1},{4,6},{5,7},{6,4},{7,5},{8,10},{9,11},{10,... | collective-permute-start | bytes 473096 | tf_op jit(solution)/shard_map/ppermute | solution.py:86
  46.0 12.3 %collective-permute-start.17 = (bf16[56,1408]{1,0:T(8,128)(2,1)S(1)}, bf16[56,1408]{1,0:T(8,128)(2,1)S(1)}, u32[]{:S(2)}, u32[]{:S(2)}) collective-permute-start(bf16[56,1408]{1,0:T(8,128)(2,1)S(1)} %get-tuple-element.135), channel_id=1, source_target_pairs={{0,3},{1,2},{2,1},{3,0},{4,7},{5,6},{6,5},{7,4},{8,11},{9,10},{10,... | collective-permute-start | bytes 473096 | tf_op jit(solution)/shard_map/ppermute | solution.py:86
  46.5 4.4 %copy-start.3 = (bf16[56,1024]{1,0:T(8,128)(2,1)S(1)}, bf16[56,1024]{1,0:T(8,128)(2,1)}, u32[]{:S(2)}) copy-start(bf16[56,1024]{1,0:T(8,128)(2,1)} %get-tuple-element.125.refs_7_) | copy-start | bytes 344068
  51.0 7.3 %copy-start.1 = (bf16[56,1024]{1,0:T(8,128)(2,1)S(1)}, bf16[56,1024]{1,0:T(8,128)(2,1)}, u32[]{:S(2)}) copy-start(bf16[56,1024]{1,0:T(8,128)(2,1)} %get-tuple-element.136.refs_12_) | copy-start | bytes 344068
  51.0 7.3 %copy-start.2 = (bf16[56,1024]{1,0:T(8,128)(2,1)S(1)}, bf16[56,1024]{1,0:T(8,128)(2,1)}, u32[]{:S(2)}) copy-start(bf16[56,1024]{1,0:T(8,128)(2,1)} %get-tuple-element.137.refs_13_) | copy-start | bytes 344068
  60.3 6.3 %collective-permute-start.20 = (bf16[4,576,128]{2,1,0:T(8,128)(2,1)S(1)}, bf16[4,576,128]{2,1,0:T(8,128)(2,1)S(1)}, u32[]{:S(2)}, u32[]{:S(2)}) collective-permute-start(bf16[4,576,128]{2,1,0:T(8,128)(2,1)S(1)} %get-tuple-element.141), channel_id=1, source_target_pairs={{0,4},{4,0},{8,12},{12,8},{16,20},{20,16},{24,28},{28,24},{1,5},{5... | collective-permute-start | bytes 1769480 | tf_op jit(solution)/shard_map/ppermute | solution.py:97
  60.3 8.5 %collective-permute-start.15 = (bf16[56,1024]{1,0:T(8,128)(2,1)S(1)}, bf16[56,1024]{1,0:T(8,128)(2,1)S(1)}, u32[]{:S(2)}, u32[]{:S(2)}) collective-permute-start(bf16[56,1024]{1,0:T(8,128)(2,1)S(1)} %get-tuple-element.128), channel_id=1, source_target_pairs={{0,1},{1,0},{2,3},{3,2},{4,5},{5,4},{6,7},{7,6},{8,9},{9,8},{10,11... | collective-permute-start | bytes 344072 | tf_op jit(solution)/shard_map/ppermute | solution.py:86
  64.1 11.8 %collective-permute-start.18 = (bf16[56,1024]{1,0:T(8,128)(2,1)S(1)}, bf16[56,1024]{1,0:T(8,128)(2,1)S(1)}, u32[]{:S(2)}, u32[]{:S(2)}) collective-permute-start(bf16[56,1024]{1,0:T(8,128)(2,1)S(1)} %get-tuple-element.138), channel_id=1, source_target_pairs={{0,2},{1,3},{2,0},{3,1},{4,6},{5,7},{6,4},{7,5},{8,10},{9,11},{10,... | collective-permute-start | bytes 344072 | tf_op jit(solution)/shard_map/ppermute | solution.py:86
  65.1 10.8 %collective-permute-start.19 = (bf16[56,1024]{1,0:T(8,128)(2,1)S(1)}, bf16[56,1024]{1,0:T(8,128)(2,1)S(1)}, u32[]{:S(2)}, u32[]{:S(2)}) collective-permute-start(bf16[56,1024]{1,0:T(8,128)(2,1)S(1)} %get-tuple-element.139), channel_id=1, source_target_pairs={{0,3},{1,2},{2,1},{3,0},{4,7},{5,6},{6,5},{7,4},{8,11},{9,10},{10,... | collective-permute-start | bytes 344072 | tf_op jit(solution)/shard_map/ppermute | solution.py:86
  66.7 9.8 %copy-start.4 = (bf16[128,256]{1,0:T(8,128)(2,1)S(1)}, bf16[128,256]{1,0:T(8,128)(2,1)}, u32[]{:S(2)}) copy-start(bf16[128,256]{1,0:T(8,128)(2,1)} %get-tuple-element.86.refs_0_) | copy-start | bytes 196612
  66.7 9.8 %copy-start.6 = (f32[128,1]{0,1:T(1,128)S(1)}, f32[128,1]{0,1:T(1,128)}, u32[]{:S(2)}) copy-start(f32[128,1]{0,1:T(1,128)} %param.13) | copy-start | bytes 1540
  66.8 9.1 %collective-permute-start.21 = (bf16[576,128]{1,0:T(8,128)(2,1)S(1)}, bf16[576,128]{1,0:T(8,128)(2,1)S(1)}, u32[]{:S(2)}, u32[]{:S(2)}) collective-permute-start(bf16[576,128]{1,0:T(8,128)(2,1)S(1)} %get-tuple-element.149), channel_id=1, source_target_pairs={{0,24},{4,28},{8,16},{12,20},{16,8},{20,12},{24,0},{28,4},{1,25},{... | collective-permute-start | bytes 442376 | tf_op jit(solution)/shard_map/ppermute | solution.py:103
  68.3 8.2 %collective-permute-start.22 = (bf16[576,128]{1,0:T(8,128)(2,1)S(1)}, bf16[576,128]{1,0:T(8,128)(2,1)S(1)}, u32[]{:S(2)}, u32[]{:S(2)}) collective-permute-start(bf16[576,128]{1,0:T(8,128)(2,1)S(1)} %get-tuple-element.148), channel_id=1, source_target_pairs={{0,16},{4,20},{8,24},{12,28},{16,0},{20,4},{24,8},{28,12},{1,17},{... | collective-permute-start | bytes 442376 | tf_op jit(solution)/shard_map/ppermute | solution.py:103
  68.9 7.7 %collective-permute-start.23 = (bf16[576,128]{1,0:T(8,128)(2,1)S(1)}, bf16[576,128]{1,0:T(8,128)(2,1)S(1)}, u32[]{:S(2)}, u32[]{:S(2)}) collective-permute-start(bf16[576,128]{1,0:T(8,128)(2,1)S(1)} %get-tuple-element.147), channel_id=1, source_target_pairs={{0,8},{4,12},{8,0},{12,4},{16,24},{20,28},{24,16},{28,20},{1,9},{5... | collective-permute-start | bytes 442376 | tf_op jit(solution)/shard_map/ppermute | solution.py:103
